TPU v7x, 32 devices: a whole 2x2x4 slice. The times are simulated.
32 devices in a mesh: row: 4 (over y, core), sample: 8 (over z, x).
Axes of the slice: x: 2, y: 2, z: 4, core: 2. Of those that a mesh axis runs over, the one named last changes fastest.
Arguments:
- atom_feat: bfloat16 [16, 4608, 128], P('sample', 'row'), may hold values from -24 to 24
- atom_token: int32 [4608], P('row'), may hold values from 0 to 287, as said below
- pair_cond: bfloat16 [288, 288, 128], P('row', 'sample'), may hold values from -24 to 24
- token_mask: int32 [288], P('sample'), may hold values 0 or 1
- atom_wq: bfloat16 [128, 128], replicated, may hold values from -3 to 3
- atom_wk: bfloat16 [128, 128], replicated, may hold values from -3 to 3
- atom_wv: bfloat16 [128, 128], replicated, may hold values from -0.5 to 0.5
- atom_wo: bfloat16 [128, 128], replicated, may hold values from -0.5 to 0.5
- agg_weight: bfloat16 [128, 768], replicated, may hold values from -0.5 to 0.5
- pair_weight: bfloat16 [128, 16], replicated, may hold values from -64 to 64
- token_gain: float32 [768], replicated, may hold values from 0.5 to 1.5
- query_weight: bfloat16 [768, 768], replicated, may hold values from -0.21875 to 0.21875
- key_weight: bfloat16 [768, 768], replicated, may hold values from -0.21875 to 0.21875
- value_weight: bfloat16 [768, 768], replicated, may hold values from -0.21875 to 0.21875
- gate_weight: bfloat16 [768, 768], replicated, may hold values from -0.21875 to 0.21875
- out_weight: bfloat16 [768, 768], replicated, may hold values from -0.21875 to 0.21875
Outputs:
- token_out: bfloat16 [16, 288, 768], P('sample', 'row')
Inputs may be any that keep to these rules, and one draw needn't show every extreme that they name: atom_token never falls along the atoms; atoms 1152 r to 1152 (r + 1) - 1 belong to tokens 72 r to 72 (r + 1) - 1, and every token has at least one atom.
All inputs are finite; a program needn't handle non-finite values. No bound on the sum of `token_mask` on one device may be relied on, other than what follows from the above.
Results may differ from a plain program's by a relative error of at most 0.008.
The roundings to bfloat16 on the way count: a program that leaves them out, or rounds other values in their place, can miss the bound.
Values may be sent and summed in bfloat16 or wider, within the bound.
No kernel may reach another device: no remote copies, remote signals or barrier semaphores. Data moves between devices by JAX's collectives and lax.ppermute only.
A program may use at most 128 MiB of HBM per device.

v0:
```python
import jax
import jax.numpy as jnp
from jax import lax
from jax.sharding import PartitionSpec as P

HEADS = 16
HEAD_DIM = 48
AHEADS = 4
AHEAD_DIM = 32
QWIN = 32
KWIN = 128


def with_halo(shard, sides, width):
    for axis, dim in sides:
        devices, length = (lax.axis_size(axis), shard.shape[dim])
        up = [(i, (i + 1) % devices) for i in range(devices - 1)]
        down = [(j, i) for i, j in up]
        last = lax.slice_in_dim(shard, length - width, length, axis=dim)
        leading = lax.slice_in_dim(shard, 0, width, axis=dim)
        before = lax.ppermute(last, axis, up)
        after = lax.ppermute(leading, axis, down)
        shard = jnp.concatenate([before, shard, after], axis=dim)
    return shard


def layer_norm(x):
    mean = jnp.mean(x, -1, keepdims=True)
    centre = x - mean
    var = jnp.mean(centre * centre, -1, keepdims=True)
    return centre * lax.rsqrt(var + 1e-05)


def shards(
    atom_feat,
    atom_token,
    pair_cond,
    token_mask,
    atom_wq,
    atom_wk,
    atom_wv,
    atom_wo,
    agg_weight,
    pair_weight,
    token_gain,
    query_weight,
    key_weight,
    value_weight,
    gate_weight,
    out_weight,
):
    samples, atoms, chans = atom_feat.shape
    rim = (KWIN - QWIN) // 2
    windows = atoms // QWIN
    row_rank = lax.axis_index("row")
    all_atoms = atoms * lax.axis_size("row")
    normed = layer_norm(atom_feat.astype(jnp.float32)).astype(jnp.bfloat16)
    query = jnp.dot(normed, atom_wq, preferred_element_type=jnp.float32).astype(jnp.bfloat16)
    padded = with_halo(normed, (("row", 1),), rim)
    keys_pad = jnp.dot(padded, atom_wk, preferred_element_type=jnp.float32).astype(jnp.bfloat16)
    vals_pad = jnp.dot(padded, atom_wv, preferred_element_type=jnp.float32).astype(jnp.bfloat16)
    keys_pad = keys_pad.reshape(samples, windows + 3, QWIN, chans)
    vals_pad = vals_pad.reshape(samples, windows + 3, QWIN, chans)
    akeys = jnp.concatenate([keys_pad[:, k : k + windows] for k in range(4)], axis=2).reshape(
        samples, windows, KWIN, AHEADS, AHEAD_DIM
    )
    avals = jnp.concatenate([vals_pad[:, k : k + windows] for k in range(4)], axis=2).reshape(
        samples, windows, KWIN, AHEADS, AHEAD_DIM
    )
    aquery = query.reshape(samples, windows, QWIN, AHEADS, AHEAD_DIM)
    wid = jnp.arange(windows, dtype=jnp.int32)
    tid = jnp.arange(KWIN, dtype=jnp.int32)
    gidx = row_rank * atoms - rim + wid[:, None] * QWIN + tid[None, :]
    valid = (gidx >= 0) & (gidx < all_atoms)
    ascores = jnp.einsum(
        "swqhd,swkhd->swhqk", aquery, akeys, preferred_element_type=jnp.float32
    ) * (1.0 / AHEAD_DIM**0.5)
    ascores = jnp.where(valid[None, :, None, None, :], ascores, -jnp.inf)
    aexp = jnp.exp(ascores - jnp.max(ascores, -1, keepdims=True))
    atotal = jnp.sum(aexp, -1)
    amix = (
        jnp.einsum(
            "swhqk,swkhd->swhqd",
            aexp.astype(jnp.bfloat16),
            avals,
            preferred_element_type=jnp.float32,
        )
        / atotal[..., None]
    )
    amix = jnp.transpose(amix, (0, 1, 3, 2, 4)).reshape(samples, atoms, chans).astype(jnp.bfloat16)
    atom_out = (
        atom_feat.astype(jnp.float32) + jnp.dot(amix, atom_wo, preferred_element_type=jnp.float32)
    ).astype(jnp.bfloat16)
    hidden = jax.nn.relu(jnp.dot(atom_out, agg_weight, preferred_element_type=jnp.float32)).astype(
        jnp.bfloat16
    )
    rows_here, cols_here = (pair_cond.shape[0], pair_cond.shape[1])
    local_token = atom_token - row_rank * rows_here
    onehot = local_token[None, :] == jnp.arange(rows_here, dtype=jnp.int32)[:, None]
    counts = jnp.sum(onehot.astype(jnp.float32), 1)
    token_sum = jnp.einsum(
        "ta,sad->std", onehot.astype(jnp.bfloat16), hidden, preferred_element_type=jnp.float32
    )
    token_in = token_sum / counts[None, :, None]
    pnorm = layer_norm(pair_cond.astype(jnp.float32)).astype(jnp.bfloat16)
    bias_raw = jnp.dot(pnorm, pair_weight, preferred_element_type=jnp.float32)
    qidx = row_rank * rows_here + jnp.arange(rows_here, dtype=jnp.int32)
    kidx = lax.axis_index("sample") * cols_here + jnp.arange(cols_here, dtype=jnp.int32)
    allowed = (token_mask[None, :] == 1) | (qidx[:, None] == kidx[None, :])
    bias_part = jnp.transpose(
        jnp.where(allowed[:, :, None], bias_raw, -30000.0).astype(jnp.bfloat16), (2, 0, 1)
    )
    bias_rows = lax.all_gather(bias_part, "sample", axis=2, tiled=True)
    tnorm = (layer_norm(token_in) * token_gain).astype(jnp.bfloat16)
    tquery = (
        jnp.dot(tnorm, query_weight, preferred_element_type=jnp.float32)
        .astype(jnp.bfloat16)
        .reshape(samples, rows_here, HEADS, HEAD_DIM)
    )
    gate = jnp.dot(tnorm, gate_weight, preferred_element_type=jnp.float32)
    tscale = 1.0 / HEAD_DIM**0.5
    tkeys = jnp.dot(tnorm, key_weight, preferred_element_type=jnp.float32).astype(jnp.bfloat16)
    tvals = jnp.dot(tnorm, value_weight, preferred_element_type=jnp.float32).astype(jnp.bfloat16)
    attend_tkeys = lax.all_gather(tkeys, "row", axis=1, tiled=True)
    attend_tvals = lax.all_gather(tvals, "row", axis=1, tiled=True)
    running = jnp.full((samples, HEADS, rows_here), -jnp.inf, jnp.float32)
    total = jnp.zeros((samples, HEADS, rows_here), jnp.float32)
    accum = jnp.zeros((samples, HEADS, rows_here, HEAD_DIM), jnp.float32)
    count = attend_tkeys.shape[1]
    attend_tkeys = attend_tkeys.reshape(samples, count, HEADS, HEAD_DIM)
    attend_tvals = attend_tvals.reshape(samples, count, HEADS, HEAD_DIM)
    tbias = bias_rows.astype(jnp.float32)
    scores = (
        jnp.einsum("sqhd,skhd->shqk", tquery, attend_tkeys, preferred_element_type=jnp.float32)
        * tscale
        + tbias[None]
    )
    newmax = jnp.max(scores, -1)
    expd = jnp.exp(scores - newmax[..., None])
    factor = jnp.exp(running - newmax)
    total = total * factor + jnp.sum(expd, -1)
    accum = accum * factor[..., None] + jnp.einsum(
        "shqk,skhd->shqd",
        expd.astype(jnp.bfloat16),
        attend_tvals,
        preferred_element_type=jnp.float32,
    )
    tmix = accum / total[..., None]
    tmix = jnp.transpose(tmix, (0, 2, 1, 3)).reshape(samples, rows_here, HEADS * HEAD_DIM)
    gated = (tmix * jax.nn.sigmoid(gate)).astype(jnp.bfloat16)
    return (token_in + jnp.dot(gated, out_weight, preferred_element_type=jnp.float32)).astype(
        jnp.bfloat16
    )


def solution(mesh):
    placed = (
        P("sample", "row", None),
        P("row"),
        P("row", "sample", None),
        P("sample"),
        P(),
        P(),
        P(),
        P(),
        P(),
        P(),
        P(),
        P(),
        P(),
        P(),
        P(),
        P(),
    )
    return jax.shard_map(
        shards, mesh=mesh, in_specs=placed, out_specs=P("sample", "row", None), check_vma=False
    )
```

profile of v0, /device:TPU:0, one launch (start us, length us, event | category | flops | bytes accessed | tf_op | source)
XLA Modules:
  0.0 135.8 jit_solution(18014147891767708026)
XLA Ops:
  0.0 1.4 %convert_reduce_fusion = f32[2,1152]{1,0:T(2,128)S(1)} fusion(bf16[2,1152,128]{2,1,0:T(8,128)(2,1)} %param.16), kind=kLoop, calls=%fused_computation.33 | loop fusion | flops 587520 | bytes 599040 | tf_op jit(solution)/shard_map/reduce_sum | solution.py:28
  1.5 1.8 %fusion.44 = f32[2,1152]{1,0:T(2,128)S(1)} fusion(bf16[2,1152,128]{2,1,0:T(8,128)(2,1)} %param.16, f32[2,1152]{1,0:T(2,128)S(1)} %broadcast_multiply_fusion.1), kind=kLoop, calls=%fused_computation.57 | loop fusion | flops 1177344 | bytes 608256 | tf_op jit(solution)/shard_map/reduce_sum | solution.py:30
  3.3 1.8 %fusion.45 = bf16[2,1152,128]{2,1,0:T(8,128)(2,1)S(1)} fusion(bf16[2,1152,128]{2,1,0:T(8,128)(2,1)} %param.16, f32[2,1152]{1,0:T(2,128)S(1)} %add_rsqrt_fusion.1, f32[2,1152]{1,0:T(2,128)S(1)} %broadcast_multiply_fusion.1), kind=kLoop, calls=%fused_computation.58 | loop fusion | flops 1179648 | bytes 1198080 | tf_op jit(solution)/shard_map/convert_element_type | solution.py:57
  5.7 3.0 %collective-permute-start = (bf16[2,48,128]{2,1,0:T(8,128)(2,1)}, bf16[2,48,128]{2,1,0:T(8,128)(2,1)}, u32[]{:S(2)}, u32[]{:S(2)}) collective-permute-start(bf16[2,48,128]{2,1,0:T(8,128)(2,1)} %get-tuple-element.13), channel_id=1, source_target_pairs={{0,8},{8,16},{16,24},{1,9},{9,17},{17,25},{2,10},{10,18},{18,26},{... | collective-permute-start | bytes 73736 | tf_op jit(solution)/shard_map/ppermute | solution.py:21
  8.6 1.3 collective-permute-start.1
  11.9 1.1 fusion.54
  13.1 35.5 %all_gather.10 = bf16[16,72,288]{1,0,2:T(8,128)(2,1)S(1)} all-gather(bf16[16,72,36]{1,0,2:T(8,128)(2,1)S(1)} %fusion.54), channel_id=1, replica_groups=mesh['row'=4,'sample'=8] {'sample'}, dimensions={2}, use_global_device_ids=true | all-gather | bytes 746496 | tf_op jit(solution)/shard_map/all_gather | solution.py:113
  49.2 2.0 %reshape.158 = bf16[2,36,32,4,32]{4,3,2,1,0:T(4,128)(2,1)} reshape(bf16[2,1152,128]{2,1,0:T(8,128)(2,1)S(1)} %convolution_convert_fusion.2) | data formatting | bytes 1179648 | tf_op jit(solution)/shard_map/reshape | solution.py:70
  51.2 1.7 %copy.49 = bf16[16,72,288]{2,1,0:T(8,128)(2,1)} copy(bf16[16,72,288]{1,0,2:T(8,128)(2,1)S(1)} %all_gather.10) | data formatting | bytes 1327104 | tf_op jit(solution)/shard_map/all_gather | solution.py:113
  52.9 1.3 convert_element_type.90
  55.7 1.7 %pad_maximum_fusion = bf16[2,36,128,128]{3,2,1,0:T(8,128)(2,1)} fusion(bf16[2,36,32,128]{3,2,1,0:T(8,128)(2,1)S(1)} %get-tuple-element.10, bf16[2,36,32,128]{3,2,1,0:T(8,128)(2,1)S(1)} %get-tuple-element.11, bf16[2,36,32,128]{3,2,1,0:T(8,128)(2,1)S(1)} %get-tuple-element.12, bf16[2,36,32,128]{3,2,1,0:T(8,128)(2,1)S(1)} %get-tuple-element.9), kind=kLoop, calls=%fused_computation.19 | loop fusion | flops 9437184 | bytes 4718592 | tf_op jit(solution)/shard_map/concatenate | solution.py:64
  57.4 4.3 %copy.43 = bf16[2,36,128,128]{2,3,1,0:T(8,128)(2,1)} copy(bf16[2,36,128,128]{3,2,1,0:T(8,128)(2,1)} %pad_maximum_fusion) | data formatting | bytes 4718592 | tf_op jit(solution)/shard_map/concatenate | solution.py:64
  63.2 1.8 %pad_maximum_fusion.1 = bf16[2,36,128,128]{3,2,1,0:T(8,128)(2,1)} fusion(bf16[2,36,32,128]{3,2,1,0:T(8,128)(2,1)S(1)} %get-tuple-element.6, bf16[2,36,32,128]{3,2,1,0:T(8,128)(2,1)S(1)} %get-tuple-element.7, bf16[2,36,32,128]{3,2,1,0:T(8,128)(2,1)S(1)} %get-tuple-element.8, bf16[2,36,32,128]{3,2,1,0:T(8,128)(2,1)S(1)} %get-tuple-element.5), kind=kLoop, calls=%fused_computation.20 | loop fusion | flops 9437184 | bytes 4718592 | tf_op jit(solution)/shard_map/concatenate | solution.py:67
  64.9 4.3 %copy.45 = bf16[2,36,128,128]{2,3,1,0:T(8,128)(2,1)} copy(bf16[2,36,128,128]{3,2,1,0:T(8,128)(2,1)} %pad_maximum_fusion.1) | data formatting | bytes 4718592 | tf_op jit(solution)/shard_map/concatenate | solution.py:67
  69.2 3.9 %fusion.1 = (f32[2,36,4,32]{3,2,1,0:T(4,128)S(1)}, f32[2,36,4,32,128]{4,3,2,1,0:T(8,128)S(1)}) fusion(pred[36,128]{1,0:T(8,128)(4,1)S(1)} %fusion.73, bf16[2,36,128,4,32]{2,4,3,1,0:T(8,128)(2,1)} %bitcast.80, bf16[2,36,32,4,32]{4,3,2,1,0:T(4,128)(2,1)} %reshape.158), kind=kOutput, calls=%fused_computation.5 | convolution fusion | flops 79027200 | bytes 7709184 | tf_op jit(solution)/shard_map/swqhd,swkhd->swhqk/dot_general | solution.py:75
  73.2 2.9 %fusion.2 = f32[2,36,4,32]{3,2,1,0:T(4,128)S(1)} fusion(f32[2,36,4,32,128]{4,3,2,1,0:T(8,128)S(1)} %get-tuple-element.16, f32[2,36,4,32]{3,2,1,0:T(4,128)S(1)} %get-tuple-element.15, pred[36,128]{1,0:T(8,128)(4,1)S(1)} %fusion.73), kind=kLoop, calls=%fused_computation.6 | loop fusion | flops 4709376 | bytes 4796928 | tf_op jit(solution)/shard_map/reduce_sum | solution.py:80
  76.0 3.2 %fusion = bf16[2,36,32,4,32]{4,2,3,1,0:T(8,128)(2,1)S(1)} fusion(f32[2,36,32,4]{2,3,1,0:T(4,128)S(1)} %bitcast.88, bf16[2,36,128,4,32]{2,4,3,1,0:T(8,128)(2,1)S(1)} %bitcast.84, f32[2,36,4,32,128]{4,3,2,1,0:T(8,128)S(1)} %get-tuple-element.16, f32[2,36,4,32]{3,2,1,0:T(4,128)S(1)} %get-tuple-element.15, pred[36,128]{1,0:T(8,128)(4,1)S(1)} %fusion.73), kind=kOutput, calls=%fused_computation.2 | convolution fusion | flops 80805888 | bytes 7746048 | tf_op jit(solution)/shard_map/swhqk,swkhd->swhqd/dot_general | solution.py:82
  79.3 2.6 %copy.46 = bf16[2,36,32,4,32]{4,3,2,1,0:T(4,128)(2,1)} copy(bf16[2,36,32,4,32]{4,2,3,1,0:T(8,128)(2,1)S(1)} %fusion) | data formatting | bytes 1179648 | tf_op jit(solution)/shard_map/convert_element_type | solution.py:90
  81.9 4.1 %convert_element_type.79 = bf16[2,1152,128]{2,1,0:T(8,128)(2,1)} reshape(bf16[2,36,32,4,32]{4,3,2,1,0:T(4,128)(2,1)} %copy.46) | data formatting | bytes 1179648 | tf_op jit(solution)/shard_map/convert_element_type | solution.py:90
  86.0 2.2 %fusion.7 = bf16[2,1152,128]{2,1,0:T(8,128)(2,1)} fusion(bf16[2,1152,128]{2,1,0:T(8,128)(2,1)} %convert_element_type.79, bf16[2,1152,128]{2,1,0:T(8,128)(2,1)S(1)} %copy-done.2, bf16[128,128]{1,0:T(8,128)(2,1)} %param.23), kind=kOutput, calls=%fused_computation.14 | convolution fusion | flops 76382208 | bytes 1802240 | tf_op jit(solution)/shard_map/dot_general | solution.py:92
  88.2 3.4 %fusion.85 = (f32[2,72]{1,0:T(2,128)S(1)}, f32[2,72,768]{2,1,0:T(8,128)S(1)}) fusion(f32[72]{0:T(128)S(1)} %copy-done.9, s32[1152]{0:T(1024)S(1)} %broadcast_subtract_fusion, bf16[2,1152,128]{2,1,0:T(8,128)(2,1)} %fusion.7, bf16[128,768]{1,0:T(8,128)(2,1)} %param.24), kind=kOutput, calls=%fused_computation.112 | convolution fusion | flops 711631744 | bytes 1234272 | tf_op jit(solution)/shard_map/ta,sad->std/dot_general | solution.py:101
  92.3 11.3 %all_gather.9 = bf16[2,288,768]{2,1,0:T(8,128)(2,1)} all-gather(bf16[2,72,768]{2,1,0:T(8,128)(2,1)S(1)} %convolution_convert_fusion.4), channel_id=1, replica_groups=mesh['row'=4,'sample'=8] {'row'}, dimensions={1}, use_global_device_ids=true | all-gather | bytes 1105920 | tf_op jit(solution)/shard_map/all_gather | solution.py:124
  103.6 2.3 %copy.48 = bf16[2,288,768]{1,2,0:T(8,128)(2,1)} copy(bf16[2,288,768]{2,1,0:T(8,128)(2,1)} %all_gather.9) | data formatting | bytes 1769472 | tf_op jit(solution)/shard_map/all_gather | solution.py:124
  105.9 2.4 %convolution_convert_fusion.5 = bf16[2,72,768]{2,1,0:T(8,128)(2,1)} fusion(bf16[768,768]{1,0:T(8,128)(2,1)} %param.27, f32[2,72,768]{2,1,0:T(8,128)S(1)} %get-tuple-element.18, f32[768]{0:T(1024)S(1)} %copy-done.6, f32[2,72]{1,0:T(2,128)S(1)} %add_rsqrt_fusion.2, f32[2,72]{1,0:T(2,128)S(1)} %broadcast_multiply_fusion.2), kind=kOutput, calls=%fused_computation.56 | convolution fusion | flops 170422272 | bytes 1847424 | tf_op jit(solution)/shard_map/dot_general | solution.py:116
  108.3 1.9 %copy.47 = bf16[2,72,768]{1,2,0:T(8,128)(2,1)} copy(bf16[2,72,768]{2,1,0:T(8,128)(2,1)} %convolution_convert_fusion.5) | data formatting | bytes 442368 | tf_op jit(solution)/shard_map/convert_element_type | solution.py:117
  110.1 2.3 %fusion.4 = (f32[2,16,72]{2,1,0:T(8,128)S(1)}, f32[2,16,72,288]{3,2,1,0:T(8,128)S(1)}) fusion(f32[16,72,288]{2,1,0:T(8,128)S(1)} %convert_element_type.90, bf16[2,72,16,48]{1,3,2,0:T(8,128)(2,1)} %bitcast.85, bf16[2,288,16,48]{1,3,2,0:T(8,128)(2,1)} %bitcast.83), kind=kOutput, calls=%fused_computation.10 | convolution fusion | flops 65689344 | bytes 5096448 | tf_op jit(solution)/shard_map/sqhd,skhd->shqk/dot_general | solution.py:134
  112.5 1.4 fusion.5
  115.1 9.7 %all_gather.11 = bf16[2,288,768]{2,1,0:T(8,128)(2,1)} all-gather(bf16[2,72,768]{2,1,0:T(8,128)(2,1)S(1)} %convolution_convert_fusion.3), channel_id=1, replica_groups=mesh['row'=4,'sample'=8] {'row'}, dimensions={1}, use_global_device_ids=true | all-gather | bytes 1105920 | tf_op jit(solution)/shard_map/all_gather | solution.py:125
  124.8 2.3 %copy.50 = bf16[2,288,768]{1,2,0:T(8,128)(2,1)} copy(bf16[2,288,768]{2,1,0:T(8,128)(2,1)} %all_gather.11) | data formatting | bytes 1769472 | tf_op jit(solution)/shard_map/all_gather | solution.py:125
  127.1 4.2 %fusion.55 = f32[2,72,16,48]{1,3,2,0:T(8,128)} fusion(bf16[2,288,16,48]{1,3,2,0:T(8,128)(2,1)} %bitcast.86, f32[2,16,72,288]{3,2,1,0:T(8,128)} %copy-done.1, f32[2,16,72]{2,1,0:T(8,128)S(1)} %get-tuple-element.19, f32[16,72,288]{2,1,0:T(8,128)S(1)} %convert_element_type.90, f32[2,72,16]{1,2,0:T(8,128)S(1)} %bitcast_add_fusion, ...), kind=kOutput, calls=%fused_computation.67 | convolution fusion | flops 66576384 | bytes 5336064 | tf_op jit(solution)/shard_map/shqk,skhd->shqd/dot_general | solution.py:142
  131.3 1.4 %copy.51 = f32[2,72,768]{2,1,0:T(8,128)S(1)} copy(f32[2,72,768]{1,2,0:T(8,128)} %bitcast.87) | data formatting | bytes 884736 | tf_op jit(solution)/shard_map/reshape | solution.py:149
  132.7 3.0 %fusion.42 = bf16[2,72,768]{2,1,0:T(8,128)(2,1)} fusion(f32[2,72,768]{2,1,0:T(8,128)S(1)} %get-tuple-element.18, bf16[768,768]{1,0:T(8,128)(2,1)} %param.31, f32[2,72,768]{2,1,0:T(8,128)S(1)} %copy.51, bf16[768,768]{1,0:T(8,128)(2,1)} %param.30, f32[768]{0:T(1024)S(1)} %copy-done.6, f32[2,72]{1,0:T(2,128)S(1)} %add_rsqrt_fusion.2, ...), kind=kOutput, calls=%fused_computation.52 | convolution fusion | flops 340955136 | bytes 3469440 | tf_op jit(solution)/shard_map/dot_general | solution.py:151
  (55 shorter events, 8.0 us)
Async XLA Ops:
  0.0 91.9 %copy-start = (bf16[768,768]{1,0:T(8,128)(2,1)S(1)}, bf16[768,768]{1,0:T(8,128)(2,1)}, u32[]{:S(2)}) copy-start(bf16[768,768]{1,0:T(8,128)(2,1)} %param.28) | copy-start | bytes 3538948
  0.0 9.9 %copy-start.7 = (bf16[128,128]{1,0:T(8,128)(2,1)S(1)}, bf16[128,128]{1,0:T(8,128)(2,1)}, u32[]{:S(2)}) copy-start(bf16[128,128]{1,0:T(8,128)(2,1)} %param.20) | copy-start | bytes 98308
  0.0 10.3 %copy-start.8 = (s32[1152]{0:T(1024)S(1)}, s32[1152]{0:T(1024)}, u32[]{:S(2)}) copy-start(s32[1152]{0:T(1024)} %param.17) | copy-start | bytes 13828
  0.0 10.4 %copy-start.12 = (s32[36]{0:T(128)S(1)}, s32[36]{0:T(128)}, u32[]{:S(2)}) copy-start(s32[36]{0:T(128)} %param.19) | copy-start | bytes 436
  0.0 10.4 %copy-start.3 = (bf16[72,36,128]{2,0,1:T(8,128)(2,1)S(1)}, bf16[72,36,128]{2,0,1:T(8,128)(2,1)}, u32[]{:S(2)}) copy-start(bf16[72,36,128]{2,0,1:T(8,128)(2,1)} %param.18) | copy-start | bytes 1990660
  1.5 10.5 %copy-start.11 = (bf16[128,16]{0,1:T(8,128)(2,1)S(1)}, bf16[128,16]{0,1:T(8,128)(2,1)}, u32[]{:S(2)}) copy-start(bf16[128,16]{0,1:T(8,128)(2,1)} %param.25) | copy-start | bytes 12292
  5.7 48.5 %collective-permute-start = (bf16[2,48,128]{2,1,0:T(8,128)(2,1)}, bf16[2,48,128]{2,1,0:T(8,128)(2,1)}, u32[]{:S(2)}, u32[]{:S(2)}) collective-permute-start(bf16[2,48,128]{2,1,0:T(8,128)(2,1)} %get-tuple-element.13), channel_id=1, source_target_pairs={{0,8},{8,16},{16,24},{1,9},{9,17},{17,25},{2,10},{10,18},{18,26},{... | collective-permute-start | bytes 73736 | tf_op jit(solution)/shard_map/ppermute | solution.py:21
  8.6 45.6 %collective-permute-start.1 = (bf16[2,48,128]{2,1,0:T(8,128)(2,1)}, bf16[2,48,128]{2,1,0:T(8,128)(2,1)}, u32[]{:S(2)}, u32[]{:S(2)}) collective-permute-start(bf16[2,48,128]{2,1,0:T(8,128)(2,1)} %get-tuple-element.14), channel_id=1, source_target_pairs={{8,0},{16,8},{24,16},{9,1},{17,9},{25,17},{10,2},{18,10},{26,18},{... | collective-permute-start | bytes 73736 | tf_op jit(solution)/shard_map/ppermute | solution.py:22
  52.9 1.3 copy-start.10
  73.1 2.9 %copy-start.4 = (bf16[2,36,128,128]{2,3,1,0:T(8,128)(2,1)S(1)}, bf16[2,36,128,128]{2,3,1,0:T(8,128)(2,1)}, u32[]{:S(2)}) copy-start(bf16[2,36,128,128]{2,3,1,0:T(8,128)(2,1)} %copy.45) | copy-start | bytes 7077892
  81.9 4.1 %copy-start.2 = (bf16[2,1152,128]{2,1,0:T(8,128)(2,1)S(1)}, bf16[2,1152,128]{2,1,0:T(8,128)(2,1)}, u32[]{:S(2)}) copy-start(bf16[2,1152,128]{2,1,0:T(8,128)(2,1)} %param.16) | copy-start | bytes 1769476
  81.9 6.3 %copy-start.9 = (f32[72]{0:T(128)S(1)}, f32[72]{0:T(128)}, u32[]{:S(2)}) copy-start(f32[72]{0:T(128)} %convert_reduce_fusion.2) | copy-start | bytes 868
  88.2 3.7 %copy-start.6 = (f32[768]{0:T(1024)S(1)}, f32[768]{0:T(1024)}, u32[]{:S(2)}) copy-start(f32[768]{0:T(1024)} %param.26) | copy-start | bytes 9220
  112.5 1.8 %copy-start.1 = (f32[2,16,72,288]{3,2,1,0:T(8,128)}, f32[2,16,72,288]{3,2,1,0:T(8,128)S(1)}, u32[]{:S(2)}) copy-start(f32[2,16,72,288]{3,2,1,0:T(8,128)S(1)} %get-tuple-element.20) | copy-start | bytes 7962628
  112.5 2.2 %copy-start.5 = (bf16[768,768]{1,0:T(8,128)(2,1)S(1)}, bf16[768,768]{1,0:T(8,128)(2,1)}, u32[]{:S(2)}) copy-start(bf16[768,768]{1,0:T(8,128)(2,1)} %param.29) | copy-start | bytes 3538948
where the time goes:
time: 137 us; the launch traced here: 136 us
  blocking collectives  56.5 us (41%)
  local copies, waits for them, and re-layouts  29.1 us (21%)
  matrix products  29 us (21%)
  other arithmetic  16.6 us (12%)
  starting transfers between devices  4.23 us (3%)
    all_gather x1, blocking collectives, shards(): bias_rows = lax.all_gather(bias_part, 'sample', axis=2, tiled=True)  35.5 us
    all_gather x1, blocking collectives, shards(): attend_tkeys = lax.all_gather(tkeys, 'row', axis=1, tiled=True)  11.3 us
    all_gather x1, blocking collectives, shards(): attend_tvals = lax.all_gather(tvals, 'row', axis=1, tiled=True)  9.71 us
    convert_element_type x2, local copies, waits for them, and re-layouts, shards(): jnp.transpose(amix, (0, 1, 3, 2, 4)).reshape(samples, atoms, chans)  6.74 us
    concatenate x1, local copies, waits for them, and re-layouts, shards(): jnp.concatenate([vals_pad[:, k:k + windows] for k in range(4)], axis=2)  4.29 us
    concatenate x1, local copies, waits for them, and re-layouts, shards(): jnp.concatenate([keys_pad[:, k:k + windows] for k in range(4)], axis=2)  4.28 us
    dot_general x1, matrix products, shards(): jnp.einsum('shqk,skhd->shqd', expd.astype(jnp.bfloat16), attend_tvals, pr...  4.23 us
    dot_general x1, matrix products, shards(): jnp.einsum('swqhd,swkhd->swhqk', aquery, akeys, preferred_element_type=jn...  3.9 us
  transfers between devices with their start and end apart: 2, of which 0 were waited for; matrix products, arithmetic and copies ran while one was open for 6% of the time, Pallas kernels for 0%

commit v1 on v0

v1 whole, which is shorter than its diff:
```python
import functools
import math

import jax
import jax.numpy as jnp
from jax import lax
from jax.experimental import pallas as pl
from jax.experimental.pallas import tpu as pltpu
from jax.sharding import PartitionSpec as P

HEADS = 16
HEAD_DIM = 48
AHEADS = 4
AHEAD_DIM = 32
QWIN = 32
KWIN = 128
RIM = (KWIN - QWIN) // 2
LANES = 128
SUB = 8
F32 = jnp.float32
BF16 = jnp.bfloat16
VMEM_LIMIT = 48 * 1024 * 1024
NT = (((1,), (1,)), ((), ()))


def layer_norm(x):
    mean = jnp.mean(x, -1, keepdims=True)
    centre = x - mean
    var = jnp.mean(centre * centre, -1, keepdims=True)
    return centre * lax.rsqrt(var + 1e-05)


def dot(a, b):
    return jnp.dot(a, b, preferred_element_type=F32)


def dot_nt(a, b):
    return lax.dot_general(a, b, NT, preferred_element_type=F32)


def iota(shape, dim):
    return lax.broadcasted_iota(jnp.int32, shape, dim)


def skewed(items, stages):
    held = list(items)
    for t in range(len(held) + len(stages) - 1):
        for k in reversed(range(len(stages))):
            if 0 <= t - k < len(held):
                held[t - k] = stages[k](held[t - k])
    return held


def bias_kernel(offs, pair, mask, weight, out, normed):
    cols, rows, chans = pair.shape
    for k in range(cols):
        normed[k] = layer_norm(pair[k].astype(F32))
    spread = (iota((HEADS, LANES), 1) // SUB == iota((HEADS, LANES), 0)).astype(BF16)
    wide = lax.dot_general(weight[...], spread, (((0,), (0,)), ((), ())), preferred_element_type=F32).astype(BF16)
    tall = cols * SUB
    key_of = iota((tall, cols), 0) // SUB == iota((tall, cols), 1)
    open_key = dot_nt(key_of.astype(BF16), jnp.broadcast_to(mask[...], (LANES, cols)).astype(BF16)) > 0.5
    picked = (iota((cols, tall), 1) // SUB == iota((cols, tall), 0)).astype(BF16)
    row = iota((tall, LANES), 0)
    mine = iota((tall, LANES), 1) % SUB == row % SUB
    apart = offs[1] + row // SUB - offs[0] - row % SUB
    for g in range(rows // SUB):
        x = normed[:, g * SUB : (g + 1) * SUB].reshape(tall, chans).astype(BF16)
        raw = jnp.where(open_key | (apart == g * SUB), dot(x, wide), -30000.0)
        raw = jnp.where(mine, raw, 0.0).astype(BF16)
        out[:, g * LANES : (g + 1) * LANES] = dot(picked, raw).astype(BF16)


def pair_bias(offs, pair_cond, token_mask, pair_weight):
    rows, cols, chans = pair_cond.shape
    vmem = pl.BlockSpec(memory_space=pltpu.VMEM)
    return pl.pallas_call(
        bias_kernel,
        out_shape=jax.ShapeDtypeStruct((cols, rows * HEADS), BF16),
        in_specs=[pl.BlockSpec(memory_space=pltpu.SMEM), vmem, vmem, vmem],
        out_specs=vmem,
        scratch_shapes=[pltpu.VMEM((cols, rows, chans), F32)],
        compiler_params=pltpu.CompilerParams(vmem_limit_bytes=VMEM_LIMIT),
        cost_estimate=pl.CostEstimate(flops=200_000_000, bytes_accessed=800_000, transcendentals=0),
        name="pair_bias",
    )(offs, jnp.transpose(pair_cond, (1, 0, 2)), token_mask.reshape(1, cols), pair_weight.T)


def exchange_all(block, axis):
    devices = lax.axis_size(axis)
    held = block[None]
    far = devices // 2
    while far > 1:
        got = lax.ppermute(held, axis, [(i, i ^ far) for i in range(devices)])
        held = jnp.concatenate([held, got], axis=0)
        far //= 2
    return held, lax.ppermute(held, axis, [(i, i ^ 1) for i in range(devices)])


def atom_kernel(
    offs, feat, before, after, token, wq, wk, wv, wo, agg, gain, token_in, token_norm, qs, ks, vs, mixed
):
    atoms, chans = feat.shape[1:]
    rows = token_in.shape[1]
    wqkv = jnp.concatenate([wq[...], wk[...], wv[...]], axis=1)
    wkv = wqkv[:, chans:]
    for ref, at in ((before, 0), (after, RIM + atoms)):
        kv = dot(layer_norm(ref[0].astype(F32)).astype(BF16), wkv).astype(BF16)
        ks[at : at + RIM] = kv[:, :chans]
        vs[at : at + RIM] = kv[:, chans:]
    for c in range(0, atoms, 128):
        qkv = dot(layer_norm(feat[0, c : c + 128].astype(F32)).astype(BF16), wqkv).astype(BF16)
        qs[c : c + 128] = qkv[:, :chans]
        ks[RIM + c : RIM + c + 128] = qkv[:, chans : 2 * chans]
        vs[RIM + c : RIM + c + 128] = qkv[:, 2 * chans :]
    rate = math.log2(math.e) / AHEAD_DIM**0.5
    head_of = iota((QWIN, chans), 1) // AHEAD_DIM
    windows = atoms // QWIN
    keyat = iota((AHEADS * QWIN, KWIN), 1)
    batch = 2

    def score(first):
        out = []
        for at in range(first * QWIN, (first + batch) * QWIN, QWIN):
            q = qs[at : at + QWIN]
            q = jnp.concatenate([jnp.where(head_of == h, q, jnp.zeros_like(q)) for h in range(AHEADS)], axis=0)
            s = dot_nt(q, ks[at : at + KWIN])
            if at < RIM:
                s = jnp.where((offs[2] == 1) & (keyat < RIM - at), -jnp.inf, s)
            if at + KWIN > RIM + atoms:
                s = jnp.where((offs[3] == 1) & (keyat >= RIM + atoms - at), -jnp.inf, s)
            out.append(s)
        return first, jnp.concatenate(out, axis=0)

    def soften(item):
        first, s = item
        e = jnp.exp2((s - jnp.max(s, -1, keepdims=True)) * rate)
        return first, e.astype(BF16), 1.0 / jnp.sum(e, -1, keepdims=True)

    def mix(item):
        first, e, share = item
        tall = AHEADS * QWIN
        for i in range(batch):
            at = (first + i) * QWIN
            o = dot(e[i * tall : (i + 1) * tall], vs[at : at + KWIN]) * share[i * tall : (i + 1) * tall]
            acc = o[:QWIN]
            for h in range(1, AHEADS):
                acc = jnp.where(head_of == h, o[h * QWIN : (h + 1) * QWIN], acc)
            mixed[at : at + QWIN] = acc.astype(BF16)

    skewed(range(0, windows, batch), [score, soften, mix])
    local = token[...] - offs[0]
    step = 384
    tsum = jnp.zeros((rows, agg.shape[1]), F32)
    count = jnp.zeros((rows, 1), F32)
    for c in range(0, atoms, step):
        out = (feat[0, c : c + step].astype(F32) + dot(mixed[c : c + step], wo[...])).astype(BF16)
        hidden = jnp.maximum(dot(out, agg[...]), 0.0).astype(BF16)
        onehot = (iota((rows, step), 0) == local[:, c : c + step]).astype(F32)
        count = count + jnp.sum(onehot, -1, keepdims=True)
        tsum = tsum + dot(onehot.astype(BF16), hidden)
    tin = tsum / count
    token_in[0] = tin
    token_norm[0] = (layer_norm(tin) * gain[...]).astype(BF16)


def atom_stage(offs, feat, before, after, token, wq, wk, wv, wo, agg, gain, rows):
    samples, atoms, chans = feat.shape
    width = agg.shape[1]

    def per_sample(*tail):
        return pl.BlockSpec((1, *tail), lambda s: (s, 0, 0))

    def whole(*shape):
        return pl.BlockSpec(shape, lambda s: (0,) * len(shape))

    return pl.pallas_call(
        atom_kernel,
        grid=(samples,),
        out_shape=[
            jax.ShapeDtypeStruct((samples, rows, width), F32),
            jax.ShapeDtypeStruct((samples, rows, width), BF16),
        ],
        in_specs=[
            pl.BlockSpec(memory_space=pltpu.SMEM),
            per_sample(atoms, chans),
            per_sample(RIM, chans),
            per_sample(RIM, chans),
            whole(1, atoms),
            whole(chans, chans),
            whole(chans, chans),
            whole(chans, chans),
            whole(chans, chans),
            whole(chans, width),
            whole(1, width),
        ],
        out_specs=[per_sample(rows, width), per_sample(rows, width)],
        scratch_shapes=[
            pltpu.VMEM((atoms, chans), BF16),
            pltpu.VMEM((atoms + 2 * RIM, chans), BF16),
            pltpu.VMEM((atoms + 2 * RIM, chans), BF16),
            pltpu.VMEM((atoms, chans), BF16),
        ],
        compiler_params=pltpu.CompilerParams(vmem_limit_bytes=VMEM_LIMIT),
        cost_estimate=pl.CostEstimate(flops=8_000_000_000, bytes_accessed=2_000_000, transcendentals=1_200_000),
        name="atom_stage",
    )(offs, feat, before, after, token.reshape(1, atoms), wq, wk, wv, wo, agg, gain.reshape(1, width))


def head_groups(width):
    groups = []
    for base in range(0, width, 8 * HEAD_DIM):
        first = base // HEAD_DIM
        groups.append((base, range(first, first + 5)))
        groups.append((base + LANES, range(first + 5, first + 8)))
    return groups


def token_kernel(offs, norm_all, norm_own, token_in, near, far, wq, wk, wv, wg, wo, out, bt, bs, ks, vs, wbuf, sems):
    blocks, samples, rows, width = norm_all.shape
    keys = blocks * rows
    copies = [pltpu.make_async_copy(w, wbuf.at[i], sems.at[i]) for i, w in enumerate((wk, wv, wq, wg, wo))]
    for copy in copies:
        copy.start()
    half, cols, _ = near.shape
    for j in range(2 * half):
        apart = offs[4] ^ j
        place = sum(((apart // (half >> i)) % 2) * 2**i for i in range(half.bit_length() - 1))
        block = jnp.where(apart % 2 == 0, near[place], far[place])
        bt[j * cols : (j + 1) * cols] = block.astype(F32)
    for g in range(rows // SUB):
        turned = bt[:, g * LANES : (g + 1) * LANES].T
        for h in range(HEADS):
            bs[h * rows + g * SUB : h * rows + (g + 1) * SUB] = turned[h * SUB : (h + 1) * SUB]
    x_all = jnp.concatenate(
        [norm_all[j, s].astype(F32) for s in range(samples) for j in range(blocks)], axis=0
    ).astype(BF16)
    copies[0].wait()
    ks[...] = dot(x_all, wbuf[0]).astype(BF16)
    copies[1].wait()
    vs[...] = dot(x_all, wbuf[1]).astype(BF16)
    x_own = jnp.concatenate([norm_own[s].astype(F32) for s in range(samples)], axis=0).astype(BF16)
    copies[2].wait()
    q_own = dot(x_own, wbuf[2]).astype(BF16).astype(F32)
    copies[3].wait()
    gate = jax.nn.sigmoid(dot(x_own, wbuf[3]))
    scale = 1.0 / HEAD_DIM**0.5
    lane = iota((rows, 2 * LANES), 1)
    gated = []
    work = [(s, base, h) for s in range(samples) for base, heads in head_groups(width) for h in heads]

    def score(item):
        s, base, h = item
        low = h * HEAD_DIM - base
        mine = (lane >= low) & (lane < low + HEAD_DIM)
        q = q_own[s * rows : (s + 1) * rows, base : base + 2 * LANES]
        k = ks[s * keys : (s + 1) * keys, base : base + 2 * LANES]
        sc = dot_nt(jnp.where(mine, q, 0.0).astype(BF16), k)
        return item, sc * scale + bs[h * rows : (h + 1) * rows]

    def soften(item):
        place, sc = item
        e = jnp.exp(sc - jnp.max(sc, -1, keepdims=True))
        return place, e.astype(BF16), 1.0 / jnp.sum(e, -1, keepdims=True)

    mixes = {}

    def mix(item):
        (s, base, h), e, share = item
        low = h * HEAD_DIM - base
        mine = (lane >= low) & (lane < low + HEAD_DIM)
        o = dot(e, vs[s * keys : (s + 1) * keys, base : base + 2 * LANES]) * share
        mixes[s, base] = jnp.where(mine, o, mixes.get((s, base), 0.0))

    skewed(work, [score, soften, mix])
    gated = []
    for s in range(samples):
        tiles = {}
        for base, _ in head_groups(width):
            for t in range(2):
                at = base + t * LANES
                part = mixes[s, base][:, t * LANES : (t + 1) * LANES]
                tiles[at] = tiles[at] + part if at in tiles else part
        whole = jnp.concatenate([tiles[at] for at in range(0, width, LANES)], axis=1)
        gated.append(whole * gate[s * rows : (s + 1) * rows])
    copies[4].wait()
    res = dot(jnp.concatenate(gated, axis=0).astype(BF16), wbuf[4])
    for s in range(samples):
        out[s] = (token_in[s] + res[s * rows : (s + 1) * rows]).astype(BF16)


def token_stage(offs, norm_all, norm_own, token_in, near, far, wq, wk, wv, wg, wo):
    blocks, samples, rows, width = norm_all.shape
    keys = blocks * rows
    vmem = pl.BlockSpec(memory_space=pltpu.VMEM)
    hbm = pl.BlockSpec(memory_space=pl.ANY)
    return pl.pallas_call(
        token_kernel,
        out_shape=jax.ShapeDtypeStruct((samples, rows, width), BF16),
        in_specs=[pl.BlockSpec(memory_space=pltpu.SMEM)] + [vmem] * 5 + [hbm] * 5,
        out_specs=vmem,
        scratch_shapes=[
            pltpu.VMEM((keys, rows * HEADS), F32),
            pltpu.VMEM((rows * HEADS, keys), F32),
            pltpu.VMEM((samples * keys, width), BF16),
            pltpu.VMEM((samples * keys, width), BF16),
            pltpu.VMEM((5, width, width), BF16),
            pltpu.SemaphoreType.DMA((5,)),
        ],
        compiler_params=pltpu.CompilerParams(vmem_limit_bytes=VMEM_LIMIT),
        cost_estimate=pl.CostEstimate(flops=5_000_000_000, bytes_accessed=9_000_000, transcendentals=700_000),
        name="token_stage",
    )(offs, norm_all, norm_own, token_in, near, far, wq, wk, wv, wg, wo)


def shards(
    atom_feat,
    atom_token,
    pair_cond,
    token_mask,
    atom_wq,
    atom_wk,
    atom_wv,
    atom_wo,
    agg_weight,
    pair_weight,
    token_gain,
    query_weight,
    key_weight,
    value_weight,
    gate_weight,
    out_weight,
):
    rows, cols, _ = pair_cond.shape
    atoms = atom_feat.shape[1]
    ranks = lax.axis_size("row")
    rank = lax.axis_index("row")
    offs = jnp.stack(
        [
            rank * rows,
            lax.axis_index("sample") * cols,
            (rank == 0).astype(jnp.int32),
            (rank == ranks - 1).astype(jnp.int32),
            lax.axis_index("sample"),
        ]
    ).astype(jnp.int32)
    up = [(i, i + 1) for i in range(ranks - 1)]
    down = [(j, i) for i, j in up]
    before = lax.ppermute(atom_feat[:, atoms - RIM :], "row", up)
    after = lax.ppermute(atom_feat[:, :RIM], "row", down)
    bias = pair_bias(offs, pair_cond, token_mask, pair_weight)
    near, far = exchange_all(bias, "sample")
    token_in, token_norm = atom_stage(
        offs, atom_feat, before, after, atom_token, atom_wq, atom_wk, atom_wv, atom_wo, agg_weight, token_gain, rows
    )
    norm_all = lax.all_gather(token_norm, "row", axis=0)
    return token_stage(
        offs, norm_all, token_norm, token_in, near, far, query_weight, key_weight, value_weight, gate_weight, out_weight
    )


def solution(mesh):
    placed = (
        P("sample", "row", None),
        P("row"),
        P("row", "sample", None),
        P("sample"),
    ) + (P(),) * 12
    return jax.shard_map(
        shards, mesh=mesh, in_specs=placed, out_specs=P("sample", "row", None), check_vma=False
    )
```

time: 137 us -> 48.7 us (0.36)
  blocking collectives: 56.5 us -> 9.46 us
  matrix products: 29 us -> 0 us
  local copies, waits for them, and re-layouts: 29.1 us -> 4.71 us
  Pallas kernels: 0 us -> 21.9 us
  other arithmetic: 16.6 us -> 0.09 us
  starting transfers between devices: 4.23 us -> 11.6 us
    all_gather x3 -> x1, blocking collectives: 56.5 us -> 9.46 us  [shards(): norm_all = lax.all_gather(token_norm, 'row', axis=0)]
    dot_general x14 -> x0, matrix products: 29 us -> none  [the longest x1 4.23 us: shards(): jnp.einsum('shqk,skhd->shqd', expd.astype(jnp.bfloat16), attend_tvals, pr...]
    pallas_call x0 -> x3, Pallas kernels: none -> 21.9 us  [the longest x1 9.92 us: token_stage(): pl.pallas_call(token_kernel, out_shape=jax.ShapeDtypeStruct((samples, row...]
    reduce_sum x8 -> x0, other arithmetic: 9.77 us -> none  [the longest x3 3.02 us: layer_norm(): var = jnp.mean(centre * centre, -1, keepdims=True)]
    convert_element_type x3 -> x0, local copies, waits for them, and re-layouts: 8.62 us -> none  [the longest x2 6.74 us: shards(): jnp.transpose(amix, (0, 1, 3, 2, 4)).reshape(samples, atoms, chans)]
    concatenate x2 -> x0, local copies, waits for them, and re-layouts: 8.58 us -> none  [the longest x1 4.29 us: shards(): jnp.concatenate([vals_pad[:, k:k + windows] for k in range(4)], axis=2)]
    ppermute x2 -> x5, starting transfers between devices: 4.23 us -> 11.6 us  [the longest x2 5.74 us: exchange_all(): got = lax.ppermute(held, axis, [(i, i ^ far) for i in range(devices)])]
    all_gather x3 -> x0, local copies, waits for them, and re-layouts: 6.3 us -> none  [the longest x1 2.32 us: shards(): attend_tvals = lax.all_gather(tvals, 'row', axis=1, tiled=True)]
  transfers between devices with their start and end apart: 2 -> 5, of which waited for: 0 -> 1; matrix products, arithmetic and copies ran while one was open for 6% -> 5% of each run, Pallas kernels for 0% -> 20%
where the time goes in v1:
time: 48.7 us; the launch traced here: 48.3 us
  Pallas kernels  21.9 us (45%)
  starting transfers between devices  11.6 us (24%)
  blocking collectives  9.46 us (19%)
  local copies, waits for them, and re-layouts  4.71 us (10%)
    pallas_call x1, Pallas kernels, token_stage(): pl.pallas_call(token_kernel, out_shape=jax.ShapeDtypeStruct((samples, row...  9.92 us
    pallas_call x1, Pallas kernels, atom_stage(): pl.pallas_call(atom_kernel, grid=(samples,), out_shape=[jax.ShapeDtypeStr...  9.7 us
    all_gather x1, blocking collectives, shards(): norm_all = lax.all_gather(token_norm, 'row', axis=0)  9.46 us
    ppermute x2, starting transfers between devices, exchange_all(): got = lax.ppermute(held, axis, [(i, i ^ far) for i in range(devices)])  5.74 us
    ppermute x1, starting transfers between devices, shards(): before = lax.ppermute(atom_feat[:, atoms - RIM:], 'row', up)  3.03 us
    unnamed x24, local copies, waits for them, and re-layouts  2.47 us
    pallas_call x1, Pallas kernels, pair_bias(): pl.pallas_call(bias_kernel, out_shape=jax.ShapeDtypeStruct((cols, rows *...  2.29 us
    ppermute x1, starting transfers between devices, exchange_all(): lax.ppermute(held, axis, [(i, i ^ 1) for i in range(devices)])  1.55 us
  transfers between devices with their start and end apart: 5, of which 1 were waited for; matrix products, arithmetic and copies ran while one was open for 5% of the time, Pallas kernels for 20%

profile of v1, /device:TPU:0, one launch (start us, length us, event | category | flops | bytes accessed | tf_op | source)
XLA Modules:
  0.0 48.3 jit_solution(5042533160014251788)
XLA Ops:
  0.0 0.1 stack.31.offs
  0.1 1.1 %copy-done = bf16[72,36,128]{2,0,1:T(8,128)(2,1)S(1)} copy-done((bf16[72,36,128]{2,0,1:T(8,128)(2,1)S(1)}, bf16[72,36,128]{2,0,1:T(8,128)(2,1)}, u32[]{:S(2)}) %copy-start) | copy-done | bytes 663576
  1.2 0.7 %copy-done.1 = bf16[128,16]{0,1:T(8,128)(2,1)S(1)} copy-done((bf16[128,16]{0,1:T(8,128)(2,1)S(1)}, bf16[128,16]{0,1:T(8,128)(2,1)}, u32[]{:S(2)}) %copy-start.1) | copy-done | bytes 4120
  1.9 0.7 %copy-done.3 = s32[36]{0:T(128)S(1)} copy-done((s32[36]{0:T(128)S(1)}, s32[36]{0:T(128)}, u32[]{:S(2)}) %copy-start.3) | copy-done | bytes 168
  2.5 0.0 copy-start.11
  2.5 2.3 %pair_bias.1 = bf16[36,1152]{1,0:T(8,128)(2,1)S(1)} custom-call(s32[5]{0:T(128)S(1)} %stack.31.offs, bf16[36,72,128]{2,1,0:T(8,128)(2,1)S(1)} %bitcast.14, s32[1,36]{1,0:T(1,128)S(1)} %bitcast.16, bf16[16,128]{1,0:T(8,128)(2,1)S(1)} %bitcast.15), custom_call_target="tpu_custom_call" | custom-call | flops 200000000 | bytes 800000 | tf_op jit(solution)/shard_map/pair_bias/pallas_call | solution.py:77
  4.8 4.1 %collective-permute-start.2 = (bf16[1,36,1152]{2,1,0:T(8,128)(2,1)S(1)}, bf16[1,36,1152]{2,1,0:T(8,128)(2,1)S(1)}, u32[]{:S(2)}, u32[]{:S(2)}) collective-permute-start(bf16[1,36,1152]{2,1,0:T(8,128)(2,1)S(1)} %bitcast.11), channel_id=1, source_target_pairs={{0,4},{1,5},{2,6},{3,7},{4,0},{5,1},{6,2},{7,3},{8,12},{9,13},{10,... | collective-permute-start | bytes 248840 | tf_op jit(solution)/shard_map/ppermute | solution.py:94
  8.9 0.8 %fusion = (bf16[2,48,128]{2,1,0:T(8,128)(2,1)S(1)}, bf16[2,48,128]{2,1,0:T(8,128)(2,1)S(1)}) fusion(bf16[2,1152,128]{2,1,0:T(8,128)(2,1)} %feat.1), kind=kLoop, calls=%fused_computation.2 | loop fusion | bytes 98304 | tf_op jit(solution)/shard_map/slice | solution.py:350
  9.7 1.3 %collective-permute-start.1 = (bf16[2,48,128]{2,1,0:T(8,128)(2,1)S(1)}, bf16[2,48,128]{2,1,0:T(8,128)(2,1)S(1)}, u32[]{:S(2)}, u32[]{:S(2)}) collective-permute-start(bf16[2,48,128]{2,1,0:T(8,128)(2,1)S(1)} %get-tuple-element.9), channel_id=1, source_target_pairs={{8,0},{16,8},{24,16},{9,1},{17,9},{25,17},{10,2},{18,10},{26,18},{... | collective-permute-start | bytes 73736 | tf_op jit(solution)/shard_map/ppermute | solution.py:350
  11.0 3.0 %collective-permute-start = (bf16[2,48,128]{2,1,0:T(8,128)(2,1)S(1)}, bf16[2,48,128]{2,1,0:T(8,128)(2,1)S(1)}, u32[]{:S(2)}, u32[]{:S(2)}) collective-permute-start(bf16[2,48,128]{2,1,0:T(8,128)(2,1)S(1)} %get-tuple-element.10), channel_id=1, source_target_pairs={{0,8},{8,16},{16,24},{1,9},{9,17},{17,25},{2,10},{10,18},{18,26},{... | collective-permute-start | bytes 73736 | tf_op jit(solution)/shard_map/ppermute | solution.py:349
  14.0 0.7 %reshape.10.gain = f32[1,768]{1,0:T(1,128)S(1)} reshape(f32[768]{0:T(1024)} %param.26) | data formatting | bytes 6144 | tf_op jit(solution)/shard_map/reshape | solution.py:207
  14.7 0.7 %reshape.9.token = s32[1,1152]{1,0:T(1,128)S(1)} reshape(s32[1152]{0:T(1024)} %param.17) | data formatting | bytes 9216 | tf_op jit(solution)/shard_map/reshape | solution.py:207
  15.4 0.0 collective-permute-done.2
  15.5 1.6 %collective-permute-start.3 = (bf16[2,36,1152]{2,1,0:T(8,128)(2,1)S(1)}, bf16[2,36,1152]{2,1,0:T(8,128)(2,1)S(1)}, u32[]{:S(2)}, u32[]{:S(2)}) collective-permute-start(bf16[2,36,1152]{2,1,0:T(8,128)(2,1)S(1)} %pad_maximum_fusion.1), channel_id=1, source_target_pairs={{0,2},{1,3},{2,0},{3,1},{4,6},{5,7},{6,4},{7,5},{8,10},{9,11},{10,... | collective-permute-start | bytes 497672 | tf_op jit(solution)/shard_map/ppermute | solution.py:94
  17.1 0.0 collective-permute-done.1.after
  17.1 0.0 collective-permute-done.before
  17.1 0.0 copy-done.8
  17.1 0.0 copy-done.2
  17.1 0.0 copy-done.7
  17.1 0.0 copy-done.9
  17.1 0.0 copy-done.10
  17.2 0.0 copy-done.11
  17.2 0.0 copy-start.5
  17.2 0.0 copy-start.6
  17.2 9.7 %atom_stage.1 = (f32[2,72,768]{2,1,0:T(8,128)S(1)}, bf16[2,72,768]{2,1,0:T(8,128)(2,1)S(1)}) custom-call(s32[5]{0:T(128)S(1)} %stack.31.offs, bf16[2,1152,128]{2,1,0:T(8,128)(2,1)S(1)} %copy-done.2, bf16[2,48,128]{2,1,0:T(8,128)(2,1)S(1)} %collective-permute-done.before, bf16[2,48,128]{2,1,0:T(8,128)(2,1)S(1)} %collective-permute-done.1.after, ...), custom_call_target="tpu_custom_call" | custom-call | flops 8000000000 | bytes 2000000 | tf_op jit(solution)/shard_map/atom_stage/pallas_call | solution.py:177
  26.9 0.0 copy-start.4
  26.9 0.0 collective-permute-done.3
  26.9 0.1 pad_maximum_fusion.near
  27.0 1.6 %collective-permute-start.4 = (bf16[4,36,1152]{2,1,0:T(8,128)(2,1)S(1)}, bf16[4,36,1152]{2,1,0:T(8,128)(2,1)S(1)}, u32[]{:S(2)}, u32[]{:S(2)}) collective-permute-start(bf16[4,36,1152]{2,1,0:T(8,128)(2,1)S(1)} %pad_maximum_fusion.near), channel_id=1, source_target_pairs={{0,1},{1,0},{2,3},{3,2},{4,5},{5,4},{6,7},{7,6},{8,9},{9,8},{10,11... | collective-permute-start | bytes 995336 | tf_op jit(solution)/shard_map/ppermute | solution.py:97
  28.5 9.5 %all-gather = bf16[8,72,768]{2,1,0:T(8,128)(2,1)S(1)} all-gather(bf16[2,72,768]{2,1,0:T(8,128)(2,1)S(1)} %get-tuple-element.7.norm_own), channel_id=2, replica_groups=mesh['row'=4,'sample'=8] {'row'}, dimensions={0}, use_global_device_ids=true | all-gather | bytes 1105920 | tf_op jit(solution)/shard_map/all_gather | solution.py:356
  38.0 0.4 collective-permute-done.4.far
  38.4 9.9 %token_stage.1 = bf16[2,72,768]{2,1,0:T(8,128)(2,1)} custom-call(s32[5]{0:T(128)S(1)} %stack.31.offs, bf16[4,2,72,768]{3,2,1,0:T(8,128)(2,1)S(1)} %bitcast.10, bf16[2,72,768]{2,1,0:T(8,128)(2,1)S(1)} %get-tuple-element.7.norm_own, f32[2,72,768]{2,1,0:T(8,128)S(1)} %get-tuple-element.8.token_in, bf16[4,36,1152]{2,1,0:T(8,128)(2,1)S(1)} %pad_maximum_fusion.near, ...), custom_call_target="tpu_custom_call" | custom-call | flops 5000000000 | bytes 9000000 | tf_op jit(solution)/shard_map/token_stage/pallas_call | solution.py:297
  (12 shorter events, 0.0 us)
Async XLA Ops:
  0.0 17.1 %copy-start.8 = (bf16[128,128]{1,0:T(8,128)(2,1)S(1)}, bf16[128,128]{1,0:T(8,128)(2,1)}, u32[]{:S(2)}) copy-start(bf16[128,128]{1,0:T(8,128)(2,1)} %wq.2) | copy-start | bytes 98308
  0.1 1.1 %copy-start = (bf16[72,36,128]{2,0,1:T(8,128)(2,1)S(1)}, bf16[72,36,128]{2,0,1:T(8,128)(2,1)}, u32[]{:S(2)}) copy-start(bf16[72,36,128]{2,0,1:T(8,128)(2,1)} %param.18) | copy-start | bytes 1990660
  1.2 0.7 %copy-start.1 = (bf16[128,16]{0,1:T(8,128)(2,1)S(1)}, bf16[128,16]{0,1:T(8,128)(2,1)}, u32[]{:S(2)}) copy-start(bf16[128,16]{0,1:T(8,128)(2,1)} %param.25) | copy-start | bytes 12292
  1.9 0.7 %copy-start.3 = (s32[36]{0:T(128)S(1)}, s32[36]{0:T(128)}, u32[]{:S(2)}) copy-start(s32[36]{0:T(128)} %param.19) | copy-start | bytes 436
  2.5 14.6 %copy-start.2 = (bf16[2,1152,128]{2,1,0:T(8,128)(2,1)S(1)}, bf16[2,1152,128]{2,1,0:T(8,128)(2,1)}, u32[]{:S(2)}) copy-start(bf16[2,1152,128]{2,1,0:T(8,128)(2,1)} %feat.1) | copy-start | bytes 1769476
  2.5 14.6 %copy-start.7 = (bf16[128,768]{1,0:T(8,128)(2,1)S(1)}, bf16[128,768]{1,0:T(8,128)(2,1)}, u32[]{:S(2)}) copy-start(bf16[128,768]{1,0:T(8,128)(2,1)} %agg.1) | copy-start | bytes 589828
  2.5 14.6 %copy-start.9 = (bf16[128,128]{1,0:T(8,128)(2,1)S(1)}, bf16[128,128]{1,0:T(8,128)(2,1)}, u32[]{:S(2)}) copy-start(bf16[128,128]{1,0:T(8,128)(2,1)} %wk.2) | copy-start | bytes 98308
  2.5 14.6 %copy-start.10 = (bf16[128,128]{1,0:T(8,128)(2,1)S(1)}, bf16[128,128]{1,0:T(8,128)(2,1)}, u32[]{:S(2)}) copy-start(bf16[128,128]{1,0:T(8,128)(2,1)} %wv.2) | copy-start | bytes 98308
  2.5 14.6 %copy-start.11 = (bf16[128,128]{1,0:T(8,128)(2,1)S(1)}, bf16[128,128]{1,0:T(8,128)(2,1)}, u32[]{:S(2)}) copy-start(bf16[128,128]{1,0:T(8,128)(2,1)} %wo.2) | copy-start | bytes 98308
  4.8 10.6 %collective-permute-start.2 = (bf16[1,36,1152]{2,1,0:T(8,128)(2,1)S(1)}, bf16[1,36,1152]{2,1,0:T(8,128)(2,1)S(1)}, u32[]{:S(2)}, u32[]{:S(2)}) collective-permute-start(bf16[1,36,1152]{2,1,0:T(8,128)(2,1)S(1)} %bitcast.11), channel_id=1, source_target_pairs={{0,4},{1,5},{2,6},{3,7},{4,0},{5,1},{6,2},{7,3},{8,12},{9,13},{10,... | collective-permute-start | bytes 248840 | tf_op jit(solution)/shard_map/ppermute | solution.py:94
  9.7 7.4 %collective-permute-start.1 = (bf16[2,48,128]{2,1,0:T(8,128)(2,1)S(1)}, bf16[2,48,128]{2,1,0:T(8,128)(2,1)S(1)}, u32[]{:S(2)}, u32[]{:S(2)}) collective-permute-start(bf16[2,48,128]{2,1,0:T(8,128)(2,1)S(1)} %get-tuple-element.9), channel_id=1, source_target_pairs={{8,0},{16,8},{24,16},{9,1},{17,9},{25,17},{10,2},{18,10},{26,18},{... | collective-permute-start | bytes 73736 | tf_op jit(solution)/shard_map/ppermute | solution.py:350
  11.0 6.1 %collective-permute-start = (bf16[2,48,128]{2,1,0:T(8,128)(2,1)S(1)}, bf16[2,48,128]{2,1,0:T(8,128)(2,1)S(1)}, u32[]{:S(2)}, u32[]{:S(2)}) collective-permute-start(bf16[2,48,128]{2,1,0:T(8,128)(2,1)S(1)} %get-tuple-element.10), channel_id=1, source_target_pairs={{0,8},{8,16},{16,24},{1,9},{9,17},{17,25},{2,10},{10,18},{18,26},{... | collective-permute-start | bytes 73736 | tf_op jit(solution)/shard_map/ppermute | solution.py:349
  15.5 11.5 %collective-permute-start.3 = (bf16[2,36,1152]{2,1,0:T(8,128)(2,1)S(1)}, bf16[2,36,1152]{2,1,0:T(8,128)(2,1)S(1)}, u32[]{:S(2)}, u32[]{:S(2)}) collective-permute-start(bf16[2,36,1152]{2,1,0:T(8,128)(2,1)S(1)} %pad_maximum_fusion.1), channel_id=1, source_target_pairs={{0,2},{1,3},{2,0},{3,1},{4,6},{5,7},{6,4},{7,5},{8,10},{9,11},{10,... | collective-permute-start | bytes 497672 | tf_op jit(solution)/shard_map/ppermute | solution.py:94
  17.2 21.2 %copy-start.5 = (bf16[768,768]{1,0:T(8,128)(2,1)S(1)}, bf16[768,768]{1,0:T(8,128)(2,1)}, u32[]{:S(2)}) copy-start(bf16[768,768]{1,0:T(8,128)(2,1)} %wk.3) | copy-start | bytes 3538948
  17.2 21.2 %copy-start.6 = (bf16[768,768]{1,0:T(8,128)(2,1)S(1)}, bf16[768,768]{1,0:T(8,128)(2,1)}, u32[]{:S(2)}) copy-start(bf16[768,768]{1,0:T(8,128)(2,1)} %wv.3) | copy-start | bytes 3538948
  26.9 11.5 %copy-start.4 = (bf16[768,768]{1,0:T(8,128)(2,1)S(1)}, bf16[768,768]{1,0:T(8,128)(2,1)}, u32[]{:S(2)}) copy-start(bf16[768,768]{1,0:T(8,128)(2,1)} %wq.3) | copy-start | bytes 3538948
  27.0 11.4 %collective-permute-start.4 = (bf16[4,36,1152]{2,1,0:T(8,128)(2,1)S(1)}, bf16[4,36,1152]{2,1,0:T(8,128)(2,1)S(1)}, u32[]{:S(2)}, u32[]{:S(2)}) collective-permute-start(bf16[4,36,1152]{2,1,0:T(8,128)(2,1)S(1)} %pad_maximum_fusion.near), channel_id=1, source_target_pairs={{0,1},{1,0},{2,3},{3,2},{4,5},{5,4},{6,7},{7,6},{8,9},{9,8},{10,11... | collective-permute-start | bytes 995336 | tf_op jit(solution)/shard_map/ppermute | solution.py:97

commit v2 on v1

v2 whole, which is shorter than its diff:
```python
import functools
import math

import jax
import jax.numpy as jnp
from jax import lax
from jax.experimental import pallas as pl
from jax.experimental.pallas import tpu as pltpu
from jax.sharding import PartitionSpec as P

HEADS = 16
HEAD_DIM = 48
AHEADS = 4
AHEAD_DIM = 32
QWIN = 32
KWIN = 128
RIM = (KWIN - QWIN) // 2
LANES = 128
SUB = 8
F32 = jnp.float32
BF16 = jnp.bfloat16
MIB = 1024 * 1024
NT = (((1,), (1,)), ((), ()))


def layer_norm(x):
    mean = jnp.mean(x, -1, keepdims=True)
    centre = x - mean
    var = jnp.mean(centre * centre, -1, keepdims=True)
    return centre * lax.rsqrt(var + 1e-05)


def dot(a, b):
    return jnp.dot(a, b, preferred_element_type=F32)


def dot_nt(a, b):
    return lax.dot_general(a, b, NT, preferred_element_type=F32)


def iota(shape, dim):
    return lax.broadcasted_iota(jnp.int32, shape, dim)


def cost(micros):
    return pl.CostEstimate(flops=micros * 1_100_000_000, bytes_accessed=1_000_000, transcendentals=0)


def inverse(total):
    guess = pl.reciprocal(total, approx=True)
    return guess * (2.0 - total * guess)


def skewed(items, stages):
    held = list(items)
    for t in range(len(held) + len(stages) - 1):
        for k in reversed(range(len(stages))):
            if 0 <= t - k < len(held):
                held[t - k] = stages[k](held[t - k])
    return held


def bias_kernel(pair, mask, weight, out, other, normed):
    cols, rows, chans = pair.shape
    for k in range(cols):
        normed[k] = layer_norm(pair[k].astype(F32))
    spread = (iota((HEADS, LANES), 1) // SUB == iota((HEADS, LANES), 0)).astype(BF16)
    wide = lax.dot_general(weight[...], spread, (((0,), (0,)), ((), ())), preferred_element_type=F32).astype(BF16)
    tall = cols * SUB
    key_of = iota((tall, cols), 0) // SUB == iota((tall, cols), 1)
    open_row = jnp.broadcast_to(mask[...].reshape(1, cols), (LANES, cols)).astype(BF16)
    open_key = dot_nt(key_of.astype(BF16), open_row) > 0.5
    picked = (iota((cols, tall), 1) // SUB == iota((cols, tall), 0)).astype(BF16)
    row = iota((tall, LANES), 0)
    mine = iota((tall, LANES), 1) % SUB == row % SUB
    apart = lax.axis_index("sample") * cols + row // SUB - lax.axis_index("row") * rows - row % SUB
    for g in range(rows // SUB):
        x = normed[:, g * SUB : (g + 1) * SUB].reshape(tall, chans).astype(BF16)
        raw = jnp.where(open_key | (apart == g * SUB), dot(x, wide), -30000.0)
        raw = jnp.where(mine, raw, 0.0).astype(BF16)
        at = g * LANES
        ref, at = (out, at) if at < out.shape[1] else (other, at - out.shape[1])
        ref[:, at : at + LANES] = dot(picked, raw).astype(BF16)


def pair_bias(pair_cond, token_mask, pair_weight):
    rows, cols, chans = pair_cond.shape
    wide = rows * HEADS
    first = (wide // LANES + 1) // 2 * LANES
    vmem = pl.BlockSpec(memory_space=pltpu.VMEM)
    return pl.pallas_call(
        bias_kernel,
        out_shape=[jax.ShapeDtypeStruct((cols, first), BF16), jax.ShapeDtypeStruct((cols, wide - first), BF16)],
        in_specs=[vmem] * 3,
        out_specs=[vmem] * 2,
        scratch_shapes=[pltpu.VMEM((cols, rows, chans), F32)],
        compiler_params=pltpu.CompilerParams(vmem_limit_bytes=16 * MIB),
        cost_estimate=cost(3),
        name="pair_bias",
    )(jnp.transpose(pair_cond, (1, 0, 2)), token_mask, pair_weight.T)


def after(value, *others):
    return lax.optimization_barrier((value, *others))[0]


def swap(held, axis, far):
    return lax.ppermute(held, axis, [(i, i ^ far) for i in range(lax.axis_size(axis))])


def block_of(near, far, bits, me, j):
    apart = me ^ j
    place = sum((apart // bit) % 2 * 2**i for i, bit in enumerate(bits[:-1]))
    return jnp.where((apart // bits[-1]) % 2 == 0, near[place], far[place])


def bits_of(devices):
    return [devices >> i for i in range(1, devices.bit_length())]


def atom_kernel(sample, feat, before, after, wq, wk, wv, mixed, ns, ks, qt, vt):
    atoms, chans = feat.shape[1:]
    rank = lax.axis_index("row")
    at_start = rank == 0
    at_end = rank == lax.axis_size("row") - 1
    ns[:RIM] = layer_norm(before[sample].astype(F32)).astype(BF16)
    for c in range(0, atoms, LANES):
        ns[RIM + c : RIM + c + LANES] = layer_norm(feat[sample, c : c + LANES].astype(F32)).astype(BF16)
    ns[RIM + atoms : 2 * RIM + atoms] = layer_norm(after[sample].astype(F32)).astype(BF16)
    padded = ns.shape[0]
    ns[atoms + 2 * RIM :] = jnp.zeros((padded - atoms - 2 * RIM, chans), BF16)
    wqv = jnp.concatenate([wq[...].astype(F32).T, wv[...].astype(F32).T], axis=0).astype(BF16)
    for c in range(0, padded, LANES):
        normed = ns[c : c + LANES]
        ks[c : c + LANES] = dot(normed, wk[...]).astype(BF16)
        qv = dot(wqv, normed.astype(F32).T.astype(BF16)).astype(BF16)
        qt[:, c : c + LANES] = qv[:chans]
        vt[:, c : c + LANES] = qv[chans:]
    rate = math.log2(math.e) / AHEAD_DIM**0.5
    tall = AHEADS * QWIN
    group = LANES // QWIN
    wide = group * tall
    batch = 2
    keyat = iota((KWIN, tall), 0)
    col = iota((2 * LANES, wide), 1)
    spread = (iota((2 * LANES, wide), 0) == RIM + col // tall * QWIN + col % QWIN).astype(BF16)
    row = iota((wide, LANES), 0)
    fold = (iota((wide, LANES), 1) == row // tall * QWIN + row % QWIN).astype(BF16)
    own_head = iota((chans, wide), 0) // AHEAD_DIM == iota((chans, wide), 1) % tall // QWIN
    queries, sums = {}, {}

    def score(first):
        base = first // LANES * LANES
        if base not in queries:
            queries[base] = jnp.where(own_head, dot(qt[:, base : base + 2 * LANES], spread), 0.0).astype(BF16)
        out = []
        for at in range(first, first + batch * QWIN, QWIN):
            col = (at - base) // QWIN * tall
            s = dot(ks[at : at + KWIN], queries[base][:, col : col + tall])
            if at < RIM:
                s = jnp.where(at_start & (keyat < RIM - at), -jnp.inf, s)
            if at + KWIN > RIM + atoms:
                s = jnp.where(at_end & (keyat >= RIM + atoms - at), -jnp.inf, s)
            out.append(s)
        return first, out

    def soften(item):
        first, scores = item
        out = []
        for s in scores:
            e = jnp.exp2((s - jnp.max(s, 0, keepdims=True)) * rate)
            out.append((e.astype(BF16), 1.0 / jnp.sum(e, 0, keepdims=True)))
        return first, out

    def mix(item):
        first, parts = item
        base = first // LANES * LANES
        for i, (e, share) in enumerate(parts):
            skip = first + i * QWIN - base
            pads = [jnp.zeros((n, tall), BF16) for n in (skip, 2 * LANES - KWIN - skip)]
            e = jnp.concatenate([p for p in (pads[0], e, pads[1]) if p.shape[0]], axis=0)
            o = dot(vt[:, base : base + 2 * LANES], e) * share
            sums.setdefault(base, []).append(jnp.where(own_head[:, :tall], o, 0.0).astype(BF16))
        if len(sums[base]) == group:
            mixed[:, base : base + LANES] = dot(jnp.concatenate(sums[base], axis=1), fold).astype(BF16)

    skewed(range(0, atoms, batch * QWIN), [score, soften, mix])


def atom_attention(sample, feat, before, after, wq, wk, wv):
    atoms, chans = feat.shape[1:]
    padded = pl.cdiv(atoms + 2 * RIM, LANES) * LANES
    vmem = pl.BlockSpec(memory_space=pltpu.VMEM)
    return pl.pallas_call(
        functools.partial(atom_kernel, sample),
        out_shape=jax.ShapeDtypeStruct((chans, atoms), BF16),
        in_specs=[vmem] * 6,
        out_specs=vmem,
        scratch_shapes=[
            pltpu.VMEM((padded, chans), BF16),
            pltpu.VMEM((padded, chans), BF16),
            pltpu.VMEM((chans, padded), BF16),
            pltpu.VMEM((chans, padded), BF16),
        ],
        compiler_params=pltpu.CompilerParams(vmem_limit_bytes=16 * MIB),
        cost_estimate=cost(4),
        name="atom_attention",
    )(feat, before, after, wq, wk, wv)


def gather_kernel(sample, mixed, feat, token, wo, agg, gain, token_in, token_norm):
    atoms = feat.shape[1]
    rows = token_in.shape[0]
    wo_turned = wo[...].astype(F32).T.astype(BF16)
    local = token[...].reshape(1, atoms) - lax.axis_index("row") * rows
    step = 384
    tsum = jnp.zeros((rows, agg.shape[1]), F32)
    count = jnp.zeros((rows, 1), F32)
    for c in range(0, atoms, step):
        out = (feat[sample, c : c + step].astype(F32) + dot(wo_turned, mixed[:, c : c + step]).T).astype(BF16)
        hidden = jnp.maximum(dot(out, agg[...]), 0.0).astype(BF16)
        onehot = (iota((rows, step), 0) == local[:, c : c + step]).astype(F32)
        count = count + jnp.sum(onehot, -1, keepdims=True)
        tsum = tsum + dot(onehot.astype(BF16), hidden)
    tin = tsum / count
    token_in[...] = tin
    token_norm[...] = (layer_norm(tin) * gain[...].reshape(1, -1)).astype(BF16)


def gather_tokens(sample, mixed, feat, token, wo, agg, gain, rows):
    width = agg.shape[1]
    vmem = pl.BlockSpec(memory_space=pltpu.VMEM)
    return pl.pallas_call(
        functools.partial(gather_kernel, sample),
        out_shape=[jax.ShapeDtypeStruct((rows, width), F32), jax.ShapeDtypeStruct((rows, width), BF16)],
        in_specs=[vmem] * 6,
        out_specs=[vmem, vmem],
        compiler_params=pltpu.CompilerParams(vmem_limit_bytes=16 * MIB),
        cost_estimate=cost(1),
        name="gather_tokens",
    )(mixed, feat, token, wo, agg, gain)


def turn_kernel(orders, *refs):
    *halves, out, tall = refs
    rows = out.shape[0] // HEADS
    me = lax.axis_index("sample")
    at = 0
    for near, far, bits in zip(halves[::2], halves[1::2], orders):
        half, cols, wide = near.shape
        for j in range(2 * half):
            tall[j * cols : (j + 1) * cols, at : at + wide] = block_of(near, far, bits, me, j).astype(F32)
        at += wide
    for g in range(rows // SUB):
        turned = tall[:, g * LANES : (g + 1) * LANES].T
        for h in range(HEADS):
            out[h * rows + g * SUB : h * rows + (g + 1) * SUB] = turned[h * SUB : (h + 1) * SUB]


def turn_bias(orders, halves):
    half, cols, _ = halves[0].shape
    keys = 2 * half * cols
    wide = sum(near.shape[2] for near in halves[::2])
    vmem = pl.BlockSpec(memory_space=pltpu.VMEM)
    return pl.pallas_call(
        functools.partial(turn_kernel, orders),
        out_shape=jax.ShapeDtypeStruct((wide, keys), F32),
        in_specs=[vmem] * len(halves),
        out_specs=vmem,
        scratch_shapes=[pltpu.VMEM((keys, wide), F32)],
        compiler_params=pltpu.CompilerParams(vmem_limit_bytes=24 * MIB),
        cost_estimate=cost(1),
        name="turn_bias",
    )(*halves)


def head_groups(width):
    groups = []
    for base in range(0, width, 8 * HEAD_DIM):
        first = base // HEAD_DIM
        groups.append((base, range(first, first + 5)))
        groups.append((base + LANES, range(first + 5, first + 8)))
    return groups


def project_kernel(near, far, wq, wk, wv, wg, q, kt, v, gate):
    half, rows, width = near.shape
    me = lax.axis_index("row")
    x = jnp.concatenate([block_of(near, far, bits_of(2 * half), me, j).astype(F32) for j in range(2 * half)], axis=0).astype(BF16)
    own = near[0]
    q[...] = dot(own, wq[...]).astype(BF16)
    gate[...] = jax.nn.sigmoid(dot(own, wg[...]))
    for c in range(0, width, 2 * LANES):
        kt[c : c + 2 * LANES] = dot(x, wk[:, c : c + 2 * LANES]).T.astype(BF16)
    v[...] = dot(x, wv[...]).astype(BF16)


def project(near, far, wq, wk, wv, wg):
    half, rows, width = near.shape
    keys = 2 * half * rows
    vmem = pl.BlockSpec(memory_space=pltpu.VMEM)
    return pl.pallas_call(
        project_kernel,
        out_shape=[
            jax.ShapeDtypeStruct((rows, width), BF16),
            jax.ShapeDtypeStruct((width, keys), BF16),
            jax.ShapeDtypeStruct((keys, width), BF16),
            jax.ShapeDtypeStruct((rows, width), F32),
        ],
        in_specs=[vmem] * 6,
        out_specs=[vmem] * 4,
        compiler_params=pltpu.CompilerParams(vmem_limit_bytes=24 * MIB),
        cost_estimate=cost(2),
        name="project",
    )(near, far, wq, wk, wv, wg)


def attend_kernel(q, kt, v, gate, token_in, bias, wo, *rest):
    *earlier, out = rest
    rows, width = token_in.shape
    scale = 1.0 / HEAD_DIM**0.5
    lane = iota((rows, 2 * LANES), 1)
    work = [(base, h) for base, heads in head_groups(width) for h in heads]

    def channels(base, h):
        low = h * HEAD_DIM - base
        return (lane >= low) & (lane < low + HEAD_DIM)

    def score(item):
        base, h = item
        mine = q[:, base : base + 2 * LANES]
        mine = jnp.where(channels(base, h), mine, jnp.zeros_like(mine))
        return item, dot(mine, kt[base : base + 2 * LANES]) * scale + bias[h * rows : (h + 1) * rows]

    def soften(item):
        place, sc = item
        e = jnp.exp(sc - jnp.max(sc, -1, keepdims=True))
        return place, e.astype(BF16), inverse(jnp.sum(e, -1, keepdims=True))

    mixes = {}

    def mix(item):
        (base, h), e, share = item
        o = dot(e, v[:, base : base + 2 * LANES]) * share
        mixes[base] = jnp.where(channels(base, h), o, mixes.get(base, 0.0))

    skewed(work, [score, soften, mix])
    tiles = {}
    for base, _ in head_groups(width):
        for t in range(2):
            at = base + t * LANES
            part = mixes[base][:, t * LANES : (t + 1) * LANES]
            tiles[at] = tiles[at] + part if at in tiles else part
    gated = jnp.concatenate([tiles[at] for at in range(0, width, LANES)], axis=1) * gate[...]
    res = (token_in[...] + dot(gated.astype(BF16), wo[...])).astype(BF16)
    if earlier:
        for s, ref in enumerate(earlier):
            out[s] = ref[...]
        out[len(earlier)] = res
    else:
        out[...] = res


def attend(q, kt, v, gate, token_in, bias, wo, earlier):
    rows, width = token_in.shape
    vmem = pl.BlockSpec(memory_space=pltpu.VMEM)
    shape = (len(earlier) + 1, rows, width) if earlier else (rows, width)
    return pl.pallas_call(
        attend_kernel,
        out_shape=jax.ShapeDtypeStruct(shape, BF16),
        in_specs=[vmem] * (7 + len(earlier)),
        out_specs=vmem,
        compiler_params=pltpu.CompilerParams(vmem_limit_bytes=24 * MIB),
        cost_estimate=cost(3),
        name="attend",
    )(q, kt, v, gate, token_in, bias, wo, *earlier)


def shards(
    atom_feat,
    atom_token,
    pair_cond,
    token_mask,
    atom_wq,
    atom_wk,
    atom_wv,
    atom_wo,
    agg_weight,
    pair_weight,
    token_gain,
    query_weight,
    key_weight,
    value_weight,
    gate_weight,
    out_weight,
):
    samples, atoms, _ = atom_feat.shape
    rows = pair_cond.shape[0]
    ranks = lax.axis_size("row")
    up = [(i, i + 1) for i in range(ranks - 1)]
    down = [(j, i) for i, j in up]
    before = lax.ppermute(atom_feat[:, atoms - RIM :], "row", up)
    behind = lax.ppermute(atom_feat[:, :RIM], "row", down)
    bits = bits_of(lax.axis_size("sample"))
    orders = [bits, bits[-1:] + bits[:-1]]
    held = [part[None] for part in pair_bias(pair_cond, token_mask, pair_weight)]

    def wider(step, *others):
        got = after([swap(h, "sample", order[step]) for h, order in zip(held, orders)], *others)
        return [jnp.concatenate([h, g], axis=0) for h, g in zip(held, got)]

    row_bits = bits_of(ranks)
    norms, inputs = [], []
    step = 0
    for s in range(samples):
        mixed = atom_attention(s, atom_feat, before, behind, atom_wq, atom_wk, atom_wv)
        if step < len(bits) - 1:
            held = wider(step, mixed)
            step += 1
            mixed = after(mixed, held)
        if s:
            norms[-1] = jnp.concatenate([norms[-1], after(swap(norms[-1], "row", row_bits[0]), mixed)], axis=0)
            mixed = after(mixed, norms[-1])
        token_in, token_norm = gather_tokens(s, mixed, atom_feat, atom_token, atom_wo, agg_weight, token_gain, rows)
        inputs.append(token_in)
        norms.append(token_norm[None])
        before = after(before, token_norm)
    while step < len(bits) - 1:
        held = wider(step)
        step += 1
    halves = []
    for h, order in zip(held, orders):
        halves += [h, swap(h, "sample", order[-1])]
    parts = []
    for s in range(samples):
        near = norms[s]
        for i, far in enumerate(row_bits[:-1]):
            if near.shape[0] == 1 << i:
                got = swap(near, "row", far)
                near = jnp.concatenate([near, after(got, *parts[-1]) if parts else got], axis=0)
        norms[s] = near
        if s == samples - 1:
            halves = after(halves, near)
            bias = turn_bias(orders, halves)
        parts.append(project(near, swap(near, "row", row_bits[-1]), query_weight, key_weight, value_weight, gate_weight))
    done = []
    for s, part in enumerate(parts):
        earlier = done if s == samples - 1 else []
        done.append(attend(*part, inputs[s], bias, out_weight, earlier))
    return done[-1]


def solution(mesh):
    placed = (
        P("sample", "row", None),
        P("row"),
        P("row", "sample", None),
        P("sample"),
    ) + (P(),) * 12
    return jax.shard_map(
        shards, mesh=mesh, in_specs=placed, out_specs=P("sample", "row", None), check_vma=False
    )
```

time: 48.7 us -> 47.8 us (0.982)
  blocking collectives: 9.46 us -> 0 us
  starting transfers between devices: 11.6 us -> 16 us
  waiting for transfers between devices: 0.41 us -> 3.52 us
  Pallas kernels: 21.9 us -> 23.4 us
  local copies, waits for them, and re-layouts: 4.71 us -> 3.97 us
    all_gather x1 -> x0, blocking collectives: 9.46 us -> none  [shards(): norm_all = lax.all_gather(token_norm, 'row', axis=0)]
    ppermute x4 -> x11, starting transfers between devices: 8.58 us -> 13.7 us  [the longest x10 12.4 us: swap(): lax.ppermute(held, axis, [(i, i ^ far) for i in range(lax.axis_size(axis))])]
    ppermute x4 -> x11, waiting for transfers between devices: 0.4 us -> 3.51 us  [the longest x10 3.51 us: swap(): lax.ppermute(held, axis, [(i, i ^ far) for i in range(lax.axis_size(axis))])]
    pallas_call x3 -> x10, Pallas kernels: 21.9 us -> 23.4 us  [the longest x2 10.4 us: atom_attention(): pl.pallas_call(functools.partial(atom_kernel, sample), out_shape=jax.Shap...]
    reshape x2 -> x0, local copies, waits for them, and re-layouts: 1.39 us -> none  [the longest x1 0.7 us: atom_stage(): token.reshape(1, atoms)]
    unnamed x24 -> x32, local copies, waits for them, and re-layouts: 2.47 us -> 3.21 us
    ppermute x1, starting transfers between devices: 3.03 us -> 2.35 us  [shards(): before = lax.ppermute(atom_feat[:, atoms - RIM:], 'row', up)]
  transfers between devices with their start and end apart: 5 -> 12, of which waited for: 1 -> 1; matrix products, arithmetic and copies ran while one was open for 5% -> 0% of each run, Pallas kernels for 20% -> 42%
where the time goes in v2:
time: 47.8 us; the launch traced here: 47.4 us
  Pallas kernels  23.4 us (49%)
  starting transfers between devices  16 us (33%)
  local copies, waits for them, and re-layouts  3.97 us (8%)
  waiting for transfers between devices  3.52 us (7%)
    ppermute x10, starting transfers between devices, swap(): lax.ppermute(held, axis, [(i, i ^ far) for i in range(lax.axis_size(axis))])  12.4 us
    pallas_call x2, Pallas kernels, atom_attention(): pl.pallas_call(functools.partial(atom_kernel, sample), out_shape=jax.Shap...  10.4 us
    pallas_call x2, Pallas kernels, attend(): pl.pallas_call(attend_kernel, out_shape=jax.ShapeDtypeStruct(shape, BF16)...  4.27 us
    pallas_call x2, Pallas kernels, gather_tokens(): pl.pallas_call(functools.partial(gather_kernel, sample), out_shape=[jax.S...  4.04 us
    ppermute x10, waiting for transfers between devices, swap(): lax.ppermute(held, axis, [(i, i ^ far) for i in range(lax.axis_size(axis))])  3.51 us
    unnamed x32, local copies, waits for them, and re-layouts  3.21 us
    pallas_call x2, Pallas kernels, project(): pl.pallas_call(project_kernel, out_shape=[jax.ShapeDtypeStruct((rows, wid...  2.57 us
    ppermute x1, starting transfers between devices, shards(): before = lax.ppermute(atom_feat[:, atoms - RIM:], 'row', up)  2.35 us
  transfers between devices with their start and end apart: 12, of which 1 were waited for; matrix products, arithmetic and copies ran while one was open for 0% of the time, Pallas kernels for 42%

profile of v2, /device:TPU:0, one launch (start us, length us, event | category | flops | bytes accessed | tf_op | source)
XLA Modules:
  0.0 47.4 jit_solution(8374655113195443794)
XLA Ops:
  0.0 0.8 %fusion = (bf16[2,48,128]{2,1,0:T(8,128)(2,1)S(1)}, bf16[2,48,128]{2,1,0:T(8,128)(2,1)S(1)}) fusion(bf16[2,1152,128]{2,1,0:T(8,128)(2,1)} %feat.7), kind=kLoop, calls=%fused_computation.6 | loop fusion | bytes 98304 | tf_op jit(solution)/shard_map/slice | solution.py:403
  0.8 2.3 %collective-permute-start = (bf16[2,48,128]{2,1,0:T(8,128)(2,1)S(1)}, bf16[2,48,128]{2,1,0:T(8,128)(2,1)S(1)}, u32[]{:S(2)}, u32[]{:S(2)}) collective-permute-start(bf16[2,48,128]{2,1,0:T(8,128)(2,1)S(1)} %get-tuple-element.62), channel_id=1, source_target_pairs={{0,8},{8,16},{16,24},{1,9},{9,17},{17,25},{2,10},{10,18},{18,26},{... | collective-permute-start | bytes 73736 | tf_op jit(solution)/shard_map/ppermute | solution.py:402
  3.1 1.3 %collective-permute-start.1 = (bf16[2,48,128]{2,1,0:T(8,128)(2,1)S(1)}, bf16[2,48,128]{2,1,0:T(8,128)(2,1)S(1)}, u32[]{:S(2)}, u32[]{:S(2)}) collective-permute-start(bf16[2,48,128]{2,1,0:T(8,128)(2,1)S(1)} %get-tuple-element.61), channel_id=1, source_target_pairs={{8,0},{16,8},{24,16},{9,1},{17,9},{25,17},{10,2},{18,10},{26,18},{... | collective-permute-start | bytes 73736 | tf_op jit(solution)/shard_map/ppermute | solution.py:403
  4.4 0.0 copy-start.6
  4.4 1.1 %copy-done.6 = bf16[72,36,128]{2,0,1:T(8,128)(2,1)S(1)} copy-done((bf16[72,36,128]{2,0,1:T(8,128)(2,1)S(1)}, bf16[72,36,128]{2,0,1:T(8,128)(2,1)}, u32[]{:S(2)}) %copy-start.6) | copy-done | bytes 663576
  5.5 0.7 %copy-done.13 = bf16[128,16]{0,1:T(8,128)(2,1)S(1)} copy-done((bf16[128,16]{0,1:T(8,128)(2,1)S(1)}, bf16[128,16]{0,1:T(8,128)(2,1)}, u32[]{:S(2)}) %copy-start.13) | copy-done | bytes 4120
  6.2 0.7 %copy-done.15 = s32[36]{0:T(128)S(1)} copy-done((s32[36]{0:T(128)S(1)}, s32[36]{0:T(128)}, u32[]{:S(2)}) %copy-start.15) | copy-done | bytes 168
  6.9 1.7 %pair_bias.1 = (bf16[36,640]{1,0:T(8,128)(2,1)S(1)}, bf16[36,512]{1,0:T(8,128)(2,1)S(1)}) custom-call(bf16[36,72,128]{2,1,0:T(8,128)(2,1)S(1)} %bitcast.16, s32[36]{0:T(128)S(1)} %copy-done.15, bf16[16,128]{1,0:T(8,128)(2,1)S(1)} %bitcast.17), custom_call_target="tpu_custom_call" | custom-call | flops 3300000000 | bytes 1000000 | tf_op jit(solution)/shard_map/pair_bias/pallas_call | solution.py:91
  8.6 3.5 %collective-permute-start.2 = (bf16[1,36,640]{2,1,0:T(8,128)(2,1)S(1)}, bf16[1,36,640]{2,1,0:T(8,128)(2,1)S(1)}, u32[]{:S(2)}, u32[]{:S(2)}) collective-permute-start(bf16[1,36,640]{2,1,0:T(8,128)(2,1)S(1)} %bitcast.6), channel_id=1, source_target_pairs={{0,4},{1,5},{2,6},{3,7},{4,0},{5,1},{6,2},{7,3},{8,12},{9,13},{10,... | collective-permute-start | bytes 138248 | tf_op jit(solution)/shard_map/ppermute | solution.py:108
  12.1 1.6 %collective-permute-start.3 = (bf16[1,36,512]{2,1,0:T(8,128)(2,1)S(1)}, bf16[1,36,512]{2,1,0:T(8,128)(2,1)S(1)}, u32[]{:S(2)}, u32[]{:S(2)}) collective-permute-start(bf16[1,36,512]{2,1,0:T(8,128)(2,1)S(1)} %bitcast.9), channel_id=1, source_target_pairs={{0,1},{1,0},{2,3},{3,2},{4,5},{5,4},{6,7},{7,6},{8,9},{9,8},{10,11... | collective-permute-start | bytes 110600 | tf_op jit(solution)/shard_map/ppermute | solution.py:108
  13.7 5.2 %atom_attention.2.mixed = bf16[128,1152]{1,0:T(8,128)(2,1)S(1)} custom-call(bf16[2,1152,128]{2,1,0:T(8,128)(2,1)S(1)} %copy-done, bf16[2,48,128]{2,1,0:T(8,128)(2,1)S(1)} %collective-permute-done.before, bf16[2,48,128]{2,1,0:T(8,128)(2,1)S(1)} %collective-permute-done.1.after, bf16[128,128]{1,0:T(8,128)(2,1)S(1)} %copy-done.8, ...), custom_call_target="tpu_custom_call" | custom-call | flops 4400000000 | bytes 1000000 | tf_op jit(solution)/shard_map/atom_attention/pallas_call | solution.py:194
  19.0 0.4 collective-permute-start.5
  19.4 1.6 %collective-permute-start.4 = (bf16[2,36,640]{2,1,0:T(8,128)(2,1)S(1)}, bf16[2,36,640]{2,1,0:T(8,128)(2,1)S(1)}, u32[]{:S(2)}, u32[]{:S(2)}) collective-permute-start(bf16[2,36,640]{2,1,0:T(8,128)(2,1)S(1)} %pad_maximum_fusion.4), channel_id=1, source_target_pairs={{0,2},{1,3},{2,0},{3,1},{4,6},{5,7},{6,4},{7,5},{8,10},{9,11},{10,... | collective-permute-start | bytes 276488 | tf_op jit(solution)/shard_map/ppermute | solution.py:108
  21.0 1.9 %gather_tokens.2 = (f32[72,768]{1,0:T(8,128)S(1)}, bf16[72,768]{1,0:T(8,128)(2,1)S(1)}) custom-call(bf16[128,1152]{1,0:T(8,128)(2,1)S(1)} %atom_attention.2.mixed, bf16[2,1152,128]{2,1,0:T(8,128)(2,1)S(1)} %copy-done, s32[1152]{0:T(1024)S(1)} %copy-done.12, bf16[128,128]{1,0:T(8,128)(2,1)S(1)} %copy-done.11, bf16[128,768]{1,0:T(8,128)(2,1)S(1)} %copy-done.7, ...), custom_call_target="tpu_custom_call" | custom-call | flops 1100000000 | bytes 1000000 | tf_op jit(solution)/shard_map/gather_tokens/pallas_call | solution.py:233
  22.9 4.1 %collective-permute-start.6 = (bf16[1,72,768]{2,1,0:T(8,128)(2,1)S(1)}, bf16[1,72,768]{2,1,0:T(8,128)(2,1)S(1)}, u32[]{:S(2)}, u32[]{:S(2)}) collective-permute-start(bf16[1,72,768]{2,1,0:T(8,128)(2,1)S(1)} %bitcast.12), channel_id=1, source_target_pairs={{0,16},{8,24},{16,0},{24,8},{1,17},{9,25},{17,1},{25,9},{2,18},{10... | collective-permute-start | bytes 331784 | tf_op jit(solution)/shard_map/ppermute | solution.py:108
  27.0 5.2 %atom_attention.3.mixed = bf16[128,1152]{1,0:T(8,128)(2,1)S(1)} custom-call(bf16[2,1152,128]{2,1,0:T(8,128)(2,1)S(1)} %copy-done, bf16[2,48,128]{2,1,0:T(8,128)(2,1)S(1)} %collective-permute-done.before, bf16[2,48,128]{2,1,0:T(8,128)(2,1)S(1)} %collective-permute-done.1.after, bf16[128,128]{1,0:T(8,128)(2,1)S(1)} %copy-done.8, ...), custom_call_target="tpu_custom_call" | custom-call | flops 4400000000 | bytes 1000000 | tf_op jit(solution)/shard_map/atom_attention/pallas_call | solution.py:194
  32.3 0.0 copy-start.4
  32.4 0.0 copy-start.1
  32.4 0.0 copy-start.3
  32.4 0.1 collective-permute-start.8
  32.5 0.5 %collective-permute-start.11 = (bf16[4,36,512]{2,1,0:T(8,128)(2,1)S(1)}, bf16[4,36,512]{2,1,0:T(8,128)(2,1)S(1)}, u32[]{:S(2)}, u32[]{:S(2)}) collective-permute-start(bf16[4,36,512]{2,1,0:T(8,128)(2,1)S(1)} %pad_maximum_fusion.3.refs_2_), channel_id=1, source_target_pairs={{0,2},{1,3},{2,0},{3,1},{4,6},{5,7},{6,4},{7,5},{8,10},{9,11},{10,... | collective-permute-start | bytes 442376 | tf_op jit(solution)/shard_map/ppermute | solution.py:108
  33.0 0.5 %collective-permute-start.10 = (bf16[4,36,640]{2,1,0:T(8,128)(2,1)S(1)}, bf16[4,36,640]{2,1,0:T(8,128)(2,1)S(1)}, u32[]{:S(2)}, u32[]{:S(2)}) collective-permute-start(bf16[4,36,640]{2,1,0:T(8,128)(2,1)S(1)} %pad_maximum_fusion.2.refs_0_), channel_id=1, source_target_pairs={{0,1},{1,0},{2,3},{3,2},{4,5},{5,4},{6,7},{7,6},{8,9},{9,8},{10,11... | collective-permute-start | bytes 552968 | tf_op jit(solution)/shard_map/ppermute | solution.py:108
  33.5 2.1 %gather_tokens.3 = (f32[72,768]{1,0:T(8,128)S(1)}, bf16[72,768]{1,0:T(8,128)(2,1)S(1)}) custom-call(bf16[128,1152]{1,0:T(8,128)(2,1)S(1)} %atom_attention.3.mixed, bf16[2,1152,128]{2,1,0:T(8,128)(2,1)S(1)} %copy-done, s32[1152]{0:T(1024)S(1)} %copy-done.12, bf16[128,128]{1,0:T(8,128)(2,1)S(1)} %copy-done.11, bf16[128,768]{1,0:T(8,128)(2,1)S(1)} %copy-done.7, ...), custom_call_target="tpu_custom_call" | custom-call | flops 1100000000 | bytes 1000000 | tf_op jit(solution)/shard_map/gather_tokens/pallas_call | solution.py:233
  35.7 0.1 collective-permute-start.7
  35.8 1.3 %project.2 = (bf16[72,768]{1,0:T(8,128)(2,1)S(1)}, bf16[768,288]{1,0:T(8,128)(2,1)S(1)}, bf16[288,768]{1,0:T(8,128)(2,1)S(1)}, f32[72,768]{1,0:T(8,128)S(1)}) custom-call(bf16[2,72,768]{2,1,0:T(8,128)(2,1)S(1)} %pad_maximum_fusion.near, bf16[2,72,768]{2,1,0:T(8,128)(2,1)S(1)} %collective-permute-done.8.far, bf16[768,768]{1,0:T(8,128)(2,1)S(1)} %copy-done.1, ...), custom_call_target="tpu_custom_call" | custom-call | flops 2200000000 | bytes 1000000 | tf_op jit(solution)/shard_map/project/pallas_call | solution.py:302
  37.1 3.5 %collective-permute-done.7 = bf16[1,72,768]{2,1,0:T(8,128)(2,1)S(1)} collective-permute-done((bf16[1,72,768]{2,1,0:T(8,128)(2,1)S(1)}, bf16[1,72,768]{2,1,0:T(8,128)(2,1)S(1)}, u32[]{:S(2)}, u32[]{:S(2)}) %collective-permute-start.7) | collective-permute-done | bytes 110624 | tf_op jit(solution)/shard_map/ppermute | solution.py:108
  40.6 0.1 collective-permute-start.9
  40.7 0.4 turn_bias.1.bias
  41.1 0.7 %copy-done.5 = bf16[768,768]{1,0:T(8,128)(2,1)S(1)} copy-done((bf16[768,768]{1,0:T(8,128)(2,1)S(1)}, bf16[768,768]{1,0:T(8,128)(2,1)}, u32[]{:S(2)}) %copy-start.5) | copy-done | bytes 1179672
  41.9 1.8 %attend.2.rest_0_ = bf16[72,768]{1,0:T(8,128)(2,1)S(1)} custom-call(bf16[72,768]{1,0:T(8,128)(2,1)S(1)} %get-tuple-element.46.q, bf16[768,288]{1,0:T(8,128)(2,1)S(1)} %get-tuple-element.47.kt, bf16[288,768]{1,0:T(8,128)(2,1)S(1)} %get-tuple-element.48.v, f32[72,768]{1,0:T(8,128)S(1)} %get-tuple-element.49.gate, f32[72,768]{1,0:T(8,128)S(1)} %get-tuple-element.60.token_in, ...), custom_call_target="tpu_custom_call" | custom-call | flops 3300000000 | bytes 1000000 | tf_op jit(solution)/shard_map/attend/pallas_call | solution.py:368
  43.7 1.3 %project.3 = (bf16[72,768]{1,0:T(8,128)(2,1)S(1)}, bf16[768,288]{1,0:T(8,128)(2,1)S(1)}, bf16[288,768]{1,0:T(8,128)(2,1)S(1)}, f32[72,768]{1,0:T(8,128)S(1)}) custom-call(bf16[2,72,768]{2,1,0:T(8,128)(2,1)S(1)} %pad_maximum_fusion.1.near, bf16[2,72,768]{2,1,0:T(8,128)(2,1)S(1)} %collective-permute-done.9.far, bf16[768,768]{1,0:T(8,128)(2,1)S(1)} %copy-done.1, ...), custom_call_target="tpu_custom_call" | custom-call | flops 2200000000 | bytes 1000000 | tf_op jit(solution)/shard_map/project/pallas_call | solution.py:302
  45.0 2.5 %attend.3 = bf16[2,72,768]{2,1,0:T(8,128)(2,1)} custom-call(bf16[72,768]{1,0:T(8,128)(2,1)S(1)} %get-tuple-element.51.q, bf16[768,288]{1,0:T(8,128)(2,1)S(1)} %get-tuple-element.52.kt, bf16[288,768]{1,0:T(8,128)(2,1)S(1)} %get-tuple-element.53.v, f32[72,768]{1,0:T(8,128)S(1)} %get-tuple-element.54.gate, f32[72,768]{1,0:T(8,128)S(1)} %get-tuple-element.55.token_in, ...), custom_call_target="tpu_custom_call" | custom-call | flops 3300000000 | bytes 1000000 | tf_op jit(solution)/shard_map/attend/pallas_call | solution.py:368
  (41 shorter events, 0.2 us)
Async XLA Ops:
  0.8 12.9 %collective-permute-start = (bf16[2,48,128]{2,1,0:T(8,128)(2,1)S(1)}, bf16[2,48,128]{2,1,0:T(8,128)(2,1)S(1)}, u32[]{:S(2)}, u32[]{:S(2)}) collective-permute-start(bf16[2,48,128]{2,1,0:T(8,128)(2,1)S(1)} %get-tuple-element.62), channel_id=1, source_target_pairs={{0,8},{8,16},{16,24},{1,9},{9,17},{17,25},{2,10},{10,18},{18,26},{... | collective-permute-start | bytes 73736 | tf_op jit(solution)/shard_map/ppermute | solution.py:402
  3.1 10.6 %collective-permute-start.1 = (bf16[2,48,128]{2,1,0:T(8,128)(2,1)S(1)}, bf16[2,48,128]{2,1,0:T(8,128)(2,1)S(1)}, u32[]{:S(2)}, u32[]{:S(2)}) collective-permute-start(bf16[2,48,128]{2,1,0:T(8,128)(2,1)S(1)} %get-tuple-element.61), channel_id=1, source_target_pairs={{8,0},{16,8},{24,16},{9,1},{17,9},{25,17},{10,2},{18,10},{26,18},{... | collective-permute-start | bytes 73736 | tf_op jit(solution)/shard_map/ppermute | solution.py:403
  4.4 1.1 %copy-start.6 = (bf16[72,36,128]{2,0,1:T(8,128)(2,1)S(1)}, bf16[72,36,128]{2,0,1:T(8,128)(2,1)}, u32[]{:S(2)}) copy-start(bf16[72,36,128]{2,0,1:T(8,128)(2,1)} %param.18) | copy-start | bytes 1990660
  5.5 0.7 %copy-start.13 = (bf16[128,16]{0,1:T(8,128)(2,1)S(1)}, bf16[128,16]{0,1:T(8,128)(2,1)}, u32[]{:S(2)}) copy-start(bf16[128,16]{0,1:T(8,128)(2,1)} %param.25) | copy-start | bytes 12292
  6.2 0.7 %copy-start.15 = (s32[36]{0:T(128)S(1)}, s32[36]{0:T(128)}, u32[]{:S(2)}) copy-start(s32[36]{0:T(128)} %mask.1) | copy-start | bytes 436
  6.9 6.8 %copy-start = (bf16[2,1152,128]{2,1,0:T(8,128)(2,1)S(1)}, bf16[2,1152,128]{2,1,0:T(8,128)(2,1)}, u32[]{:S(2)}) copy-start(bf16[2,1152,128]{2,1,0:T(8,128)(2,1)} %feat.7) | copy-start | bytes 1769476
  6.9 6.8 %copy-start.8 = (bf16[128,128]{1,0:T(8,128)(2,1)S(1)}, bf16[128,128]{1,0:T(8,128)(2,1)}, u32[]{:S(2)}) copy-start(bf16[128,128]{1,0:T(8,128)(2,1)} %wq.5) | copy-start | bytes 98308
  6.9 6.8 %copy-start.9 = (bf16[128,128]{1,0:T(8,128)(2,1)S(1)}, bf16[128,128]{1,0:T(8,128)(2,1)}, u32[]{:S(2)}) copy-start(bf16[128,128]{1,0:T(8,128)(2,1)} %wk.5) | copy-start | bytes 98308
  6.9 6.8 %copy-start.10 = (bf16[128,128]{1,0:T(8,128)(2,1)S(1)}, bf16[128,128]{1,0:T(8,128)(2,1)}, u32[]{:S(2)}) copy-start(bf16[128,128]{1,0:T(8,128)(2,1)} %wv.5) | copy-start | bytes 98308
  8.6 10.3 %collective-permute-start.2 = (bf16[1,36,640]{2,1,0:T(8,128)(2,1)S(1)}, bf16[1,36,640]{2,1,0:T(8,128)(2,1)S(1)}, u32[]{:S(2)}, u32[]{:S(2)}) collective-permute-start(bf16[1,36,640]{2,1,0:T(8,128)(2,1)S(1)} %bitcast.6), channel_id=1, source_target_pairs={{0,4},{1,5},{2,6},{3,7},{4,0},{5,1},{6,2},{7,3},{8,12},{9,13},{10,... | collective-permute-start | bytes 138248 | tf_op jit(solution)/shard_map/ppermute | solution.py:108
  12.1 8.9 %copy-start.7 = (bf16[128,768]{1,0:T(8,128)(2,1)S(1)}, bf16[128,768]{1,0:T(8,128)(2,1)}, u32[]{:S(2)}) copy-start(bf16[128,768]{1,0:T(8,128)(2,1)} %agg.3) | copy-start | bytes 589828
  12.1 8.9 %copy-start.11 = (bf16[128,128]{1,0:T(8,128)(2,1)S(1)}, bf16[128,128]{1,0:T(8,128)(2,1)}, u32[]{:S(2)}) copy-start(bf16[128,128]{1,0:T(8,128)(2,1)} %wo.5) | copy-start | bytes 98308
  12.1 8.9 %copy-start.12 = (s32[1152]{0:T(1024)S(1)}, s32[1152]{0:T(1024)}, u32[]{:S(2)}) copy-start(s32[1152]{0:T(1024)} %token_.3) | copy-start | bytes 13828
  12.1 8.9 %copy-start.14 = (f32[768]{0:T(1024)S(1)}, f32[768]{0:T(1024)}, u32[]{:S(2)}) copy-start(f32[768]{0:T(1024)} %gain.3) | copy-start | bytes 9220
  12.1 6.8 %collective-permute-start.3 = (bf16[1,36,512]{2,1,0:T(8,128)(2,1)S(1)}, bf16[1,36,512]{2,1,0:T(8,128)(2,1)S(1)}, u32[]{:S(2)}, u32[]{:S(2)}) collective-permute-start(bf16[1,36,512]{2,1,0:T(8,128)(2,1)S(1)} %bitcast.9), channel_id=1, source_target_pairs={{0,1},{1,0},{2,3},{3,2},{4,5},{5,4},{6,7},{7,6},{8,9},{9,8},{10,11... | collective-permute-start | bytes 110600 | tf_op jit(solution)/shard_map/ppermute | solution.py:108
  19.0 13.2 %collective-permute-start.5 = (bf16[2,36,512]{2,1,0:T(8,128)(2,1)S(1)}, bf16[2,36,512]{2,1,0:T(8,128)(2,1)S(1)}, u32[]{:S(2)}, u32[]{:S(2)}) collective-permute-start(bf16[2,36,512]{2,1,0:T(8,128)(2,1)S(1)} %pad_maximum_fusion.5), channel_id=1, source_target_pairs={{0,4},{1,5},{2,6},{3,7},{4,0},{5,1},{6,2},{7,3},{8,12},{9,13},{10,... | collective-permute-start | bytes 221192 | tf_op jit(solution)/shard_map/ppermute | solution.py:108
  19.4 12.9 %collective-permute-start.4 = (bf16[2,36,640]{2,1,0:T(8,128)(2,1)S(1)}, bf16[2,36,640]{2,1,0:T(8,128)(2,1)S(1)}, u32[]{:S(2)}, u32[]{:S(2)}) collective-permute-start(bf16[2,36,640]{2,1,0:T(8,128)(2,1)S(1)} %pad_maximum_fusion.4), channel_id=1, source_target_pairs={{0,2},{1,3},{2,0},{3,1},{4,6},{5,7},{6,4},{7,5},{8,10},{9,11},{10,... | collective-permute-start | bytes 276488 | tf_op jit(solution)/shard_map/ppermute | solution.py:108
  22.9 9.4 %collective-permute-start.6 = (bf16[1,72,768]{2,1,0:T(8,128)(2,1)S(1)}, bf16[1,72,768]{2,1,0:T(8,128)(2,1)S(1)}, u32[]{:S(2)}, u32[]{:S(2)}) collective-permute-start(bf16[1,72,768]{2,1,0:T(8,128)(2,1)S(1)} %bitcast.12), channel_id=1, source_target_pairs={{0,16},{8,24},{16,0},{24,8},{1,17},{9,25},{17,1},{25,9},{2,18},{10... | collective-permute-start | bytes 331784 | tf_op jit(solution)/shard_map/ppermute | solution.py:108
  32.3 3.5 %copy-start.4 = (bf16[768,768]{1,0:T(8,128)(2,1)S(1)}, bf16[768,768]{1,0:T(8,128)(2,1)}, u32[]{:S(2)}) copy-start(bf16[768,768]{1,0:T(8,128)(2,1)} %wg.3) | copy-start | bytes 3538948
  32.4 3.4 %copy-start.1 = (bf16[768,768]{1,0:T(8,128)(2,1)S(1)}, bf16[768,768]{1,0:T(8,128)(2,1)}, u32[]{:S(2)}) copy-start(bf16[768,768]{1,0:T(8,128)(2,1)} %wq.7) | copy-start | bytes 3538948
  32.4 3.4 %copy-start.2 = (bf16[768,768]{1,0:T(8,128)(2,1)S(1)}, bf16[768,768]{1,0:T(8,128)(2,1)}, u32[]{:S(2)}) copy-start(bf16[768,768]{1,0:T(8,128)(2,1)} %wk.7) | copy-start | bytes 3538948
  32.4 3.4 %copy-start.3 = (bf16[768,768]{1,0:T(8,128)(2,1)S(1)}, bf16[768,768]{1,0:T(8,128)(2,1)}, u32[]{:S(2)}) copy-start(bf16[768,768]{1,0:T(8,128)(2,1)} %wv.7) | copy-start | bytes 3538948
  32.4 3.3 %collective-permute-start.8 = (bf16[2,72,768]{2,1,0:T(8,128)(2,1)S(1)}, bf16[2,72,768]{2,1,0:T(8,128)(2,1)S(1)}, u32[]{:S(2)}, u32[]{:S(2)}) collective-permute-start(bf16[2,72,768]{2,1,0:T(8,128)(2,1)S(1)} %pad_maximum_fusion.near), channel_id=1, source_target_pairs={{0,8},{8,0},{16,24},{24,16},{1,9},{9,1},{17,25},{25,17},{2,10},{10... | collective-permute-start | bytes 663560 | tf_op jit(solution)/shard_map/ppermute | solution.py:108
  32.5 8.2 %collective-permute-start.11 = (bf16[4,36,512]{2,1,0:T(8,128)(2,1)S(1)}, bf16[4,36,512]{2,1,0:T(8,128)(2,1)S(1)}, u32[]{:S(2)}, u32[]{:S(2)}) collective-permute-start(bf16[4,36,512]{2,1,0:T(8,128)(2,1)S(1)} %pad_maximum_fusion.3.refs_2_), channel_id=1, source_target_pairs={{0,2},{1,3},{2,0},{3,1},{4,6},{5,7},{6,4},{7,5},{8,10},{9,11},{10,... | collective-permute-start | bytes 442376 | tf_op jit(solution)/shard_map/ppermute | solution.py:108
  33.0 7.7 %collective-permute-start.10 = (bf16[4,36,640]{2,1,0:T(8,128)(2,1)S(1)}, bf16[4,36,640]{2,1,0:T(8,128)(2,1)S(1)}, u32[]{:S(2)}, u32[]{:S(2)}) collective-permute-start(bf16[4,36,640]{2,1,0:T(8,128)(2,1)S(1)} %pad_maximum_fusion.2.refs_0_), channel_id=1, source_target_pairs={{0,1},{1,0},{2,3},{3,2},{4,5},{5,4},{6,7},{7,6},{8,9},{9,8},{10,11... | collective-permute-start | bytes 552968 | tf_op jit(solution)/shard_map/ppermute | solution.py:108
  35.7 4.9 %collective-permute-start.7 = (bf16[1,72,768]{2,1,0:T(8,128)(2,1)S(1)}, bf16[1,72,768]{2,1,0:T(8,128)(2,1)S(1)}, u32[]{:S(2)}, u32[]{:S(2)}) collective-permute-start(bf16[1,72,768]{2,1,0:T(8,128)(2,1)S(1)} %bitcast.14), channel_id=1, source_target_pairs={{0,16},{8,24},{16,0},{24,8},{1,17},{9,25},{17,1},{25,9},{2,18},{10... | collective-permute-start | bytes 331784 | tf_op jit(solution)/shard_map/ppermute | solution.py:108
  40.6 1.3 %copy-start.5 = (bf16[768,768]{1,0:T(8,128)(2,1)S(1)}, bf16[768,768]{1,0:T(8,128)(2,1)}, u32[]{:S(2)}) copy-start(bf16[768,768]{1,0:T(8,128)(2,1)} %wo.7) | copy-start | bytes 3538948
  40.6 3.1 %collective-permute-start.9 = (bf16[2,72,768]{2,1,0:T(8,128)(2,1)S(1)}, bf16[2,72,768]{2,1,0:T(8,128)(2,1)S(1)}, u32[]{:S(2)}, u32[]{:S(2)}) collective-permute-start(bf16[2,72,768]{2,1,0:T(8,128)(2,1)S(1)} %pad_maximum_fusion.1.near), channel_id=1, source_target_pairs={{0,8},{8,0},{16,24},{24,16},{1,9},{9,1},{17,25},{25,17},{2,10},{10... | collective-permute-start | bytes 663560 | tf_op jit(solution)/shard_map/ppermute | solution.py:108

commit v3 on v2

--- a/solution.py
+++ b/solution.py
@@ -60,10 +60,26 @@
     return held
 
 
-def bias_kernel(pair, mask, weight, out, other, normed):
+def bias_kernel(feat, pair_hbm, mask_hbm, weight_hbm, out, first, last, pair, mask, weight, normed, sems):
     cols, rows, chans = pair.shape
-    for k in range(cols):
-        normed[k] = layer_norm(pair[k].astype(F32))
+    atoms = feat.shape[1]
+    moves = [
+        (weight_hbm, weight),
+        (mask_hbm, mask),
+        (feat.at[:, :RIM], first),
+        (feat.at[:, atoms - RIM :], last),
+    ]
+    step = cols // 4
+    moves += [(pair_hbm.at[k : k + step], pair.at[k : k + step]) for k in range(0, cols, step)]
+    copies = [pltpu.make_async_copy(src, dst, sems.at[i]) for i, (src, dst) in enumerate(moves)]
+    for copy in copies:
+        copy.start()
+    for i, copy in enumerate(copies[4:]):
+        copy.wait()
+        for k in range(i * step, (i + 1) * step):
+            normed[k] = layer_norm(pair[k].astype(F32))
+    for copy in copies[:4]:
+        copy.wait()
     spread = (iota((HEADS, LANES), 1) // SUB == iota((HEADS, LANES), 0)).astype(BF16)
     wide = lax.dot_general(weight[...], spread, (((0,), (0,)), ((), ())), preferred_element_type=F32).astype(BF16)
     tall = cols * SUB
@@ -78,26 +94,33 @@
         x = normed[:, g * SUB : (g + 1) * SUB].reshape(tall, chans).astype(BF16)
         raw = jnp.where(open_key | (apart == g * SUB), dot(x, wide), -30000.0)
         raw = jnp.where(mine, raw, 0.0).astype(BF16)
-        at = g * LANES
-        ref, at = (out, at) if at < out.shape[1] else (other, at - out.shape[1])
-        ref[:, at : at + LANES] = dot(picked, raw).astype(BF16)
-
-
-def pair_bias(pair_cond, token_mask, pair_weight):
+        out[:, g * LANES : (g + 1) * LANES] = dot(picked, raw).astype(BF16)
+
+
+def pair_bias(feat, pair_cond, token_mask, pair_weight):
     rows, cols, chans = pair_cond.shape
-    wide = rows * HEADS
-    first = (wide // LANES + 1) // 2 * LANES
-    vmem = pl.BlockSpec(memory_space=pltpu.VMEM)
+    edge = (feat.shape[0], RIM, feat.shape[2])
+    hbm = pl.BlockSpec(memory_space=pltpu.HBM)
     return pl.pallas_call(
         bias_kernel,
-        out_shape=[jax.ShapeDtypeStruct((cols, first), BF16), jax.ShapeDtypeStruct((cols, wide - first), BF16)],
-        in_specs=[vmem] * 3,
-        out_specs=[vmem] * 2,
-        scratch_shapes=[pltpu.VMEM((cols, rows, chans), F32)],
-        compiler_params=pltpu.CompilerParams(vmem_limit_bytes=16 * MIB),
+        out_shape=[
+            jax.ShapeDtypeStruct((cols, rows * HEADS), BF16),
+            jax.ShapeDtypeStruct(edge, BF16),
+            jax.ShapeDtypeStruct(edge, BF16),
+        ],
+        in_specs=[hbm] * 4,
+        out_specs=[pl.BlockSpec(memory_space=pltpu.VMEM)] * 3,
+        scratch_shapes=[
+            pltpu.VMEM((cols, rows, chans), BF16),
+            pltpu.VMEM((cols,), jnp.int32),
+            pltpu.VMEM((HEADS, chans), BF16),
+            pltpu.VMEM((cols, rows, chans), F32),
+            pltpu.SemaphoreType.DMA((8,)),
+        ],
+        compiler_params=pltpu.CompilerParams(vmem_limit_bytes=60 * MIB),
         cost_estimate=cost(3),
         name="pair_bias",
-    )(jnp.transpose(pair_cond, (1, 0, 2)), token_mask, pair_weight.T)
+    )(feat, jnp.transpose(pair_cond, (1, 0, 2)), token_mask, pair_weight.T)
 
 
 def after(value, *others):
@@ -118,89 +141,70 @@
     return [devices >> i for i in range(1, devices.bit_length())]
 
 
-def atom_kernel(sample, feat, before, after, wq, wk, wv, mixed, ns, ks, qt, vt):
+def atom_kernel(sample, feat, before, after, wq, wk, wv, mixed, qs, ks, vs):
     atoms, chans = feat.shape[1:]
     rank = lax.axis_index("row")
     at_start = rank == 0
     at_end = rank == lax.axis_size("row") - 1
-    ns[:RIM] = layer_norm(before[sample].astype(F32)).astype(BF16)
+    wqkv = jnp.concatenate([wq[...], wk[...], wv[...]], axis=1)
+    for ref, at in ((before, 0), (after, RIM + atoms)):
+        kv = dot(layer_norm(ref[sample].astype(F32)).astype(BF16), wqkv[:, chans:]).astype(BF16)
+        ks[at : at + RIM] = kv[:, :chans]
+        vs[at : at + RIM] = kv[:, chans:]
     for c in range(0, atoms, LANES):
-        ns[RIM + c : RIM + c + LANES] = layer_norm(feat[sample, c : c + LANES].astype(F32)).astype(BF16)
-    ns[RIM + atoms : 2 * RIM + atoms] = layer_norm(after[sample].astype(F32)).astype(BF16)
-    padded = ns.shape[0]
-    ns[atoms + 2 * RIM :] = jnp.zeros((padded - atoms - 2 * RIM, chans), BF16)
-    wqv = jnp.concatenate([wq[...].astype(F32).T, wv[...].astype(F32).T], axis=0).astype(BF16)
-    for c in range(0, padded, LANES):
-        normed = ns[c : c + LANES]
-        ks[c : c + LANES] = dot(normed, wk[...]).astype(BF16)
-        qv = dot(wqv, normed.astype(F32).T.astype(BF16)).astype(BF16)
-        qt[:, c : c + LANES] = qv[:chans]
-        vt[:, c : c + LANES] = qv[chans:]
+        qkv = dot(layer_norm(feat[sample, c : c + LANES].astype(F32)).astype(BF16), wqkv).astype(BF16)
+        qs[c : c + LANES] = qkv[:, :chans]
+        ks[RIM + c : RIM + c + LANES] = qkv[:, chans : 2 * chans]
+        vs[RIM + c : RIM + c + LANES] = qkv[:, 2 * chans :]
     rate = math.log2(math.e) / AHEAD_DIM**0.5
     tall = AHEADS * QWIN
-    group = LANES // QWIN
-    wide = group * tall
+    head_of = iota((QWIN, chans), 1) // AHEAD_DIM
+    keyat = iota((tall, KWIN), 1)
     batch = 2
-    keyat = iota((KWIN, tall), 0)
-    col = iota((2 * LANES, wide), 1)
-    spread = (iota((2 * LANES, wide), 0) == RIM + col // tall * QWIN + col % QWIN).astype(BF16)
-    row = iota((wide, LANES), 0)
-    fold = (iota((wide, LANES), 1) == row // tall * QWIN + row % QWIN).astype(BF16)
-    own_head = iota((chans, wide), 0) // AHEAD_DIM == iota((chans, wide), 1) % tall // QWIN
-    queries, sums = {}, {}
 
     def score(first):
-        base = first // LANES * LANES
-        if base not in queries:
-            queries[base] = jnp.where(own_head, dot(qt[:, base : base + 2 * LANES], spread), 0.0).astype(BF16)
         out = []
         for at in range(first, first + batch * QWIN, QWIN):
-            col = (at - base) // QWIN * tall
-            s = dot(ks[at : at + KWIN], queries[base][:, col : col + tall])
+            q = qs[at : at + QWIN]
+            q = jnp.concatenate([jnp.where(head_of == h, q, jnp.zeros_like(q)) for h in range(AHEADS)], axis=0)
+            s = dot_nt(q, ks[at : at + KWIN])
             if at < RIM:
                 s = jnp.where(at_start & (keyat < RIM - at), -jnp.inf, s)
             if at + KWIN > RIM + atoms:
                 s = jnp.where(at_end & (keyat >= RIM + atoms - at), -jnp.inf, s)
             out.append(s)
-        return first, out
+        return first, jnp.concatenate(out, axis=0)
 
     def soften(item):
-        first, scores = item
-        out = []
-        for s in scores:
-            e = jnp.exp2((s - jnp.max(s, 0, keepdims=True)) * rate)
-            out.append((e.astype(BF16), 1.0 / jnp.sum(e, 0, keepdims=True)))
-        return first, out
+        first, s = item
+        e = jnp.exp2((s - jnp.max(s, -1, keepdims=True)) * rate)
+        return first, e.astype(BF16), inverse(jnp.sum(e, -1, keepdims=True))
 
     def mix(item):
-        first, parts = item
-        base = first // LANES * LANES
-        for i, (e, share) in enumerate(parts):
-            skip = first + i * QWIN - base
-            pads = [jnp.zeros((n, tall), BF16) for n in (skip, 2 * LANES - KWIN - skip)]
-            e = jnp.concatenate([p for p in (pads[0], e, pads[1]) if p.shape[0]], axis=0)
-            o = dot(vt[:, base : base + 2 * LANES], e) * share
-            sums.setdefault(base, []).append(jnp.where(own_head[:, :tall], o, 0.0).astype(BF16))
-        if len(sums[base]) == group:
-            mixed[:, base : base + LANES] = dot(jnp.concatenate(sums[base], axis=1), fold).astype(BF16)
+        first, e, share = item
+        for i in range(batch):
+            at = first + i * QWIN
+            o = dot(e[i * tall : (i + 1) * tall], vs[at : at + KWIN]) * share[i * tall : (i + 1) * tall]
+            acc = o[:QWIN]
+            for h in range(1, AHEADS):
+                acc = jnp.where(head_of == h, o[h * QWIN : (h + 1) * QWIN], acc)
+            mixed[at : at + QWIN] = acc.astype(BF16)
 
     skewed(range(0, atoms, batch * QWIN), [score, soften, mix])
 
 
 def atom_attention(sample, feat, before, after, wq, wk, wv):
     atoms, chans = feat.shape[1:]
-    padded = pl.cdiv(atoms + 2 * RIM, LANES) * LANES
     vmem = pl.BlockSpec(memory_space=pltpu.VMEM)
     return pl.pallas_call(
         functools.partial(atom_kernel, sample),
-        out_shape=jax.ShapeDtypeStruct((chans, atoms), BF16),
+        out_shape=jax.ShapeDtypeStruct((atoms, chans), BF16),
         in_specs=[vmem] * 6,
         out_specs=vmem,
         scratch_shapes=[
-            pltpu.VMEM((padded, chans), BF16),
-            pltpu.VMEM((padded, chans), BF16),
-            pltpu.VMEM((chans, padded), BF16),
-            pltpu.VMEM((chans, padded), BF16),
+            pltpu.VMEM((atoms, chans), BF16),
+            pltpu.VMEM((atoms + 2 * RIM, chans), BF16),
+            pltpu.VMEM((atoms + 2 * RIM, chans), BF16),
         ],
         compiler_params=pltpu.CompilerParams(vmem_limit_bytes=16 * MIB),
         cost_estimate=cost(4),
@@ -211,13 +215,12 @@
 def gather_kernel(sample, mixed, feat, token, wo, agg, gain, token_in, token_norm):
     atoms = feat.shape[1]
     rows = token_in.shape[0]
-    wo_turned = wo[...].astype(F32).T.astype(BF16)
     local = token[...].reshape(1, atoms) - lax.axis_index("row") * rows
     step = 384
     tsum = jnp.zeros((rows, agg.shape[1]), F32)
     count = jnp.zeros((rows, 1), F32)
     for c in range(0, atoms, step):
-        out = (feat[sample, c : c + step].astype(F32) + dot(wo_turned, mixed[:, c : c + step]).T).astype(BF16)
+        out = (feat[sample, c : c + step].astype(F32) + dot(mixed[c : c + step], wo[...])).astype(BF16)
         hidden = jnp.maximum(dot(out, agg[...]), 0.0).astype(BF16)
         onehot = (iota((rows, step), 0) == local[:, c : c + step]).astype(F32)
         count = count + jnp.sum(onehot, -1, keepdims=True)
@@ -399,11 +402,12 @@
     ranks = lax.axis_size("row")
     up = [(i, i + 1) for i in range(ranks - 1)]
     down = [(j, i) for i, j in up]
-    before = lax.ppermute(atom_feat[:, atoms - RIM :], "row", up)
-    behind = lax.ppermute(atom_feat[:, :RIM], "row", down)
+    bias, first, last = pair_bias(atom_feat, pair_cond, token_mask, pair_weight)
+    before = lax.ppermute(last, "row", up)
+    behind = lax.ppermute(first, "row", down)
     bits = bits_of(lax.axis_size("sample"))
-    orders = [bits, bits[-1:] + bits[:-1]]
-    held = [part[None] for part in pair_bias(pair_cond, token_mask, pair_weight)]
+    orders = [bits]
+    held = [bias[None]]
 
     def wider(step, *others):
         got = after([swap(h, "sample", order[step]) for h, order in zip(held, orders)], *others)

time: 47.8 us -> 43.6 us (0.912)
  local copies, waits for them, and re-layouts: 3.97 us -> 0.08 us
  waiting for transfers between devices: 3.52 us -> 6.31 us
  Pallas kernels: 23.4 us -> 21.4 us
  starting transfers between devices: 16 us -> 15.3 us
    pallas_call x2, Pallas kernels: 10.4 us -> 6.12 us  [atom_attention(): pl.pallas_call(functools.partial(atom_kernel, sample), out_shape=jax.Shap...]
    unnamed x32 -> x28, local copies, waits for them, and re-layouts: 3.21 us -> 0.08 us
    pallas_call x1, Pallas kernels: 1.74 us -> 4.71 us  [pair_bias(): pl.pallas_call(bias_kernel, out_shape=[jax.ShapeDtypeStruct((cols, rows *...]
    ppermute x10 -> x7, waiting for transfers between devices: 3.51 us -> 5.71 us  [swap(): lax.ppermute(held, axis, [(i, i ^ far) for i in range(lax.axis_size(axis))])]
    ppermute x10 -> x7, starting transfers between devices: 12.4 us -> 11.6 us  [swap(): lax.ppermute(held, axis, [(i, i ^ far) for i in range(lax.axis_size(axis))])]
    slice x1 -> x0, local copies, waits for them, and re-layouts: 0.76 us -> none  [shards(): behind = lax.ppermute(atom_feat[:, :RIM], 'row', down)]
    pallas_call x2, Pallas kernels: 4.04 us -> 3.3 us  [gather_tokens(): pl.pallas_call(functools.partial(gather_kernel, sample), out_shape=[jax.S...]
    ppermute x2, waiting for transfers between devices: 0.01 us -> 0.59 us  [the longest x1 0.59 us: shards(): behind = lax.ppermute(first, 'row', down)]
  transfers between devices with their start and end apart: 12 -> 9, of which waited for: 1 -> 4; matrix products, arithmetic and copies ran while one was open for 0% -> 0% of each run, Pallas kernels for 42% -> 30%
where the time goes in v3:
time: 43.6 us; the launch traced here: 43.4 us
  Pallas kernels  21.4 us (49%)
  starting transfers between devices  15.3 us (35%)
  waiting for transfers between devices  6.31 us (14%)
    ppermute x7, starting transfers between devices, swap(): lax.ppermute(held, axis, [(i, i ^ far) for i in range(lax.axis_size(axis))])  11.6 us
    pallas_call x2, Pallas kernels, atom_attention(): pl.pallas_call(functools.partial(atom_kernel, sample), out_shape=jax.Shap...  6.12 us
    ppermute x7, waiting for transfers between devices, swap(): lax.ppermute(held, axis, [(i, i ^ far) for i in range(lax.axis_size(axis))])  5.71 us
    pallas_call x1, Pallas kernels, pair_bias(): pl.pallas_call(bias_kernel, out_shape=[jax.ShapeDtypeStruct((cols, rows *...  4.71 us
    pallas_call x2, Pallas kernels, attend(): pl.pallas_call(attend_kernel, out_shape=jax.ShapeDtypeStruct(shape, BF16)...  4.21 us
    pallas_call x2, Pallas kernels, gather_tokens(): pl.pallas_call(functools.partial(gather_kernel, sample), out_shape=[jax.S...  3.3 us
    pallas_call x2, Pallas kernels, project(): pl.pallas_call(project_kernel, out_shape=[jax.ShapeDtypeStruct((rows, wid...  2.6 us
    ppermute x1, starting transfers between devices, shards(): before = lax.ppermute(last, 'row', up)  2.37 us
  transfers between devices with their start and end apart: 9, of which 4 were waited for; matrix products, arithmetic and copies ran while one was open for 0% of the time, Pallas kernels for 30%

profile of v3, /device:TPU:0, one launch (start us, length us, event | category | flops | bytes accessed | tf_op | source)
XLA Modules:
  0.0 43.4 jit_solution(15339253308983533711)
XLA Ops:
  0.0 4.7 %pair_bias.1 = (bf16[36,1152]{1,0:T(8,128)(2,1)}, bf16[2,48,128]{2,1,0:T(8,128)(2,1)}, bf16[2,48,128]{2,1,0:T(8,128)(2,1)}) custom-call(bf16[2,1152,128]{2,1,0:T(8,128)(2,1)} %feat.9, bf16[36,72,128]{2,1,0:T(8,128)(2,1)} %bitcast.12, s32[36]{0:T(128)} %mask_hbm.1, bf16[16,128]{1,0:T(8,128)(2,1)} %bitcast.13), custom_call_target="tpu_custom_call" | custom-call | flops 3300000000 | bytes 1000000 | tf_op jit(solution)/shard_map/pair_bias/pallas_call | solution.py:104
  4.7 2.4 %collective-permute-start = (bf16[2,48,128]{2,1,0:T(8,128)(2,1)}, bf16[2,48,128]{2,1,0:T(8,128)(2,1)S(1)}, u32[]{:S(2)}, u32[]{:S(2)}) collective-permute-start(bf16[2,48,128]{2,1,0:T(8,128)(2,1)} %get-tuple-element.30), channel_id=1, source_target_pairs={{0,8},{8,16},{16,24},{1,9},{9,17},{17,25},{2,10},{10,18},{18,26},{... | collective-permute-start | bytes 73736 | tf_op jit(solution)/shard_map/ppermute | solution.py:406
  7.1 1.3 %collective-permute-start.1 = (bf16[2,48,128]{2,1,0:T(8,128)(2,1)}, bf16[2,48,128]{2,1,0:T(8,128)(2,1)S(1)}, u32[]{:S(2)}, u32[]{:S(2)}) collective-permute-start(bf16[2,48,128]{2,1,0:T(8,128)(2,1)} %get-tuple-element.31), channel_id=1, source_target_pairs={{8,0},{16,8},{24,16},{9,1},{17,9},{25,17},{10,2},{18,10},{26,18},{... | collective-permute-start | bytes 73736 | tf_op jit(solution)/shard_map/ppermute | solution.py:407
  8.4 0.0 copy-start.13
  8.4 0.0 copy-start.6
  8.4 0.0 copy-start.10
  8.5 0.0 copy-start.12
  8.5 3.5 %collective-permute-start.2 = (bf16[1,36,1152]{2,1,0:T(8,128)(2,1)}, bf16[1,36,1152]{2,1,0:T(8,128)(2,1)S(1)}, u32[]{:S(2)}, u32[]{:S(2)}) collective-permute-start(bf16[1,36,1152]{2,1,0:T(8,128)(2,1)} %bitcast.9), channel_id=1, source_target_pairs={{0,4},{1,5},{2,6},{3,7},{4,0},{5,1},{6,2},{7,3},{8,12},{9,13},{10,... | collective-permute-start | bytes 248840 | tf_op jit(solution)/shard_map/ppermute | solution.py:131
  11.9 0.6 %collective-permute-done.1.after = bf16[2,48,128]{2,1,0:T(8,128)(2,1)S(1)} collective-permute-done((bf16[2,48,128]{2,1,0:T(8,128)(2,1)}, bf16[2,48,128]{2,1,0:T(8,128)(2,1)S(1)}, u32[]{:S(2)}, u32[]{:S(2)}) %collective-permute-start.1) | collective-permute-done | bytes 24608 | tf_op jit(solution)/shard_map/ppermute | solution.py:407
  12.6 3.1 %atom_attention.2.mixed = bf16[1152,128]{1,0:T(8,128)(2,1)S(1)} custom-call(bf16[2,1152,128]{2,1,0:T(8,128)(2,1)S(1)} %copy-done.5, bf16[2,48,128]{2,1,0:T(8,128)(2,1)S(1)} %collective-permute-done.before, bf16[2,48,128]{2,1,0:T(8,128)(2,1)S(1)} %collective-permute-done.1.after, bf16[128,128]{1,0:T(8,128)(2,1)S(1)} %copy-done.7, ...), custom_call_target="tpu_custom_call" | custom-call | flops 4400000000 | bytes 1000000 | tf_op jit(solution)/shard_map/atom_attention/pallas_call | solution.py:199
  15.7 2.6 %collective-permute-start.3 = (bf16[2,36,1152]{2,1,0:T(8,128)(2,1)S(1)}, bf16[2,36,1152]{2,1,0:T(8,128)(2,1)S(1)}, u32[]{:S(2)}, u32[]{:S(2)}) collective-permute-start(bf16[2,36,1152]{2,1,0:T(8,128)(2,1)S(1)} %pad_maximum_fusion.3), channel_id=1, source_target_pairs={{0,2},{1,3},{2,0},{3,1},{4,6},{5,7},{6,4},{7,5},{8,10},{9,11},{10,... | collective-permute-start | bytes 497672 | tf_op jit(solution)/shard_map/ppermute | solution.py:131
  18.3 1.6 %gather_tokens.2 = (f32[72,768]{1,0:T(8,128)S(1)}, bf16[72,768]{1,0:T(8,128)(2,1)S(1)}) custom-call(bf16[1152,128]{1,0:T(8,128)(2,1)S(1)} %atom_attention.2.mixed, bf16[2,1152,128]{2,1,0:T(8,128)(2,1)S(1)} %copy-done.5, s32[1152]{0:T(1024)S(1)} %copy-done.11, bf16[128,128]{1,0:T(8,128)(2,1)S(1)} %copy-done.10, bf16[128,768]{1,0:T(8,128)(2,1)S(1)} %copy-done.6, ...), custom_call_target="tpu_custom_call" | custom-call | flops 1100000000 | bytes 1000000 | tf_op jit(solution)/shard_map/gather_tokens/pallas_call | solution.py:236
  20.0 2.7 %collective-permute-start.4 = (bf16[1,72,768]{2,1,0:T(8,128)(2,1)S(1)}, bf16[1,72,768]{2,1,0:T(8,128)(2,1)S(1)}, u32[]{:S(2)}, u32[]{:S(2)}) collective-permute-start(bf16[1,72,768]{2,1,0:T(8,128)(2,1)S(1)} %bitcast.5), channel_id=1, source_target_pairs={{0,16},{8,24},{16,0},{24,8},{1,17},{9,25},{17,1},{25,9},{2,18},{10... | collective-permute-start | bytes 331784 | tf_op jit(solution)/shard_map/ppermute | solution.py:131
  22.7 3.1 %atom_attention.3.mixed = bf16[1152,128]{1,0:T(8,128)(2,1)S(1)} custom-call(bf16[2,1152,128]{2,1,0:T(8,128)(2,1)S(1)} %copy-done.5, bf16[2,48,128]{2,1,0:T(8,128)(2,1)S(1)} %collective-permute-done.before, bf16[2,48,128]{2,1,0:T(8,128)(2,1)S(1)} %collective-permute-done.1.after, bf16[128,128]{1,0:T(8,128)(2,1)S(1)} %copy-done.7, ...), custom_call_target="tpu_custom_call" | custom-call | flops 4400000000 | bytes 1000000 | tf_op jit(solution)/shard_map/atom_attention/pallas_call | solution.py:199
  25.7 0.0 copy-start.3
  25.8 0.1 pad_maximum_fusion.refs_0_
  25.8 0.5 %collective-permute-done.4 = bf16[1,72,768]{2,1,0:T(8,128)(2,1)S(1)} collective-permute-done((bf16[1,72,768]{2,1,0:T(8,128)(2,1)S(1)}, bf16[1,72,768]{2,1,0:T(8,128)(2,1)S(1)}, u32[]{:S(2)}, u32[]{:S(2)}) %collective-permute-start.4) | collective-permute-done | bytes 110624 | tf_op jit(solution)/shard_map/ppermute | solution.py:131
  26.4 0.0 copy-start.1
  26.4 0.0 copy-start.2
  26.4 0.1 collective-permute-start.6
  26.5 1.6 %collective-permute-start.8 = (bf16[4,36,1152]{2,1,0:T(8,128)(2,1)S(1)}, bf16[4,36,1152]{2,1,0:T(8,128)(2,1)S(1)}, u32[]{:S(2)}, u32[]{:S(2)}) collective-permute-start(bf16[4,36,1152]{2,1,0:T(8,128)(2,1)S(1)} %pad_maximum_fusion.refs_0_), channel_id=1, source_target_pairs={{0,1},{1,0},{2,3},{3,2},{4,5},{5,4},{6,7},{7,6},{8,9},{9,8},{10,11... | collective-permute-start | bytes 995336 | tf_op jit(solution)/shard_map/ppermute | solution.py:131
  28.0 1.7 %gather_tokens.3 = (f32[72,768]{1,0:T(8,128)S(1)}, bf16[72,768]{1,0:T(8,128)(2,1)S(1)}) custom-call(bf16[1152,128]{1,0:T(8,128)(2,1)S(1)} %atom_attention.3.mixed, bf16[2,1152,128]{2,1,0:T(8,128)(2,1)S(1)} %copy-done.5, s32[1152]{0:T(1024)S(1)} %copy-done.11, bf16[128,128]{1,0:T(8,128)(2,1)S(1)} %copy-done.10, bf16[128,768]{1,0:T(8,128)(2,1)S(1)} %copy-done.6, ...), custom_call_target="tpu_custom_call" | custom-call | flops 1100000000 | bytes 1000000 | tf_op jit(solution)/shard_map/gather_tokens/pallas_call | solution.py:236
  29.7 1.1 %collective-permute-start.5 = (bf16[1,72,768]{2,1,0:T(8,128)(2,1)S(1)}, bf16[1,72,768]{2,1,0:T(8,128)(2,1)S(1)}, u32[]{:S(2)}, u32[]{:S(2)}) collective-permute-start(bf16[1,72,768]{2,1,0:T(8,128)(2,1)S(1)} %bitcast.7), channel_id=1, source_target_pairs={{0,16},{8,24},{16,0},{24,8},{1,17},{9,25},{17,1},{25,9},{2,18},{10... | collective-permute-start | bytes 331784 | tf_op jit(solution)/shard_map/ppermute | solution.py:131
  30.9 1.3 %project.2 = (bf16[72,768]{1,0:T(8,128)(2,1)S(1)}, bf16[768,288]{1,0:T(8,128)(2,1)S(1)}, bf16[288,768]{1,0:T(8,128)(2,1)S(1)}, f32[72,768]{1,0:T(8,128)S(1)}) custom-call(bf16[2,72,768]{2,1,0:T(8,128)(2,1)S(1)} %pad_maximum_fusion.1.near, bf16[2,72,768]{2,1,0:T(8,128)(2,1)S(1)} %collective-permute-done.6.far, bf16[768,768]{1,0:T(8,128)(2,1)S(1)} %copy-done, ...), custom_call_target="tpu_custom_call" | custom-call | flops 2200000000 | bytes 1000000 | tf_op jit(solution)/shard_map/project/pallas_call | solution.py:305
  32.2 2.7 %collective-permute-done.5 = bf16[1,72,768]{2,1,0:T(8,128)(2,1)S(1)} collective-permute-done((bf16[1,72,768]{2,1,0:T(8,128)(2,1)S(1)}, bf16[1,72,768]{2,1,0:T(8,128)(2,1)S(1)}, u32[]{:S(2)}, u32[]{:S(2)}) %collective-permute-start.5) | collective-permute-done | bytes 110624 | tf_op jit(solution)/shard_map/ppermute | solution.py:131
  34.9 0.0 copy-start.4
  34.9 0.1 collective-permute-start.7
  35.0 2.5 %collective-permute-done.8.refs_1_ = bf16[4,36,1152]{2,1,0:T(8,128)(2,1)S(1)} collective-permute-done((bf16[4,36,1152]{2,1,0:T(8,128)(2,1)S(1)}, bf16[4,36,1152]{2,1,0:T(8,128)(2,1)S(1)}, u32[]{:S(2)}, u32[]{:S(2)}) %collective-permute-start.8) | collective-permute-done | bytes 331808 | tf_op jit(solution)/shard_map/ppermute | solution.py:131
  37.5 0.4 turn_bias.1.bias
  37.9 1.8 %attend.2.rest_0_ = bf16[72,768]{1,0:T(8,128)(2,1)S(1)} custom-call(bf16[72,768]{1,0:T(8,128)(2,1)S(1)} %get-tuple-element.42.q, bf16[768,288]{1,0:T(8,128)(2,1)S(1)} %get-tuple-element.43.kt, bf16[288,768]{1,0:T(8,128)(2,1)S(1)} %get-tuple-element.44.v, f32[72,768]{1,0:T(8,128)S(1)} %get-tuple-element.45.gate, f32[72,768]{1,0:T(8,128)S(1)} %get-tuple-element.54.token_in, ...), custom_call_target="tpu_custom_call" | custom-call | flops 3300000000 | bytes 1000000 | tf_op jit(solution)/shard_map/attend/pallas_call | solution.py:371
  39.7 1.3 %project.3 = (bf16[72,768]{1,0:T(8,128)(2,1)S(1)}, bf16[768,288]{1,0:T(8,128)(2,1)S(1)}, bf16[288,768]{1,0:T(8,128)(2,1)S(1)}, f32[72,768]{1,0:T(8,128)S(1)}) custom-call(bf16[2,72,768]{2,1,0:T(8,128)(2,1)S(1)} %pad_maximum_fusion.2.near, bf16[2,72,768]{2,1,0:T(8,128)(2,1)S(1)} %collective-permute-done.7.far, bf16[768,768]{1,0:T(8,128)(2,1)S(1)} %copy-done, ...), custom_call_target="tpu_custom_call" | custom-call | flops 2200000000 | bytes 1000000 | tf_op jit(solution)/shard_map/project/pallas_call | solution.py:305
  41.0 2.5 %attend.3 = bf16[2,72,768]{2,1,0:T(8,128)(2,1)} custom-call(bf16[72,768]{1,0:T(8,128)(2,1)S(1)} %get-tuple-element.47.q, bf16[768,288]{1,0:T(8,128)(2,1)S(1)} %get-tuple-element.48.kt, bf16[288,768]{1,0:T(8,128)(2,1)S(1)} %get-tuple-element.49.v, f32[72,768]{1,0:T(8,128)S(1)} %get-tuple-element.50.gate, f32[72,768]{1,0:T(8,128)S(1)} %get-tuple-element.51.token_in, ...), custom_call_target="tpu_custom_call" | custom-call | flops 3300000000 | bytes 1000000 | tf_op jit(solution)/shard_map/attend/pallas_call | solution.py:371
  (28 shorter events, 0.1 us)
Async XLA Ops:
  0.0 12.5 %copy-start.5 = (bf16[2,1152,128]{2,1,0:T(8,128)(2,1)S(1)}, bf16[2,1152,128]{2,1,0:T(8,128)(2,1)}, u32[]{:S(2)}) copy-start(bf16[2,1152,128]{2,1,0:T(8,128)(2,1)} %feat.9) | copy-start | bytes 1769476
  0.0 12.5 %copy-start.7 = (bf16[128,128]{1,0:T(8,128)(2,1)S(1)}, bf16[128,128]{1,0:T(8,128)(2,1)}, u32[]{:S(2)}) copy-start(bf16[128,128]{1,0:T(8,128)(2,1)} %wq.5) | copy-start | bytes 98308
  0.0 12.5 %copy-start.8 = (bf16[128,128]{1,0:T(8,128)(2,1)S(1)}, bf16[128,128]{1,0:T(8,128)(2,1)}, u32[]{:S(2)}) copy-start(bf16[128,128]{1,0:T(8,128)(2,1)} %wk.5) | copy-start | bytes 98308
  0.0 12.5 %copy-start.9 = (bf16[128,128]{1,0:T(8,128)(2,1)S(1)}, bf16[128,128]{1,0:T(8,128)(2,1)}, u32[]{:S(2)}) copy-start(bf16[128,128]{1,0:T(8,128)(2,1)} %wv.5) | copy-start | bytes 98308
  4.7 7.2 %collective-permute-start = (bf16[2,48,128]{2,1,0:T(8,128)(2,1)}, bf16[2,48,128]{2,1,0:T(8,128)(2,1)S(1)}, u32[]{:S(2)}, u32[]{:S(2)}) collective-permute-start(bf16[2,48,128]{2,1,0:T(8,128)(2,1)} %get-tuple-element.30), channel_id=1, source_target_pairs={{0,8},{8,16},{16,24},{1,9},{9,17},{17,25},{2,10},{10,18},{18,26},{... | collective-permute-start | bytes 73736 | tf_op jit(solution)/shard_map/ppermute | solution.py:406
  7.1 5.4 %collective-permute-start.1 = (bf16[2,48,128]{2,1,0:T(8,128)(2,1)}, bf16[2,48,128]{2,1,0:T(8,128)(2,1)S(1)}, u32[]{:S(2)}, u32[]{:S(2)}) collective-permute-start(bf16[2,48,128]{2,1,0:T(8,128)(2,1)} %get-tuple-element.31), channel_id=1, source_target_pairs={{8,0},{16,8},{24,16},{9,1},{17,9},{25,17},{10,2},{18,10},{26,18},{... | collective-permute-start | bytes 73736 | tf_op jit(solution)/shard_map/ppermute | solution.py:407
  8.4 7.2 %copy-start.13 = (bf16[36,1152]{1,0:T(8,128)(2,1)S(1)}, bf16[36,1152]{1,0:T(8,128)(2,1)}, u32[]{:S(2)}) copy-start(bf16[36,1152]{1,0:T(8,128)(2,1)} %get-tuple-element.32) | copy-start | bytes 248836
  8.4 9.9 %copy-start.6 = (bf16[128,768]{1,0:T(8,128)(2,1)S(1)}, bf16[128,768]{1,0:T(8,128)(2,1)}, u32[]{:S(2)}) copy-start(bf16[128,768]{1,0:T(8,128)(2,1)} %agg.3) | copy-start | bytes 589828
  8.4 9.9 %copy-start.10 = (bf16[128,128]{1,0:T(8,128)(2,1)S(1)}, bf16[128,128]{1,0:T(8,128)(2,1)}, u32[]{:S(2)}) copy-start(bf16[128,128]{1,0:T(8,128)(2,1)} %wo.5) | copy-start | bytes 98308
  8.4 9.9 %copy-start.11 = (s32[1152]{0:T(1024)S(1)}, s32[1152]{0:T(1024)}, u32[]{:S(2)}) copy-start(s32[1152]{0:T(1024)} %token_.3) | copy-start | bytes 13828
  8.5 9.9 %copy-start.12 = (f32[768]{0:T(1024)S(1)}, f32[768]{0:T(1024)}, u32[]{:S(2)}) copy-start(f32[768]{0:T(1024)} %gain.3) | copy-start | bytes 9220
  8.5 7.2 %collective-permute-start.2 = (bf16[1,36,1152]{2,1,0:T(8,128)(2,1)}, bf16[1,36,1152]{2,1,0:T(8,128)(2,1)S(1)}, u32[]{:S(2)}, u32[]{:S(2)}) collective-permute-start(bf16[1,36,1152]{2,1,0:T(8,128)(2,1)} %bitcast.9), channel_id=1, source_target_pairs={{0,4},{1,5},{2,6},{3,7},{4,0},{5,1},{6,2},{7,3},{8,12},{9,13},{10,... | collective-permute-start | bytes 248840 | tf_op jit(solution)/shard_map/ppermute | solution.py:131
  15.7 10.0 %collective-permute-start.3 = (bf16[2,36,1152]{2,1,0:T(8,128)(2,1)S(1)}, bf16[2,36,1152]{2,1,0:T(8,128)(2,1)S(1)}, u32[]{:S(2)}, u32[]{:S(2)}) collective-permute-start(bf16[2,36,1152]{2,1,0:T(8,128)(2,1)S(1)} %pad_maximum_fusion.3), channel_id=1, source_target_pairs={{0,2},{1,3},{2,0},{3,1},{4,6},{5,7},{6,4},{7,5},{8,10},{9,11},{10,... | collective-permute-start | bytes 497672 | tf_op jit(solution)/shard_map/ppermute | solution.py:131
  20.0 6.3 %collective-permute-start.4 = (bf16[1,72,768]{2,1,0:T(8,128)(2,1)S(1)}, bf16[1,72,768]{2,1,0:T(8,128)(2,1)S(1)}, u32[]{:S(2)}, u32[]{:S(2)}) collective-permute-start(bf16[1,72,768]{2,1,0:T(8,128)(2,1)S(1)} %bitcast.5), channel_id=1, source_target_pairs={{0,16},{8,24},{16,0},{24,8},{1,17},{9,25},{17,1},{25,9},{2,18},{10... | collective-permute-start | bytes 331784 | tf_op jit(solution)/shard_map/ppermute | solution.py:131
  25.7 5.1 %copy-start.3 = (bf16[768,768]{1,0:T(8,128)(2,1)S(1)}, bf16[768,768]{1,0:T(8,128)(2,1)}, u32[]{:S(2)}) copy-start(bf16[768,768]{1,0:T(8,128)(2,1)} %wg.3) | copy-start | bytes 3538948
  26.4 4.5 %copy-start = (bf16[768,768]{1,0:T(8,128)(2,1)S(1)}, bf16[768,768]{1,0:T(8,128)(2,1)}, u32[]{:S(2)}) copy-start(bf16[768,768]{1,0:T(8,128)(2,1)} %wq.7) | copy-start | bytes 3538948
  26.4 4.5 %copy-start.1 = (bf16[768,768]{1,0:T(8,128)(2,1)S(1)}, bf16[768,768]{1,0:T(8,128)(2,1)}, u32[]{:S(2)}) copy-start(bf16[768,768]{1,0:T(8,128)(2,1)} %wk.7) | copy-start | bytes 3538948
  26.4 4.5 %copy-start.2 = (bf16[768,768]{1,0:T(8,128)(2,1)S(1)}, bf16[768,768]{1,0:T(8,128)(2,1)}, u32[]{:S(2)}) copy-start(bf16[768,768]{1,0:T(8,128)(2,1)} %wv.7) | copy-start | bytes 3538948
  26.4 4.4 %collective-permute-start.6 = (bf16[2,72,768]{2,1,0:T(8,128)(2,1)S(1)}, bf16[2,72,768]{2,1,0:T(8,128)(2,1)S(1)}, u32[]{:S(2)}, u32[]{:S(2)}) collective-permute-start(bf16[2,72,768]{2,1,0:T(8,128)(2,1)S(1)} %pad_maximum_fusion.1.near), channel_id=1, source_target_pairs={{0,8},{8,0},{16,24},{24,16},{1,9},{9,1},{17,25},{25,17},{2,10},{10... | collective-permute-start | bytes 663560 | tf_op jit(solution)/shard_map/ppermute | solution.py:131
  26.5 11.0 %collective-permute-start.8 = (bf16[4,36,1152]{2,1,0:T(8,128)(2,1)S(1)}, bf16[4,36,1152]{2,1,0:T(8,128)(2,1)S(1)}, u32[]{:S(2)}, u32[]{:S(2)}) collective-permute-start(bf16[4,36,1152]{2,1,0:T(8,128)(2,1)S(1)} %pad_maximum_fusion.refs_0_), channel_id=1, source_target_pairs={{0,1},{1,0},{2,3},{3,2},{4,5},{5,4},{6,7},{7,6},{8,9},{9,8},{10,11... | collective-permute-start | bytes 995336 | tf_op jit(solution)/shard_map/ppermute | solution.py:131
  29.7 5.2 %collective-permute-start.5 = (bf16[1,72,768]{2,1,0:T(8,128)(2,1)S(1)}, bf16[1,72,768]{2,1,0:T(8,128)(2,1)S(1)}, u32[]{:S(2)}, u32[]{:S(2)}) collective-permute-start(bf16[1,72,768]{2,1,0:T(8,128)(2,1)S(1)} %bitcast.7), channel_id=1, source_target_pairs={{0,16},{8,24},{16,0},{24,8},{1,17},{9,25},{17,1},{25,9},{2,18},{10... | collective-permute-start | bytes 331784 | tf_op jit(solution)/shard_map/ppermute | solution.py:131
  34.9 3.0 %copy-start.4 = (bf16[768,768]{1,0:T(8,128)(2,1)S(1)}, bf16[768,768]{1,0:T(8,128)(2,1)}, u32[]{:S(2)}) copy-start(bf16[768,768]{1,0:T(8,128)(2,1)} %wo.7) | copy-start | bytes 3538948
  34.9 4.7 %collective-permute-start.7 = (bf16[2,72,768]{2,1,0:T(8,128)(2,1)S(1)}, bf16[2,72,768]{2,1,0:T(8,128)(2,1)S(1)}, u32[]{:S(2)}, u32[]{:S(2)}) collective-permute-start(bf16[2,72,768]{2,1,0:T(8,128)(2,1)S(1)} %pad_maximum_fusion.2.near), channel_id=1, source_target_pairs={{0,8},{8,0},{16,24},{24,16},{1,9},{9,1},{17,25},{25,17},{2,10},{10... | collective-permute-start | bytes 663560 | tf_op jit(solution)/shard_map/ppermute | solution.py:131

commit v4 on v3

--- a/solution.py
+++ b/solution.py
@@ -43,7 +43,7 @@
 
 
 def cost(micros):
-    return pl.CostEstimate(flops=micros * 1_100_000_000, bytes_accessed=1_000_000, transcendentals=0)
+    return pl.CostEstimate(flops=micros * 20_000_000, bytes_accessed=1_000, transcendentals=0)
 
 
 def inverse(total):
@@ -60,26 +60,13 @@
     return held
 
 
-def bias_kernel(feat, pair_hbm, mask_hbm, weight_hbm, out, first, last, pair, mask, weight, normed, sems):
+def bias_kernel(head, tail, pair, mask, weight, out, inner, outer, normed):
+    odd = lax.axis_index("row") % 2 == 1
+    inner[...] = jnp.where(odd, head[...], tail[...])
+    outer[...] = jnp.where(odd, tail[...], head[...])
     cols, rows, chans = pair.shape
-    atoms = feat.shape[1]
-    moves = [
-        (weight_hbm, weight),
-        (mask_hbm, mask),
-        (feat.at[:, :RIM], first),
-        (feat.at[:, atoms - RIM :], last),
-    ]
-    step = cols // 4
-    moves += [(pair_hbm.at[k : k + step], pair.at[k : k + step]) for k in range(0, cols, step)]
-    copies = [pltpu.make_async_copy(src, dst, sems.at[i]) for i, (src, dst) in enumerate(moves)]
-    for copy in copies:
-        copy.start()
-    for i, copy in enumerate(copies[4:]):
-        copy.wait()
-        for k in range(i * step, (i + 1) * step):
-            normed[k] = layer_norm(pair[k].astype(F32))
-    for copy in copies[:4]:
-        copy.wait()
+    for k in range(cols):
+        normed[k] = layer_norm(pair[k].astype(F32))
     spread = (iota((HEADS, LANES), 1) // SUB == iota((HEADS, LANES), 0)).astype(BF16)
     wide = lax.dot_general(weight[...], spread, (((0,), (0,)), ((), ())), preferred_element_type=F32).astype(BF16)
     tall = cols * SUB
@@ -99,28 +86,33 @@
 
 def pair_bias(feat, pair_cond, token_mask, pair_weight):
     rows, cols, chans = pair_cond.shape
-    edge = (feat.shape[0], RIM, feat.shape[2])
-    hbm = pl.BlockSpec(memory_space=pltpu.HBM)
+    samples, atoms, width = feat.shape
+    edge = (samples, RIM, width)
+
+    def whole(*shape):
+        return pl.BlockSpec(shape, lambda i: (0,) * len(shape))
+
     return pl.pallas_call(
         bias_kernel,
+        grid=(1,),
         out_shape=[
             jax.ShapeDtypeStruct((cols, rows * HEADS), BF16),
             jax.ShapeDtypeStruct(edge, BF16),
             jax.ShapeDtypeStruct(edge, BF16),
         ],
-        in_specs=[hbm] * 4,
-        out_specs=[pl.BlockSpec(memory_space=pltpu.VMEM)] * 3,
-        scratch_shapes=[
-            pltpu.VMEM((cols, rows, chans), BF16),
-            pltpu.VMEM((cols,), jnp.int32),
-            pltpu.VMEM((HEADS, chans), BF16),
-            pltpu.VMEM((cols, rows, chans), F32),
-            pltpu.SemaphoreType.DMA((8,)),
+        in_specs=[
+            pl.BlockSpec(edge, lambda i: (0, 0, 0)),
+            pl.BlockSpec(edge, lambda i: (0, atoms // RIM - 1, 0)),
+            whole(cols, rows, chans),
+            whole(cols),
+            whole(HEADS, chans),
         ],
+        out_specs=[whole(cols, rows * HEADS), whole(*edge), whole(*edge)],
+        scratch_shapes=[pltpu.VMEM((cols, rows, chans), F32)],
         compiler_params=pltpu.CompilerParams(vmem_limit_bytes=60 * MIB),
         cost_estimate=cost(3),
         name="pair_bias",
-    )(feat, jnp.transpose(pair_cond, (1, 0, 2)), token_mask, pair_weight.T)
+    )(feat, feat, jnp.transpose(pair_cond, (1, 0, 2)), token_mask, pair_weight.T)
 
 
 def after(value, *others):
@@ -131,24 +123,27 @@
     return lax.ppermute(held, axis, [(i, i ^ far) for i in range(lax.axis_size(axis))])
 
 
-def block_of(near, far, bits, me, j):
-    apart = me ^ j
-    place = sum((apart // bit) % 2 * 2**i for i, bit in enumerate(bits[:-1]))
-    return jnp.where((apart // bits[-1]) % 2 == 0, near[place], far[place])
-
-
 def bits_of(devices):
     return [devices >> i for i in range(1, devices.bit_length())]
 
 
-def atom_kernel(sample, feat, before, after, wq, wk, wv, mixed, qs, ks, vs):
+def block_of(near, far, me, j):
+    apart = me ^ j
+    place = sum((apart // bit) % 2 * 2**i for i, bit in enumerate(bits_of(2 * near.shape[0])[:-1]))
+    return jnp.where(apart % 2 == 0, near[place], far[place])
+
+
+def atom_kernel(sample, feat, inner, outer, wq, wk, wv, mixed, qs, ks, vs):
     atoms, chans = feat.shape[1:]
     rank = lax.axis_index("row")
     at_start = rank == 0
     at_end = rank == lax.axis_size("row") - 1
     wqkv = jnp.concatenate([wq[...], wk[...], wv[...]], axis=1)
-    for ref, at in ((before, 0), (after, RIM + atoms)):
-        kv = dot(layer_norm(ref[sample].astype(F32)).astype(BF16), wqkv[:, chans:]).astype(BF16)
+    odd = rank % 2 == 1
+    before = jnp.where(odd, inner[sample], outer[sample])
+    behind = jnp.where(odd, outer[sample], inner[sample])
+    for part, at in ((before, 0), (behind, RIM + atoms)):
+        kv = dot(layer_norm(part.astype(F32)).astype(BF16), wqkv[:, chans:]).astype(BF16)
         ks[at : at + RIM] = kv[:, :chans]
         vs[at : at + RIM] = kv[:, chans:]
     for c in range(0, atoms, LANES):
@@ -193,7 +188,7 @@
     skewed(range(0, atoms, batch * QWIN), [score, soften, mix])
 
 
-def atom_attention(sample, feat, before, after, wq, wk, wv):
+def atom_attention(sample, feat, inner, outer, wq, wk, wv):
     atoms, chans = feat.shape[1:]
     vmem = pl.BlockSpec(memory_space=pltpu.VMEM)
     return pl.pallas_call(
@@ -209,7 +204,7 @@
         compiler_params=pltpu.CompilerParams(vmem_limit_bytes=16 * MIB),
         cost_estimate=cost(4),
         name="atom_attention",
-    )(feat, before, after, wq, wk, wv)
+    )(feat, inner, outer, wq, wk, wv)
 
 
 def gather_kernel(sample, mixed, feat, token, wo, agg, gain, token_in, token_norm):
@@ -244,37 +239,32 @@
     )(mixed, feat, token, wo, agg, gain)
 
 
-def turn_kernel(orders, *refs):
-    *halves, out, tall = refs
+def turn_kernel(near, far, out, tall):
+    half, cols, _ = near.shape
     rows = out.shape[0] // HEADS
     me = lax.axis_index("sample")
-    at = 0
-    for near, far, bits in zip(halves[::2], halves[1::2], orders):
-        half, cols, wide = near.shape
-        for j in range(2 * half):
-            tall[j * cols : (j + 1) * cols, at : at + wide] = block_of(near, far, bits, me, j).astype(F32)
-        at += wide
+    for j in range(2 * half):
+        tall[j * cols : (j + 1) * cols] = block_of(near, far, me, j).astype(F32)
     for g in range(rows // SUB):
         turned = tall[:, g * LANES : (g + 1) * LANES].T
         for h in range(HEADS):
             out[h * rows + g * SUB : h * rows + (g + 1) * SUB] = turned[h * SUB : (h + 1) * SUB]
 
 
-def turn_bias(orders, halves):
-    half, cols, _ = halves[0].shape
+def turn_bias(near, far):
+    half, cols, wide = near.shape
     keys = 2 * half * cols
-    wide = sum(near.shape[2] for near in halves[::2])
     vmem = pl.BlockSpec(memory_space=pltpu.VMEM)
     return pl.pallas_call(
-        functools.partial(turn_kernel, orders),
+        turn_kernel,
         out_shape=jax.ShapeDtypeStruct((wide, keys), F32),
-        in_specs=[vmem] * len(halves),
+        in_specs=[vmem, vmem],
         out_specs=vmem,
         scratch_shapes=[pltpu.VMEM((keys, wide), F32)],
         compiler_params=pltpu.CompilerParams(vmem_limit_bytes=24 * MIB),
         cost_estimate=cost(1),
         name="turn_bias",
-    )(*halves)
+    )(near, far)
 
 
 def head_groups(width):
@@ -289,7 +279,7 @@
 def project_kernel(near, far, wq, wk, wv, wg, q, kt, v, gate):
     half, rows, width = near.shape
     me = lax.axis_index("row")
-    x = jnp.concatenate([block_of(near, far, bits_of(2 * half), me, j).astype(F32) for j in range(2 * half)], axis=0).astype(BF16)
+    x = jnp.concatenate([block_of(near, far, me, j).astype(F32) for j in range(2 * half)], axis=0).astype(BF16)
     own = near[0]
     q[...] = dot(own, wq[...]).astype(BF16)
     gate[...] = jax.nn.sigmoid(dot(own, wg[...]))
@@ -397,58 +387,42 @@
     gate_weight,
     out_weight,
 ):
-    samples, atoms, _ = atom_feat.shape
+    samples = atom_feat.shape[0]
     rows = pair_cond.shape[0]
     ranks = lax.axis_size("row")
-    up = [(i, i + 1) for i in range(ranks - 1)]
-    down = [(j, i) for i, j in up]
-    bias, first, last = pair_bias(atom_feat, pair_cond, token_mask, pair_weight)
-    before = lax.ppermute(last, "row", up)
-    behind = lax.ppermute(first, "row", down)
-    bits = bits_of(lax.axis_size("sample"))
-    orders = [bits]
-    held = [bias[None]]
-
-    def wider(step, *others):
-        got = after([swap(h, "sample", order[step]) for h, order in zip(held, orders)], *others)
-        return [jnp.concatenate([h, g], axis=0) for h, g in zip(held, got)]
-
-    row_bits = bits_of(ranks)
-    norms, inputs = [], []
-    step = 0
+    bias, inner, outer = pair_bias(atom_feat, pair_cond, token_mask, pair_weight)
+    inner = swap(inner, "row", 1)
+    odd_pairs = [(i, i + 1) for i in range(1, ranks - 1, 2)]
+    outer = lax.ppermute(outer, "row", odd_pairs + [(j, i) for i, j in odd_pairs])
+
+    def widen(held, axis, bit, *others):
+        return jnp.concatenate([held, after(swap(held, axis, bit), *others)], axis=0)
+
+    bits, row_bits = bits_of(lax.axis_size("sample")), bits_of(ranks)
+    held, norms, inputs = bias[None], [], []
     for s in range(samples):
-        mixed = atom_attention(s, atom_feat, before, behind, atom_wq, atom_wk, atom_wv)
-        if step < len(bits) - 1:
-            held = wider(step, mixed)
-            step += 1
-            mixed = after(mixed, held)
+        if s < len(bits) - 1:
+            held = widen(held, "sample", bits[s], inner, outer, *norms[-1:])
+        inner = after(inner, held, *norms[-1:])
+        mixed = atom_attention(s, atom_feat, inner, outer, atom_wq, atom_wk, atom_wv)
         if s:
-            norms[-1] = jnp.concatenate([norms[-1], after(swap(norms[-1], "row", row_bits[0]), mixed)], axis=0)
+            norms[-1] = widen(norms[-1], "row", row_bits[0], mixed)
             mixed = after(mixed, norms[-1])
         token_in, token_norm = gather_tokens(s, mixed, atom_feat, atom_token, atom_wo, agg_weight, token_gain, rows)
         inputs.append(token_in)
         norms.append(token_norm[None])
-        before = after(before, token_norm)
-    while step < len(bits) - 1:
-        held = wider(step)
-        step += 1
-    halves = []
-    for h, order in zip(held, orders):
-        halves += [h, swap(h, "sample", order[-1])]
-    parts = []
+    for bit in bits[samples:-1]:
+        held = widen(held, "sample", bit)
+    far_bias = swap(held, "sample", bits[-1])
+    done = []
     for s in range(samples):
         near = norms[s]
-        for i, far in enumerate(row_bits[:-1]):
-            if near.shape[0] == 1 << i:
-                got = swap(near, "row", far)
-                near = jnp.concatenate([near, after(got, *parts[-1]) if parts else got], axis=0)
-        norms[s] = near
-        if s == samples - 1:
-            halves = after(halves, near)
-            bias = turn_bias(orders, halves)
-        parts.append(project(near, swap(near, "row", row_bits[-1]), query_weight, key_weight, value_weight, gate_weight))
-    done = []
-    for s, part in enumerate(parts):
+        for bit in row_bits[near.shape[0].bit_length() - 1 : -1]:
+            near = widen(near, "row", bit, *done)
+        far = swap(near, "row", row_bits[-1])
+        part = project(near, far, query_weight, key_weight, value_weight, gate_weight)
+        if s == 0:
+            bias = turn_bias(held, after(far_bias, part))
         earlier = done if s == samples - 1 else []
         done.append(attend(*part, inputs[s], bias, out_weight, earlier))
     return done[-1]

time: 43.6 us -> 40.2 us (0.922)
  starting transfers between devices: 15.3 us -> 10.7 us
  Pallas kernels: 21.4 us -> 20.1 us
  other arithmetic: 0.13 us -> 1.02 us
  local copies, waits for them, and re-layouts: 0.08 us -> 0.91 us
  waiting for transfers between devices: 6.31 us -> 7.03 us
    ppermute x2 -> x1, starting transfers between devices: 3.66 us -> 0.78 us  [shards(): lax.ppermute(outer, 'row', odd_pairs + [(j, i) for i, j in odd_pairs])]
    ppermute x7 -> x8, starting transfers between devices: 11.6 us -> 9.87 us  [swap(): lax.ppermute(held, axis, [(i, i ^ far) for i in range(lax.axis_size(axis))])]
    ppermute x7 -> x8, waiting for transfers between devices: 5.71 us -> 7.03 us  [swap(): lax.ppermute(held, axis, [(i, i ^ far) for i in range(lax.axis_size(axis))])]
    pallas_call x2, Pallas kernels: 5.12 us -> 3.99 us  [the longest x1 3.57 us: pair_bias(): pl.pallas_call(bias_kernel, grid=(1,), out_shape=[jax.ShapeDtypeStruct((c...]
    concatenate x4, other arithmetic: 0.13 us -> 1.02 us  [widen(): jnp.concatenate([held, after(swap(held, axis, bit), *others)], axis=0)]
    unnamed x28, local copies, waits for them, and re-layouts: 0.08 us -> 0.91 us
    ppermute x2 -> x1, waiting for transfers between devices: 0.59 us -> 0.01 us  [shards(): lax.ppermute(outer, 'row', odd_pairs + [(j, i) for i, j in odd_pairs])]
  transfers between devices with their start and end apart: 9 -> 9, of which waited for: 4 -> 4; matrix products, arithmetic and copies ran while one was open for 0% -> 0% of each run, Pallas kernels for 30% -> 32%
where the time goes in v4:
time: 40.2 us; the launch traced here: 40 us
  Pallas kernels  20.1 us (50%)
  starting transfers between devices  10.7 us (27%)
  waiting for transfers between devices  7.03 us (17%)
  other arithmetic  1.02 us (3%)
  local copies, waits for them, and re-layouts  0.91 us (2%)
    ppermute x8, starting transfers between devices, swap(): lax.ppermute(held, axis, [(i, i ^ far) for i in range(lax.axis_size(axis))])  9.87 us
    ppermute x8, waiting for transfers between devices, swap(): lax.ppermute(held, axis, [(i, i ^ far) for i in range(lax.axis_size(axis))])  7.03 us
    pallas_call x2, Pallas kernels, atom_attention(): pl.pallas_call(functools.partial(atom_kernel, sample), out_shape=jax.Shap...  6.03 us
    pallas_call x2, Pallas kernels, attend(): pl.pallas_call(attend_kernel, out_shape=jax.ShapeDtypeStruct(shape, BF16)...  4.24 us
    pallas_call x1, Pallas kernels, pair_bias(): pl.pallas_call(bias_kernel, grid=(1,), out_shape=[jax.ShapeDtypeStruct((c...  3.57 us
    pallas_call x2, Pallas kernels, gather_tokens(): pl.pallas_call(functools.partial(gather_kernel, sample), out_shape=[jax.S...  3.3 us
    pallas_call x2, Pallas kernels, project(): pl.pallas_call(project_kernel, out_shape=[jax.ShapeDtypeStruct((rows, wid...  2.56 us
    concatenate x4, other arithmetic, widen(): jnp.concatenate([held, after(swap(held, axis, bit), *others)], axis=0)  1.02 us
  transfers between devices with their start and end apart: 9, of which 4 were waited for; matrix products, arithmetic and copies ran while one was open for 0% of the time, Pallas kernels for 32%

profile of v4, /device:TPU:0, one launch (start us, length us, event | category | flops | bytes accessed | tf_op | source)
XLA Modules:
  0.0 40.0 jit_solution(18223385183454206991)
XLA Ops:
  0.0 3.6 %pair_bias.1 = (bf16[36,1152]{1,0:T(8,128)(2,1)}, bf16[2,48,128]{2,1,0:T(8,128)(2,1)}, bf16[2,48,128]{2,1,0:T(8,128)(2,1)}) custom-call(bf16[2,1152,128]{2,1,0:T(8,128)(2,1)} %feat.7, bf16[2,1152,128]{2,1,0:T(8,128)(2,1)} %feat.7, bf16[36,72,128]{2,1,0:T(8,128)(2,1)} %bitcast.9, s32[36]{0:T(128)} %mask.1, bf16[16,128]{1,0:T(8,128)(2,1)} %bitcast.13), custom_call_target="tpu_custom_call" | custom-call | flops 60000000 | bytes 1000 | tf_op jit(solution)/shard_map/pair_bias/pallas_call | solution.py:95
  3.6 4.0 %collective-permute-start.1 = (bf16[1,36,1152]{2,1,0:T(8,128)(2,1)}, bf16[1,36,1152]{2,1,0:T(8,128)(2,1)S(1)}, u32[]{:S(2)}, u32[]{:S(2)}) collective-permute-start(bf16[1,36,1152]{2,1,0:T(8,128)(2,1)} %bitcast.10), channel_id=1, source_target_pairs={{0,4},{1,5},{2,6},{3,7},{4,0},{5,1},{6,2},{7,3},{8,12},{9,13},{10,... | collective-permute-start | bytes 248840 | tf_op jit(solution)/shard_map/ppermute | solution.py:123
  7.7 0.0 collective-permute-start
  7.7 0.8 %collective-permute-start.2 = (bf16[2,48,128]{2,1,0:T(8,128)(2,1)}, bf16[2,48,128]{2,1,0:T(8,128)(2,1)S(1)}, u32[]{:S(2)}, u32[]{:S(2)}) collective-permute-start(bf16[2,48,128]{2,1,0:T(8,128)(2,1)} %get-tuple-element.30), channel_id=1, source_target_pairs={{8,16},{16,8},{9,17},{17,9},{10,18},{18,10},{11,19},{19,11},{12,20... | collective-permute-start | bytes 73736 | tf_op jit(solution)/shard_map/ppermute | solution.py:396
  8.5 0.6 %collective-permute-done.inner = bf16[2,48,128]{2,1,0:T(8,128)(2,1)S(1)} collective-permute-done((bf16[2,48,128]{2,1,0:T(8,128)(2,1)}, bf16[2,48,128]{2,1,0:T(8,128)(2,1)S(1)}, u32[]{:S(2)}, u32[]{:S(2)}) %collective-permute-start) | collective-permute-done | bytes 24608 | tf_op jit(solution)/shard_map/ppermute | solution.py:123
  9.1 0.0 collective-permute-done.2.outer
  9.1 3.4 %collective-permute-done.1 = bf16[1,36,1152]{2,1,0:T(8,128)(2,1)S(1)} collective-permute-done((bf16[1,36,1152]{2,1,0:T(8,128)(2,1)}, bf16[1,36,1152]{2,1,0:T(8,128)(2,1)S(1)}, u32[]{:S(2)}, u32[]{:S(2)}) %collective-permute-start.1) | collective-permute-done | bytes 82976 | tf_op jit(solution)/shard_map/ppermute | solution.py:123
  12.5 0.9 %pad_maximum_fusion.3 = bf16[2,36,1152]{2,1,0:T(8,128)(2,1)S(1)} fusion(bf16[1,36,1152]{2,1,0:T(8,128)(2,1)S(1)} %collective-permute-done.1, bf16[1,36,1152]{2,1,0:T(8,128)(2,1)} %bitcast.11), kind=kLoop, calls=%fused_computation.3 | loop fusion | flops 82944 | bytes 331776 | tf_op jit(solution)/shard_map/concatenate | solution.py:399
  13.4 0.9 %collective-permute-start.3 = (bf16[2,36,1152]{2,1,0:T(8,128)(2,1)S(1)}, bf16[2,36,1152]{2,1,0:T(8,128)(2,1)S(1)}, u32[]{:S(2)}, u32[]{:S(2)}) collective-permute-start(bf16[2,36,1152]{2,1,0:T(8,128)(2,1)S(1)} %pad_maximum_fusion.3), channel_id=1, source_target_pairs={{0,2},{1,3},{2,0},{3,1},{4,6},{5,7},{6,4},{7,5},{8,10},{9,11},{10,... | collective-permute-start | bytes 497672 | tf_op jit(solution)/shard_map/ppermute | solution.py:123
  14.3 0.0 copy-start.4
  14.4 3.0 %atom_attention.2.mixed = bf16[1152,128]{1,0:T(8,128)(2,1)S(1)} custom-call(bf16[2,1152,128]{2,1,0:T(8,128)(2,1)S(1)} %copy-done, bf16[2,48,128]{2,1,0:T(8,128)(2,1)S(1)} %collective-permute-done.inner, bf16[2,48,128]{2,1,0:T(8,128)(2,1)S(1)} %collective-permute-done.2.outer, bf16[128,128]{1,0:T(8,128)(2,1)S(1)} %copy-done.7, ...), custom_call_target="tpu_custom_call" | custom-call | flops 80000000 | bytes 1000 | tf_op jit(solution)/shard_map/atom_attention/pallas_call | solution.py:194
  17.4 0.0 copy-start.3
  17.4 1.7 %gather_tokens.2 = (f32[72,768]{1,0:T(8,128)S(1)}, bf16[72,768]{1,0:T(8,128)(2,1)S(1)}) custom-call(bf16[1152,128]{1,0:T(8,128)(2,1)S(1)} %atom_attention.2.mixed, bf16[2,1152,128]{2,1,0:T(8,128)(2,1)S(1)} %copy-done, s32[1152]{0:T(1024)S(1)} %copy-done.11, bf16[128,128]{1,0:T(8,128)(2,1)S(1)} %copy-done.10, bf16[128,768]{1,0:T(8,128)(2,1)S(1)} %copy-done.6, ...), custom_call_target="tpu_custom_call" | custom-call | flops 20000000 | bytes 1000 | tf_op jit(solution)/shard_map/gather_tokens/pallas_call | solution.py:231
  19.1 3.0 %collective-permute-start.4 = (bf16[1,72,768]{2,1,0:T(8,128)(2,1)S(1)}, bf16[1,72,768]{2,1,0:T(8,128)(2,1)S(1)}, u32[]{:S(2)}, u32[]{:S(2)}) collective-permute-start(bf16[1,72,768]{2,1,0:T(8,128)(2,1)S(1)} %bitcast.7), channel_id=1, source_target_pairs={{0,16},{8,24},{16,0},{24,8},{1,17},{9,25},{17,1},{25,9},{2,18},{10... | collective-permute-start | bytes 331784 | tf_op jit(solution)/shard_map/ppermute | solution.py:123
  22.1 0.1 pad_maximum_fusion.near
  22.1 0.0 copy-start.1
  22.1 0.0 copy-start.2
  22.2 1.6 %collective-permute-start.7 = (bf16[4,36,1152]{2,1,0:T(8,128)(2,1)S(1)}, bf16[4,36,1152]{2,1,0:T(8,128)(2,1)S(1)}, u32[]{:S(2)}, u32[]{:S(2)}) collective-permute-start(bf16[4,36,1152]{2,1,0:T(8,128)(2,1)S(1)} %pad_maximum_fusion.near), channel_id=1, source_target_pairs={{0,1},{1,0},{2,3},{3,2},{4,5},{5,4},{6,7},{7,6},{8,9},{9,8},{10,11... | collective-permute-start | bytes 995336 | tf_op jit(solution)/shard_map/ppermute | solution.py:123
  23.7 3.0 %atom_attention.3.mixed = bf16[1152,128]{1,0:T(8,128)(2,1)S(1)} custom-call(bf16[2,1152,128]{2,1,0:T(8,128)(2,1)S(1)} %copy-done, bf16[2,48,128]{2,1,0:T(8,128)(2,1)S(1)} %collective-permute-done.inner, bf16[2,48,128]{2,1,0:T(8,128)(2,1)S(1)} %collective-permute-done.2.outer, bf16[128,128]{1,0:T(8,128)(2,1)S(1)} %copy-done.7, ...), custom_call_target="tpu_custom_call" | custom-call | flops 80000000 | bytes 1000 | tf_op jit(solution)/shard_map/atom_attention/pallas_call | solution.py:194
  26.7 0.0 collective-permute-done.4
  26.8 0.1 collective-permute-start.6
  26.9 1.6 %gather_tokens.3 = (f32[72,768]{1,0:T(8,128)S(1)}, bf16[72,768]{1,0:T(8,128)(2,1)S(1)}) custom-call(bf16[1152,128]{1,0:T(8,128)(2,1)S(1)} %atom_attention.3.mixed, bf16[2,1152,128]{2,1,0:T(8,128)(2,1)S(1)} %copy-done, s32[1152]{0:T(1024)S(1)} %copy-done.11, bf16[128,128]{1,0:T(8,128)(2,1)S(1)} %copy-done.10, bf16[128,768]{1,0:T(8,128)(2,1)S(1)} %copy-done.6, ...), custom_call_target="tpu_custom_call" | custom-call | flops 20000000 | bytes 1000 | tf_op jit(solution)/shard_map/gather_tokens/pallas_call | solution.py:231
  28.5 0.3 collective-permute-start.5
  28.8 1.3 %project.2 = (bf16[72,768]{1,0:T(8,128)(2,1)S(1)}, bf16[768,288]{1,0:T(8,128)(2,1)S(1)}, bf16[288,768]{1,0:T(8,128)(2,1)S(1)}, f32[72,768]{1,0:T(8,128)S(1)}) custom-call(bf16[2,72,768]{2,1,0:T(8,128)(2,1)S(1)} %pad_maximum_fusion.1.near, bf16[2,72,768]{2,1,0:T(8,128)(2,1)S(1)} %collective-permute-done.6.far, bf16[768,768]{1,0:T(8,128)(2,1)S(1)} %copy-done.1, ...), custom_call_target="tpu_custom_call" | custom-call | flops 40000000 | bytes 1000 | tf_op jit(solution)/shard_map/project/pallas_call | solution.py:295
  30.1 1.5 %collective-permute-done.7.far = bf16[4,36,1152]{2,1,0:T(8,128)(2,1)S(1)} collective-permute-done((bf16[4,36,1152]{2,1,0:T(8,128)(2,1)S(1)}, bf16[4,36,1152]{2,1,0:T(8,128)(2,1)S(1)}, u32[]{:S(2)}, u32[]{:S(2)}) %collective-permute-start.7) | collective-permute-done | bytes 331808 | tf_op jit(solution)/shard_map/ppermute | solution.py:123
  31.6 0.4 %turn_bias.1.bias = f32[1152,288]{1,0:T(8,128)S(1)} custom-call(bf16[4,36,1152]{2,1,0:T(8,128)(2,1)S(1)} %pad_maximum_fusion.near, bf16[4,36,1152]{2,1,0:T(8,128)(2,1)S(1)} %collective-permute-done.7.far), custom_call_target="tpu_custom_call" | custom-call | flops 20000000 | bytes 1000 | tf_op jit(solution)/shard_map/turn_bias/pallas_call | solution.py:258
  32.0 0.8 %copy-done.5 = bf16[768,768]{1,0:T(8,128)(2,1)S(1)} copy-done((bf16[768,768]{1,0:T(8,128)(2,1)S(1)}, bf16[768,768]{1,0:T(8,128)(2,1)}, u32[]{:S(2)}) %copy-start.5) | copy-done | bytes 1179672
  32.9 1.8 %attend.2.rest_0_ = bf16[72,768]{1,0:T(8,128)(2,1)S(1)} custom-call(bf16[72,768]{1,0:T(8,128)(2,1)S(1)} %get-tuple-element.39.q, bf16[768,288]{1,0:T(8,128)(2,1)S(1)} %get-tuple-element.40.kt, bf16[288,768]{1,0:T(8,128)(2,1)S(1)} %get-tuple-element.41.v, f32[72,768]{1,0:T(8,128)S(1)} %get-tuple-element.42.gate, f32[72,768]{1,0:T(8,128)S(1)} %get-tuple-element.43.token_in, ...), custom_call_target="tpu_custom_call" | custom-call | flops 60000000 | bytes 1000 | tf_op jit(solution)/shard_map/attend/pallas_call | solution.py:361
  34.7 0.1 collective-permute-start.8
  34.8 1.5 %collective-permute-done.8.far = bf16[2,72,768]{2,1,0:T(8,128)(2,1)S(1)} collective-permute-done((bf16[2,72,768]{2,1,0:T(8,128)(2,1)S(1)}, bf16[2,72,768]{2,1,0:T(8,128)(2,1)S(1)}, u32[]{:S(2)}, u32[]{:S(2)}) %collective-permute-start.8) | collective-permute-done | bytes 221216 | tf_op jit(solution)/shard_map/ppermute | solution.py:123
  36.2 1.3 %project.3 = (bf16[72,768]{1,0:T(8,128)(2,1)S(1)}, bf16[768,288]{1,0:T(8,128)(2,1)S(1)}, bf16[288,768]{1,0:T(8,128)(2,1)S(1)}, f32[72,768]{1,0:T(8,128)S(1)}) custom-call(bf16[2,72,768]{2,1,0:T(8,128)(2,1)S(1)} %pad_maximum_fusion.2.near, bf16[2,72,768]{2,1,0:T(8,128)(2,1)S(1)} %collective-permute-done.8.far, bf16[768,768]{1,0:T(8,128)(2,1)S(1)} %copy-done.1, ...), custom_call_target="tpu_custom_call" | custom-call | flops 40000000 | bytes 1000 | tf_op jit(solution)/shard_map/project/pallas_call | solution.py:295
  37.5 2.5 %attend.3 = bf16[2,72,768]{2,1,0:T(8,128)(2,1)} custom-call(bf16[72,768]{1,0:T(8,128)(2,1)S(1)} %get-tuple-element.46.q, bf16[768,288]{1,0:T(8,128)(2,1)S(1)} %get-tuple-element.47.kt, bf16[288,768]{1,0:T(8,128)(2,1)S(1)} %get-tuple-element.48.v, f32[72,768]{1,0:T(8,128)S(1)} %get-tuple-element.49.gate, f32[72,768]{1,0:T(8,128)S(1)} %get-tuple-element.50.token_in, ...), custom_call_target="tpu_custom_call" | custom-call | flops 60000000 | bytes 1000 | tf_op jit(solution)/shard_map/attend/pallas_call | solution.py:361
  (28 shorter events, 0.1 us)
Async XLA Ops:
  0.0 14.3 %copy-start = (bf16[2,1152,128]{2,1,0:T(8,128)(2,1)S(1)}, bf16[2,1152,128]{2,1,0:T(8,128)(2,1)}, u32[]{:S(2)}) copy-start(bf16[2,1152,128]{2,1,0:T(8,128)(2,1)} %feat.7) | copy-start | bytes 1769476
  0.0 14.3 %copy-start.9 = (bf16[128,128]{1,0:T(8,128)(2,1)S(1)}, bf16[128,128]{1,0:T(8,128)(2,1)}, u32[]{:S(2)}) copy-start(bf16[128,128]{1,0:T(8,128)(2,1)} %wv.5) | copy-start | bytes 98308
  0.0 14.3 %copy-start.8 = (bf16[128,128]{1,0:T(8,128)(2,1)S(1)}, bf16[128,128]{1,0:T(8,128)(2,1)}, u32[]{:S(2)}) copy-start(bf16[128,128]{1,0:T(8,128)(2,1)} %wk.5) | copy-start | bytes 98308
  0.0 14.3 %copy-start.7 = (bf16[128,128]{1,0:T(8,128)(2,1)S(1)}, bf16[128,128]{1,0:T(8,128)(2,1)}, u32[]{:S(2)}) copy-start(bf16[128,128]{1,0:T(8,128)(2,1)} %wq.5) | copy-start | bytes 98308
  0.0 17.4 %copy-start.6 = (bf16[128,768]{1,0:T(8,128)(2,1)S(1)}, bf16[128,768]{1,0:T(8,128)(2,1)}, u32[]{:S(2)}) copy-start(bf16[128,768]{1,0:T(8,128)(2,1)} %agg.3) | copy-start | bytes 589828
  0.0 17.4 %copy-start.10 = (bf16[128,128]{1,0:T(8,128)(2,1)S(1)}, bf16[128,128]{1,0:T(8,128)(2,1)}, u32[]{:S(2)}) copy-start(bf16[128,128]{1,0:T(8,128)(2,1)} %wo.5) | copy-start | bytes 98308
  0.0 17.4 %copy-start.11 = (s32[1152]{0:T(1024)S(1)}, s32[1152]{0:T(1024)}, u32[]{:S(2)}) copy-start(s32[1152]{0:T(1024)} %token_.3) | copy-start | bytes 13828
  0.0 17.4 %copy-start.12 = (f32[768]{0:T(1024)S(1)}, f32[768]{0:T(1024)}, u32[]{:S(2)}) copy-start(f32[768]{0:T(1024)} %gain.3) | copy-start | bytes 9220
  3.6 8.9 %collective-permute-start.1 = (bf16[1,36,1152]{2,1,0:T(8,128)(2,1)}, bf16[1,36,1152]{2,1,0:T(8,128)(2,1)S(1)}, u32[]{:S(2)}, u32[]{:S(2)}) collective-permute-start(bf16[1,36,1152]{2,1,0:T(8,128)(2,1)} %bitcast.10), channel_id=1, source_target_pairs={{0,4},{1,5},{2,6},{3,7},{4,0},{5,1},{6,2},{7,3},{8,12},{9,13},{10,... | collective-permute-start | bytes 248840 | tf_op jit(solution)/shard_map/ppermute | solution.py:123
  7.7 1.4 %collective-permute-start = (bf16[2,48,128]{2,1,0:T(8,128)(2,1)}, bf16[2,48,128]{2,1,0:T(8,128)(2,1)S(1)}, u32[]{:S(2)}, u32[]{:S(2)}) collective-permute-start(bf16[2,48,128]{2,1,0:T(8,128)(2,1)} %get-tuple-element.28), channel_id=1, source_target_pairs={{0,8},{8,0},{16,24},{24,16},{1,9},{9,1},{17,25},{25,17},{2,10},{10... | collective-permute-start | bytes 73736 | tf_op jit(solution)/shard_map/ppermute | solution.py:123
  7.7 14.4 %copy-start.13 = (bf16[36,1152]{1,0:T(8,128)(2,1)S(1)}, bf16[36,1152]{1,0:T(8,128)(2,1)}, u32[]{:S(2)}) copy-start(bf16[36,1152]{1,0:T(8,128)(2,1)} %get-tuple-element.29) | copy-start | bytes 248836
  7.7 1.4 %collective-permute-start.2 = (bf16[2,48,128]{2,1,0:T(8,128)(2,1)}, bf16[2,48,128]{2,1,0:T(8,128)(2,1)S(1)}, u32[]{:S(2)}, u32[]{:S(2)}) collective-permute-start(bf16[2,48,128]{2,1,0:T(8,128)(2,1)} %get-tuple-element.30), channel_id=1, source_target_pairs={{8,16},{16,8},{9,17},{17,9},{10,18},{18,10},{11,19},{19,11},{12,20... | collective-permute-start | bytes 73736 | tf_op jit(solution)/shard_map/ppermute | solution.py:396
  13.4 8.6 %collective-permute-start.3 = (bf16[2,36,1152]{2,1,0:T(8,128)(2,1)S(1)}, bf16[2,36,1152]{2,1,0:T(8,128)(2,1)S(1)}, u32[]{:S(2)}, u32[]{:S(2)}) collective-permute-start(bf16[2,36,1152]{2,1,0:T(8,128)(2,1)S(1)} %pad_maximum_fusion.3), channel_id=1, source_target_pairs={{0,2},{1,3},{2,0},{3,1},{4,6},{5,7},{6,4},{7,5},{8,10},{9,11},{10,... | collective-permute-start | bytes 497672 | tf_op jit(solution)/shard_map/ppermute | solution.py:123
  14.3 14.4 %copy-start.4 = (bf16[768,768]{1,0:T(8,128)(2,1)S(1)}, bf16[768,768]{1,0:T(8,128)(2,1)}, u32[]{:S(2)}) copy-start(bf16[768,768]{1,0:T(8,128)(2,1)} %wg.3) | copy-start | bytes 3538948
  17.4 11.4 %copy-start.3 = (bf16[768,768]{1,0:T(8,128)(2,1)S(1)}, bf16[768,768]{1,0:T(8,128)(2,1)}, u32[]{:S(2)}) copy-start(bf16[768,768]{1,0:T(8,128)(2,1)} %wv.7) | copy-start | bytes 3538948
  19.1 7.6 %collective-permute-start.4 = (bf16[1,72,768]{2,1,0:T(8,128)(2,1)S(1)}, bf16[1,72,768]{2,1,0:T(8,128)(2,1)S(1)}, u32[]{:S(2)}, u32[]{:S(2)}) collective-permute-start(bf16[1,72,768]{2,1,0:T(8,128)(2,1)S(1)} %bitcast.7), channel_id=1, source_target_pairs={{0,16},{8,24},{16,0},{24,8},{1,17},{9,25},{17,1},{25,9},{2,18},{10... | collective-permute-start | bytes 331784 | tf_op jit(solution)/shard_map/ppermute | solution.py:123
  22.1 6.7 %copy-start.1 = (bf16[768,768]{1,0:T(8,128)(2,1)S(1)}, bf16[768,768]{1,0:T(8,128)(2,1)}, u32[]{:S(2)}) copy-start(bf16[768,768]{1,0:T(8,128)(2,1)} %wq.7) | copy-start | bytes 3538948
  22.1 6.7 %copy-start.2 = (bf16[768,768]{1,0:T(8,128)(2,1)S(1)}, bf16[768,768]{1,0:T(8,128)(2,1)}, u32[]{:S(2)}) copy-start(bf16[768,768]{1,0:T(8,128)(2,1)} %wk.7) | copy-start | bytes 3538948
  22.2 9.4 %collective-permute-start.7 = (bf16[4,36,1152]{2,1,0:T(8,128)(2,1)S(1)}, bf16[4,36,1152]{2,1,0:T(8,128)(2,1)S(1)}, u32[]{:S(2)}, u32[]{:S(2)}) collective-permute-start(bf16[4,36,1152]{2,1,0:T(8,128)(2,1)S(1)} %pad_maximum_fusion.near), channel_id=1, source_target_pairs={{0,1},{1,0},{2,3},{3,2},{4,5},{5,4},{6,7},{7,6},{8,9},{9,8},{10,11... | collective-permute-start | bytes 995336 | tf_op jit(solution)/shard_map/ppermute | solution.py:123
  26.8 2.0 %collective-permute-start.6 = (bf16[2,72,768]{2,1,0:T(8,128)(2,1)S(1)}, bf16[2,72,768]{2,1,0:T(8,128)(2,1)S(1)}, u32[]{:S(2)}, u32[]{:S(2)}) collective-permute-start(bf16[2,72,768]{2,1,0:T(8,128)(2,1)S(1)} %pad_maximum_fusion.1.near), channel_id=1, source_target_pairs={{0,8},{8,0},{16,24},{24,16},{1,9},{9,1},{17,25},{25,17},{2,10},{10... | collective-permute-start | bytes 663560 | tf_op jit(solution)/shard_map/ppermute | solution.py:123
  28.5 6.1 %collective-permute-start.5 = (bf16[1,72,768]{2,1,0:T(8,128)(2,1)S(1)}, bf16[1,72,768]{2,1,0:T(8,128)(2,1)S(1)}, u32[]{:S(2)}, u32[]{:S(2)}) collective-permute-start(bf16[1,72,768]{2,1,0:T(8,128)(2,1)S(1)} %bitcast.5), channel_id=1, source_target_pairs={{0,16},{8,24},{16,0},{24,8},{1,17},{9,25},{17,1},{25,9},{2,18},{10... | collective-permute-start | bytes 331784 | tf_op jit(solution)/shard_map/ppermute | solution.py:123
  31.6 1.3 %copy-start.5 = (bf16[768,768]{1,0:T(8,128)(2,1)S(1)}, bf16[768,768]{1,0:T(8,128)(2,1)}, u32[]{:S(2)}) copy-start(bf16[768,768]{1,0:T(8,128)(2,1)} %wo.7) | copy-start | bytes 3538948
  34.7 1.5 %collective-permute-start.8 = (bf16[2,72,768]{2,1,0:T(8,128)(2,1)S(1)}, bf16[2,72,768]{2,1,0:T(8,128)(2,1)S(1)}, u32[]{:S(2)}, u32[]{:S(2)}) collective-permute-start(bf16[2,72,768]{2,1,0:T(8,128)(2,1)S(1)} %pad_maximum_fusion.2.near), channel_id=1, source_target_pairs={{0,8},{8,0},{16,24},{24,16},{1,9},{9,1},{17,25},{25,17},{2,10},{10... | collective-permute-start | bytes 663560 | tf_op jit(solution)/shard_map/ppermute | solution.py:123

commit v5 on v4

--- a/solution.py
+++ b/solution.py
@@ -142,20 +142,32 @@
     odd = rank % 2 == 1
     before = jnp.where(odd, inner[sample], outer[sample])
     behind = jnp.where(odd, outer[sample], inner[sample])
-    for part, at in ((before, 0), (behind, RIM + atoms)):
-        kv = dot(layer_norm(part.astype(F32)).astype(BF16), wqkv[:, chans:]).astype(BF16)
-        ks[at : at + RIM] = kv[:, :chans]
-        vs[at : at + RIM] = kv[:, chans:]
-    for c in range(0, atoms, LANES):
-        qkv = dot(layer_norm(feat[sample, c : c + LANES].astype(F32)).astype(BF16), wqkv).astype(BF16)
-        qs[c : c + LANES] = qkv[:, :chans]
-        ks[RIM + c : RIM + c + LANES] = qkv[:, chans : 2 * chans]
-        vs[RIM + c : RIM + c + LANES] = qkv[:, 2 * chans :]
+
+    def normalise(at):
+        if isinstance(at, int):
+            part = feat[sample, at : at + LANES]
+        else:
+            at, part = at
+        return at, layer_norm(part.astype(F32)).astype(BF16)
+
+    def project_atoms(item):
+        at, normed = item
+        count = normed.shape[0]
+        if count == RIM:
+            kv = dot(normed, wqkv[:, chans:]).astype(BF16)
+        else:
+            qkv = dot(normed, wqkv).astype(BF16)
+            qs[at : at + count] = qkv[:, :chans]
+            kv = qkv[:, chans:]
+        ks[RIM + at : RIM + at + count] = kv[:, :chans]
+        vs[RIM + at : RIM + at + count] = kv[:, chans:]
+
+    skewed([*range(0, atoms, LANES), (-RIM, before), (atoms, behind)], [normalise, project_atoms])
     rate = math.log2(math.e) / AHEAD_DIM**0.5
     tall = AHEADS * QWIN
     head_of = iota((QWIN, chans), 1) // AHEAD_DIM
     keyat = iota((tall, KWIN), 1)
-    batch = 2
+    batch = 4
 
     def score(first):
         out = []
@@ -211,16 +223,18 @@
     atoms = feat.shape[1]
     rows = token_in.shape[0]
     local = token[...].reshape(1, atoms) - lax.axis_index("row") * rows
-    step = 384
-    tsum = jnp.zeros((rows, agg.shape[1]), F32)
-    count = jnp.zeros((rows, 1), F32)
-    for c in range(0, atoms, step):
-        out = (feat[sample, c : c + step].astype(F32) + dot(mixed[c : c + step], wo[...])).astype(BF16)
-        hidden = jnp.maximum(dot(out, agg[...]), 0.0).astype(BF16)
-        onehot = (iota((rows, step), 0) == local[:, c : c + step]).astype(F32)
-        count = count + jnp.sum(onehot, -1, keepdims=True)
-        tsum = tsum + dot(onehot.astype(BF16), hidden)
-    tin = tsum / count
+    step = 192
+
+    def finish(c):
+        return c, (feat[sample, c : c + step].astype(F32) + dot(mixed[c : c + step], wo[...])).astype(BF16)
+
+    def hide(item):
+        c, out = item
+        return c, jnp.maximum(dot(out, agg[...]), 0.0).astype(BF16)
+
+    hidden = jnp.concatenate([h for _, h in skewed(range(0, atoms, step), [finish, hide])], axis=0)
+    onehot = (iota((rows, atoms), 0) == local).astype(F32)
+    tin = dot(onehot.astype(BF16), hidden) / jnp.sum(onehot, -1, keepdims=True)
     token_in[...] = tin
     token_norm[...] = (layer_norm(tin) * gain[...].reshape(1, -1)).astype(BF16)
 
@@ -313,17 +327,18 @@
     rows, width = token_in.shape
     scale = 1.0 / HEAD_DIM**0.5
     lane = iota((rows, 2 * LANES), 1)
-    work = [(base, h) for base, heads in head_groups(width) for h in heads]
+    work = [(base, heads[i : i + 2]) for base, heads in head_groups(width) for i in range(0, len(heads), 2)]
 
     def channels(base, h):
         low = h * HEAD_DIM - base
         return (lane >= low) & (lane < low + HEAD_DIM)
 
     def score(item):
-        base, h = item
-        mine = q[:, base : base + 2 * LANES]
-        mine = jnp.where(channels(base, h), mine, jnp.zeros_like(mine))
-        return item, dot(mine, kt[base : base + 2 * LANES]) * scale + bias[h * rows : (h + 1) * rows]
+        base, heads = item
+        mine = q[:, base : base + 2 * LANES].astype(F32)
+        mine = jnp.concatenate([jnp.where(channels(base, h), mine, 0.0) for h in heads], axis=0).astype(BF16)
+        some = bias[heads[0] * rows : (heads[-1] + 1) * rows]
+        return item, dot(mine, kt[base : base + 2 * LANES]) * scale + some
 
     def soften(item):
         place, sc = item
@@ -333,9 +348,10 @@
     mixes = {}
 
     def mix(item):
-        (base, h), e, share = item
+        (base, heads), e, share = item
         o = dot(e, v[:, base : base + 2 * LANES]) * share
-        mixes[base] = jnp.where(channels(base, h), o, mixes.get(base, 0.0))
+        for i, h in enumerate(heads):
+            mixes[base] = jnp.where(channels(base, h), o[i * rows : (i + 1) * rows], mixes.get(base, 0.0))
 
     skewed(work, [score, soften, mix])
     tiles = {}
@@ -392,7 +408,7 @@
     ranks = lax.axis_size("row")
     bias, inner, outer = pair_bias(atom_feat, pair_cond, token_mask, pair_weight)
     inner = swap(inner, "row", 1)
-    odd_pairs = [(i, i + 1) for i in range(1, ranks - 1, 2)]
+    odd_pairs = [(i, (i + 1) % ranks) for i in range(1, ranks, 2)]
     outer = lax.ppermute(outer, "row", odd_pairs + [(j, i) for i, j in odd_pairs])
 
     def widen(held, axis, bit, *others):

time: 40.2 us -> 38.6 us (0.960)
  Pallas kernels: 20.1 us -> 18.9 us
  waiting for transfers between devices: 7.03 us -> 6.61 us
    ppermute x8, waiting for transfers between devices: 7.03 us -> 4.79 us  [swap(): lax.ppermute(held, axis, [(i, i ^ far) for i in range(lax.axis_size(axis))])]
    ppermute x1, waiting for transfers between devices: 0.01 us -> 1.83 us  [shards(): lax.ppermute(outer, 'row', odd_pairs + [(j, i) for i, j in odd_pairs])]
    pallas_call x2, Pallas kernels: 6.03 us -> 4.78 us  [atom_attention(): pl.pallas_call(functools.partial(atom_kernel, sample), out_shape=jax.Shap...]
    ppermute x1, starting transfers between devices: 0.78 us -> 1.63 us  [shards(): lax.ppermute(outer, 'row', odd_pairs + [(j, i) for i, j in odd_pairs])]
    ppermute x8, starting transfers between devices: 9.87 us -> 9.07 us  [swap(): lax.ppermute(held, axis, [(i, i ^ far) for i in range(lax.axis_size(axis))])]
  transfers between devices with their start and end apart: 9 -> 9, of which waited for: 4 -> 4; matrix products, arithmetic and copies ran while one was open for 0% -> 0% of each run, Pallas kernels for 32% -> 30%
where the time goes in v5:
time: 38.6 us; the launch traced here: 38.4 us
  Pallas kernels  18.9 us (49%)
  starting transfers between devices  10.7 us (28%)
  waiting for transfers between devices  6.61 us (17%)
  other arithmetic  1.02 us (3%)
  local copies, waits for them, and re-layouts  0.91 us (2%)
    ppermute x8, starting transfers between devices, swap(): lax.ppermute(held, axis, [(i, i ^ far) for i in range(lax.axis_size(axis))])  9.07 us
    ppermute x8, waiting for transfers between devices, swap(): lax.ppermute(held, axis, [(i, i ^ far) for i in range(lax.axis_size(axis))])  4.79 us
    pallas_call x2, Pallas kernels, atom_attention(): pl.pallas_call(functools.partial(atom_kernel, sample), out_shape=jax.Shap...  4.78 us
    pallas_call x2, Pallas kernels, attend(): pl.pallas_call(attend_kernel, out_shape=jax.ShapeDtypeStruct(shape, BF16)...  3.93 us
    pallas_call x2, Pallas kernels, gather_tokens(): pl.pallas_call(functools.partial(gather_kernel, sample), out_shape=[jax.S...  3.63 us
    pallas_call x1, Pallas kernels, pair_bias(): pl.pallas_call(bias_kernel, grid=(1,), out_shape=[jax.ShapeDtypeStruct((c...  3.57 us
    pallas_call x2, Pallas kernels, project(): pl.pallas_call(project_kernel, out_shape=[jax.ShapeDtypeStruct((rows, wid...  2.57 us
    ppermute x1, waiting for transfers between devices, shards(): lax.ppermute(outer, 'row', odd_pairs + [(j, i) for i, j in odd_pairs])  1.83 us
  transfers between devices with their start and end apart: 9, of which 4 were waited for; matrix products, arithmetic and copies ran while one was open for 0% of the time, Pallas kernels for 30%

profile of v5, /device:TPU:0, one launch (start us, length us, event | category | flops | bytes accessed | tf_op | source)
XLA Modules:
  0.0 38.4 jit_solution(15703749526045313520)
XLA Ops:
  0.0 3.6 %pair_bias.1 = (bf16[36,1152]{1,0:T(8,128)(2,1)}, bf16[2,48,128]{2,1,0:T(8,128)(2,1)}, bf16[2,48,128]{2,1,0:T(8,128)(2,1)}) custom-call(bf16[2,1152,128]{2,1,0:T(8,128)(2,1)} %feat.7, bf16[2,1152,128]{2,1,0:T(8,128)(2,1)} %feat.7, bf16[36,72,128]{2,1,0:T(8,128)(2,1)} %bitcast.9, s32[36]{0:T(128)} %mask.1, bf16[16,128]{1,0:T(8,128)(2,1)} %bitcast.13), custom_call_target="tpu_custom_call" | custom-call | flops 60000000 | bytes 1000 | tf_op jit(solution)/shard_map/pair_bias/pallas_call | solution.py:95
  3.6 4.0 %collective-permute-start.1 = (bf16[1,36,1152]{2,1,0:T(8,128)(2,1)}, bf16[1,36,1152]{2,1,0:T(8,128)(2,1)S(1)}, u32[]{:S(2)}, u32[]{:S(2)}) collective-permute-start(bf16[1,36,1152]{2,1,0:T(8,128)(2,1)} %bitcast.10), channel_id=1, source_target_pairs={{0,4},{1,5},{2,6},{3,7},{4,0},{5,1},{6,2},{7,3},{8,12},{9,13},{10,... | collective-permute-start | bytes 248840 | tf_op jit(solution)/shard_map/ppermute | solution.py:123
  7.7 0.0 collective-permute-start
  7.7 1.6 %collective-permute-start.2 = (bf16[2,48,128]{2,1,0:T(8,128)(2,1)}, bf16[2,48,128]{2,1,0:T(8,128)(2,1)S(1)}, u32[]{:S(2)}, u32[]{:S(2)}) collective-permute-start(bf16[2,48,128]{2,1,0:T(8,128)(2,1)} %get-tuple-element.30), channel_id=1, source_target_pairs={{8,16},{24,0},{16,8},{0,24},{9,17},{25,1},{17,9},{1,25},{10,18},{2... | collective-permute-start | bytes 73736 | tf_op jit(solution)/shard_map/ppermute | solution.py:412
  9.3 1.8 %collective-permute-done.2.outer = bf16[2,48,128]{2,1,0:T(8,128)(2,1)S(1)} collective-permute-done((bf16[2,48,128]{2,1,0:T(8,128)(2,1)}, bf16[2,48,128]{2,1,0:T(8,128)(2,1)S(1)}, u32[]{:S(2)}, u32[]{:S(2)}) %collective-permute-start.2) | collective-permute-done | bytes 24608 | tf_op jit(solution)/shard_map/ppermute | solution.py:412
  11.1 1.4 %collective-permute-done.1 = bf16[1,36,1152]{2,1,0:T(8,128)(2,1)S(1)} collective-permute-done((bf16[1,36,1152]{2,1,0:T(8,128)(2,1)}, bf16[1,36,1152]{2,1,0:T(8,128)(2,1)S(1)}, u32[]{:S(2)}, u32[]{:S(2)}) %collective-permute-start.1) | collective-permute-done | bytes 82976 | tf_op jit(solution)/shard_map/ppermute | solution.py:123
  12.5 0.9 %pad_maximum_fusion.3 = bf16[2,36,1152]{2,1,0:T(8,128)(2,1)S(1)} fusion(bf16[1,36,1152]{2,1,0:T(8,128)(2,1)S(1)} %collective-permute-done.1, bf16[1,36,1152]{2,1,0:T(8,128)(2,1)} %bitcast.11), kind=kLoop, calls=%fused_computation.3 | loop fusion | flops 82944 | bytes 331776 | tf_op jit(solution)/shard_map/concatenate | solution.py:415
  13.4 0.9 %collective-permute-start.3 = (bf16[2,36,1152]{2,1,0:T(8,128)(2,1)S(1)}, bf16[2,36,1152]{2,1,0:T(8,128)(2,1)S(1)}, u32[]{:S(2)}, u32[]{:S(2)}) collective-permute-start(bf16[2,36,1152]{2,1,0:T(8,128)(2,1)S(1)} %pad_maximum_fusion.3), channel_id=1, source_target_pairs={{0,2},{1,3},{2,0},{3,1},{4,6},{5,7},{6,4},{7,5},{8,10},{9,11},{10,... | collective-permute-start | bytes 497672 | tf_op jit(solution)/shard_map/ppermute | solution.py:123
  14.3 0.0 copy-start.4
  14.4 2.4 %atom_attention.2.mixed = bf16[1152,128]{1,0:T(8,128)(2,1)S(1)} custom-call(bf16[2,1152,128]{2,1,0:T(8,128)(2,1)S(1)} %copy-done, bf16[2,48,128]{2,1,0:T(8,128)(2,1)S(1)} %collective-permute-done.inner, bf16[2,48,128]{2,1,0:T(8,128)(2,1)S(1)} %collective-permute-done.2.outer, bf16[128,128]{1,0:T(8,128)(2,1)S(1)} %copy-done.7, ...), custom_call_target="tpu_custom_call" | custom-call | flops 80000000 | bytes 1000 | tf_op jit(solution)/shard_map/atom_attention/pallas_call | solution.py:206
  16.8 0.0 copy-start.3
  16.8 1.8 %gather_tokens.2 = (f32[72,768]{1,0:T(8,128)S(1)}, bf16[72,768]{1,0:T(8,128)(2,1)S(1)}) custom-call(bf16[1152,128]{1,0:T(8,128)(2,1)S(1)} %atom_attention.2.mixed, bf16[2,1152,128]{2,1,0:T(8,128)(2,1)S(1)} %copy-done, s32[1152]{0:T(1024)S(1)} %copy-done.11, bf16[128,128]{1,0:T(8,128)(2,1)S(1)} %copy-done.10, bf16[128,768]{1,0:T(8,128)(2,1)S(1)} %copy-done.6, ...), custom_call_target="tpu_custom_call" | custom-call | flops 20000000 | bytes 1000 | tf_op jit(solution)/shard_map/gather_tokens/pallas_call | solution.py:245
  18.6 1.6 %collective-permute-start.4 = (bf16[1,72,768]{2,1,0:T(8,128)(2,1)S(1)}, bf16[1,72,768]{2,1,0:T(8,128)(2,1)S(1)}, u32[]{:S(2)}, u32[]{:S(2)}) collective-permute-start(bf16[1,72,768]{2,1,0:T(8,128)(2,1)S(1)} %bitcast.7), channel_id=1, source_target_pairs={{0,16},{8,24},{16,0},{24,8},{1,17},{9,25},{17,1},{25,9},{2,18},{10... | collective-permute-start | bytes 331784 | tf_op jit(solution)/shard_map/ppermute | solution.py:123
  20.2 0.0 collective-permute-done.3
  20.2 0.1 pad_maximum_fusion.near
  20.3 0.0 copy-start.1
  20.3 0.0 copy-start.2
  20.3 1.6 %collective-permute-start.7 = (bf16[4,36,1152]{2,1,0:T(8,128)(2,1)S(1)}, bf16[4,36,1152]{2,1,0:T(8,128)(2,1)S(1)}, u32[]{:S(2)}, u32[]{:S(2)}) collective-permute-start(bf16[4,36,1152]{2,1,0:T(8,128)(2,1)S(1)} %pad_maximum_fusion.near), channel_id=1, source_target_pairs={{0,1},{1,0},{2,3},{3,2},{4,5},{5,4},{6,7},{7,6},{8,9},{9,8},{10,11... | collective-permute-start | bytes 995336 | tf_op jit(solution)/shard_map/ppermute | solution.py:123
  21.9 2.4 %atom_attention.3.mixed = bf16[1152,128]{1,0:T(8,128)(2,1)S(1)} custom-call(bf16[2,1152,128]{2,1,0:T(8,128)(2,1)S(1)} %copy-done, bf16[2,48,128]{2,1,0:T(8,128)(2,1)S(1)} %collective-permute-done.inner, bf16[2,48,128]{2,1,0:T(8,128)(2,1)S(1)} %collective-permute-done.2.outer, bf16[128,128]{1,0:T(8,128)(2,1)S(1)} %copy-done.7, ...), custom_call_target="tpu_custom_call" | custom-call | flops 80000000 | bytes 1000 | tf_op jit(solution)/shard_map/atom_attention/pallas_call | solution.py:206
  24.3 0.0 collective-permute-done.4
  24.3 0.1 collective-permute-start.6
  24.4 1.8 %gather_tokens.3 = (f32[72,768]{1,0:T(8,128)S(1)}, bf16[72,768]{1,0:T(8,128)(2,1)S(1)}) custom-call(bf16[1152,128]{1,0:T(8,128)(2,1)S(1)} %atom_attention.3.mixed, bf16[2,1152,128]{2,1,0:T(8,128)(2,1)S(1)} %copy-done, s32[1152]{0:T(1024)S(1)} %copy-done.11, bf16[128,128]{1,0:T(8,128)(2,1)S(1)} %copy-done.10, bf16[128,768]{1,0:T(8,128)(2,1)S(1)} %copy-done.6, ...), custom_call_target="tpu_custom_call" | custom-call | flops 20000000 | bytes 1000 | tf_op jit(solution)/shard_map/gather_tokens/pallas_call | solution.py:245
  26.2 0.8 %collective-permute-start.5 = (bf16[1,72,768]{2,1,0:T(8,128)(2,1)S(1)}, bf16[1,72,768]{2,1,0:T(8,128)(2,1)S(1)}, u32[]{:S(2)}, u32[]{:S(2)}) collective-permute-start(bf16[1,72,768]{2,1,0:T(8,128)(2,1)S(1)} %bitcast.5), channel_id=1, source_target_pairs={{0,16},{8,24},{16,0},{24,8},{1,17},{9,25},{17,1},{25,9},{2,18},{10... | collective-permute-start | bytes 331784 | tf_op jit(solution)/shard_map/ppermute | solution.py:123
  27.1 1.3 %project.2 = (bf16[72,768]{1,0:T(8,128)(2,1)S(1)}, bf16[768,288]{1,0:T(8,128)(2,1)S(1)}, bf16[288,768]{1,0:T(8,128)(2,1)S(1)}, f32[72,768]{1,0:T(8,128)S(1)}) custom-call(bf16[2,72,768]{2,1,0:T(8,128)(2,1)S(1)} %pad_maximum_fusion.1.near, bf16[2,72,768]{2,1,0:T(8,128)(2,1)S(1)} %collective-permute-done.6.far, bf16[768,768]{1,0:T(8,128)(2,1)S(1)} %copy-done.1, ...), custom_call_target="tpu_custom_call" | custom-call | flops 40000000 | bytes 1000 | tf_op jit(solution)/shard_map/project/pallas_call | solution.py:309
  28.4 1.9 %collective-permute-done.7.far = bf16[4,36,1152]{2,1,0:T(8,128)(2,1)S(1)} collective-permute-done((bf16[4,36,1152]{2,1,0:T(8,128)(2,1)S(1)}, bf16[4,36,1152]{2,1,0:T(8,128)(2,1)S(1)}, u32[]{:S(2)}, u32[]{:S(2)}) %collective-permute-start.7) | collective-permute-done | bytes 331808 | tf_op jit(solution)/shard_map/ppermute | solution.py:123
  30.3 0.4 %turn_bias.1.bias = f32[1152,288]{1,0:T(8,128)S(1)} custom-call(bf16[4,36,1152]{2,1,0:T(8,128)(2,1)S(1)} %pad_maximum_fusion.near, bf16[4,36,1152]{2,1,0:T(8,128)(2,1)S(1)} %collective-permute-done.7.far), custom_call_target="tpu_custom_call" | custom-call | flops 20000000 | bytes 1000 | tf_op jit(solution)/shard_map/turn_bias/pallas_call | solution.py:272
  30.7 0.8 %copy-done.5 = bf16[768,768]{1,0:T(8,128)(2,1)S(1)} copy-done((bf16[768,768]{1,0:T(8,128)(2,1)S(1)}, bf16[768,768]{1,0:T(8,128)(2,1)}, u32[]{:S(2)}) %copy-start.5) | copy-done | bytes 1179672
  31.6 1.6 %attend.2.rest_0_ = bf16[72,768]{1,0:T(8,128)(2,1)S(1)} custom-call(bf16[72,768]{1,0:T(8,128)(2,1)S(1)} %get-tuple-element.39.q, bf16[768,288]{1,0:T(8,128)(2,1)S(1)} %get-tuple-element.40.kt, bf16[288,768]{1,0:T(8,128)(2,1)S(1)} %get-tuple-element.41.v, f32[72,768]{1,0:T(8,128)S(1)} %get-tuple-element.42.gate, f32[72,768]{1,0:T(8,128)S(1)} %get-tuple-element.43.token_in, ...), custom_call_target="tpu_custom_call" | custom-call | flops 60000000 | bytes 1000 | tf_op jit(solution)/shard_map/attend/pallas_call | solution.py:377
  33.2 0.1 collective-permute-start.8
  33.3 1.5 %collective-permute-done.8.far = bf16[2,72,768]{2,1,0:T(8,128)(2,1)S(1)} collective-permute-done((bf16[2,72,768]{2,1,0:T(8,128)(2,1)S(1)}, bf16[2,72,768]{2,1,0:T(8,128)(2,1)S(1)}, u32[]{:S(2)}, u32[]{:S(2)}) %collective-permute-start.8) | collective-permute-done | bytes 221216 | tf_op jit(solution)/shard_map/ppermute | solution.py:123
  34.8 1.3 %project.3 = (bf16[72,768]{1,0:T(8,128)(2,1)S(1)}, bf16[768,288]{1,0:T(8,128)(2,1)S(1)}, bf16[288,768]{1,0:T(8,128)(2,1)S(1)}, f32[72,768]{1,0:T(8,128)S(1)}) custom-call(bf16[2,72,768]{2,1,0:T(8,128)(2,1)S(1)} %pad_maximum_fusion.2.near, bf16[2,72,768]{2,1,0:T(8,128)(2,1)S(1)} %collective-permute-done.8.far, bf16[768,768]{1,0:T(8,128)(2,1)S(1)} %copy-done.1, ...), custom_call_target="tpu_custom_call" | custom-call | flops 40000000 | bytes 1000 | tf_op jit(solution)/shard_map/project/pallas_call | solution.py:309
  36.1 2.3 %attend.3 = bf16[2,72,768]{2,1,0:T(8,128)(2,1)} custom-call(bf16[72,768]{1,0:T(8,128)(2,1)S(1)} %get-tuple-element.46.q, bf16[768,288]{1,0:T(8,128)(2,1)S(1)} %get-tuple-element.47.kt, bf16[288,768]{1,0:T(8,128)(2,1)S(1)} %get-tuple-element.48.v, f32[72,768]{1,0:T(8,128)S(1)} %get-tuple-element.49.gate, f32[72,768]{1,0:T(8,128)S(1)} %get-tuple-element.50.token_in, ...), custom_call_target="tpu_custom_call" | custom-call | flops 60000000 | bytes 1000 | tf_op jit(solution)/shard_map/attend/pallas_call | solution.py:377
  (28 shorter events, 0.1 us)
Async XLA Ops:
  0.0 14.3 %copy-start = (bf16[2,1152,128]{2,1,0:T(8,128)(2,1)S(1)}, bf16[2,1152,128]{2,1,0:T(8,128)(2,1)}, u32[]{:S(2)}) copy-start(bf16[2,1152,128]{2,1,0:T(8,128)(2,1)} %feat.7) | copy-start | bytes 1769476
  0.0 14.3 %copy-start.9 = (bf16[128,128]{1,0:T(8,128)(2,1)S(1)}, bf16[128,128]{1,0:T(8,128)(2,1)}, u32[]{:S(2)}) copy-start(bf16[128,128]{1,0:T(8,128)(2,1)} %wv.5) | copy-start | bytes 98308
  0.0 14.3 %copy-start.8 = (bf16[128,128]{1,0:T(8,128)(2,1)S(1)}, bf16[128,128]{1,0:T(8,128)(2,1)}, u32[]{:S(2)}) copy-start(bf16[128,128]{1,0:T(8,128)(2,1)} %wk.5) | copy-start | bytes 98308
  0.0 14.3 %copy-start.7 = (bf16[128,128]{1,0:T(8,128)(2,1)S(1)}, bf16[128,128]{1,0:T(8,128)(2,1)}, u32[]{:S(2)}) copy-start(bf16[128,128]{1,0:T(8,128)(2,1)} %wq.5) | copy-start | bytes 98308
  0.0 16.7 %copy-start.6 = (bf16[128,768]{1,0:T(8,128)(2,1)S(1)}, bf16[128,768]{1,0:T(8,128)(2,1)}, u32[]{:S(2)}) copy-start(bf16[128,768]{1,0:T(8,128)(2,1)} %agg.3) | copy-start | bytes 589828
  0.0 16.7 %copy-start.10 = (bf16[128,128]{1,0:T(8,128)(2,1)S(1)}, bf16[128,128]{1,0:T(8,128)(2,1)}, u32[]{:S(2)}) copy-start(bf16[128,128]{1,0:T(8,128)(2,1)} %wo.5) | copy-start | bytes 98308
  0.0 16.7 %copy-start.11 = (s32[1152]{0:T(1024)S(1)}, s32[1152]{0:T(1024)}, u32[]{:S(2)}) copy-start(s32[1152]{0:T(1024)} %token_.3) | copy-start | bytes 13828
  0.0 16.7 %copy-start.12 = (f32[768]{0:T(1024)S(1)}, f32[768]{0:T(1024)}, u32[]{:S(2)}) copy-start(f32[768]{0:T(1024)} %gain.3) | copy-start | bytes 9220
  3.6 8.9 %collective-permute-start.1 = (bf16[1,36,1152]{2,1,0:T(8,128)(2,1)}, bf16[1,36,1152]{2,1,0:T(8,128)(2,1)S(1)}, u32[]{:S(2)}, u32[]{:S(2)}) collective-permute-start(bf16[1,36,1152]{2,1,0:T(8,128)(2,1)} %bitcast.10), channel_id=1, source_target_pairs={{0,4},{1,5},{2,6},{3,7},{4,0},{5,1},{6,2},{7,3},{8,12},{9,13},{10,... | collective-permute-start | bytes 248840 | tf_op jit(solution)/shard_map/ppermute | solution.py:123
  7.7 1.6 %collective-permute-start = (bf16[2,48,128]{2,1,0:T(8,128)(2,1)}, bf16[2,48,128]{2,1,0:T(8,128)(2,1)S(1)}, u32[]{:S(2)}, u32[]{:S(2)}) collective-permute-start(bf16[2,48,128]{2,1,0:T(8,128)(2,1)} %get-tuple-element.28), channel_id=1, source_target_pairs={{0,8},{8,0},{16,24},{24,16},{1,9},{9,1},{17,25},{25,17},{2,10},{10... | collective-permute-start | bytes 73736 | tf_op jit(solution)/shard_map/ppermute | solution.py:123
  7.7 12.5 %copy-start.13 = (bf16[36,1152]{1,0:T(8,128)(2,1)S(1)}, bf16[36,1152]{1,0:T(8,128)(2,1)}, u32[]{:S(2)}) copy-start(bf16[36,1152]{1,0:T(8,128)(2,1)} %get-tuple-element.29) | copy-start | bytes 248836
  7.7 3.5 %collective-permute-start.2 = (bf16[2,48,128]{2,1,0:T(8,128)(2,1)}, bf16[2,48,128]{2,1,0:T(8,128)(2,1)S(1)}, u32[]{:S(2)}, u32[]{:S(2)}) collective-permute-start(bf16[2,48,128]{2,1,0:T(8,128)(2,1)} %get-tuple-element.30), channel_id=1, source_target_pairs={{8,16},{24,0},{16,8},{0,24},{9,17},{25,1},{17,9},{1,25},{10,18},{2... | collective-permute-start | bytes 73736 | tf_op jit(solution)/shard_map/ppermute | solution.py:412
  13.4 6.8 %collective-permute-start.3 = (bf16[2,36,1152]{2,1,0:T(8,128)(2,1)S(1)}, bf16[2,36,1152]{2,1,0:T(8,128)(2,1)S(1)}, u32[]{:S(2)}, u32[]{:S(2)}) collective-permute-start(bf16[2,36,1152]{2,1,0:T(8,128)(2,1)S(1)} %pad_maximum_fusion.3), channel_id=1, source_target_pairs={{0,2},{1,3},{2,0},{3,1},{4,6},{5,7},{6,4},{7,5},{8,10},{9,11},{10,... | collective-permute-start | bytes 497672 | tf_op jit(solution)/shard_map/ppermute | solution.py:123
  14.3 12.7 %copy-start.4 = (bf16[768,768]{1,0:T(8,128)(2,1)S(1)}, bf16[768,768]{1,0:T(8,128)(2,1)}, u32[]{:S(2)}) copy-start(bf16[768,768]{1,0:T(8,128)(2,1)} %wg.3) | copy-start | bytes 3538948
  16.8 10.3 %copy-start.3 = (bf16[768,768]{1,0:T(8,128)(2,1)S(1)}, bf16[768,768]{1,0:T(8,128)(2,1)}, u32[]{:S(2)}) copy-start(bf16[768,768]{1,0:T(8,128)(2,1)} %wv.7) | copy-start | bytes 3538948
  18.6 5.6 %collective-permute-start.4 = (bf16[1,72,768]{2,1,0:T(8,128)(2,1)S(1)}, bf16[1,72,768]{2,1,0:T(8,128)(2,1)S(1)}, u32[]{:S(2)}, u32[]{:S(2)}) collective-permute-start(bf16[1,72,768]{2,1,0:T(8,128)(2,1)S(1)} %bitcast.7), channel_id=1, source_target_pairs={{0,16},{8,24},{16,0},{24,8},{1,17},{9,25},{17,1},{25,9},{2,18},{10... | collective-permute-start | bytes 331784 | tf_op jit(solution)/shard_map/ppermute | solution.py:123
  20.3 6.8 %copy-start.1 = (bf16[768,768]{1,0:T(8,128)(2,1)S(1)}, bf16[768,768]{1,0:T(8,128)(2,1)}, u32[]{:S(2)}) copy-start(bf16[768,768]{1,0:T(8,128)(2,1)} %wq.7) | copy-start | bytes 3538948
  20.3 6.8 %copy-start.2 = (bf16[768,768]{1,0:T(8,128)(2,1)S(1)}, bf16[768,768]{1,0:T(8,128)(2,1)}, u32[]{:S(2)}) copy-start(bf16[768,768]{1,0:T(8,128)(2,1)} %wk.7) | copy-start | bytes 3538948
  20.3 10.0 %collective-permute-start.7 = (bf16[4,36,1152]{2,1,0:T(8,128)(2,1)S(1)}, bf16[4,36,1152]{2,1,0:T(8,128)(2,1)S(1)}, u32[]{:S(2)}, u32[]{:S(2)}) collective-permute-start(bf16[4,36,1152]{2,1,0:T(8,128)(2,1)S(1)} %pad_maximum_fusion.near), channel_id=1, source_target_pairs={{0,1},{1,0},{2,3},{3,2},{4,5},{5,4},{6,7},{7,6},{8,9},{9,8},{10,11... | collective-permute-start | bytes 995336 | tf_op jit(solution)/shard_map/ppermute | solution.py:123
  24.3 2.7 %collective-permute-start.6 = (bf16[2,72,768]{2,1,0:T(8,128)(2,1)S(1)}, bf16[2,72,768]{2,1,0:T(8,128)(2,1)S(1)}, u32[]{:S(2)}, u32[]{:S(2)}) collective-permute-start(bf16[2,72,768]{2,1,0:T(8,128)(2,1)S(1)} %pad_maximum_fusion.1.near), channel_id=1, source_target_pairs={{0,8},{8,0},{16,24},{24,16},{1,9},{9,1},{17,25},{25,17},{2,10},{10... | collective-permute-start | bytes 663560 | tf_op jit(solution)/shard_map/ppermute | solution.py:123
  26.2 7.0 %collective-permute-start.5 = (bf16[1,72,768]{2,1,0:T(8,128)(2,1)S(1)}, bf16[1,72,768]{2,1,0:T(8,128)(2,1)S(1)}, u32[]{:S(2)}, u32[]{:S(2)}) collective-permute-start(bf16[1,72,768]{2,1,0:T(8,128)(2,1)S(1)} %bitcast.5), channel_id=1, source_target_pairs={{0,16},{8,24},{16,0},{24,8},{1,17},{9,25},{17,1},{25,9},{2,18},{10... | collective-permute-start | bytes 331784 | tf_op jit(solution)/shard_map/ppermute | solution.py:123
  30.3 1.3 %copy-start.5 = (bf16[768,768]{1,0:T(8,128)(2,1)S(1)}, bf16[768,768]{1,0:T(8,128)(2,1)}, u32[]{:S(2)}) copy-start(bf16[768,768]{1,0:T(8,128)(2,1)} %wo.7) | copy-start | bytes 3538948
  33.2 1.5 %collective-permute-start.8 = (bf16[2,72,768]{2,1,0:T(8,128)(2,1)S(1)}, bf16[2,72,768]{2,1,0:T(8,128)(2,1)S(1)}, u32[]{:S(2)}, u32[]{:S(2)}) collective-permute-start(bf16[2,72,768]{2,1,0:T(8,128)(2,1)S(1)} %pad_maximum_fusion.2.near), channel_id=1, source_target_pairs={{0,8},{8,0},{16,24},{24,16},{1,9},{9,1},{17,25},{25,17},{2,10},{10... | collective-permute-start | bytes 663560 | tf_op jit(solution)/shard_map/ppermute | solution.py:123

commit v6 on v5

--- a/solution.py
+++ b/solution.py
@@ -127,10 +127,11 @@
     return [devices >> i for i in range(1, devices.bit_length())]
 
 
-def block_of(near, far, me, j):
-    apart = me ^ j
-    place = sum((apart // bit) % 2 * 2**i for i, bit in enumerate(bits_of(2 * near.shape[0])[:-1]))
-    return jnp.where(apart % 2 == 0, near[place], far[place])
+def places_of(bits):
+    places = [0]
+    for bit in bits:
+        places += [p ^ bit for p in places]
+    return places
 
 
 def atom_kernel(sample, feat, inner, outer, wq, wk, wv, mixed, qs, ks, vs):
@@ -167,7 +168,7 @@
     tall = AHEADS * QWIN
     head_of = iota((QWIN, chans), 1) // AHEAD_DIM
     keyat = iota((tall, KWIN), 1)
-    batch = 4
+    batch = 6
 
     def score(first):
         out = []
@@ -223,7 +224,8 @@
     atoms = feat.shape[1]
     rows = token_in.shape[0]
     local = token[...].reshape(1, atoms) - lax.axis_index("row") * rows
-    step = 192
+    step = 384
+    sums = []
 
     def finish(c):
         return c, (feat[sample, c : c + step].astype(F32) + dot(mixed[c : c + step], wo[...])).astype(BF16)
@@ -232,9 +234,14 @@
         c, out = item
         return c, jnp.maximum(dot(out, agg[...]), 0.0).astype(BF16)
 
-    hidden = jnp.concatenate([h for _, h in skewed(range(0, atoms, step), [finish, hide])], axis=0)
-    onehot = (iota((rows, atoms), 0) == local).astype(F32)
-    tin = dot(onehot.astype(BF16), hidden) / jnp.sum(onehot, -1, keepdims=True)
+    def add(item):
+        c, hidden = item
+        onehot = (iota((rows, step), 0) == local[:, c : c + step]).astype(F32)
+        part = dot(onehot.astype(BF16), hidden), jnp.sum(onehot, -1, keepdims=True)
+        sums[:] = [a + b for a, b in zip(sums, part)] if sums else part
+
+    skewed(range(0, atoms, step), [finish, hide, add])
+    tin = sums[0] / sums[1]
     token_in[...] = tin
     token_norm[...] = (layer_norm(tin) * gain[...].reshape(1, -1)).astype(BF16)
 
@@ -253,32 +260,42 @@
     )(mixed, feat, token, wo, agg, gain)
 
 
-def turn_kernel(near, far, out, tall):
-    half, cols, _ = near.shape
+def turn_kernel(orders, row_bits, *refs):
+    *halves, out, tall = refs
     rows = out.shape[0] // HEADS
     me = lax.axis_index("sample")
-    for j in range(2 * half):
-        tall[j * cols : (j + 1) * cols] = block_of(near, far, me, j).astype(F32)
+    at = 0
+    for near, far, bits in zip(halves[::2], halves[1::2], orders):
+        half, cols, wide = near.shape
+        places = places_of(bits)
+        for j in range(2 * half):
+            place = sum(jnp.where(me ^ j == p, i, 0) for i, p in enumerate(places))
+            block = jnp.where(place < half, near[place % half], far[place % half])
+            tall[j * cols : (j + 1) * cols, at : at + wide] = block.astype(F32)
+        at += wide
+    starts = [pl.multiple_of((lax.axis_index("row") ^ p) * rows, SUB) for p in places_of(row_bits)]
     for g in range(rows // SUB):
-        turned = tall[:, g * LANES : (g + 1) * LANES].T
+        lanes = slice(g * LANES, (g + 1) * LANES)
+        turned = jnp.concatenate([tall[pl.ds(start, rows), lanes] for start in starts], axis=0).T
         for h in range(HEADS):
             out[h * rows + g * SUB : h * rows + (g + 1) * SUB] = turned[h * SUB : (h + 1) * SUB]
 
 
-def turn_bias(near, far):
-    half, cols, wide = near.shape
+def turn_bias(orders, row_bits, halves):
+    half, cols, _ = halves[0].shape
     keys = 2 * half * cols
+    wide = sum(near.shape[2] for near in halves[::2])
     vmem = pl.BlockSpec(memory_space=pltpu.VMEM)
     return pl.pallas_call(
-        turn_kernel,
+        functools.partial(turn_kernel, orders, row_bits),
         out_shape=jax.ShapeDtypeStruct((wide, keys), F32),
-        in_specs=[vmem, vmem],
+        in_specs=[vmem] * len(halves),
         out_specs=vmem,
         scratch_shapes=[pltpu.VMEM((keys, wide), F32)],
         compiler_params=pltpu.CompilerParams(vmem_limit_bytes=24 * MIB),
         cost_estimate=cost(1),
         name="turn_bias",
-    )(near, far)
+    )(*halves)
 
 
 def head_groups(width):
@@ -290,28 +307,27 @@
     return groups
 
 
-def project_kernel(near, far, wq, wk, wv, wg, q, kt, v, gate):
+def stack(blocks):
+    return jnp.concatenate([blocks[j].astype(F32) for j in range(blocks.shape[0])], axis=0).astype(BF16)
+
+
+def project_kernel(near, wq, wk, wv, wg, wo, q, k, v, gate):
+    x = stack(near)
+    q[...] = dot(near[0], wq[...]).astype(BF16)
+    gate[...] = jax.nn.sigmoid(dot(near[0], wg[...]))
+    k[...] = dot(x, wk[...]).astype(BF16)
+    v[...] = dot(x, wv[...]).astype(BF16)
+
+
+def project(near, wq, wk, wv, wg, wo):
     half, rows, width = near.shape
-    me = lax.axis_index("row")
-    x = jnp.concatenate([block_of(near, far, me, j).astype(F32) for j in range(2 * half)], axis=0).astype(BF16)
-    own = near[0]
-    q[...] = dot(own, wq[...]).astype(BF16)
-    gate[...] = jax.nn.sigmoid(dot(own, wg[...]))
-    for c in range(0, width, 2 * LANES):
-        kt[c : c + 2 * LANES] = dot(x, wk[:, c : c + 2 * LANES]).T.astype(BF16)
-    v[...] = dot(x, wv[...]).astype(BF16)
-
-
-def project(near, far, wq, wk, wv, wg):
-    half, rows, width = near.shape
-    keys = 2 * half * rows
     vmem = pl.BlockSpec(memory_space=pltpu.VMEM)
     return pl.pallas_call(
         project_kernel,
         out_shape=[
             jax.ShapeDtypeStruct((rows, width), BF16),
-            jax.ShapeDtypeStruct((width, keys), BF16),
-            jax.ShapeDtypeStruct((keys, width), BF16),
+            jax.ShapeDtypeStruct((half * rows, width), BF16),
+            jax.ShapeDtypeStruct((half * rows, width), BF16),
             jax.ShapeDtypeStruct((rows, width), F32),
         ],
         in_specs=[vmem] * 6,
@@ -319,12 +335,19 @@
         compiler_params=pltpu.CompilerParams(vmem_limit_bytes=24 * MIB),
         cost_estimate=cost(2),
         name="project",
-    )(near, far, wq, wk, wv, wg)
-
-
-def attend_kernel(q, kt, v, gate, token_in, bias, wo, *rest):
-    *earlier, out = rest
+    )(near, wq, wk, wv, wg, wo)
+
+
+def attend_kernel(far, q, k_near, v_near, gate, token_in, bias, wk, wv, wo, *rest):
+    *earlier, out, kt, v = rest
     rows, width = token_in.shape
+    x = stack(far)
+    for c in range(0, width, 2 * LANES):
+        lanes = slice(c, c + 2 * LANES)
+        k = jnp.concatenate([k_near[:, lanes].astype(F32), dot(x, wk[:, lanes])], axis=0)
+        kt[lanes] = k.T.astype(BF16)
+    v[: v_near.shape[0]] = v_near[...]
+    v[v_near.shape[0] :] = dot(x, wv[...]).astype(BF16)
     scale = 1.0 / HEAD_DIM**0.5
     lane = iota((rows, 2 * LANES), 1)
     work = [(base, heads[i : i + 2]) for base, heads in head_groups(width) for i in range(0, len(heads), 2)]
@@ -370,19 +393,21 @@
         out[...] = res
 
 
-def attend(q, kt, v, gate, token_in, bias, wo, earlier):
+def attend(far, q, k, v, gate, token_in, bias, wk, wv, wo, earlier):
     rows, width = token_in.shape
+    keys = 2 * k.shape[0]
     vmem = pl.BlockSpec(memory_space=pltpu.VMEM)
     shape = (len(earlier) + 1, rows, width) if earlier else (rows, width)
     return pl.pallas_call(
         attend_kernel,
         out_shape=jax.ShapeDtypeStruct(shape, BF16),
-        in_specs=[vmem] * (7 + len(earlier)),
+        in_specs=[vmem] * (10 + len(earlier)),
         out_specs=vmem,
+        scratch_shapes=[pltpu.VMEM((width, keys), BF16), pltpu.VMEM((keys, width), BF16)],
         compiler_params=pltpu.CompilerParams(vmem_limit_bytes=24 * MIB),
         cost_estimate=cost(3),
         name="attend",
-    )(q, kt, v, gate, token_in, bias, wo, *earlier)
+    )(far, q, k, v, gate, token_in, bias, wk, wv, wo, *earlier)
 
 
 def shards(
@@ -415,32 +440,39 @@
         return jnp.concatenate([held, after(swap(held, axis, bit), *others)], axis=0)
 
     bits, row_bits = bits_of(lax.axis_size("sample")), bits_of(ranks)
-    held, norms, inputs = bias[None], [], []
+    orders = [bits, bits[:1] + bits[-1:] + bits[1:-1]]
+    split = (bias.shape[1] // LANES + 1) // 2 * LANES
+    mixed = atom_attention(0, atom_feat, inner, outer, atom_wq, atom_wk, atom_wv)
+    got = after(swap(bias, "sample", bits[0]), mixed)
+    held = [jnp.stack([bias[:, lanes], got[:, lanes]]) for lanes in (slice(0, split), slice(split, None))]
+    mixed = after(mixed, held)
+    norms, inputs = [], []
     for s in range(samples):
-        if s < len(bits) - 1:
-            held = widen(held, "sample", bits[s], inner, outer, *norms[-1:])
-        inner = after(inner, held, *norms[-1:])
-        mixed = atom_attention(s, atom_feat, inner, outer, atom_wq, atom_wk, atom_wv)
         if s:
+            mixed = atom_attention(s, atom_feat, inner, outer, atom_wq, atom_wk, atom_wv)
             norms[-1] = widen(norms[-1], "row", row_bits[0], mixed)
             mixed = after(mixed, norms[-1])
         token_in, token_norm = gather_tokens(s, mixed, atom_feat, atom_token, atom_wo, agg_weight, token_gain, rows)
         inputs.append(token_in)
         norms.append(token_norm[None])
-    for bit in bits[samples:-1]:
-        held = widen(held, "sample", bit)
-    far_bias = swap(held, "sample", bits[-1])
+        if s == 0:
+            for i in range(1, len(bits) - 1):
+                held = [widen(h, "sample", order[i], token_norm) for h, order in zip(held, orders)]
+            inner = after(inner, held, token_norm)
+    halves = []
+    for h, order in zip(held, orders):
+        halves += [h, swap(h, "sample", order[-1])]
     done = []
     for s in range(samples):
         near = norms[s]
         for bit in row_bits[near.shape[0].bit_length() - 1 : -1]:
             near = widen(near, "row", bit, *done)
         far = swap(near, "row", row_bits[-1])
-        part = project(near, far, query_weight, key_weight, value_weight, gate_weight)
+        part = project(near, query_weight, key_weight, value_weight, gate_weight, out_weight)
         if s == 0:
-            bias = turn_bias(held, after(far_bias, part))
+            bias = turn_bias(orders, row_bits, after(halves, part))
         earlier = done if s == samples - 1 else []
-        done.append(attend(*part, inputs[s], bias, out_weight, earlier))
+        done.append(attend(far, *part, inputs[s], bias, key_weight, value_weight, out_weight, earlier))
     return done[-1]
 
 

time: 38.6 us -> 38.6 us (level)
  other arithmetic: 1.02 us -> 0.13 us
  local copies, waits for them, and re-layouts: 0.91 us -> 1.7 us
  starting transfers between devices: 10.7 us -> 11.2 us
    ppermute x1, waiting for transfers between devices: 1.83 us -> 0.01 us  [shards(): lax.ppermute(outer, 'row', odd_pairs + [(j, i) for i, j in odd_pairs])]
    another operation x0 -> x4, local copies, waits for them, and re-layouts: none -> 1.63 us  [shards(): jnp.stack([bias[:, lanes], got[:, lanes]])]
    ppermute x8 -> x10, waiting for transfers between devices: 4.79 us -> 6.32 us  [swap(): lax.ppermute(held, axis, [(i, i ^ far) for i in range(lax.axis_size(axis))])]
    pallas_call x2, Pallas kernels: 3.93 us -> 5.14 us  [attend(): pl.pallas_call(attend_kernel, out_shape=jax.ShapeDtypeStruct(shape, BF16)...]
    ppermute x1, starting transfers between devices: 1.63 us -> 2.64 us  [shards(): lax.ppermute(outer, 'row', odd_pairs + [(j, i) for i, j in odd_pairs])]
    concatenate x4, other arithmetic: 1.02 us -> 0.1 us  [widen(): jnp.concatenate([held, after(swap(held, axis, bit), *others)], axis=0)]
    unnamed x28 -> x26, local copies, waits for them, and re-layouts: 0.91 us -> 0.06 us
    pallas_call x2, Pallas kernels: 3.63 us -> 2.82 us  [gather_tokens(): pl.pallas_call(functools.partial(gather_kernel, sample), out_shape=[jax.S...]
  transfers between devices with their start and end apart: 9 -> 11, of which waited for: 4 -> 6; matrix products, arithmetic and copies ran while one was open for 0% -> 4% of each run, Pallas kernels for 30% -> 32%
where the time goes in v6:
time: 38.6 us; the launch traced here: 38.3 us
  Pallas kernels  18.7 us (48%)
  starting transfers between devices  11.2 us (29%)
  waiting for transfers between devices  6.33 us (16%)
  local copies, waits for them, and re-layouts  1.7 us (4%)
    ppermute x10, starting transfers between devices, swap(): lax.ppermute(held, axis, [(i, i ^ far) for i in range(lax.axis_size(axis))])  8.6 us
    ppermute x10, waiting for transfers between devices, swap(): lax.ppermute(held, axis, [(i, i ^ far) for i in range(lax.axis_size(axis))])  6.32 us
    pallas_call x2, Pallas kernels, attend(): pl.pallas_call(attend_kernel, out_shape=jax.ShapeDtypeStruct(shape, BF16)...  5.14 us
    pallas_call x2, Pallas kernels, atom_attention(): pl.pallas_call(functools.partial(atom_kernel, sample), out_shape=jax.Shap...  4.53 us
    pallas_call x1, Pallas kernels, pair_bias(): pl.pallas_call(bias_kernel, grid=(1,), out_shape=[jax.ShapeDtypeStruct((c...  3.59 us
    pallas_call x2, Pallas kernels, gather_tokens(): pl.pallas_call(functools.partial(gather_kernel, sample), out_shape=[jax.S...  2.82 us
    ppermute x1, starting transfers between devices, shards(): lax.ppermute(outer, 'row', odd_pairs + [(j, i) for i, j in odd_pairs])  2.64 us
    pallas_call x2, Pallas kernels, project(): pl.pallas_call(project_kernel, out_shape=[jax.ShapeDtypeStruct((rows, wid...  1.86 us
  transfers between devices with their start and end apart: 11, of which 6 were waited for; matrix products, arithmetic and copies ran while one was open for 4% of the time, Pallas kernels for 32%

profile of v6, /device:TPU:0, one launch (start us, length us, event | category | flops | bytes accessed | tf_op | source)
XLA Modules:
  0.0 38.3 jit_solution(6795427041915249293)
XLA Ops:
  0.0 3.6 %pair_bias.1 = (bf16[36,1152]{1,0:T(8,128)(2,1)}, bf16[2,48,128]{2,1,0:T(8,128)(2,1)}, bf16[2,48,128]{2,1,0:T(8,128)(2,1)}) custom-call(bf16[2,1152,128]{2,1,0:T(8,128)(2,1)} %feat.7, bf16[2,1152,128]{2,1,0:T(8,128)(2,1)} %feat.7, bf16[36,72,128]{2,1,0:T(8,128)(2,1)} %bitcast.16, s32[36]{0:T(128)} %mask.1, bf16[16,128]{1,0:T(8,128)(2,1)} %bitcast.17), custom_call_target="tpu_custom_call" | custom-call | flops 60000000 | bytes 1000 | tf_op jit(solution)/shard_map/pair_bias/pallas_call | solution.py:95
  3.6 0.0 copy-start.12
  3.6 0.5 %collective-permute-start = (bf16[2,48,128]{2,1,0:T(8,128)(2,1)}, bf16[2,48,128]{2,1,0:T(8,128)(2,1)S(1)}, u32[]{:S(2)}, u32[]{:S(2)}) collective-permute-start(bf16[2,48,128]{2,1,0:T(8,128)(2,1)} %get-tuple-element.32), channel_id=1, source_target_pairs={{0,8},{8,0},{16,24},{24,16},{1,9},{9,1},{17,25},{25,17},{2,10},{10... | collective-permute-start | bytes 73736 | tf_op jit(solution)/shard_map/ppermute | solution.py:123
  4.2 2.6 %collective-permute-start.2 = (bf16[2,48,128]{2,1,0:T(8,128)(2,1)}, bf16[2,48,128]{2,1,0:T(8,128)(2,1)S(1)}, u32[]{:S(2)}, u32[]{:S(2)}) collective-permute-start(bf16[2,48,128]{2,1,0:T(8,128)(2,1)} %get-tuple-element.34), channel_id=1, source_target_pairs={{8,16},{24,0},{16,8},{0,24},{9,17},{25,1},{17,9},{1,25},{10,18},{2... | collective-permute-start | bytes 73736 | tf_op jit(solution)/shard_map/ppermute | solution.py:437
  6.8 2.6 %collective-permute-start.1 = (bf16[36,1152]{1,0:T(8,128)(2,1)}, bf16[36,1152]{1,0:T(8,128)(2,1)S(1)}, u32[]{:S(2)}, u32[]{:S(2)}) collective-permute-start(bf16[36,1152]{1,0:T(8,128)(2,1)} %get-tuple-element.33), channel_id=1, source_target_pairs={{0,4},{1,5},{2,6},{3,7},{4,0},{5,1},{6,2},{7,3},{8,12},{9,13},{10,... | collective-permute-start | bytes 248840 | tf_op jit(solution)/shard_map/ppermute | solution.py:123
  9.4 0.8 %slice_bitcast_fusion.1 = bf16[1,36,640]{2,1,0:T(8,128)(2,1)S(1)} fusion(bf16[36,1152]{1,0:T(8,128)(2,1)} %get-tuple-element.33), kind=kLoop, calls=%fused_computation.7 | loop fusion | bytes 92160 | tf_op jit(solution)/shard_map/stack | solution.py:447
  10.2 0.8 %slice_bitcast_fusion.3 = bf16[1,36,512]{2,1,0:T(8,128)(2,1)S(1)} fusion(bf16[36,1152]{1,0:T(8,128)(2,1)} %get-tuple-element.33), kind=kLoop, calls=%fused_computation.9 | loop fusion | bytes 73728 | tf_op jit(solution)/shard_map/stack | solution.py:447
  11.1 2.3 %atom_attention.2.mixed = bf16[1152,128]{1,0:T(8,128)(2,1)S(1)} custom-call(bf16[2,1152,128]{2,1,0:T(8,128)(2,1)S(1)} %copy-done, bf16[2,48,128]{2,1,0:T(8,128)(2,1)S(1)} %collective-permute-done.inner, bf16[2,48,128]{2,1,0:T(8,128)(2,1)S(1)} %collective-permute-done.2.outer, bf16[128,128]{1,0:T(8,128)(2,1)S(1)} %copy-done.7, ...), custom_call_target="tpu_custom_call" | custom-call | flops 80000000 | bytes 1000 | tf_op jit(solution)/shard_map/atom_attention/pallas_call | solution.py:207
  13.3 1.2 %collective-permute-done.1 = bf16[36,1152]{1,0:T(8,128)(2,1)S(1)} collective-permute-done((bf16[36,1152]{1,0:T(8,128)(2,1)}, bf16[36,1152]{1,0:T(8,128)(2,1)S(1)}, u32[]{:S(2)}, u32[]{:S(2)}) %collective-permute-start.1) | collective-permute-done | bytes 82976 | tf_op jit(solution)/shard_map/ppermute | solution.py:123
  14.6 1.6 %collective-permute-start.4 = (bf16[2,36,512]{2,1,0:T(8,128)(2,1)S(1)}, bf16[2,36,512]{2,1,0:T(8,128)(2,1)S(1)}, u32[]{:S(2)}, u32[]{:S(2)}) collective-permute-start(bf16[2,36,512]{2,1,0:T(8,128)(2,1)S(1)} %pad_maximum_fusion.5), channel_id=1, source_target_pairs={{0,1},{1,0},{2,3},{3,2},{4,5},{5,4},{6,7},{7,6},{8,9},{9,8},{10,11... | collective-permute-start | bytes 221192 | tf_op jit(solution)/shard_map/ppermute | solution.py:123
  16.1 0.8 %collective-permute-start.3 = (bf16[2,36,640]{2,1,0:T(8,128)(2,1)S(1)}, bf16[2,36,640]{2,1,0:T(8,128)(2,1)S(1)}, u32[]{:S(2)}, u32[]{:S(2)}) collective-permute-start(bf16[2,36,640]{2,1,0:T(8,128)(2,1)S(1)} %pad_maximum_fusion.4), channel_id=1, source_target_pairs={{0,2},{1,3},{2,0},{3,1},{4,6},{5,7},{6,4},{7,5},{8,10},{9,11},{10,... | collective-permute-start | bytes 276488 | tf_op jit(solution)/shard_map/ppermute | solution.py:123
  17.0 0.0 copy-start.3
  17.0 1.4 %gather_tokens.2 = (f32[72,768]{1,0:T(8,128)S(1)}, bf16[72,768]{1,0:T(8,128)(2,1)S(1)}) custom-call(bf16[1152,128]{1,0:T(8,128)(2,1)S(1)} %atom_attention.2.mixed, bf16[2,1152,128]{2,1,0:T(8,128)(2,1)S(1)} %copy-done, s32[1152]{0:T(1024)S(1)} %copy-done.11, bf16[128,128]{1,0:T(8,128)(2,1)S(1)} %copy-done.10, bf16[128,768]{1,0:T(8,128)(2,1)S(1)} %copy-done.6, ...), custom_call_target="tpu_custom_call" | custom-call | flops 20000000 | bytes 1000 | tf_op jit(solution)/shard_map/gather_tokens/pallas_call | solution.py:252
  18.4 0.6 %collective-permute-start.5 = (bf16[1,72,768]{2,1,0:T(8,128)(2,1)S(1)}, bf16[1,72,768]{2,1,0:T(8,128)(2,1)S(1)}, u32[]{:S(2)}, u32[]{:S(2)}) collective-permute-start(bf16[1,72,768]{2,1,0:T(8,128)(2,1)S(1)} %bitcast.14), channel_id=1, source_target_pairs={{0,16},{8,24},{16,0},{24,8},{1,17},{9,25},{17,1},{25,9},{2,18},{10... | collective-permute-start | bytes 331784 | tf_op jit(solution)/shard_map/ppermute | solution.py:123
  19.0 0.1 collective-permute-done.4
  19.1 1.8 %collective-permute-done.3 = bf16[2,36,640]{2,1,0:T(8,128)(2,1)S(1)} collective-permute-done((bf16[2,36,640]{2,1,0:T(8,128)(2,1)S(1)}, bf16[2,36,640]{2,1,0:T(8,128)(2,1)S(1)}, u32[]{:S(2)}, u32[]{:S(2)}) %collective-permute-start.3) | collective-permute-done | bytes 92192 | tf_op jit(solution)/shard_map/ppermute | solution.py:123
  20.9 2.3 %atom_attention.3.mixed = bf16[1152,128]{1,0:T(8,128)(2,1)S(1)} custom-call(bf16[2,1152,128]{2,1,0:T(8,128)(2,1)S(1)} %copy-done, bf16[2,48,128]{2,1,0:T(8,128)(2,1)S(1)} %collective-permute-done.inner, bf16[2,48,128]{2,1,0:T(8,128)(2,1)S(1)} %collective-permute-done.2.outer, bf16[128,128]{1,0:T(8,128)(2,1)S(1)} %copy-done.7, ...), custom_call_target="tpu_custom_call" | custom-call | flops 80000000 | bytes 1000 | tf_op jit(solution)/shard_map/atom_attention/pallas_call | solution.py:207
  23.2 0.0 collective-permute-done.5
  23.3 0.1 collective-permute-start.7
  23.3 0.6 %collective-permute-start.8 = (bf16[4,36,640]{2,1,0:T(8,128)(2,1)S(1)}, bf16[4,36,640]{2,1,0:T(8,128)(2,1)S(1)}, u32[]{:S(2)}, u32[]{:S(2)}) collective-permute-start(bf16[4,36,640]{2,1,0:T(8,128)(2,1)S(1)} %pad_maximum_fusion.2.refs_0_), channel_id=1, source_target_pairs={{0,1},{1,0},{2,3},{3,2},{4,5},{5,4},{6,7},{7,6},{8,9},{9,8},{10,11... | collective-permute-start | bytes 552968 | tf_op jit(solution)/shard_map/ppermute | solution.py:123
  24.0 1.2 %collective-permute-start.9 = (bf16[4,36,512]{2,1,0:T(8,128)(2,1)S(1)}, bf16[4,36,512]{2,1,0:T(8,128)(2,1)S(1)}, u32[]{:S(2)}, u32[]{:S(2)}) collective-permute-start(bf16[4,36,512]{2,1,0:T(8,128)(2,1)S(1)} %pad_maximum_fusion.3.refs_2_), channel_id=1, source_target_pairs={{0,2},{1,3},{2,0},{3,1},{4,6},{5,7},{6,4},{7,5},{8,10},{9,11},{10,... | collective-permute-start | bytes 442376 | tf_op jit(solution)/shard_map/ppermute | solution.py:123
  25.2 1.4 %gather_tokens.3 = (f32[72,768]{1,0:T(8,128)S(1)}, bf16[72,768]{1,0:T(8,128)(2,1)S(1)}) custom-call(bf16[1152,128]{1,0:T(8,128)(2,1)S(1)} %atom_attention.3.mixed, bf16[2,1152,128]{2,1,0:T(8,128)(2,1)S(1)} %copy-done, s32[1152]{0:T(1024)S(1)} %copy-done.11, bf16[128,128]{1,0:T(8,128)(2,1)S(1)} %copy-done.10, bf16[128,768]{1,0:T(8,128)(2,1)S(1)} %copy-done.6, ...), custom_call_target="tpu_custom_call" | custom-call | flops 20000000 | bytes 1000 | tf_op jit(solution)/shard_map/gather_tokens/pallas_call | solution.py:252
  26.6 0.5 %collective-permute-start.6 = (bf16[1,72,768]{2,1,0:T(8,128)(2,1)S(1)}, bf16[1,72,768]{2,1,0:T(8,128)(2,1)S(1)}, u32[]{:S(2)}, u32[]{:S(2)}) collective-permute-start(bf16[1,72,768]{2,1,0:T(8,128)(2,1)S(1)} %bitcast.12), channel_id=1, source_target_pairs={{0,16},{8,24},{16,0},{24,8},{1,17},{9,25},{17,1},{25,9},{2,18},{10... | collective-permute-start | bytes 331784 | tf_op jit(solution)/shard_map/ppermute | solution.py:123
  27.2 0.9 %project.2 = (bf16[72,768]{1,0:T(8,128)(2,1)S(1)}, bf16[144,768]{1,0:T(8,128)(2,1)S(1)}, bf16[144,768]{1,0:T(8,128)(2,1)S(1)}, f32[72,768]{1,0:T(8,128)S(1)}) custom-call(bf16[2,72,768]{2,1,0:T(8,128)(2,1)S(1)} %pad_maximum_fusion.near, bf16[768,768]{1,0:T(8,128)(2,1)S(1)} %copy-done.4, bf16[768,768]{1,0:T(8,128)(2,1)S(1)} %copy-done.1, ...), custom_call_target="tpu_custom_call" | custom-call | flops 40000000 | bytes 1000 | tf_op jit(solution)/shard_map/project/pallas_call | solution.py:325
  28.1 2.1 %collective-permute-done.9.refs_3_ = bf16[4,36,512]{2,1,0:T(8,128)(2,1)S(1)} collective-permute-done((bf16[4,36,512]{2,1,0:T(8,128)(2,1)S(1)}, bf16[4,36,512]{2,1,0:T(8,128)(2,1)S(1)}, u32[]{:S(2)}, u32[]{:S(2)}) %collective-permute-start.9) | collective-permute-done | bytes 147488 | tf_op jit(solution)/shard_map/ppermute | solution.py:123
  30.2 0.6 %collective-permute-done.8.refs_1_ = bf16[4,36,640]{2,1,0:T(8,128)(2,1)S(1)} collective-permute-done((bf16[4,36,640]{2,1,0:T(8,128)(2,1)S(1)}, bf16[4,36,640]{2,1,0:T(8,128)(2,1)S(1)}, u32[]{:S(2)}, u32[]{:S(2)}) %collective-permute-start.8) | collective-permute-done | bytes 184352 | tf_op jit(solution)/shard_map/ppermute | solution.py:123
  30.8 0.7 %turn_bias.1.bias = f32[1152,288]{1,0:T(8,128)S(1)} custom-call(bf16[4,36,640]{2,1,0:T(8,128)(2,1)S(1)} %pad_maximum_fusion.2.refs_0_, bf16[4,36,640]{2,1,0:T(8,128)(2,1)S(1)} %collective-permute-done.8.refs_1_, bf16[4,36,512]{2,1,0:T(8,128)(2,1)S(1)} %pad_maximum_fusion.3.refs_2_, bf16[4,36,512]{2,1,0:T(8,128)(2,1)S(1)} %collective-permute-done.9.refs_3_), custom_call_target="tpu_custom_call" | custom-call | flops 20000000 | bytes 1000 | tf_op jit(solution)/shard_map/turn_bias/pallas_call | solution.py:289
  31.6 2.2 %attend.2.rest_0_ = bf16[72,768]{1,0:T(8,128)(2,1)S(1)} custom-call(bf16[2,72,768]{2,1,0:T(8,128)(2,1)S(1)} %collective-permute-done.7.far, bf16[72,768]{1,0:T(8,128)(2,1)S(1)} %get-tuple-element.44.q, bf16[144,768]{1,0:T(8,128)(2,1)S(1)} %get-tuple-element.45.k_near, bf16[144,768]{1,0:T(8,128)(2,1)S(1)} %get-tuple-element.46.v_near, ...), custom_call_target="tpu_custom_call" | custom-call | flops 60000000 | bytes 1000 | tf_op jit(solution)/shard_map/attend/pallas_call | solution.py:401
  33.9 0.1 collective-permute-start.10
  33.9 0.9 %project.3 = (bf16[72,768]{1,0:T(8,128)(2,1)S(1)}, bf16[144,768]{1,0:T(8,128)(2,1)S(1)}, bf16[144,768]{1,0:T(8,128)(2,1)S(1)}, f32[72,768]{1,0:T(8,128)S(1)}) custom-call(bf16[2,72,768]{2,1,0:T(8,128)(2,1)S(1)} %pad_maximum_fusion.1.near, bf16[768,768]{1,0:T(8,128)(2,1)S(1)} %copy-done.4, bf16[768,768]{1,0:T(8,128)(2,1)S(1)} %copy-done.1, ...), custom_call_target="tpu_custom_call" | custom-call | flops 40000000 | bytes 1000 | tf_op jit(solution)/shard_map/project/pallas_call | solution.py:325
  34.9 0.5 %collective-permute-done.10.far = bf16[2,72,768]{2,1,0:T(8,128)(2,1)S(1)} collective-permute-done((bf16[2,72,768]{2,1,0:T(8,128)(2,1)S(1)}, bf16[2,72,768]{2,1,0:T(8,128)(2,1)S(1)}, u32[]{:S(2)}, u32[]{:S(2)}) %collective-permute-start.10) | collective-permute-done | bytes 221216 | tf_op jit(solution)/shard_map/ppermute | solution.py:123
  35.4 2.9 %attend.3 = bf16[2,72,768]{2,1,0:T(8,128)(2,1)} custom-call(bf16[2,72,768]{2,1,0:T(8,128)(2,1)S(1)} %collective-permute-done.10.far, bf16[72,768]{1,0:T(8,128)(2,1)S(1)} %get-tuple-element.54.q, bf16[144,768]{1,0:T(8,128)(2,1)S(1)} %get-tuple-element.55.k_near, bf16[144,768]{1,0:T(8,128)(2,1)S(1)} %get-tuple-element.56.v_near, ...), custom_call_target="tpu_custom_call" | custom-call | flops 60000000 | bytes 1000 | tf_op jit(solution)/shard_map/attend/pallas_call | solution.py:401
  (36 shorter events, 0.2 us)
Async XLA Ops:
  0.0 11.0 %copy-start = (bf16[2,1152,128]{2,1,0:T(8,128)(2,1)S(1)}, bf16[2,1152,128]{2,1,0:T(8,128)(2,1)}, u32[]{:S(2)}) copy-start(bf16[2,1152,128]{2,1,0:T(8,128)(2,1)} %feat.7) | copy-start | bytes 1769476
  0.0 11.0 %copy-start.7 = (bf16[128,128]{1,0:T(8,128)(2,1)S(1)}, bf16[128,128]{1,0:T(8,128)(2,1)}, u32[]{:S(2)}) copy-start(bf16[128,128]{1,0:T(8,128)(2,1)} %wq.5) | copy-start | bytes 98308
  0.0 11.0 %copy-start.8 = (bf16[128,128]{1,0:T(8,128)(2,1)S(1)}, bf16[128,128]{1,0:T(8,128)(2,1)}, u32[]{:S(2)}) copy-start(bf16[128,128]{1,0:T(8,128)(2,1)} %wk.7) | copy-start | bytes 98308
  0.0 11.0 %copy-start.9 = (bf16[128,128]{1,0:T(8,128)(2,1)S(1)}, bf16[128,128]{1,0:T(8,128)(2,1)}, u32[]{:S(2)}) copy-start(bf16[128,128]{1,0:T(8,128)(2,1)} %wv.7) | copy-start | bytes 98308
  3.6 13.4 %copy-start.6 = (bf16[128,768]{1,0:T(8,128)(2,1)S(1)}, bf16[128,768]{1,0:T(8,128)(2,1)}, u32[]{:S(2)}) copy-start(bf16[128,768]{1,0:T(8,128)(2,1)} %agg.3) | copy-start | bytes 589828
  3.6 13.4 %copy-start.10 = (bf16[128,128]{1,0:T(8,128)(2,1)S(1)}, bf16[128,128]{1,0:T(8,128)(2,1)}, u32[]{:S(2)}) copy-start(bf16[128,128]{1,0:T(8,128)(2,1)} %wo.7) | copy-start | bytes 98308
  3.6 13.4 %copy-start.11 = (s32[1152]{0:T(1024)S(1)}, s32[1152]{0:T(1024)}, u32[]{:S(2)}) copy-start(s32[1152]{0:T(1024)} %token_.3) | copy-start | bytes 13828
  3.6 13.4 %copy-start.12 = (f32[768]{0:T(1024)S(1)}, f32[768]{0:T(1024)}, u32[]{:S(2)}) copy-start(f32[768]{0:T(1024)} %gain.3) | copy-start | bytes 9220
  3.6 7.4 %collective-permute-start = (bf16[2,48,128]{2,1,0:T(8,128)(2,1)}, bf16[2,48,128]{2,1,0:T(8,128)(2,1)S(1)}, u32[]{:S(2)}, u32[]{:S(2)}) collective-permute-start(bf16[2,48,128]{2,1,0:T(8,128)(2,1)} %get-tuple-element.32), channel_id=1, source_target_pairs={{0,8},{8,0},{16,24},{24,16},{1,9},{9,1},{17,25},{25,17},{2,10},{10... | collective-permute-start | bytes 73736 | tf_op jit(solution)/shard_map/ppermute | solution.py:123
  4.2 6.9 %collective-permute-start.2 = (bf16[2,48,128]{2,1,0:T(8,128)(2,1)}, bf16[2,48,128]{2,1,0:T(8,128)(2,1)S(1)}, u32[]{:S(2)}, u32[]{:S(2)}) collective-permute-start(bf16[2,48,128]{2,1,0:T(8,128)(2,1)} %get-tuple-element.34), channel_id=1, source_target_pairs={{8,16},{24,0},{16,8},{0,24},{9,17},{25,1},{17,9},{1,25},{10,18},{2... | collective-permute-start | bytes 73736 | tf_op jit(solution)/shard_map/ppermute | solution.py:437
  6.8 7.7 %collective-permute-start.1 = (bf16[36,1152]{1,0:T(8,128)(2,1)}, bf16[36,1152]{1,0:T(8,128)(2,1)S(1)}, u32[]{:S(2)}, u32[]{:S(2)}) collective-permute-start(bf16[36,1152]{1,0:T(8,128)(2,1)} %get-tuple-element.33), channel_id=1, source_target_pairs={{0,4},{1,5},{2,6},{3,7},{4,0},{5,1},{6,2},{7,3},{8,12},{9,13},{10,... | collective-permute-start | bytes 248840 | tf_op jit(solution)/shard_map/ppermute | solution.py:123
  11.1 16.1 %copy-start.5 = (bf16[768,768]{1,0:T(8,128)(2,1)S(1)}, bf16[768,768]{1,0:T(8,128)(2,1)}, u32[]{:S(2)}) copy-start(bf16[768,768]{1,0:T(8,128)(2,1)} %wg.3) | copy-start | bytes 3538948
  14.5 12.6 %copy-start.4 = (bf16[768,768]{1,0:T(8,128)(2,1)S(1)}, bf16[768,768]{1,0:T(8,128)(2,1)}, u32[]{:S(2)}) copy-start(bf16[768,768]{1,0:T(8,128)(2,1)} %wq.7) | copy-start | bytes 3538948
  14.6 4.5 %collective-permute-start.4 = (bf16[2,36,512]{2,1,0:T(8,128)(2,1)S(1)}, bf16[2,36,512]{2,1,0:T(8,128)(2,1)S(1)}, u32[]{:S(2)}, u32[]{:S(2)}) collective-permute-start(bf16[2,36,512]{2,1,0:T(8,128)(2,1)S(1)} %pad_maximum_fusion.5), channel_id=1, source_target_pairs={{0,1},{1,0},{2,3},{3,2},{4,5},{5,4},{6,7},{7,6},{8,9},{9,8},{10,11... | collective-permute-start | bytes 221192 | tf_op jit(solution)/shard_map/ppermute | solution.py:123
  16.1 4.7 %collective-permute-start.3 = (bf16[2,36,640]{2,1,0:T(8,128)(2,1)S(1)}, bf16[2,36,640]{2,1,0:T(8,128)(2,1)S(1)}, u32[]{:S(2)}, u32[]{:S(2)}) collective-permute-start(bf16[2,36,640]{2,1,0:T(8,128)(2,1)S(1)} %pad_maximum_fusion.4), channel_id=1, source_target_pairs={{0,2},{1,3},{2,0},{3,1},{4,6},{5,7},{6,4},{7,5},{8,10},{9,11},{10,... | collective-permute-start | bytes 276488 | tf_op jit(solution)/shard_map/ppermute | solution.py:123
  17.0 10.1 %copy-start.3 = (bf16[768,768]{1,0:T(8,128)(2,1)S(1)}, bf16[768,768]{1,0:T(8,128)(2,1)}, u32[]{:S(2)}) copy-start(bf16[768,768]{1,0:T(8,128)(2,1)} %wo.11) | copy-start | bytes 3538948
  18.4 4.8 %collective-permute-start.5 = (bf16[1,72,768]{2,1,0:T(8,128)(2,1)S(1)}, bf16[1,72,768]{2,1,0:T(8,128)(2,1)S(1)}, u32[]{:S(2)}, u32[]{:S(2)}) collective-permute-start(bf16[1,72,768]{2,1,0:T(8,128)(2,1)S(1)} %bitcast.14), channel_id=1, source_target_pairs={{0,16},{8,24},{16,0},{24,8},{1,17},{9,25},{17,1},{25,9},{2,18},{10... | collective-permute-start | bytes 331784 | tf_op jit(solution)/shard_map/ppermute | solution.py:123
  20.9 6.2 %copy-start.1 = (bf16[768,768]{1,0:T(8,128)(2,1)S(1)}, bf16[768,768]{1,0:T(8,128)(2,1)}, u32[]{:S(2)}) copy-start(bf16[768,768]{1,0:T(8,128)(2,1)} %wk.11) | copy-start | bytes 3538948
  20.9 6.2 %copy-start.2 = (bf16[768,768]{1,0:T(8,128)(2,1)S(1)}, bf16[768,768]{1,0:T(8,128)(2,1)}, u32[]{:S(2)}) copy-start(bf16[768,768]{1,0:T(8,128)(2,1)} %wv.11) | copy-start | bytes 3538948
  23.3 8.3 %collective-permute-start.7 = (bf16[2,72,768]{2,1,0:T(8,128)(2,1)S(1)}, bf16[2,72,768]{2,1,0:T(8,128)(2,1)S(1)}, u32[]{:S(2)}, u32[]{:S(2)}) collective-permute-start(bf16[2,72,768]{2,1,0:T(8,128)(2,1)S(1)} %pad_maximum_fusion.near), channel_id=1, source_target_pairs={{0,8},{8,0},{16,24},{24,16},{1,9},{9,1},{17,25},{25,17},{2,10},{10... | collective-permute-start | bytes 663560 | tf_op jit(solution)/shard_map/ppermute | solution.py:123
  23.3 7.5 %collective-permute-start.8 = (bf16[4,36,640]{2,1,0:T(8,128)(2,1)S(1)}, bf16[4,36,640]{2,1,0:T(8,128)(2,1)S(1)}, u32[]{:S(2)}, u32[]{:S(2)}) collective-permute-start(bf16[4,36,640]{2,1,0:T(8,128)(2,1)S(1)} %pad_maximum_fusion.2.refs_0_), channel_id=1, source_target_pairs={{0,1},{1,0},{2,3},{3,2},{4,5},{5,4},{6,7},{7,6},{8,9},{9,8},{10,11... | collective-permute-start | bytes 552968 | tf_op jit(solution)/shard_map/ppermute | solution.py:123
  24.0 6.3 %collective-permute-start.9 = (bf16[4,36,512]{2,1,0:T(8,128)(2,1)S(1)}, bf16[4,36,512]{2,1,0:T(8,128)(2,1)S(1)}, u32[]{:S(2)}, u32[]{:S(2)}) collective-permute-start(bf16[4,36,512]{2,1,0:T(8,128)(2,1)S(1)} %pad_maximum_fusion.3.refs_2_), channel_id=1, source_target_pairs={{0,2},{1,3},{2,0},{3,1},{4,6},{5,7},{6,4},{7,5},{8,10},{9,11},{10,... | collective-permute-start | bytes 442376 | tf_op jit(solution)/shard_map/ppermute | solution.py:123
  26.6 7.2 %collective-permute-start.6 = (bf16[1,72,768]{2,1,0:T(8,128)(2,1)S(1)}, bf16[1,72,768]{2,1,0:T(8,128)(2,1)S(1)}, u32[]{:S(2)}, u32[]{:S(2)}) collective-permute-start(bf16[1,72,768]{2,1,0:T(8,128)(2,1)S(1)} %bitcast.12), channel_id=1, source_target_pairs={{0,16},{8,24},{16,0},{24,8},{1,17},{9,25},{17,1},{25,9},{2,18},{10... | collective-permute-start | bytes 331784 | tf_op jit(solution)/shard_map/ppermute | solution.py:123
  33.9 1.5 %collective-permute-start.10 = (bf16[2,72,768]{2,1,0:T(8,128)(2,1)S(1)}, bf16[2,72,768]{2,1,0:T(8,128)(2,1)S(1)}, u32[]{:S(2)}, u32[]{:S(2)}) collective-permute-start(bf16[2,72,768]{2,1,0:T(8,128)(2,1)S(1)} %pad_maximum_fusion.1.near), channel_id=1, source_target_pairs={{0,8},{8,0},{16,24},{24,16},{1,9},{9,1},{17,25},{25,17},{2,10},{10... | collective-permute-start | bytes 663560 | tf_op jit(solution)/shard_map/ppermute | solution.py:123

commit v7 on v6

--- a/solution.py
+++ b/solution.py
@@ -20,6 +20,7 @@
 F32 = jnp.float32
 BF16 = jnp.bfloat16
 MIB = 1024 * 1024
+LOG2E = math.log2(math.e)
 NT = (((1,), (1,)), ((), ()))
 
 
@@ -65,8 +66,8 @@
     inner[...] = jnp.where(odd, head[...], tail[...])
     outer[...] = jnp.where(odd, tail[...], head[...])
     cols, rows, chans = pair.shape
-    for k in range(cols):
-        normed[k] = layer_norm(pair[k].astype(F32))
+    for k in range(0, cols, 6):
+        normed[k : k + 6] = layer_norm(pair[k : k + 6].astype(F32))
     spread = (iota((HEADS, LANES), 1) // SUB == iota((HEADS, LANES), 0)).astype(BF16)
     wide = lax.dot_general(weight[...], spread, (((0,), (0,)), ((), ())), preferred_element_type=F32).astype(BF16)
     tall = cols * SUB
@@ -77,11 +78,17 @@
     row = iota((tall, LANES), 0)
     mine = iota((tall, LANES), 1) % SUB == row % SUB
     apart = lax.axis_index("sample") * cols + row // SUB - lax.axis_index("row") * rows - row % SUB
-    for g in range(rows // SUB):
+
+    def weigh(g):
         x = normed[:, g * SUB : (g + 1) * SUB].reshape(tall, chans).astype(BF16)
         raw = jnp.where(open_key | (apart == g * SUB), dot(x, wide), -30000.0)
-        raw = jnp.where(mine, raw, 0.0).astype(BF16)
+        return g, jnp.where(mine, raw, 0.0).astype(BF16)
+
+    def pick(item):
+        g, raw = item
         out[:, g * LANES : (g + 1) * LANES] = dot(picked, raw).astype(BF16)
+
+    skewed(range(rows // SUB), [weigh, pick])
 
 
 def pair_bias(feat, pair_cond, token_mask, pair_weight):
@@ -164,7 +171,7 @@
         vs[RIM + at : RIM + at + count] = kv[:, chans:]
 
     skewed([*range(0, atoms, LANES), (-RIM, before), (atoms, behind)], [normalise, project_atoms])
-    rate = math.log2(math.e) / AHEAD_DIM**0.5
+    rate = LOG2E / AHEAD_DIM**0.5
     tall = AHEADS * QWIN
     head_of = iota((QWIN, chans), 1) // AHEAD_DIM
     keyat = iota((tall, KWIN), 1)
@@ -186,17 +193,21 @@
     def soften(item):
         first, s = item
         e = jnp.exp2((s - jnp.max(s, -1, keepdims=True)) * rate)
-        return first, e.astype(BF16), inverse(jnp.sum(e, -1, keepdims=True))
+        return first, e.astype(BF16), jnp.sum(e, -1, keepdims=True)
+
+    def own_head(parts):
+        acc = parts[:QWIN]
+        for h in range(1, AHEADS):
+            acc = jnp.where(head_of == h, parts[h * QWIN : (h + 1) * QWIN], acc)
+        return acc
 
     def mix(item):
-        first, e, share = item
+        first, e, total = item
         for i in range(batch):
             at = first + i * QWIN
-            o = dot(e[i * tall : (i + 1) * tall], vs[at : at + KWIN]) * share[i * tall : (i + 1) * tall]
-            acc = o[:QWIN]
-            for h in range(1, AHEADS):
-                acc = jnp.where(head_of == h, o[h * QWIN : (h + 1) * QWIN], acc)
-            mixed[at : at + QWIN] = acc.astype(BF16)
+            part = slice(i * tall, (i + 1) * tall)
+            o = own_head(dot(e[part], vs[at : at + KWIN])) * inverse(own_head(total[part]))
+            mixed[at : at + QWIN] = o.astype(BF16)
 
     skewed(range(0, atoms, batch * QWIN), [score, soften, mix])
 
@@ -278,7 +289,7 @@
         lanes = slice(g * LANES, (g + 1) * LANES)
         turned = jnp.concatenate([tall[pl.ds(start, rows), lanes] for start in starts], axis=0).T
         for h in range(HEADS):
-            out[h * rows + g * SUB : h * rows + (g + 1) * SUB] = turned[h * SUB : (h + 1) * SUB]
+            out[h * rows + g * SUB : h * rows + (g + 1) * SUB] = turned[h * SUB : (h + 1) * SUB] * LOG2E
 
 
 def turn_bias(orders, row_bits, halves):
@@ -348,7 +359,7 @@
         kt[lanes] = k.T.astype(BF16)
     v[: v_near.shape[0]] = v_near[...]
     v[v_near.shape[0] :] = dot(x, wv[...]).astype(BF16)
-    scale = 1.0 / HEAD_DIM**0.5
+    scale = LOG2E / HEAD_DIM**0.5
     lane = iota((rows, 2 * LANES), 1)
     work = [(base, heads[i : i + 2]) for base, heads in head_groups(width) for i in range(0, len(heads), 2)]
 
@@ -365,7 +376,7 @@
 
     def soften(item):
         place, sc = item
-        e = jnp.exp(sc - jnp.max(sc, -1, keepdims=True))
+        e = jnp.exp2(sc - jnp.max(sc, -1, keepdims=True))
         return place, e.astype(BF16), inverse(jnp.sum(e, -1, keepdims=True))
 
     mixes = {}
@@ -442,22 +453,23 @@
     bits, row_bits = bits_of(lax.axis_size("sample")), bits_of(ranks)
     orders = [bits, bits[:1] + bits[-1:] + bits[1:-1]]
     split = (bias.shape[1] // LANES + 1) // 2 * LANES
-    mixed = atom_attention(0, atom_feat, inner, outer, atom_wq, atom_wk, atom_wv)
-    got = after(swap(bias, "sample", bits[0]), mixed)
-    held = [jnp.stack([bias[:, lanes], got[:, lanes]]) for lanes in (slice(0, split), slice(split, None))]
-    mixed = after(mixed, held)
+    got = swap(bias, "sample", bits[0])
     norms, inputs = [], []
     for s in range(samples):
+        mixed = atom_attention(s, atom_feat, inner, outer, atom_wq, atom_wk, atom_wv)
         if s:
-            mixed = atom_attention(s, atom_feat, inner, outer, atom_wq, atom_wk, atom_wv)
             norms[-1] = widen(norms[-1], "row", row_bits[0], mixed)
+            if s == 1:
+                for i in range(1, len(bits) - 1):
+                    held = [widen(h, "sample", order[i], mixed) for h, order in zip(held, orders)]
+                mixed = after(mixed, held)
             mixed = after(mixed, norms[-1])
         token_in, token_norm = gather_tokens(s, mixed, atom_feat, atom_token, atom_wo, agg_weight, token_gain, rows)
         inputs.append(token_in)
         norms.append(token_norm[None])
         if s == 0:
-            for i in range(1, len(bits) - 1):
-                held = [widen(h, "sample", order[i], token_norm) for h, order in zip(held, orders)]
+            bias, got, _ = lax.optimization_barrier((bias, got, token_norm))
+            held = [jnp.stack([bias[:, lanes], got[:, lanes]]) for lanes in (slice(0, split), slice(split, None))]
             inner = after(inner, held, token_norm)
     halves = []
     for h, order in zip(held, orders):

time: 38.6 us -> 37.4 us (0.969)
  starting transfers between devices: 11.2 us -> 13.1 us
  local copies, waits for them, and re-layouts: 1.7 us -> 0.08 us
  waiting for transfers between devices: 6.33 us -> 4.81 us
    ppermute x10, waiting for transfers between devices: 6.32 us -> 2.98 us  [swap(): lax.ppermute(held, axis, [(i, i ^ far) for i in range(lax.axis_size(axis))])]
    ppermute x10, starting transfers between devices: 8.6 us -> 11.5 us  [swap(): lax.ppermute(held, axis, [(i, i ^ far) for i in range(lax.axis_size(axis))])]
    ppermute x1, waiting for transfers between devices: 0.01 us -> 1.83 us  [shards(): lax.ppermute(outer, 'row', odd_pairs + [(j, i) for i, j in odd_pairs])]
    another operation x4 -> x2, local copies, waits for them, and re-layouts: 1.63 us -> 0.02 us  [shards(): jnp.stack([bias[:, lanes], got[:, lanes]])]
    ppermute x1, starting transfers between devices: 2.64 us -> 1.63 us  [shards(): lax.ppermute(outer, 'row', odd_pairs + [(j, i) for i, j in odd_pairs])]
  transfers between devices with their start and end apart: 11 -> 11, of which waited for: 6 -> 5; matrix products, arithmetic and copies ran while one was open for 4% -> 0% of each run, Pallas kernels for 32% -> 33%
where the time goes in v7:
time: 37.4 us; the launch traced here: 37.3 us
  Pallas kernels  18.8 us (50%)
  starting transfers between devices  13.1 us (35%)
  waiting for transfers between devices  4.81 us (13%)
    ppermute x10, starting transfers between devices, swap(): lax.ppermute(held, axis, [(i, i ^ far) for i in range(lax.axis_size(axis))])  11.5 us
    pallas_call x2, Pallas kernels, attend(): pl.pallas_call(attend_kernel, out_shape=jax.ShapeDtypeStruct(shape, BF16)...  5.14 us
    pallas_call x2, Pallas kernels, atom_attention(): pl.pallas_call(functools.partial(atom_kernel, sample), out_shape=jax.Shap...  4.53 us
    pallas_call x1, Pallas kernels, pair_bias(): pl.pallas_call(bias_kernel, grid=(1,), out_shape=[jax.ShapeDtypeStruct((c...  3.57 us
    ppermute x10, waiting for transfers between devices, swap(): lax.ppermute(held, axis, [(i, i ^ far) for i in range(lax.axis_size(axis))])  2.98 us
    pallas_call x2, Pallas kernels, gather_tokens(): pl.pallas_call(functools.partial(gather_kernel, sample), out_shape=[jax.S...  2.82 us
    pallas_call x2, Pallas kernels, project(): pl.pallas_call(project_kernel, out_shape=[jax.ShapeDtypeStruct((rows, wid...  2.04 us
    ppermute x1, waiting for transfers between devices, shards(): lax.ppermute(outer, 'row', odd_pairs + [(j, i) for i, j in odd_pairs])  1.83 us
  transfers between devices with their start and end apart: 11, of which 5 were waited for; matrix products, arithmetic and copies ran while one was open for 0% of the time, Pallas kernels for 33%

profile of v7, /device:TPU:0, one launch (start us, length us, event | category | flops | bytes accessed | tf_op | source)
XLA Modules:
  0.0 37.3 jit_solution(14765460496011899424)
XLA Ops:
  0.0 3.6 %pair_bias.1 = (bf16[36,1152]{1,0:T(8,128)(2,1)}, bf16[2,48,128]{2,1,0:T(8,128)(2,1)}, bf16[2,48,128]{2,1,0:T(8,128)(2,1)}) custom-call(bf16[2,1152,128]{2,1,0:T(8,128)(2,1)} %feat.7, bf16[2,1152,128]{2,1,0:T(8,128)(2,1)} %feat.7, bf16[36,72,128]{2,1,0:T(8,128)(2,1)} %bitcast.16, s32[36]{0:T(128)} %mask.1, bf16[16,128]{1,0:T(8,128)(2,1)} %bitcast.17), custom_call_target="tpu_custom_call" | custom-call | flops 60000000 | bytes 1000 | tf_op jit(solution)/shard_map/pair_bias/pallas_call | solution.py:102
  3.6 4.0 %collective-permute-start.1 = (bf16[36,1152]{1,0:T(8,128)(2,1)}, bf16[36,1152]{1,0:T(8,128)(2,1)S(1)}, u32[]{:S(2)}, u32[]{:S(2)}) collective-permute-start(bf16[36,1152]{1,0:T(8,128)(2,1)} %get-tuple-element.37), channel_id=1, source_target_pairs={{0,4},{1,5},{2,6},{3,7},{4,0},{5,1},{6,2},{7,3},{8,12},{9,13},{10,... | collective-permute-start | bytes 248840 | tf_op jit(solution)/shard_map/ppermute | solution.py:130
  7.7 0.0 collective-permute-start
  7.7 1.6 %collective-permute-start.2 = (bf16[2,48,128]{2,1,0:T(8,128)(2,1)}, bf16[2,48,128]{2,1,0:T(8,128)(2,1)S(1)}, u32[]{:S(2)}, u32[]{:S(2)}) collective-permute-start(bf16[2,48,128]{2,1,0:T(8,128)(2,1)} %get-tuple-element.35), channel_id=1, source_target_pairs={{8,16},{24,0},{16,8},{0,24},{9,17},{25,1},{17,9},{1,25},{10,18},{2... | collective-permute-start | bytes 73736 | tf_op jit(solution)/shard_map/ppermute | solution.py:448
  9.3 0.0 collective-permute-done.inner
  9.3 1.8 %collective-permute-done.2.outer = bf16[2,48,128]{2,1,0:T(8,128)(2,1)S(1)} collective-permute-done((bf16[2,48,128]{2,1,0:T(8,128)(2,1)}, bf16[2,48,128]{2,1,0:T(8,128)(2,1)S(1)}, u32[]{:S(2)}, u32[]{:S(2)}) %collective-permute-start.2) | collective-permute-done | bytes 24608 | tf_op jit(solution)/shard_map/ppermute | solution.py:448
  11.2 0.0 copy-start.5
  11.2 2.3 %atom_attention.2.mixed = bf16[1152,128]{1,0:T(8,128)(2,1)S(1)} custom-call(bf16[2,1152,128]{2,1,0:T(8,128)(2,1)S(1)} %copy-done, bf16[2,48,128]{2,1,0:T(8,128)(2,1)S(1)} %collective-permute-done.inner, bf16[2,48,128]{2,1,0:T(8,128)(2,1)S(1)} %collective-permute-done.2.outer, bf16[128,128]{1,0:T(8,128)(2,1)S(1)} %copy-done.7, ...), custom_call_target="tpu_custom_call" | custom-call | flops 80000000 | bytes 1000 | tf_op jit(solution)/shard_map/atom_attention/pallas_call | solution.py:218
  13.5 0.0 copy-start.4
  13.5 1.4 %gather_tokens.2 = (f32[72,768]{1,0:T(8,128)S(1)}, bf16[72,768]{1,0:T(8,128)(2,1)S(1)}) custom-call(bf16[1152,128]{1,0:T(8,128)(2,1)S(1)} %atom_attention.2.mixed, bf16[2,1152,128]{2,1,0:T(8,128)(2,1)S(1)} %copy-done, s32[1152]{0:T(1024)S(1)} %copy-done.11, bf16[128,128]{1,0:T(8,128)(2,1)S(1)} %copy-done.10, bf16[128,768]{1,0:T(8,128)(2,1)S(1)} %copy-done.6, ...), custom_call_target="tpu_custom_call" | custom-call | flops 20000000 | bytes 1000 | tf_op jit(solution)/shard_map/gather_tokens/pallas_call | solution.py:263
  14.9 1.6 %collective-permute-start.5 = (bf16[1,72,768]{2,1,0:T(8,128)(2,1)S(1)}, bf16[1,72,768]{2,1,0:T(8,128)(2,1)S(1)}, u32[]{:S(2)}, u32[]{:S(2)}) collective-permute-start(bf16[1,72,768]{2,1,0:T(8,128)(2,1)S(1)} %bitcast.14), channel_id=1, source_target_pairs={{0,16},{8,24},{16,0},{24,8},{1,17},{9,25},{17,1},{25,9},{2,18},{10... | collective-permute-start | bytes 331784 | tf_op jit(solution)/shard_map/ppermute | solution.py:130
  16.5 0.0 collective-permute-done.1
  16.6 1.6 %collective-permute-start.4 = (bf16[2,36,512]{2,1,0:T(8,128)(2,1)S(1)}, bf16[2,36,512]{2,1,0:T(8,128)(2,1)S(1)}, u32[]{:S(2)}, u32[]{:S(2)}) collective-permute-start(bf16[2,36,512]{2,1,0:T(8,128)(2,1)S(1)} %pad_maximum_fusion.5), channel_id=1, source_target_pairs={{0,1},{1,0},{2,3},{3,2},{4,5},{5,4},{6,7},{7,6},{8,9},{9,8},{10,11... | collective-permute-start | bytes 221192 | tf_op jit(solution)/shard_map/ppermute | solution.py:130
  18.1 1.6 %collective-permute-start.3 = (bf16[2,36,640]{2,1,0:T(8,128)(2,1)S(1)}, bf16[2,36,640]{2,1,0:T(8,128)(2,1)S(1)}, u32[]{:S(2)}, u32[]{:S(2)}) collective-permute-start(bf16[2,36,640]{2,1,0:T(8,128)(2,1)S(1)} %pad_maximum_fusion.4), channel_id=1, source_target_pairs={{0,2},{1,3},{2,0},{3,1},{4,6},{5,7},{6,4},{7,5},{8,10},{9,11},{10,... | collective-permute-start | bytes 276488 | tf_op jit(solution)/shard_map/ppermute | solution.py:130
  19.8 2.3 %atom_attention.3.mixed = bf16[1152,128]{1,0:T(8,128)(2,1)S(1)} custom-call(bf16[2,1152,128]{2,1,0:T(8,128)(2,1)S(1)} %copy-done, bf16[2,48,128]{2,1,0:T(8,128)(2,1)S(1)} %collective-permute-done.inner, bf16[2,48,128]{2,1,0:T(8,128)(2,1)S(1)} %collective-permute-done.2.outer, bf16[128,128]{1,0:T(8,128)(2,1)S(1)} %copy-done.7, ...), custom_call_target="tpu_custom_call" | custom-call | flops 80000000 | bytes 1000 | tf_op jit(solution)/shard_map/atom_attention/pallas_call | solution.py:218
  22.1 0.0 copy-start.1
  22.1 0.0 collective-permute-done.5
  22.1 0.1 collective-permute-start.7
  22.2 1.0 %collective-permute-done.3 = bf16[2,36,640]{2,1,0:T(8,128)(2,1)S(1)} collective-permute-done((bf16[2,36,640]{2,1,0:T(8,128)(2,1)S(1)}, bf16[2,36,640]{2,1,0:T(8,128)(2,1)S(1)}, u32[]{:S(2)}, u32[]{:S(2)}) %collective-permute-start.3) | collective-permute-done | bytes 92192 | tf_op jit(solution)/shard_map/ppermute | solution.py:130
  23.3 0.6 %collective-permute-start.8 = (bf16[4,36,640]{2,1,0:T(8,128)(2,1)S(1)}, bf16[4,36,640]{2,1,0:T(8,128)(2,1)S(1)}, u32[]{:S(2)}, u32[]{:S(2)}) collective-permute-start(bf16[4,36,640]{2,1,0:T(8,128)(2,1)S(1)} %pad_maximum_fusion.2.refs_0_), channel_id=1, source_target_pairs={{0,1},{1,0},{2,3},{3,2},{4,5},{5,4},{6,7},{7,6},{8,9},{9,8},{10,11... | collective-permute-start | bytes 552968 | tf_op jit(solution)/shard_map/ppermute | solution.py:130
  23.9 1.3 %collective-permute-start.9 = (bf16[4,36,512]{2,1,0:T(8,128)(2,1)S(1)}, bf16[4,36,512]{2,1,0:T(8,128)(2,1)S(1)}, u32[]{:S(2)}, u32[]{:S(2)}) collective-permute-start(bf16[4,36,512]{2,1,0:T(8,128)(2,1)S(1)} %pad_maximum_fusion.3.refs_2_), channel_id=1, source_target_pairs={{0,2},{1,3},{2,0},{3,1},{4,6},{5,7},{6,4},{7,5},{8,10},{9,11},{10,... | collective-permute-start | bytes 442376 | tf_op jit(solution)/shard_map/ppermute | solution.py:130
  25.2 1.4 %gather_tokens.3 = (f32[72,768]{1,0:T(8,128)S(1)}, bf16[72,768]{1,0:T(8,128)(2,1)S(1)}) custom-call(bf16[1152,128]{1,0:T(8,128)(2,1)S(1)} %atom_attention.3.mixed, bf16[2,1152,128]{2,1,0:T(8,128)(2,1)S(1)} %copy-done, s32[1152]{0:T(1024)S(1)} %copy-done.11, bf16[128,128]{1,0:T(8,128)(2,1)S(1)} %copy-done.10, bf16[128,768]{1,0:T(8,128)(2,1)S(1)} %copy-done.6, ...), custom_call_target="tpu_custom_call" | custom-call | flops 20000000 | bytes 1000 | tf_op jit(solution)/shard_map/gather_tokens/pallas_call | solution.py:263
  26.7 0.6 %collective-permute-start.6 = (bf16[1,72,768]{2,1,0:T(8,128)(2,1)S(1)}, bf16[1,72,768]{2,1,0:T(8,128)(2,1)S(1)}, u32[]{:S(2)}, u32[]{:S(2)}) collective-permute-start(bf16[1,72,768]{2,1,0:T(8,128)(2,1)S(1)} %bitcast.12), channel_id=1, source_target_pairs={{0,16},{8,24},{16,0},{24,8},{1,17},{9,25},{17,1},{25,9},{2,18},{10... | collective-permute-start | bytes 331784 | tf_op jit(solution)/shard_map/ppermute | solution.py:130
  27.3 0.9 %project.2 = (bf16[72,768]{1,0:T(8,128)(2,1)S(1)}, bf16[144,768]{1,0:T(8,128)(2,1)S(1)}, bf16[144,768]{1,0:T(8,128)(2,1)S(1)}, f32[72,768]{1,0:T(8,128)S(1)}) custom-call(bf16[2,72,768]{2,1,0:T(8,128)(2,1)S(1)} %pad_maximum_fusion.near, bf16[768,768]{1,0:T(8,128)(2,1)S(1)} %copy-done.4, bf16[768,768]{1,0:T(8,128)(2,1)S(1)} %copy-done.1, ...), custom_call_target="tpu_custom_call" | custom-call | flops 40000000 | bytes 1000 | tf_op jit(solution)/shard_map/project/pallas_call | solution.py:336
  28.2 1.1 %collective-permute-done.9.refs_3_ = bf16[4,36,512]{2,1,0:T(8,128)(2,1)S(1)} collective-permute-done((bf16[4,36,512]{2,1,0:T(8,128)(2,1)S(1)}, bf16[4,36,512]{2,1,0:T(8,128)(2,1)S(1)}, u32[]{:S(2)}, u32[]{:S(2)}) %collective-permute-start.9) | collective-permute-done | bytes 147488 | tf_op jit(solution)/shard_map/ppermute | solution.py:130
  29.3 0.5 %collective-permute-done.8.refs_1_ = bf16[4,36,640]{2,1,0:T(8,128)(2,1)S(1)} collective-permute-done((bf16[4,36,640]{2,1,0:T(8,128)(2,1)S(1)}, bf16[4,36,640]{2,1,0:T(8,128)(2,1)S(1)}, u32[]{:S(2)}, u32[]{:S(2)}) %collective-permute-start.8) | collective-permute-done | bytes 184352 | tf_op jit(solution)/shard_map/ppermute | solution.py:130
  29.8 0.7 %turn_bias.1.bias = f32[1152,288]{1,0:T(8,128)S(1)} custom-call(bf16[4,36,640]{2,1,0:T(8,128)(2,1)S(1)} %pad_maximum_fusion.2.refs_0_, bf16[4,36,640]{2,1,0:T(8,128)(2,1)S(1)} %collective-permute-done.8.refs_1_, bf16[4,36,512]{2,1,0:T(8,128)(2,1)S(1)} %pad_maximum_fusion.3.refs_2_, bf16[4,36,512]{2,1,0:T(8,128)(2,1)S(1)} %collective-permute-done.9.refs_3_), custom_call_target="tpu_custom_call" | custom-call | flops 20000000 | bytes 1000 | tf_op jit(solution)/shard_map/turn_bias/pallas_call | solution.py:300
  30.5 2.2 %attend.2.rest_0_ = bf16[72,768]{1,0:T(8,128)(2,1)S(1)} custom-call(bf16[2,72,768]{2,1,0:T(8,128)(2,1)S(1)} %collective-permute-done.7.far, bf16[72,768]{1,0:T(8,128)(2,1)S(1)} %get-tuple-element.46.q, bf16[144,768]{1,0:T(8,128)(2,1)S(1)} %get-tuple-element.47.k_near, bf16[144,768]{1,0:T(8,128)(2,1)S(1)} %get-tuple-element.48.v_near, ...), custom_call_target="tpu_custom_call" | custom-call | flops 60000000 | bytes 1000 | tf_op jit(solution)/shard_map/attend/pallas_call | solution.py:412
  32.8 0.1 collective-permute-start.10
  32.9 1.1 %project.3 = (bf16[72,768]{1,0:T(8,128)(2,1)S(1)}, bf16[144,768]{1,0:T(8,128)(2,1)S(1)}, bf16[144,768]{1,0:T(8,128)(2,1)S(1)}, f32[72,768]{1,0:T(8,128)S(1)}) custom-call(bf16[2,72,768]{2,1,0:T(8,128)(2,1)S(1)} %pad_maximum_fusion.1.near, bf16[768,768]{1,0:T(8,128)(2,1)S(1)} %copy-done.4, bf16[768,768]{1,0:T(8,128)(2,1)S(1)} %copy-done.1, ...), custom_call_target="tpu_custom_call" | custom-call | flops 40000000 | bytes 1000 | tf_op jit(solution)/shard_map/project/pallas_call | solution.py:336
  34.0 0.3 collective-permute-done.10.far
  34.3 2.9 %attend.3 = bf16[2,72,768]{2,1,0:T(8,128)(2,1)} custom-call(bf16[2,72,768]{2,1,0:T(8,128)(2,1)S(1)} %collective-permute-done.10.far, bf16[72,768]{1,0:T(8,128)(2,1)S(1)} %get-tuple-element.56.q, bf16[144,768]{1,0:T(8,128)(2,1)S(1)} %get-tuple-element.57.k_near, bf16[144,768]{1,0:T(8,128)(2,1)S(1)} %get-tuple-element.58.v_near, ...), custom_call_target="tpu_custom_call" | custom-call | flops 60000000 | bytes 1000 | tf_op jit(solution)/shard_map/attend/pallas_call | solution.py:412
  (36 shorter events, 0.2 us)
Async XLA Ops:
  0.0 11.1 %copy-start = (bf16[2,1152,128]{2,1,0:T(8,128)(2,1)S(1)}, bf16[2,1152,128]{2,1,0:T(8,128)(2,1)}, u32[]{:S(2)}) copy-start(bf16[2,1152,128]{2,1,0:T(8,128)(2,1)} %feat.7) | copy-start | bytes 1769476
  0.0 11.1 %copy-start.7 = (bf16[128,128]{1,0:T(8,128)(2,1)S(1)}, bf16[128,128]{1,0:T(8,128)(2,1)}, u32[]{:S(2)}) copy-start(bf16[128,128]{1,0:T(8,128)(2,1)} %wq.5) | copy-start | bytes 98308
  0.0 11.1 %copy-start.8 = (bf16[128,128]{1,0:T(8,128)(2,1)S(1)}, bf16[128,128]{1,0:T(8,128)(2,1)}, u32[]{:S(2)}) copy-start(bf16[128,128]{1,0:T(8,128)(2,1)} %wk.7) | copy-start | bytes 98308
  0.0 11.1 %copy-start.9 = (bf16[128,128]{1,0:T(8,128)(2,1)S(1)}, bf16[128,128]{1,0:T(8,128)(2,1)}, u32[]{:S(2)}) copy-start(bf16[128,128]{1,0:T(8,128)(2,1)} %wv.7) | copy-start | bytes 98308
  0.0 13.4 %copy-start.6 = (bf16[128,768]{1,0:T(8,128)(2,1)S(1)}, bf16[128,768]{1,0:T(8,128)(2,1)}, u32[]{:S(2)}) copy-start(bf16[128,768]{1,0:T(8,128)(2,1)} %agg.3) | copy-start | bytes 589828
  0.0 13.4 %copy-start.10 = (bf16[128,128]{1,0:T(8,128)(2,1)S(1)}, bf16[128,128]{1,0:T(8,128)(2,1)}, u32[]{:S(2)}) copy-start(bf16[128,128]{1,0:T(8,128)(2,1)} %wo.7) | copy-start | bytes 98308
  0.0 13.4 %copy-start.11 = (s32[1152]{0:T(1024)S(1)}, s32[1152]{0:T(1024)}, u32[]{:S(2)}) copy-start(s32[1152]{0:T(1024)} %token_.3) | copy-start | bytes 13828
  0.0 13.4 %copy-start.12 = (f32[768]{0:T(1024)S(1)}, f32[768]{0:T(1024)}, u32[]{:S(2)}) copy-start(f32[768]{0:T(1024)} %gain.3) | copy-start | bytes 9220
  3.6 12.9 %copy-start.13 = (bf16[36,1152]{1,0:T(8,128)(2,1)S(1)}, bf16[36,1152]{1,0:T(8,128)(2,1)}, u32[]{:S(2)}) copy-start(bf16[36,1152]{1,0:T(8,128)(2,1)} %get-tuple-element.37) | copy-start | bytes 248836
  3.6 12.9 %collective-permute-start.1 = (bf16[36,1152]{1,0:T(8,128)(2,1)}, bf16[36,1152]{1,0:T(8,128)(2,1)S(1)}, u32[]{:S(2)}, u32[]{:S(2)}) collective-permute-start(bf16[36,1152]{1,0:T(8,128)(2,1)} %get-tuple-element.37), channel_id=1, source_target_pairs={{0,4},{1,5},{2,6},{3,7},{4,0},{5,1},{6,2},{7,3},{8,12},{9,13},{10,... | collective-permute-start | bytes 248840 | tf_op jit(solution)/shard_map/ppermute | solution.py:130
  7.7 1.6 %collective-permute-start = (bf16[2,48,128]{2,1,0:T(8,128)(2,1)}, bf16[2,48,128]{2,1,0:T(8,128)(2,1)S(1)}, u32[]{:S(2)}, u32[]{:S(2)}) collective-permute-start(bf16[2,48,128]{2,1,0:T(8,128)(2,1)} %get-tuple-element.33), channel_id=1, source_target_pairs={{0,8},{8,0},{16,24},{24,16},{1,9},{9,1},{17,25},{25,17},{2,10},{10... | collective-permute-start | bytes 73736 | tf_op jit(solution)/shard_map/ppermute | solution.py:130
  7.7 3.5 %collective-permute-start.2 = (bf16[2,48,128]{2,1,0:T(8,128)(2,1)}, bf16[2,48,128]{2,1,0:T(8,128)(2,1)S(1)}, u32[]{:S(2)}, u32[]{:S(2)}) collective-permute-start(bf16[2,48,128]{2,1,0:T(8,128)(2,1)} %get-tuple-element.35), channel_id=1, source_target_pairs={{8,16},{24,0},{16,8},{0,24},{9,17},{25,1},{17,9},{1,25},{10,18},{2... | collective-permute-start | bytes 73736 | tf_op jit(solution)/shard_map/ppermute | solution.py:448
  11.2 16.1 %copy-start.5 = (bf16[768,768]{1,0:T(8,128)(2,1)S(1)}, bf16[768,768]{1,0:T(8,128)(2,1)}, u32[]{:S(2)}) copy-start(bf16[768,768]{1,0:T(8,128)(2,1)} %wg.3) | copy-start | bytes 3538948
  13.5 13.8 %copy-start.4 = (bf16[768,768]{1,0:T(8,128)(2,1)S(1)}, bf16[768,768]{1,0:T(8,128)(2,1)}, u32[]{:S(2)}) copy-start(bf16[768,768]{1,0:T(8,128)(2,1)} %wq.7) | copy-start | bytes 3538948
  14.9 7.2 %collective-permute-start.5 = (bf16[1,72,768]{2,1,0:T(8,128)(2,1)S(1)}, bf16[1,72,768]{2,1,0:T(8,128)(2,1)S(1)}, u32[]{:S(2)}, u32[]{:S(2)}) collective-permute-start(bf16[1,72,768]{2,1,0:T(8,128)(2,1)S(1)} %bitcast.14), channel_id=1, source_target_pairs={{0,16},{8,24},{16,0},{24,8},{1,17},{9,25},{17,1},{25,9},{2,18},{10... | collective-permute-start | bytes 331784 | tf_op jit(solution)/shard_map/ppermute | solution.py:130
  16.6 5.6 %collective-permute-start.4 = (bf16[2,36,512]{2,1,0:T(8,128)(2,1)S(1)}, bf16[2,36,512]{2,1,0:T(8,128)(2,1)S(1)}, u32[]{:S(2)}, u32[]{:S(2)}) collective-permute-start(bf16[2,36,512]{2,1,0:T(8,128)(2,1)S(1)} %pad_maximum_fusion.5), channel_id=1, source_target_pairs={{0,1},{1,0},{2,3},{3,2},{4,5},{5,4},{6,7},{7,6},{8,9},{9,8},{10,11... | collective-permute-start | bytes 221192 | tf_op jit(solution)/shard_map/ppermute | solution.py:130
  18.1 9.1 %copy-start.3 = (bf16[768,768]{1,0:T(8,128)(2,1)S(1)}, bf16[768,768]{1,0:T(8,128)(2,1)}, u32[]{:S(2)}) copy-start(bf16[768,768]{1,0:T(8,128)(2,1)} %wo.11) | copy-start | bytes 3538948
  18.1 5.1 %collective-permute-start.3 = (bf16[2,36,640]{2,1,0:T(8,128)(2,1)S(1)}, bf16[2,36,640]{2,1,0:T(8,128)(2,1)S(1)}, u32[]{:S(2)}, u32[]{:S(2)}) collective-permute-start(bf16[2,36,640]{2,1,0:T(8,128)(2,1)S(1)} %pad_maximum_fusion.4), channel_id=1, source_target_pairs={{0,2},{1,3},{2,0},{3,1},{4,6},{5,7},{6,4},{7,5},{8,10},{9,11},{10,... | collective-permute-start | bytes 276488 | tf_op jit(solution)/shard_map/ppermute | solution.py:130
  19.8 7.5 %copy-start.2 = (bf16[768,768]{1,0:T(8,128)(2,1)S(1)}, bf16[768,768]{1,0:T(8,128)(2,1)}, u32[]{:S(2)}) copy-start(bf16[768,768]{1,0:T(8,128)(2,1)} %wv.11) | copy-start | bytes 3538948
  22.1 5.2 %copy-start.1 = (bf16[768,768]{1,0:T(8,128)(2,1)S(1)}, bf16[768,768]{1,0:T(8,128)(2,1)}, u32[]{:S(2)}) copy-start(bf16[768,768]{1,0:T(8,128)(2,1)} %wk.11) | copy-start | bytes 3538948
  22.1 8.4 %collective-permute-start.7 = (bf16[2,72,768]{2,1,0:T(8,128)(2,1)S(1)}, bf16[2,72,768]{2,1,0:T(8,128)(2,1)S(1)}, u32[]{:S(2)}, u32[]{:S(2)}) collective-permute-start(bf16[2,72,768]{2,1,0:T(8,128)(2,1)S(1)} %pad_maximum_fusion.near), channel_id=1, source_target_pairs={{0,8},{8,0},{16,24},{24,16},{1,9},{9,1},{17,25},{25,17},{2,10},{10... | collective-permute-start | bytes 663560 | tf_op jit(solution)/shard_map/ppermute | solution.py:130
  23.3 6.5 %collective-permute-start.8 = (bf16[4,36,640]{2,1,0:T(8,128)(2,1)S(1)}, bf16[4,36,640]{2,1,0:T(8,128)(2,1)S(1)}, u32[]{:S(2)}, u32[]{:S(2)}) collective-permute-start(bf16[4,36,640]{2,1,0:T(8,128)(2,1)S(1)} %pad_maximum_fusion.2.refs_0_), channel_id=1, source_target_pairs={{0,1},{1,0},{2,3},{3,2},{4,5},{5,4},{6,7},{7,6},{8,9},{9,8},{10,11... | collective-permute-start | bytes 552968 | tf_op jit(solution)/shard_map/ppermute | solution.py:130
  23.9 5.4 %collective-permute-start.9 = (bf16[4,36,512]{2,1,0:T(8,128)(2,1)S(1)}, bf16[4,36,512]{2,1,0:T(8,128)(2,1)S(1)}, u32[]{:S(2)}, u32[]{:S(2)}) collective-permute-start(bf16[4,36,512]{2,1,0:T(8,128)(2,1)S(1)} %pad_maximum_fusion.3.refs_2_), channel_id=1, source_target_pairs={{0,2},{1,3},{2,0},{3,1},{4,6},{5,7},{6,4},{7,5},{8,10},{9,11},{10,... | collective-permute-start | bytes 442376 | tf_op jit(solution)/shard_map/ppermute | solution.py:130
  26.7 6.1 %collective-permute-start.6 = (bf16[1,72,768]{2,1,0:T(8,128)(2,1)S(1)}, bf16[1,72,768]{2,1,0:T(8,128)(2,1)S(1)}, u32[]{:S(2)}, u32[]{:S(2)}) collective-permute-start(bf16[1,72,768]{2,1,0:T(8,128)(2,1)S(1)} %bitcast.12), channel_id=1, source_target_pairs={{0,16},{8,24},{16,0},{24,8},{1,17},{9,25},{17,1},{25,9},{2,18},{10... | collective-permute-start | bytes 331784 | tf_op jit(solution)/shard_map/ppermute | solution.py:130
  32.8 1.5 %collective-permute-start.10 = (bf16[2,72,768]{2,1,0:T(8,128)(2,1)S(1)}, bf16[2,72,768]{2,1,0:T(8,128)(2,1)S(1)}, u32[]{:S(2)}, u32[]{:S(2)}) collective-permute-start(bf16[2,72,768]{2,1,0:T(8,128)(2,1)S(1)} %pad_maximum_fusion.1.near), channel_id=1, source_target_pairs={{0,8},{8,0},{16,24},{24,16},{1,9},{9,1},{17,25},{25,17},{2,10},{10... | collective-permute-start | bytes 663560 | tf_op jit(solution)/shard_map/ppermute | solution.py:130

commit v8 on v7

--- a/solution.py
+++ b/solution.py
@@ -141,15 +141,65 @@
     return places
 
 
-def atom_kernel(sample, feat, inner, outer, wq, wk, wv, mixed, qs, ks, vs):
-    atoms, chans = feat.shape[1:]
+def windows_attend(starts, qs, ks, vs, mixed, shift, hide):
+    rate = LOG2E / AHEAD_DIM**0.5
+    tall = AHEADS * QWIN
+    head_of = iota((QWIN, qs.shape[1]), 1) // AHEAD_DIM
+
+    def score(batch):
+        out = []
+        for at in batch:
+            q = qs[at - shift : at - shift + QWIN]
+            q = jnp.concatenate([jnp.where(head_of == h, q, jnp.zeros_like(q)) for h in range(AHEADS)], axis=0)
+            out.append(hide(at, dot_nt(q, ks[at : at + KWIN])))
+        return batch, jnp.concatenate(out, axis=0)
+
+    def soften(item):
+        batch, s = item
+        e = jnp.exp2((s - jnp.max(s, -1, keepdims=True)) * rate)
+        return batch, e.astype(BF16), jnp.sum(e, -1, keepdims=True)
+
+    def own_head(parts):
+        acc = parts[:QWIN]
+        for h in range(1, AHEADS):
+            acc = jnp.where(head_of == h, parts[h * QWIN : (h + 1) * QWIN], acc)
+        return acc
+
+    def mix(item):
+        batch, e, total = item
+        for i, at in enumerate(batch):
+            part = slice(i * tall, (i + 1) * tall)
+            o = own_head(dot(e[part], vs[at : at + KWIN])) * inverse(own_head(total[part]))
+            mixed[at - shift : at - shift + QWIN] = o.astype(BF16)
+
+    skewed(starts, [score, soften, mix])
+
+
+def halo_of(sample, inner, outer):
+    odd = lax.axis_index("row") % 2 == 1
+    return jnp.where(odd, inner[sample], outer[sample]), jnp.where(odd, outer[sample], inner[sample])
+
+
+def hide_outside(atoms):
     rank = lax.axis_index("row")
     at_start = rank == 0
     at_end = rank == lax.axis_size("row") - 1
+    keyat = iota((AHEADS * QWIN, KWIN), 1)
+
+    def hide(at, s):
+        if at < RIM:
+            s = jnp.where(at_start & (keyat < RIM - at), -jnp.inf, s)
+        if at + KWIN > RIM + atoms:
+            s = jnp.where(at_end & (keyat >= RIM + atoms - at), -jnp.inf, s)
+        return s
+
+    return hide
+
+
+def atom_kernel(sample, feat, *refs):
+    *halo, wq, wk, wv, mixed, qs, ks, vs = refs
+    atoms, chans = feat.shape[1:]
     wqkv = jnp.concatenate([wq[...], wk[...], wv[...]], axis=1)
-    odd = rank % 2 == 1
-    before = jnp.where(odd, inner[sample], outer[sample])
-    behind = jnp.where(odd, outer[sample], inner[sample])
 
     def normalise(at):
         if isinstance(at, int):
@@ -170,55 +220,26 @@
         ks[RIM + at : RIM + at + count] = kv[:, :chans]
         vs[RIM + at : RIM + at + count] = kv[:, chans:]
 
-    skewed([*range(0, atoms, LANES), (-RIM, before), (atoms, behind)], [normalise, project_atoms])
-    rate = LOG2E / AHEAD_DIM**0.5
-    tall = AHEADS * QWIN
-    head_of = iota((QWIN, chans), 1) // AHEAD_DIM
-    keyat = iota((tall, KWIN), 1)
-    batch = 6
-
-    def score(first):
-        out = []
-        for at in range(first, first + batch * QWIN, QWIN):
-            q = qs[at : at + QWIN]
-            q = jnp.concatenate([jnp.where(head_of == h, q, jnp.zeros_like(q)) for h in range(AHEADS)], axis=0)
-            s = dot_nt(q, ks[at : at + KWIN])
-            if at < RIM:
-                s = jnp.where(at_start & (keyat < RIM - at), -jnp.inf, s)
-            if at + KWIN > RIM + atoms:
-                s = jnp.where(at_end & (keyat >= RIM + atoms - at), -jnp.inf, s)
-            out.append(s)
-        return first, jnp.concatenate(out, axis=0)
-
-    def soften(item):
-        first, s = item
-        e = jnp.exp2((s - jnp.max(s, -1, keepdims=True)) * rate)
-        return first, e.astype(BF16), jnp.sum(e, -1, keepdims=True)
-
-    def own_head(parts):
-        acc = parts[:QWIN]
-        for h in range(1, AHEADS):
-            acc = jnp.where(head_of == h, parts[h * QWIN : (h + 1) * QWIN], acc)
-        return acc
-
-    def mix(item):
-        first, e, total = item
-        for i in range(batch):
-            at = first + i * QWIN
-            part = slice(i * tall, (i + 1) * tall)
-            o = own_head(dot(e[part], vs[at : at + KWIN])) * inverse(own_head(total[part]))
-            mixed[at : at + QWIN] = o.astype(BF16)
-
-    skewed(range(0, atoms, batch * QWIN), [score, soften, mix])
-
-
-def atom_attention(sample, feat, inner, outer, wq, wk, wv):
+    parts = list(range(0, atoms, LANES))
+    if halo:
+        before, behind = halo_of(sample, *halo)
+        parts += [(-RIM, before), (atoms, behind)]
+    skewed(parts, [normalise, project_atoms])
+    starts = list(range(0, atoms, QWIN))
+    if not halo:
+        starts = [at for at in starts if RIM <= at <= atoms + RIM - KWIN]
+    batch = 8 if len(starts) % 8 == 0 else 6
+    batches = [starts[i : i + batch] for i in range(0, len(starts), batch)]
+    windows_attend(batches, qs, ks, vs, mixed, 0, hide_outside(atoms))
+
+
+def atom_attention(sample, feat, halo, wq, wk, wv):
     atoms, chans = feat.shape[1:]
     vmem = pl.BlockSpec(memory_space=pltpu.VMEM)
     return pl.pallas_call(
         functools.partial(atom_kernel, sample),
         out_shape=jax.ShapeDtypeStruct((atoms, chans), BF16),
-        in_specs=[vmem] * 6,
+        in_specs=[vmem] * (4 + len(halo)),
         out_specs=vmem,
         scratch_shapes=[
             pltpu.VMEM((atoms, chans), BF16),
@@ -228,20 +249,42 @@
         compiler_params=pltpu.CompilerParams(vmem_limit_bytes=16 * MIB),
         cost_estimate=cost(4),
         name="atom_attention",
-    )(feat, inner, outer, wq, wk, wv)
-
-
-def gather_kernel(sample, mixed, feat, token, wo, agg, gain, token_in, token_norm):
-    atoms = feat.shape[1]
+    )(feat, *halo, wq, wk, wv)
+
+
+def gather_kernel(sample, mixed, feat, token, wo, agg, gain, *refs):
+    *outside, token_in, token_norm, qs, ks, vs, ends = refs
+    atoms, chans = feat.shape[1:]
     rows = token_in.shape[0]
     local = token[...].reshape(1, atoms) - lax.axis_index("row") * rows
     step = 384
     sums = []
+    edge = 2 * QWIN
+    if outside:
+        inner, outer, wq, wk, wv = outside
+        before, behind = halo_of(sample, inner, outer)
+        wqkv = jnp.concatenate([wq[...], wk[...], wv[...]], axis=1)
+        near = edge + KWIN - QWIN - RIM
+        both = [before, feat[sample, :near], feat[sample, atoms - near :], behind]
+        qkv = dot(layer_norm(jnp.concatenate([p.astype(F32) for p in both], axis=0)).astype(BF16), wqkv).astype(BF16)
+        qs[...] = qkv[:, :chans]
+        ks[...] = qkv[:, chans : 2 * chans]
+        vs[...] = qkv[:, 2 * chans :]
+        apart = atoms - 2 * near
+        starts = [0, QWIN, RIM + near, RIM + near + QWIN]
+        hide = hide_outside(atoms)
+        windows_attend([starts], qs, ks, vs, ends, -RIM, lambda at, s: hide(at if at < RIM else at + apart, s))
 
     def finish(c):
-        return c, (feat[sample, c : c + step].astype(F32) + dot(mixed[c : c + step], wo[...])).astype(BF16)
-
-    def hide(item):
+        part = mixed[c : c + step]
+        if outside and c == 0:
+            part = jnp.concatenate([ends[RIM : RIM + edge], part[edge:]], axis=0)
+        if outside and c + step == atoms:
+            at = ends.shape[0] - RIM - edge
+            part = jnp.concatenate([part[: step - edge], ends[at : at + edge]], axis=0)
+        return c, (feat[sample, c : c + step].astype(F32) + dot(part, wo[...])).astype(BF16)
+
+    def hide_below(item):
         c, out = item
         return c, jnp.maximum(dot(out, agg[...]), 0.0).astype(BF16)
 
@@ -251,24 +294,28 @@
         part = dot(onehot.astype(BF16), hidden), jnp.sum(onehot, -1, keepdims=True)
         sums[:] = [a + b for a, b in zip(sums, part)] if sums else part
 
-    skewed(range(0, atoms, step), [finish, hide, add])
+    chunks = list(range(0, atoms, step))
+    skewed(chunks[1:-1] + [chunks[0], chunks[-1]], [finish, hide_below, add])
     tin = sums[0] / sums[1]
     token_in[...] = tin
     token_norm[...] = (layer_norm(tin) * gain[...].reshape(1, -1)).astype(BF16)
 
 
-def gather_tokens(sample, mixed, feat, token, wo, agg, gain, rows):
+def gather_tokens(sample, mixed, feat, token, wo, agg, gain, outside, rows):
     width = agg.shape[1]
+    chans = feat.shape[2]
+    reach = 2 * (KWIN + QWIN)
     vmem = pl.BlockSpec(memory_space=pltpu.VMEM)
     return pl.pallas_call(
         functools.partial(gather_kernel, sample),
         out_shape=[jax.ShapeDtypeStruct((rows, width), F32), jax.ShapeDtypeStruct((rows, width), BF16)],
-        in_specs=[vmem] * 6,
+        in_specs=[vmem] * (6 + len(outside)),
         out_specs=[vmem, vmem],
+        scratch_shapes=[pltpu.VMEM((reach, chans), BF16)] * 4,
         compiler_params=pltpu.CompilerParams(vmem_limit_bytes=16 * MIB),
         cost_estimate=cost(1),
         name="gather_tokens",
-    )(mixed, feat, token, wo, agg, gain)
+    )(mixed, feat, token, wo, agg, gain, *outside)
 
 
 def turn_kernel(orders, row_bits, *refs):
@@ -456,7 +503,8 @@
     got = swap(bias, "sample", bits[0])
     norms, inputs = [], []
     for s in range(samples):
-        mixed = atom_attention(s, atom_feat, inner, outer, atom_wq, atom_wk, atom_wv)
+        halo = (inner, outer)
+        mixed = atom_attention(s, atom_feat, halo if s else (), atom_wq, atom_wk, atom_wv)
         if s:
             norms[-1] = widen(norms[-1], "row", row_bits[0], mixed)
             if s == 1:
@@ -464,7 +512,10 @@
                     held = [widen(h, "sample", order[i], mixed) for h, order in zip(held, orders)]
                 mixed = after(mixed, held)
             mixed = after(mixed, norms[-1])
-        token_in, token_norm = gather_tokens(s, mixed, atom_feat, atom_token, atom_wo, agg_weight, token_gain, rows)
+        outside = () if s else (*halo, atom_wq, atom_wk, atom_wv)
+        token_in, token_norm = gather_tokens(
+            s, mixed, atom_feat, atom_token, atom_wo, agg_weight, token_gain, outside, rows
+        )
         inputs.append(token_in)
         norms.append(token_norm[None])
         if s == 0:

time: 37.4 us -> 35.9 us (0.960)
  waiting for transfers between devices: 4.81 us -> 2.55 us
  Pallas kernels: 18.8 us -> 19.7 us
    ppermute x1, waiting for transfers between devices: 1.83 us -> 0.01 us  [shards(): lax.ppermute(outer, 'row', odd_pairs + [(j, i) for i, j in odd_pairs])]
    pallas_call x2, Pallas kernels: 2.82 us -> 3.49 us  [gather_tokens(): pl.pallas_call(functools.partial(gather_kernel, sample), out_shape=[jax.S...]
    ppermute x10, waiting for transfers between devices: 2.98 us -> 2.54 us  [swap(): lax.ppermute(held, axis, [(i, i ^ far) for i in range(lax.axis_size(axis))])]
  transfers between devices with their start and end apart: 11 -> 11, of which waited for: 5 -> 4; matrix products, arithmetic and copies ran while one was open for 0% -> 0% of each run, Pallas kernels for 33% -> 37%
where the time goes in v8:
time: 35.9 us; the launch traced here: 35.8 us
  Pallas kernels  19.7 us (55%)
  starting transfers between devices  13.1 us (36%)
  waiting for transfers between devices  2.55 us (7%)
    ppermute x10, starting transfers between devices, swap(): lax.ppermute(held, axis, [(i, i ^ far) for i in range(lax.axis_size(axis))])  11.4 us
    pallas_call x2, Pallas kernels, attend(): pl.pallas_call(attend_kernel, out_shape=jax.ShapeDtypeStruct(shape, BF16)...  5.31 us
    pallas_call x2, Pallas kernels, atom_attention(): pl.pallas_call(functools.partial(atom_kernel, sample), out_shape=jax.Shap...  4.73 us
    pallas_call x1, Pallas kernels, pair_bias(): pl.pallas_call(bias_kernel, grid=(1,), out_shape=[jax.ShapeDtypeStruct((c...  3.57 us
    pallas_call x2, Pallas kernels, gather_tokens(): pl.pallas_call(functools.partial(gather_kernel, sample), out_shape=[jax.S...  3.49 us
    ppermute x10, waiting for transfers between devices, swap(): lax.ppermute(held, axis, [(i, i ^ far) for i in range(lax.axis_size(axis))])  2.54 us
    pallas_call x2, Pallas kernels, project(): pl.pallas_call(project_kernel, out_shape=[jax.ShapeDtypeStruct((rows, wid...  1.86 us
    ppermute x1, starting transfers between devices, shards(): lax.ppermute(outer, 'row', odd_pairs + [(j, i) for i, j in odd_pairs])  1.63 us
  transfers between devices with their start and end apart: 11, of which 4 were waited for; matrix products, arithmetic and copies ran while one was open for 0% of the time, Pallas kernels for 37%

profile of v8, /device:TPU:0, one launch (start us, length us, event | category | flops | bytes accessed | tf_op | source)
XLA Modules:
  0.0 35.8 jit_solution(130587863873290692)
XLA Ops:
  0.0 3.6 %pair_bias.1 = (bf16[36,1152]{1,0:T(8,128)(2,1)}, bf16[2,48,128]{2,1,0:T(8,128)(2,1)}, bf16[2,48,128]{2,1,0:T(8,128)(2,1)}) custom-call(bf16[2,1152,128]{2,1,0:T(8,128)(2,1)} %feat.7, bf16[2,1152,128]{2,1,0:T(8,128)(2,1)} %feat.7, bf16[36,72,128]{2,1,0:T(8,128)(2,1)} %bitcast.16, s32[36]{0:T(128)} %mask.1, bf16[16,128]{1,0:T(8,128)(2,1)} %bitcast.17), custom_call_target="tpu_custom_call" | custom-call | flops 60000000 | bytes 1000 | tf_op jit(solution)/shard_map/pair_bias/pallas_call | solution.py:102
  3.6 4.0 %collective-permute-start.1 = (bf16[36,1152]{1,0:T(8,128)(2,1)}, bf16[36,1152]{1,0:T(8,128)(2,1)S(1)}, u32[]{:S(2)}, u32[]{:S(2)}) collective-permute-start(bf16[36,1152]{1,0:T(8,128)(2,1)} %get-tuple-element.37), channel_id=1, source_target_pairs={{0,4},{1,5},{2,6},{3,7},{4,0},{5,1},{6,2},{7,3},{8,12},{9,13},{10,... | collective-permute-start | bytes 248840 | tf_op jit(solution)/shard_map/ppermute | solution.py:130
  7.7 0.0 collective-permute-start
  7.7 1.6 %collective-permute-start.2 = (bf16[2,48,128]{2,1,0:T(8,128)(2,1)}, bf16[2,48,128]{2,1,0:T(8,128)(2,1)S(1)}, u32[]{:S(2)}, u32[]{:S(2)}) collective-permute-start(bf16[2,48,128]{2,1,0:T(8,128)(2,1)} %get-tuple-element.35), channel_id=1, source_target_pairs={{8,16},{24,0},{16,8},{0,24},{9,17},{25,1},{17,9},{1,25},{10,18},{2... | collective-permute-start | bytes 73736 | tf_op jit(solution)/shard_map/ppermute | solution.py:495
  9.3 0.0 copy-start.5
  9.3 2.5 %atom_attention.2.mixed = bf16[1152,128]{1,0:T(8,128)(2,1)S(1)} custom-call(bf16[2,1152,128]{2,1,0:T(8,128)(2,1)S(1)} %copy-done, bf16[128,128]{1,0:T(8,128)(2,1)S(1)} %copy-done.7, bf16[128,128]{1,0:T(8,128)(2,1)S(1)} %copy-done.8, bf16[128,128]{1,0:T(8,128)(2,1)S(1)} %copy-done.9), custom_call_target="tpu_custom_call" | custom-call | flops 80000000 | bytes 1000 | tf_op jit(solution)/shard_map/atom_attention/pallas_call | solution.py:239
  11.8 0.0 collective-permute-done.refs_0_
  11.8 0.0 collective-permute-done.2.refs_1_
  11.9 0.0 copy-start.4
  11.9 2.1 %gather_tokens.2 = (f32[72,768]{1,0:T(8,128)S(1)}, bf16[72,768]{1,0:T(8,128)(2,1)S(1)}) custom-call(bf16[1152,128]{1,0:T(8,128)(2,1)S(1)} %atom_attention.2.mixed, bf16[2,1152,128]{2,1,0:T(8,128)(2,1)S(1)} %copy-done, s32[1152]{0:T(1024)S(1)} %copy-done.11, bf16[128,128]{1,0:T(8,128)(2,1)S(1)} %copy-done.10, bf16[128,768]{1,0:T(8,128)(2,1)S(1)} %copy-done.6, ...), custom_call_target="tpu_custom_call" | custom-call | flops 20000000 | bytes 1000 | tf_op jit(solution)/shard_map/gather_tokens/pallas_call | solution.py:309
  14.0 0.9 %collective-permute-start.5 = (bf16[1,72,768]{2,1,0:T(8,128)(2,1)S(1)}, bf16[1,72,768]{2,1,0:T(8,128)(2,1)S(1)}, u32[]{:S(2)}, u32[]{:S(2)}) collective-permute-start(bf16[1,72,768]{2,1,0:T(8,128)(2,1)S(1)} %bitcast.14), channel_id=1, source_target_pairs={{0,16},{8,24},{16,0},{24,8},{1,17},{9,25},{17,1},{25,9},{2,18},{10... | collective-permute-start | bytes 331784 | tf_op jit(solution)/shard_map/ppermute | solution.py:130
  14.9 1.5 %collective-permute-start.4 = (bf16[2,36,512]{2,1,0:T(8,128)(2,1)S(1)}, bf16[2,36,512]{2,1,0:T(8,128)(2,1)S(1)}, u32[]{:S(2)}, u32[]{:S(2)}) collective-permute-start(bf16[2,36,512]{2,1,0:T(8,128)(2,1)S(1)} %pad_maximum_fusion.5), channel_id=1, source_target_pairs={{0,1},{1,0},{2,3},{3,2},{4,5},{5,4},{6,7},{7,6},{8,9},{9,8},{10,11... | collective-permute-start | bytes 221192 | tf_op jit(solution)/shard_map/ppermute | solution.py:130
  16.5 1.6 %collective-permute-start.3 = (bf16[2,36,640]{2,1,0:T(8,128)(2,1)S(1)}, bf16[2,36,640]{2,1,0:T(8,128)(2,1)S(1)}, u32[]{:S(2)}, u32[]{:S(2)}) collective-permute-start(bf16[2,36,640]{2,1,0:T(8,128)(2,1)S(1)} %pad_maximum_fusion.4), channel_id=1, source_target_pairs={{0,2},{1,3},{2,0},{3,1},{4,6},{5,7},{6,4},{7,5},{8,10},{9,11},{10,... | collective-permute-start | bytes 276488 | tf_op jit(solution)/shard_map/ppermute | solution.py:130
  18.1 2.3 %atom_attention.3.mixed = bf16[1152,128]{1,0:T(8,128)(2,1)S(1)} custom-call(bf16[2,1152,128]{2,1,0:T(8,128)(2,1)S(1)} %copy-done, bf16[2,48,128]{2,1,0:T(8,128)(2,1)S(1)} %collective-permute-done.refs_0_, bf16[2,48,128]{2,1,0:T(8,128)(2,1)S(1)} %collective-permute-done.2.refs_1_, bf16[128,128]{1,0:T(8,128)(2,1)S(1)} %copy-done.7, ...), custom_call_target="tpu_custom_call" | custom-call | flops 80000000 | bytes 1000 | tf_op jit(solution)/shard_map/atom_attention/pallas_call | solution.py:239
  20.4 0.0 copy-start.1
  20.5 0.1 collective-permute-start.7
  20.5 0.0 collective-permute-done.4
  20.6 1.0 %collective-permute-done.3 = bf16[2,36,640]{2,1,0:T(8,128)(2,1)S(1)} collective-permute-done((bf16[2,36,640]{2,1,0:T(8,128)(2,1)S(1)}, bf16[2,36,640]{2,1,0:T(8,128)(2,1)S(1)}, u32[]{:S(2)}, u32[]{:S(2)}) %collective-permute-start.3) | collective-permute-done | bytes 92192 | tf_op jit(solution)/shard_map/ppermute | solution.py:130
  21.6 0.6 %collective-permute-start.8 = (bf16[4,36,640]{2,1,0:T(8,128)(2,1)S(1)}, bf16[4,36,640]{2,1,0:T(8,128)(2,1)S(1)}, u32[]{:S(2)}, u32[]{:S(2)}) collective-permute-start(bf16[4,36,640]{2,1,0:T(8,128)(2,1)S(1)} %pad_maximum_fusion.2.refs_0_), channel_id=1, source_target_pairs={{0,1},{1,0},{2,3},{3,2},{4,5},{5,4},{6,7},{7,6},{8,9},{9,8},{10,11... | collective-permute-start | bytes 552968 | tf_op jit(solution)/shard_map/ppermute | solution.py:130
  22.3 1.3 %collective-permute-start.9 = (bf16[4,36,512]{2,1,0:T(8,128)(2,1)S(1)}, bf16[4,36,512]{2,1,0:T(8,128)(2,1)S(1)}, u32[]{:S(2)}, u32[]{:S(2)}) collective-permute-start(bf16[4,36,512]{2,1,0:T(8,128)(2,1)S(1)} %pad_maximum_fusion.3.refs_2_), channel_id=1, source_target_pairs={{0,2},{1,3},{2,0},{3,1},{4,6},{5,7},{6,4},{7,5},{8,10},{9,11},{10,... | collective-permute-start | bytes 442376 | tf_op jit(solution)/shard_map/ppermute | solution.py:130
  23.6 1.4 %gather_tokens.3 = (f32[72,768]{1,0:T(8,128)S(1)}, bf16[72,768]{1,0:T(8,128)(2,1)S(1)}) custom-call(bf16[1152,128]{1,0:T(8,128)(2,1)S(1)} %atom_attention.3.mixed, bf16[2,1152,128]{2,1,0:T(8,128)(2,1)S(1)} %copy-done, s32[1152]{0:T(1024)S(1)} %copy-done.11, bf16[128,128]{1,0:T(8,128)(2,1)S(1)} %copy-done.10, bf16[128,768]{1,0:T(8,128)(2,1)S(1)} %copy-done.6, ...), custom_call_target="tpu_custom_call" | custom-call | flops 20000000 | bytes 1000 | tf_op jit(solution)/shard_map/gather_tokens/pallas_call | solution.py:309
  25.0 1.2 %collective-permute-start.6 = (bf16[1,72,768]{2,1,0:T(8,128)(2,1)S(1)}, bf16[1,72,768]{2,1,0:T(8,128)(2,1)S(1)}, u32[]{:S(2)}, u32[]{:S(2)}) collective-permute-start(bf16[1,72,768]{2,1,0:T(8,128)(2,1)S(1)} %bitcast.12), channel_id=1, source_target_pairs={{0,16},{8,24},{16,0},{24,8},{1,17},{9,25},{17,1},{25,9},{2,18},{10... | collective-permute-start | bytes 331784 | tf_op jit(solution)/shard_map/ppermute | solution.py:130
  26.2 0.9 %project.2 = (bf16[72,768]{1,0:T(8,128)(2,1)S(1)}, bf16[144,768]{1,0:T(8,128)(2,1)S(1)}, bf16[144,768]{1,0:T(8,128)(2,1)S(1)}, f32[72,768]{1,0:T(8,128)S(1)}) custom-call(bf16[2,72,768]{2,1,0:T(8,128)(2,1)S(1)} %pad_maximum_fusion.near, bf16[768,768]{1,0:T(8,128)(2,1)S(1)} %copy-done.4, bf16[768,768]{1,0:T(8,128)(2,1)S(1)} %copy-done.1, ...), custom_call_target="tpu_custom_call" | custom-call | flops 40000000 | bytes 1000 | tf_op jit(solution)/shard_map/project/pallas_call | solution.py:383
  27.2 0.5 %collective-permute-done.9.refs_3_ = bf16[4,36,512]{2,1,0:T(8,128)(2,1)S(1)} collective-permute-done((bf16[4,36,512]{2,1,0:T(8,128)(2,1)S(1)}, bf16[4,36,512]{2,1,0:T(8,128)(2,1)S(1)}, u32[]{:S(2)}, u32[]{:S(2)}) %collective-permute-start.9) | collective-permute-done | bytes 147488 | tf_op jit(solution)/shard_map/ppermute | solution.py:130
  27.6 0.5 %collective-permute-done.8.refs_1_ = bf16[4,36,640]{2,1,0:T(8,128)(2,1)S(1)} collective-permute-done((bf16[4,36,640]{2,1,0:T(8,128)(2,1)S(1)}, bf16[4,36,640]{2,1,0:T(8,128)(2,1)S(1)}, u32[]{:S(2)}, u32[]{:S(2)}) %collective-permute-start.8) | collective-permute-done | bytes 184352 | tf_op jit(solution)/shard_map/ppermute | solution.py:130
  28.1 0.7 %turn_bias.1.bias = f32[1152,288]{1,0:T(8,128)S(1)} custom-call(bf16[4,36,640]{2,1,0:T(8,128)(2,1)S(1)} %pad_maximum_fusion.2.refs_0_, bf16[4,36,640]{2,1,0:T(8,128)(2,1)S(1)} %collective-permute-done.8.refs_1_, bf16[4,36,512]{2,1,0:T(8,128)(2,1)S(1)} %pad_maximum_fusion.3.refs_2_, bf16[4,36,512]{2,1,0:T(8,128)(2,1)S(1)} %collective-permute-done.9.refs_3_), custom_call_target="tpu_custom_call" | custom-call | flops 20000000 | bytes 1000 | tf_op jit(solution)/shard_map/turn_bias/pallas_call | solution.py:347
  28.9 0.0 collective-permute-done.7.far
  28.9 2.4 %attend.2.rest_0_ = bf16[72,768]{1,0:T(8,128)(2,1)S(1)} custom-call(bf16[2,72,768]{2,1,0:T(8,128)(2,1)S(1)} %collective-permute-done.7.far, bf16[72,768]{1,0:T(8,128)(2,1)S(1)} %get-tuple-element.46.q, bf16[144,768]{1,0:T(8,128)(2,1)S(1)} %get-tuple-element.47.k_near, bf16[144,768]{1,0:T(8,128)(2,1)S(1)} %get-tuple-element.48.v_near, ...), custom_call_target="tpu_custom_call" | custom-call | flops 60000000 | bytes 1000 | tf_op jit(solution)/shard_map/attend/pallas_call | solution.py:459
  31.3 0.1 collective-permute-start.10
  31.4 0.9 %project.3 = (bf16[72,768]{1,0:T(8,128)(2,1)S(1)}, bf16[144,768]{1,0:T(8,128)(2,1)S(1)}, bf16[144,768]{1,0:T(8,128)(2,1)S(1)}, f32[72,768]{1,0:T(8,128)S(1)}) custom-call(bf16[2,72,768]{2,1,0:T(8,128)(2,1)S(1)} %pad_maximum_fusion.1.near, bf16[768,768]{1,0:T(8,128)(2,1)S(1)} %copy-done.4, bf16[768,768]{1,0:T(8,128)(2,1)S(1)} %copy-done.1, ...), custom_call_target="tpu_custom_call" | custom-call | flops 40000000 | bytes 1000 | tf_op jit(solution)/shard_map/project/pallas_call | solution.py:383
  32.4 0.5 %collective-permute-done.10.far = bf16[2,72,768]{2,1,0:T(8,128)(2,1)S(1)} collective-permute-done((bf16[2,72,768]{2,1,0:T(8,128)(2,1)S(1)}, bf16[2,72,768]{2,1,0:T(8,128)(2,1)S(1)}, u32[]{:S(2)}, u32[]{:S(2)}) %collective-permute-start.10) | collective-permute-done | bytes 221216 | tf_op jit(solution)/shard_map/ppermute | solution.py:130
  32.9 2.9 %attend.3 = bf16[2,72,768]{2,1,0:T(8,128)(2,1)} custom-call(bf16[2,72,768]{2,1,0:T(8,128)(2,1)S(1)} %collective-permute-done.10.far, bf16[72,768]{1,0:T(8,128)(2,1)S(1)} %get-tuple-element.56.q, bf16[144,768]{1,0:T(8,128)(2,1)S(1)} %get-tuple-element.57.k_near, bf16[144,768]{1,0:T(8,128)(2,1)S(1)} %get-tuple-element.58.v_near, ...), custom_call_target="tpu_custom_call" | custom-call | flops 60000000 | bytes 1000 | tf_op jit(solution)/shard_map/attend/pallas_call | solution.py:459
  (36 shorter events, 0.2 us)
Async XLA Ops:
  0.0 9.3 %copy-start = (bf16[2,1152,128]{2,1,0:T(8,128)(2,1)S(1)}, bf16[2,1152,128]{2,1,0:T(8,128)(2,1)}, u32[]{:S(2)}) copy-start(bf16[2,1152,128]{2,1,0:T(8,128)(2,1)} %feat.7) | copy-start | bytes 1769476
  0.0 9.3 %copy-start.7 = (bf16[128,128]{1,0:T(8,128)(2,1)S(1)}, bf16[128,128]{1,0:T(8,128)(2,1)}, u32[]{:S(2)}) copy-start(bf16[128,128]{1,0:T(8,128)(2,1)} %refs_2_.5) | copy-start | bytes 98308
  0.0 9.3 %copy-start.8 = (bf16[128,128]{1,0:T(8,128)(2,1)S(1)}, bf16[128,128]{1,0:T(8,128)(2,1)}, u32[]{:S(2)}) copy-start(bf16[128,128]{1,0:T(8,128)(2,1)} %refs_3_.3) | copy-start | bytes 98308
  0.0 9.3 %copy-start.9 = (bf16[128,128]{1,0:T(8,128)(2,1)S(1)}, bf16[128,128]{1,0:T(8,128)(2,1)}, u32[]{:S(2)}) copy-start(bf16[128,128]{1,0:T(8,128)(2,1)} %refs_4_.3) | copy-start | bytes 98308
  0.0 11.8 %copy-start.6 = (bf16[128,768]{1,0:T(8,128)(2,1)S(1)}, bf16[128,768]{1,0:T(8,128)(2,1)}, u32[]{:S(2)}) copy-start(bf16[128,768]{1,0:T(8,128)(2,1)} %agg.3) | copy-start | bytes 589828
  0.0 11.8 %copy-start.10 = (bf16[128,128]{1,0:T(8,128)(2,1)S(1)}, bf16[128,128]{1,0:T(8,128)(2,1)}, u32[]{:S(2)}) copy-start(bf16[128,128]{1,0:T(8,128)(2,1)} %wo.7) | copy-start | bytes 98308
  0.0 11.8 %copy-start.11 = (s32[1152]{0:T(1024)S(1)}, s32[1152]{0:T(1024)}, u32[]{:S(2)}) copy-start(s32[1152]{0:T(1024)} %token_.3) | copy-start | bytes 13828
  0.0 11.8 %copy-start.12 = (f32[768]{0:T(1024)S(1)}, f32[768]{0:T(1024)}, u32[]{:S(2)}) copy-start(f32[768]{0:T(1024)} %gain.3) | copy-start | bytes 9220
  3.6 11.3 %copy-start.13 = (bf16[36,1152]{1,0:T(8,128)(2,1)S(1)}, bf16[36,1152]{1,0:T(8,128)(2,1)}, u32[]{:S(2)}) copy-start(bf16[36,1152]{1,0:T(8,128)(2,1)} %get-tuple-element.37) | copy-start | bytes 248836
  3.6 11.2 %collective-permute-start.1 = (bf16[36,1152]{1,0:T(8,128)(2,1)}, bf16[36,1152]{1,0:T(8,128)(2,1)S(1)}, u32[]{:S(2)}, u32[]{:S(2)}) collective-permute-start(bf16[36,1152]{1,0:T(8,128)(2,1)} %get-tuple-element.37), channel_id=1, source_target_pairs={{0,4},{1,5},{2,6},{3,7},{4,0},{5,1},{6,2},{7,3},{8,12},{9,13},{10,... | collective-permute-start | bytes 248840 | tf_op jit(solution)/shard_map/ppermute | solution.py:130
  7.7 4.1 %collective-permute-start = (bf16[2,48,128]{2,1,0:T(8,128)(2,1)}, bf16[2,48,128]{2,1,0:T(8,128)(2,1)S(1)}, u32[]{:S(2)}, u32[]{:S(2)}) collective-permute-start(bf16[2,48,128]{2,1,0:T(8,128)(2,1)} %get-tuple-element.33), channel_id=1, source_target_pairs={{0,8},{8,0},{16,24},{24,16},{1,9},{9,1},{17,25},{25,17},{2,10},{10... | collective-permute-start | bytes 73736 | tf_op jit(solution)/shard_map/ppermute | solution.py:130
  7.7 4.1 %collective-permute-start.2 = (bf16[2,48,128]{2,1,0:T(8,128)(2,1)}, bf16[2,48,128]{2,1,0:T(8,128)(2,1)S(1)}, u32[]{:S(2)}, u32[]{:S(2)}) collective-permute-start(bf16[2,48,128]{2,1,0:T(8,128)(2,1)} %get-tuple-element.35), channel_id=1, source_target_pairs={{8,16},{24,0},{16,8},{0,24},{9,17},{25,1},{17,9},{1,25},{10,18},{2... | collective-permute-start | bytes 73736 | tf_op jit(solution)/shard_map/ppermute | solution.py:495
  9.3 16.9 %copy-start.5 = (bf16[768,768]{1,0:T(8,128)(2,1)S(1)}, bf16[768,768]{1,0:T(8,128)(2,1)}, u32[]{:S(2)}) copy-start(bf16[768,768]{1,0:T(8,128)(2,1)} %wg.3) | copy-start | bytes 3538948
  11.9 14.3 %copy-start.4 = (bf16[768,768]{1,0:T(8,128)(2,1)S(1)}, bf16[768,768]{1,0:T(8,128)(2,1)}, u32[]{:S(2)}) copy-start(bf16[768,768]{1,0:T(8,128)(2,1)} %wq.3) | copy-start | bytes 3538948
  14.0 6.5 %collective-permute-start.5 = (bf16[1,72,768]{2,1,0:T(8,128)(2,1)S(1)}, bf16[1,72,768]{2,1,0:T(8,128)(2,1)S(1)}, u32[]{:S(2)}, u32[]{:S(2)}) collective-permute-start(bf16[1,72,768]{2,1,0:T(8,128)(2,1)S(1)} %bitcast.14), channel_id=1, source_target_pairs={{0,16},{8,24},{16,0},{24,8},{1,17},{9,25},{17,1},{25,9},{2,18},{10... | collective-permute-start | bytes 331784 | tf_op jit(solution)/shard_map/ppermute | solution.py:130
  14.9 5.6 %collective-permute-start.4 = (bf16[2,36,512]{2,1,0:T(8,128)(2,1)S(1)}, bf16[2,36,512]{2,1,0:T(8,128)(2,1)S(1)}, u32[]{:S(2)}, u32[]{:S(2)}) collective-permute-start(bf16[2,36,512]{2,1,0:T(8,128)(2,1)S(1)} %pad_maximum_fusion.5), channel_id=1, source_target_pairs={{0,1},{1,0},{2,3},{3,2},{4,5},{5,4},{6,7},{7,6},{8,9},{9,8},{10,11... | collective-permute-start | bytes 221192 | tf_op jit(solution)/shard_map/ppermute | solution.py:130
  16.5 9.7 %copy-start.3 = (bf16[768,768]{1,0:T(8,128)(2,1)S(1)}, bf16[768,768]{1,0:T(8,128)(2,1)}, u32[]{:S(2)}) copy-start(bf16[768,768]{1,0:T(8,128)(2,1)} %wo.11) | copy-start | bytes 3538948
  16.5 5.1 %collective-permute-start.3 = (bf16[2,36,640]{2,1,0:T(8,128)(2,1)S(1)}, bf16[2,36,640]{2,1,0:T(8,128)(2,1)S(1)}, u32[]{:S(2)}, u32[]{:S(2)}) collective-permute-start(bf16[2,36,640]{2,1,0:T(8,128)(2,1)S(1)} %pad_maximum_fusion.4), channel_id=1, source_target_pairs={{0,2},{1,3},{2,0},{3,1},{4,6},{5,7},{6,4},{7,5},{8,10},{9,11},{10,... | collective-permute-start | bytes 276488 | tf_op jit(solution)/shard_map/ppermute | solution.py:130
  18.1 8.1 %copy-start.2 = (bf16[768,768]{1,0:T(8,128)(2,1)S(1)}, bf16[768,768]{1,0:T(8,128)(2,1)}, u32[]{:S(2)}) copy-start(bf16[768,768]{1,0:T(8,128)(2,1)} %wv.7) | copy-start | bytes 3538948
  20.4 5.8 %copy-start.1 = (bf16[768,768]{1,0:T(8,128)(2,1)S(1)}, bf16[768,768]{1,0:T(8,128)(2,1)}, u32[]{:S(2)}) copy-start(bf16[768,768]{1,0:T(8,128)(2,1)} %wk.7) | copy-start | bytes 3538948
  20.5 8.4 %collective-permute-start.7 = (bf16[2,72,768]{2,1,0:T(8,128)(2,1)S(1)}, bf16[2,72,768]{2,1,0:T(8,128)(2,1)S(1)}, u32[]{:S(2)}, u32[]{:S(2)}) collective-permute-start(bf16[2,72,768]{2,1,0:T(8,128)(2,1)S(1)} %pad_maximum_fusion.near), channel_id=1, source_target_pairs={{0,8},{8,0},{16,24},{24,16},{1,9},{9,1},{17,25},{25,17},{2,10},{10... | collective-permute-start | bytes 663560 | tf_op jit(solution)/shard_map/ppermute | solution.py:130
  21.6 6.5 %collective-permute-start.8 = (bf16[4,36,640]{2,1,0:T(8,128)(2,1)S(1)}, bf16[4,36,640]{2,1,0:T(8,128)(2,1)S(1)}, u32[]{:S(2)}, u32[]{:S(2)}) collective-permute-start(bf16[4,36,640]{2,1,0:T(8,128)(2,1)S(1)} %pad_maximum_fusion.2.refs_0_), channel_id=1, source_target_pairs={{0,1},{1,0},{2,3},{3,2},{4,5},{5,4},{6,7},{7,6},{8,9},{9,8},{10,11... | collective-permute-start | bytes 552968 | tf_op jit(solution)/shard_map/ppermute | solution.py:130
  22.3 5.4 %collective-permute-start.9 = (bf16[4,36,512]{2,1,0:T(8,128)(2,1)S(1)}, bf16[4,36,512]{2,1,0:T(8,128)(2,1)S(1)}, u32[]{:S(2)}, u32[]{:S(2)}) collective-permute-start(bf16[4,36,512]{2,1,0:T(8,128)(2,1)S(1)} %pad_maximum_fusion.3.refs_2_), channel_id=1, source_target_pairs={{0,2},{1,3},{2,0},{3,1},{4,6},{5,7},{6,4},{7,5},{8,10},{9,11},{10,... | collective-permute-start | bytes 442376 | tf_op jit(solution)/shard_map/ppermute | solution.py:130
  25.0 6.3 %collective-permute-start.6 = (bf16[1,72,768]{2,1,0:T(8,128)(2,1)S(1)}, bf16[1,72,768]{2,1,0:T(8,128)(2,1)S(1)}, u32[]{:S(2)}, u32[]{:S(2)}) collective-permute-start(bf16[1,72,768]{2,1,0:T(8,128)(2,1)S(1)} %bitcast.12), channel_id=1, source_target_pairs={{0,16},{8,24},{16,0},{24,8},{1,17},{9,25},{17,1},{25,9},{2,18},{10... | collective-permute-start | bytes 331784 | tf_op jit(solution)/shard_map/ppermute | solution.py:130
  31.3 1.5 %collective-permute-start.10 = (bf16[2,72,768]{2,1,0:T(8,128)(2,1)S(1)}, bf16[2,72,768]{2,1,0:T(8,128)(2,1)S(1)}, u32[]{:S(2)}, u32[]{:S(2)}) collective-permute-start(bf16[2,72,768]{2,1,0:T(8,128)(2,1)S(1)} %pad_maximum_fusion.1.near), channel_id=1, source_target_pairs={{0,8},{8,0},{16,24},{24,16},{1,9},{9,1},{17,25},{25,17},{2,10},{10... | collective-permute-start | bytes 663560 | tf_op jit(solution)/shard_map/ppermute | solution.py:130

commit v9 on v8

--- a/solution.py
+++ b/solution.py
@@ -228,7 +228,7 @@
     starts = list(range(0, atoms, QWIN))
     if not halo:
         starts = [at for at in starts if RIM <= at <= atoms + RIM - KWIN]
-    batch = 8 if len(starts) % 8 == 0 else 6
+    batch = 6
     batches = [starts[i : i + batch] for i in range(0, len(starts), batch)]
     windows_attend(batches, qs, ks, vs, mixed, 0, hide_outside(atoms))
 
@@ -318,6 +318,52 @@
     )(mixed, feat, token, wo, agg, gain, *outside)
 
 
+def head_groups(width):
+    groups = []
+    for base in range(0, width, 8 * HEAD_DIM):
+        first = base // HEAD_DIM
+        groups.append((base, range(first, first + 5)))
+        groups.append((base + LANES, range(first + 5, first + 8)))
+    return groups
+
+
+def stack(blocks):
+    return jnp.concatenate([blocks[j].astype(F32) for j in range(blocks.shape[0])], axis=0).astype(BF16)
+
+
+def project_kernel(near, *refs):
+    *far, wq, wk, wv, wg, wo, q, k, v, gate = refs
+    x = jnp.concatenate([stack(blocks) for blocks in (near, *far)], axis=0)
+    q[...] = dot(near[0], wq[...]).astype(BF16)
+    gate[...] = jax.nn.sigmoid(dot(near[0], wg[...]))
+    if far:
+        for c in range(0, x.shape[1], 2 * LANES):
+            k[c : c + 2 * LANES] = dot(x, wk[:, c : c + 2 * LANES]).T.astype(BF16)
+    else:
+        k[...] = dot(x, wk[...]).astype(BF16)
+    v[...] = dot(x, wv[...]).astype(BF16)
+
+
+def project(blocks, wq, wk, wv, wg, wo):
+    half, rows, width = blocks[0].shape
+    keys = len(blocks) * half * rows
+    vmem = pl.BlockSpec(memory_space=pltpu.VMEM)
+    return pl.pallas_call(
+        project_kernel,
+        out_shape=[
+            jax.ShapeDtypeStruct((rows, width), BF16),
+            jax.ShapeDtypeStruct((width, keys) if len(blocks) > 1 else (keys, width), BF16),
+            jax.ShapeDtypeStruct((keys, width), BF16),
+            jax.ShapeDtypeStruct((rows, width), F32),
+        ],
+        in_specs=[vmem] * (5 + len(blocks)),
+        out_specs=[vmem] * 4,
+        compiler_params=pltpu.CompilerParams(vmem_limit_bytes=24 * MIB),
+        cost_estimate=cost(2),
+        name="project",
+    )(*blocks, wq, wk, wv, wg, wo)
+
+
 def turn_kernel(orders, row_bits, *refs):
     *halves, out, tall = refs
     rows = out.shape[0] // HEADS
@@ -356,49 +402,11 @@
     )(*halves)
 
 
-def head_groups(width):
-    groups = []
-    for base in range(0, width, 8 * HEAD_DIM):
-        first = base // HEAD_DIM
-        groups.append((base, range(first, first + 5)))
-        groups.append((base + LANES, range(first + 5, first + 8)))
-    return groups
-
-
-def stack(blocks):
-    return jnp.concatenate([blocks[j].astype(F32) for j in range(blocks.shape[0])], axis=0).astype(BF16)
-
-
-def project_kernel(near, wq, wk, wv, wg, wo, q, k, v, gate):
-    x = stack(near)
-    q[...] = dot(near[0], wq[...]).astype(BF16)
-    gate[...] = jax.nn.sigmoid(dot(near[0], wg[...]))
-    k[...] = dot(x, wk[...]).astype(BF16)
-    v[...] = dot(x, wv[...]).astype(BF16)
-
-
-def project(near, wq, wk, wv, wg, wo):
-    half, rows, width = near.shape
-    vmem = pl.BlockSpec(memory_space=pltpu.VMEM)
-    return pl.pallas_call(
-        project_kernel,
-        out_shape=[
-            jax.ShapeDtypeStruct((rows, width), BF16),
-            jax.ShapeDtypeStruct((half * rows, width), BF16),
-            jax.ShapeDtypeStruct((half * rows, width), BF16),
-            jax.ShapeDtypeStruct((rows, width), F32),
-        ],
-        in_specs=[vmem] * 6,
-        out_specs=[vmem] * 4,
-        compiler_params=pltpu.CompilerParams(vmem_limit_bytes=24 * MIB),
-        cost_estimate=cost(2),
-        name="project",
-    )(near, wq, wk, wv, wg, wo)
-
-
-def attend_kernel(far, q, k_near, v_near, gate, token_in, bias, wk, wv, wo, *rest):
-    *earlier, out, kt, v = rest
-    rows, width = token_in.shape
+def attend_kernel(samples, bias, *refs):
+    parts, refs = [refs[5 * s : 5 * s + 5] for s in range(samples)], refs[5 * samples :]
+    far, wk, wv, wo, out, kt, v = refs
+    _, k_near, v_near, _, _ = parts[-1]
+    rows, width = parts[-1][4].shape
     x = stack(far)
     for c in range(0, width, 2 * LANES):
         lanes = slice(c, c + 2 * LANES)
@@ -408,18 +416,24 @@
     v[v_near.shape[0] :] = dot(x, wv[...]).astype(BF16)
     scale = LOG2E / HEAD_DIM**0.5
     lane = iota((rows, 2 * LANES), 1)
-    work = [(base, heads[i : i + 2]) for base, heads in head_groups(width) for i in range(0, len(heads), 2)]
+    work = [
+        (s, base, heads[i : i + 2])
+        for s in range(samples)
+        for base, heads in head_groups(width)
+        for i in range(0, len(heads), 2)
+    ]
 
     def channels(base, h):
         low = h * HEAD_DIM - base
         return (lane >= low) & (lane < low + HEAD_DIM)
 
     def score(item):
-        base, heads = item
+        s, base, heads = item
+        q, keys = parts[s][0], parts[s][1] if s < samples - 1 else kt
         mine = q[:, base : base + 2 * LANES].astype(F32)
         mine = jnp.concatenate([jnp.where(channels(base, h), mine, 0.0) for h in heads], axis=0).astype(BF16)
         some = bias[heads[0] * rows : (heads[-1] + 1) * rows]
-        return item, dot(mine, kt[base : base + 2 * LANES]) * scale + some
+        return item, dot(mine, keys[base : base + 2 * LANES]) * scale + some
 
     def soften(item):
         place, sc = item
@@ -429,43 +443,43 @@
     mixes = {}
 
     def mix(item):
-        (base, heads), e, share = item
-        o = dot(e, v[:, base : base + 2 * LANES]) * share
+        (s, base, heads), e, share = item
+        values = parts[s][2] if s < samples - 1 else v
+        o = dot(e, values[:, base : base + 2 * LANES]) * share
         for i, h in enumerate(heads):
-            mixes[base] = jnp.where(channels(base, h), o[i * rows : (i + 1) * rows], mixes.get(base, 0.0))
+            mixes[s, base] = jnp.where(channels(base, h), o[i * rows : (i + 1) * rows], mixes.get((s, base), 0.0))
+        if h == HEADS - 1:
+            close(s)
+
+    def close(s):
+        tiles = {}
+        for base, _ in head_groups(width):
+            for t in range(2):
+                at = base + t * LANES
+                part = mixes[s, base][:, t * LANES : (t + 1) * LANES]
+                tiles[at] = tiles[at] + part if at in tiles else part
+        gate, token_in = parts[s][3:]
+        gated = jnp.concatenate([tiles[at] for at in range(0, width, LANES)], axis=1) * gate[...]
+        out[s] = (token_in[...] + dot(gated.astype(BF16), wo[...])).astype(BF16)
 
     skewed(work, [score, soften, mix])
-    tiles = {}
-    for base, _ in head_groups(width):
-        for t in range(2):
-            at = base + t * LANES
-            part = mixes[base][:, t * LANES : (t + 1) * LANES]
-            tiles[at] = tiles[at] + part if at in tiles else part
-    gated = jnp.concatenate([tiles[at] for at in range(0, width, LANES)], axis=1) * gate[...]
-    res = (token_in[...] + dot(gated.astype(BF16), wo[...])).astype(BF16)
-    if earlier:
-        for s, ref in enumerate(earlier):
-            out[s] = ref[...]
-        out[len(earlier)] = res
-    else:
-        out[...] = res
-
-
-def attend(far, q, k, v, gate, token_in, bias, wk, wv, wo, earlier):
-    rows, width = token_in.shape
-    keys = 2 * k.shape[0]
+
+
+def attend(bias, parts, far, wk, wv, wo):
+    rows, width = parts[-1][4].shape
+    keys = 2 * parts[-1][1].shape[0]
     vmem = pl.BlockSpec(memory_space=pltpu.VMEM)
-    shape = (len(earlier) + 1, rows, width) if earlier else (rows, width)
+    operands = [bias, *(ref for part in parts for ref in part), far, wk, wv, wo]
     return pl.pallas_call(
-        attend_kernel,
-        out_shape=jax.ShapeDtypeStruct(shape, BF16),
-        in_specs=[vmem] * (10 + len(earlier)),
+        functools.partial(attend_kernel, len(parts)),
+        out_shape=jax.ShapeDtypeStruct((len(parts), rows, width), BF16),
+        in_specs=[vmem] * len(operands),
         out_specs=vmem,
         scratch_shapes=[pltpu.VMEM((width, keys), BF16), pltpu.VMEM((keys, width), BF16)],
-        compiler_params=pltpu.CompilerParams(vmem_limit_bytes=24 * MIB),
+        compiler_params=pltpu.CompilerParams(vmem_limit_bytes=32 * MIB),
         cost_estimate=cost(3),
         name="attend",
-    )(far, q, k, v, gate, token_in, bias, wk, wv, wo, *earlier)
+    )(*operands)
 
 
 def shards(
@@ -505,13 +519,6 @@
     for s in range(samples):
         halo = (inner, outer)
         mixed = atom_attention(s, atom_feat, halo if s else (), atom_wq, atom_wk, atom_wv)
-        if s:
-            norms[-1] = widen(norms[-1], "row", row_bits[0], mixed)
-            if s == 1:
-                for i in range(1, len(bits) - 1):
-                    held = [widen(h, "sample", order[i], mixed) for h, order in zip(held, orders)]
-                mixed = after(mixed, held)
-            mixed = after(mixed, norms[-1])
         outside = () if s else (*halo, atom_wq, atom_wk, atom_wv)
         token_in, token_norm = gather_tokens(
             s, mixed, atom_feat, atom_token, atom_wo, agg_weight, token_gain, outside, rows
@@ -522,21 +529,23 @@
             bias, got, _ = lax.optimization_barrier((bias, got, token_norm))
             held = [jnp.stack([bias[:, lanes], got[:, lanes]]) for lanes in (slice(0, split), slice(split, None))]
             inner = after(inner, held, token_norm)
+    for i in range(1, len(bits) - 1):
+        held = [widen(h, "sample", order[i], token_norm) for h, order in zip(held, orders)]
     halves = []
     for h, order in zip(held, orders):
         halves += [h, swap(h, "sample", order[-1])]
-    done = []
+    parts = []
+    weights = (query_weight, key_weight, value_weight, gate_weight, out_weight)
     for s in range(samples):
         near = norms[s]
-        for bit in row_bits[near.shape[0].bit_length() - 1 : -1]:
-            near = widen(near, "row", bit, *done)
+        for bit in row_bits[:-1]:
+            near = widen(near, "row", bit, mixed, *((parts, halves) if s == samples - 1 else parts))
         far = swap(near, "row", row_bits[-1])
-        part = project(near, query_weight, key_weight, value_weight, gate_weight, out_weight)
-        if s == 0:
-            bias = turn_bias(orders, row_bits, after(halves, part))
-        earlier = done if s == samples - 1 else []
-        done.append(attend(far, *part, inputs[s], bias, key_weight, value_weight, out_weight, earlier))
-    return done[-1]
+        near = after(near, held)
+        blocks = (near, far) if s < samples - 1 else (near,)
+        parts.append((*project(blocks, *weights), inputs[s]))
+    bias = turn_bias(orders, row_bits, after(halves, near))
+    return attend(bias, parts, far, key_weight, value_weight, out_weight)
 
 
 def solution(mesh):

time: 35.9 us -> 35.8 us (level)
  waiting for transfers between devices: 2.55 us -> 3.94 us
  Pallas kernels: 19.7 us -> 18.9 us
  starting transfers between devices: 13.1 us -> 12.3 us
    ppermute x10, waiting for transfers between devices: 2.54 us -> 3.94 us  [swap(): lax.ppermute(held, axis, [(i, i ^ far) for i in range(lax.axis_size(axis))])]
    pallas_call x2 -> x1, Pallas kernels: 5.31 us -> 4.26 us  [attend(): pl.pallas_call(functools.partial(attend_kernel, len(parts)), out_shape=ja...]
    ppermute x10, starting transfers between devices: 11.4 us -> 10.6 us  [swap(): lax.ppermute(held, axis, [(i, i ^ far) for i in range(lax.axis_size(axis))])]
  transfers between devices with their start and end apart: 11 -> 11, of which waited for: 4 -> 3; matrix products, arithmetic and copies ran while one was open for 0% -> 0% of each run, Pallas kernels for 37% -> 31%
where the time goes in v9:
time: 35.8 us; the launch traced here: 35.7 us
  Pallas kernels  18.9 us (53%)
  starting transfers between devices  12.3 us (34%)
  waiting for transfers between devices  3.94 us (11%)
    ppermute x10, starting transfers between devices, swap(): lax.ppermute(held, axis, [(i, i ^ far) for i in range(lax.axis_size(axis))])  10.6 us
    pallas_call x2, Pallas kernels, atom_attention(): pl.pallas_call(functools.partial(atom_kernel, sample), out_shape=jax.Shap...  4.62 us
    pallas_call x1, Pallas kernels, attend(): pl.pallas_call(functools.partial(attend_kernel, len(parts)), out_shape=ja...  4.26 us
    ppermute x10, waiting for transfers between devices, swap(): lax.ppermute(held, axis, [(i, i ^ far) for i in range(lax.axis_size(axis))])  3.94 us
    pallas_call x1, Pallas kernels, pair_bias(): pl.pallas_call(bias_kernel, grid=(1,), out_shape=[jax.ShapeDtypeStruct((c...  3.57 us
    pallas_call x2, Pallas kernels, gather_tokens(): pl.pallas_call(functools.partial(gather_kernel, sample), out_shape=[jax.S...  3.51 us
    pallas_call x2, Pallas kernels, project(): pl.pallas_call(project_kernel, out_shape=[jax.ShapeDtypeStruct((rows, wid...  2.21 us
    ppermute x1, starting transfers between devices, shards(): lax.ppermute(outer, 'row', odd_pairs + [(j, i) for i, j in odd_pairs])  1.63 us
  transfers between devices with their start and end apart: 11, of which 3 were waited for; matrix products, arithmetic and copies ran while one was open for 0% of the time, Pallas kernels for 31%

profile of v9, /device:TPU:0, one launch (start us, length us, event | category | flops | bytes accessed | tf_op | source)
XLA Modules:
  0.0 35.7 jit_solution(11201217835271267619)
XLA Ops:
  0.0 3.6 %pair_bias.1 = (bf16[36,1152]{1,0:T(8,128)(2,1)}, bf16[2,48,128]{2,1,0:T(8,128)(2,1)}, bf16[2,48,128]{2,1,0:T(8,128)(2,1)}) custom-call(bf16[2,1152,128]{2,1,0:T(8,128)(2,1)} %feat.7, bf16[2,1152,128]{2,1,0:T(8,128)(2,1)} %feat.7, bf16[36,72,128]{2,1,0:T(8,128)(2,1)} %bitcast.16, s32[36]{0:T(128)} %mask.1, bf16[16,128]{1,0:T(8,128)(2,1)} %bitcast.17), custom_call_target="tpu_custom_call" | custom-call | flops 60000000 | bytes 1000 | tf_op jit(solution)/shard_map/pair_bias/pallas_call | solution.py:102
  3.6 4.0 %collective-permute-start = (bf16[36,1152]{1,0:T(8,128)(2,1)}, bf16[36,1152]{1,0:T(8,128)(2,1)S(1)}, u32[]{:S(2)}, u32[]{:S(2)}) collective-permute-start(bf16[36,1152]{1,0:T(8,128)(2,1)} %get-tuple-element.37), channel_id=1, source_target_pairs={{0,4},{1,5},{2,6},{3,7},{4,0},{5,1},{6,2},{7,3},{8,12},{9,13},{10,... | collective-permute-start | bytes 248840 | tf_op jit(solution)/shard_map/ppermute | solution.py:130
  7.7 0.0 collective-permute-start.1
  7.7 1.6 %collective-permute-start.2 = (bf16[2,48,128]{2,1,0:T(8,128)(2,1)}, bf16[2,48,128]{2,1,0:T(8,128)(2,1)S(1)}, u32[]{:S(2)}, u32[]{:S(2)}) collective-permute-start(bf16[2,48,128]{2,1,0:T(8,128)(2,1)} %get-tuple-element.35), channel_id=1, source_target_pairs={{8,16},{24,0},{16,8},{0,24},{9,17},{25,1},{17,9},{1,25},{10,18},{2... | collective-permute-start | bytes 73736 | tf_op jit(solution)/shard_map/ppermute | solution.py:509
  9.3 0.0 copy-start.5
  9.3 2.4 %atom_attention.2.mixed = bf16[1152,128]{1,0:T(8,128)(2,1)S(1)} custom-call(bf16[2,1152,128]{2,1,0:T(8,128)(2,1)S(1)} %copy-done, bf16[128,128]{1,0:T(8,128)(2,1)S(1)} %copy-done.7, bf16[128,128]{1,0:T(8,128)(2,1)S(1)} %copy-done.8, bf16[128,128]{1,0:T(8,128)(2,1)S(1)} %copy-done.9), custom_call_target="tpu_custom_call" | custom-call | flops 80000000 | bytes 1000 | tf_op jit(solution)/shard_map/atom_attention/pallas_call | solution.py:239
  11.7 0.0 collective-permute-done.2.refs_1_
  11.7 0.0 copy-start.4
  11.8 2.1 %gather_tokens.2 = (f32[72,768]{1,0:T(8,128)S(1)}, bf16[72,768]{1,0:T(8,128)(2,1)S(1)}) custom-call(bf16[1152,128]{1,0:T(8,128)(2,1)S(1)} %atom_attention.2.mixed, bf16[2,1152,128]{2,1,0:T(8,128)(2,1)S(1)} %copy-done, s32[1152]{0:T(1024)S(1)} %copy-done.11, bf16[128,128]{1,0:T(8,128)(2,1)S(1)} %copy-done.10, bf16[128,768]{1,0:T(8,128)(2,1)S(1)} %copy-done.6, ...), custom_call_target="tpu_custom_call" | custom-call | flops 20000000 | bytes 1000 | tf_op jit(solution)/shard_map/gather_tokens/pallas_call | solution.py:309
  13.9 1.0 %collective-permute-start.8 = (bf16[1,72,768]{2,1,0:T(8,128)(2,1)S(1)}, bf16[1,72,768]{2,1,0:T(8,128)(2,1)S(1)}, u32[]{:S(2)}, u32[]{:S(2)}) collective-permute-start(bf16[1,72,768]{2,1,0:T(8,128)(2,1)S(1)} %bitcast.14), channel_id=1, source_target_pairs={{0,16},{8,24},{16,0},{24,8},{1,17},{9,25},{17,1},{25,9},{2,18},{10... | collective-permute-start | bytes 331784 | tf_op jit(solution)/shard_map/ppermute | solution.py:130
  14.9 0.0 copy-start.3
  14.9 1.6 %collective-permute-start.3 = (bf16[2,36,640]{2,1,0:T(8,128)(2,1)S(1)}, bf16[2,36,640]{2,1,0:T(8,128)(2,1)S(1)}, u32[]{:S(2)}, u32[]{:S(2)}) collective-permute-start(bf16[2,36,640]{2,1,0:T(8,128)(2,1)S(1)} %pad_maximum_fusion.4), channel_id=1, source_target_pairs={{0,2},{1,3},{2,0},{3,1},{4,6},{5,7},{6,4},{7,5},{8,10},{9,11},{10,... | collective-permute-start | bytes 276488 | tf_op jit(solution)/shard_map/ppermute | solution.py:130
  16.6 1.6 %collective-permute-start.5 = (bf16[2,36,512]{2,1,0:T(8,128)(2,1)S(1)}, bf16[2,36,512]{2,1,0:T(8,128)(2,1)S(1)}, u32[]{:S(2)}, u32[]{:S(2)}) collective-permute-start(bf16[2,36,512]{2,1,0:T(8,128)(2,1)S(1)} %pad_maximum_fusion.5), channel_id=1, source_target_pairs={{0,1},{1,0},{2,3},{3,2},{4,5},{5,4},{6,7},{7,6},{8,9},{9,8},{10,11... | collective-permute-start | bytes 221192 | tf_op jit(solution)/shard_map/ppermute | solution.py:130
  18.2 2.3 %atom_attention.3.mixed = bf16[1152,128]{1,0:T(8,128)(2,1)S(1)} custom-call(bf16[2,1152,128]{2,1,0:T(8,128)(2,1)S(1)} %copy-done, bf16[2,48,128]{2,1,0:T(8,128)(2,1)S(1)} %collective-permute-done.1.refs_0_, bf16[2,48,128]{2,1,0:T(8,128)(2,1)S(1)} %collective-permute-done.2.refs_1_, bf16[128,128]{1,0:T(8,128)(2,1)S(1)} %copy-done.7, ...), custom_call_target="tpu_custom_call" | custom-call | flops 80000000 | bytes 1000 | tf_op jit(solution)/shard_map/atom_attention/pallas_call | solution.py:239
  20.4 0.0 copy-start.1
  20.4 1.4 %gather_tokens.3 = (f32[72,768]{1,0:T(8,128)S(1)}, bf16[72,768]{1,0:T(8,128)(2,1)S(1)}) custom-call(bf16[1152,128]{1,0:T(8,128)(2,1)S(1)} %atom_attention.3.mixed, bf16[2,1152,128]{2,1,0:T(8,128)(2,1)S(1)} %copy-done, s32[1152]{0:T(1024)S(1)} %copy-done.11, bf16[128,128]{1,0:T(8,128)(2,1)S(1)} %copy-done.10, bf16[128,768]{1,0:T(8,128)(2,1)S(1)} %copy-done.6, ...), custom_call_target="tpu_custom_call" | custom-call | flops 20000000 | bytes 1000 | tf_op jit(solution)/shard_map/gather_tokens/pallas_call | solution.py:309
  21.9 0.0 collective-permute-done.8
  21.9 0.1 collective-permute-start.9
  22.0 0.0 collective-permute-done.5
  22.0 0.7 %collective-permute-start.4 = (bf16[4,36,640]{2,1,0:T(8,128)(2,1)S(1)}, bf16[4,36,640]{2,1,0:T(8,128)(2,1)S(1)}, u32[]{:S(2)}, u32[]{:S(2)}) collective-permute-start(bf16[4,36,640]{2,1,0:T(8,128)(2,1)S(1)} %pad_maximum_fusion.2.refs_0_), channel_id=1, source_target_pairs={{0,1},{1,0},{2,3},{3,2},{4,5},{5,4},{6,7},{7,6},{8,9},{9,8},{10,11... | collective-permute-start | bytes 552968 | tf_op jit(solution)/shard_map/ppermute | solution.py:130
  22.7 0.7 %collective-permute-start.6 = (bf16[4,36,512]{2,1,0:T(8,128)(2,1)S(1)}, bf16[4,36,512]{2,1,0:T(8,128)(2,1)S(1)}, u32[]{:S(2)}, u32[]{:S(2)}) collective-permute-start(bf16[4,36,512]{2,1,0:T(8,128)(2,1)S(1)} %pad_maximum_fusion.3.refs_2_), channel_id=1, source_target_pairs={{0,2},{1,3},{2,0},{3,1},{4,6},{5,7},{6,4},{7,5},{8,10},{9,11},{10,... | collective-permute-start | bytes 442376 | tf_op jit(solution)/shard_map/ppermute | solution.py:130
  23.4 0.9 %collective-permute-start.7 = (bf16[1,72,768]{2,1,0:T(8,128)(2,1)S(1)}, bf16[1,72,768]{2,1,0:T(8,128)(2,1)S(1)}, u32[]{:S(2)}, u32[]{:S(2)}) collective-permute-start(bf16[1,72,768]{2,1,0:T(8,128)(2,1)S(1)} %bitcast.12), channel_id=1, source_target_pairs={{0,16},{8,24},{16,0},{24,8},{1,17},{9,25},{17,1},{25,9},{2,18},{10... | collective-permute-start | bytes 331784 | tf_op jit(solution)/shard_map/ppermute | solution.py:130
  24.3 0.0 collective-permute-done.9.refs_0_
  24.4 1.3 %project.2 = (bf16[72,768]{1,0:T(8,128)(2,1)S(1)}, bf16[768,288]{1,0:T(8,128)(2,1)S(1)}, bf16[288,768]{1,0:T(8,128)(2,1)S(1)}, f32[72,768]{1,0:T(8,128)S(1)}) custom-call(bf16[2,72,768]{2,1,0:T(8,128)(2,1)S(1)} %pad_maximum_fusion.near, bf16[2,72,768]{2,1,0:T(8,128)(2,1)S(1)} %collective-permute-done.9.refs_0_, bf16[768,768]{1,0:T(8,128)(2,1)S(1)} %copy-done.4, ...), custom_call_target="tpu_custom_call" | custom-call | flops 40000000 | bytes 1000 | tf_op jit(solution)/shard_map/project/pallas_call | solution.py:351
  25.6 2.5 %collective-permute-done.7 = bf16[1,72,768]{2,1,0:T(8,128)(2,1)S(1)} collective-permute-done((bf16[1,72,768]{2,1,0:T(8,128)(2,1)S(1)}, bf16[1,72,768]{2,1,0:T(8,128)(2,1)S(1)}, u32[]{:S(2)}, u32[]{:S(2)}) %collective-permute-start.7) | collective-permute-done | bytes 110624 | tf_op jit(solution)/shard_map/ppermute | solution.py:130
  28.1 0.9 %collective-permute-done.6.refs_3_ = bf16[4,36,512]{2,1,0:T(8,128)(2,1)S(1)} collective-permute-done((bf16[4,36,512]{2,1,0:T(8,128)(2,1)S(1)}, bf16[4,36,512]{2,1,0:T(8,128)(2,1)S(1)}, u32[]{:S(2)}, u32[]{:S(2)}) %collective-permute-start.6) | collective-permute-done | bytes 147488 | tf_op jit(solution)/shard_map/ppermute | solution.py:130
  29.0 0.5 %collective-permute-done.4.refs_1_ = bf16[4,36,640]{2,1,0:T(8,128)(2,1)S(1)} collective-permute-done((bf16[4,36,640]{2,1,0:T(8,128)(2,1)S(1)}, bf16[4,36,640]{2,1,0:T(8,128)(2,1)S(1)}, u32[]{:S(2)}, u32[]{:S(2)}) %collective-permute-start.4) | collective-permute-done | bytes 184352 | tf_op jit(solution)/shard_map/ppermute | solution.py:130
  29.6 0.1 collective-permute-start.10
  29.7 0.8 %turn_bias.1.bias = f32[1152,288]{1,0:T(8,128)S(1)} custom-call(bf16[4,36,640]{2,1,0:T(8,128)(2,1)S(1)} %pad_maximum_fusion.2.refs_0_, bf16[4,36,640]{2,1,0:T(8,128)(2,1)S(1)} %collective-permute-done.4.refs_1_, bf16[4,36,512]{2,1,0:T(8,128)(2,1)S(1)} %pad_maximum_fusion.3.refs_2_, bf16[4,36,512]{2,1,0:T(8,128)(2,1)S(1)} %collective-permute-done.6.refs_3_), custom_call_target="tpu_custom_call" | custom-call | flops 20000000 | bytes 1000 | tf_op jit(solution)/shard_map/turn_bias/pallas_call | solution.py:393
  30.4 0.9 %project.3 = (bf16[72,768]{1,0:T(8,128)(2,1)S(1)}, bf16[144,768]{1,0:T(8,128)(2,1)S(1)}, bf16[144,768]{1,0:T(8,128)(2,1)S(1)}, f32[72,768]{1,0:T(8,128)S(1)}) custom-call(bf16[2,72,768]{2,1,0:T(8,128)(2,1)S(1)} %pad_maximum_fusion.1.near, bf16[768,768]{1,0:T(8,128)(2,1)S(1)} %copy-done.4, bf16[768,768]{1,0:T(8,128)(2,1)S(1)} %copy-done.1, ...), custom_call_target="tpu_custom_call" | custom-call | flops 40000000 | bytes 1000 | tf_op jit(solution)/shard_map/project/pallas_call | solution.py:351
  31.4 0.0 collective-permute-done.10.refs_10_
  31.4 4.3 %attend.1 = bf16[2,72,768]{2,1,0:T(8,128)(2,1)} custom-call(f32[1152,288]{1,0:T(8,128)S(1)} %turn_bias.1.bias, bf16[72,768]{1,0:T(8,128)(2,1)S(1)} %get-tuple-element.45.refs_0_, bf16[768,288]{1,0:T(8,128)(2,1)S(1)} %get-tuple-element.46.refs_1_, bf16[288,768]{1,0:T(8,128)(2,1)S(1)} %get-tuple-element.47.refs_2_, f32[72,768]{1,0:T(8,128)S(1)} %get-tuple-element.48.refs_3_, ...), custom_call_target="tpu_custom_call" | custom-call | flops 60000000 | bytes 1000 | tf_op jit(solution)/shard_map/attend/pallas_call | solution.py:473
  (35 shorter events, 0.2 us)
Async XLA Ops:
  0.0 9.3 %copy-start = (bf16[2,1152,128]{2,1,0:T(8,128)(2,1)S(1)}, bf16[2,1152,128]{2,1,0:T(8,128)(2,1)}, u32[]{:S(2)}) copy-start(bf16[2,1152,128]{2,1,0:T(8,128)(2,1)} %feat.7) | copy-start | bytes 1769476
  0.0 9.3 %copy-start.7 = (bf16[128,128]{1,0:T(8,128)(2,1)S(1)}, bf16[128,128]{1,0:T(8,128)(2,1)}, u32[]{:S(2)}) copy-start(bf16[128,128]{1,0:T(8,128)(2,1)} %refs_2_.7) | copy-start | bytes 98308
  0.0 9.3 %copy-start.8 = (bf16[128,128]{1,0:T(8,128)(2,1)S(1)}, bf16[128,128]{1,0:T(8,128)(2,1)}, u32[]{:S(2)}) copy-start(bf16[128,128]{1,0:T(8,128)(2,1)} %refs_3_.5) | copy-start | bytes 98308
  0.0 9.3 %copy-start.9 = (bf16[128,128]{1,0:T(8,128)(2,1)S(1)}, bf16[128,128]{1,0:T(8,128)(2,1)}, u32[]{:S(2)}) copy-start(bf16[128,128]{1,0:T(8,128)(2,1)} %refs_4_.5) | copy-start | bytes 98308
  0.0 11.7 %copy-start.6 = (bf16[128,768]{1,0:T(8,128)(2,1)S(1)}, bf16[128,768]{1,0:T(8,128)(2,1)}, u32[]{:S(2)}) copy-start(bf16[128,768]{1,0:T(8,128)(2,1)} %agg.3) | copy-start | bytes 589828
  0.0 11.7 %copy-start.10 = (bf16[128,128]{1,0:T(8,128)(2,1)S(1)}, bf16[128,128]{1,0:T(8,128)(2,1)}, u32[]{:S(2)}) copy-start(bf16[128,128]{1,0:T(8,128)(2,1)} %wo.3) | copy-start | bytes 98308
  0.0 11.7 %copy-start.11 = (s32[1152]{0:T(1024)S(1)}, s32[1152]{0:T(1024)}, u32[]{:S(2)}) copy-start(s32[1152]{0:T(1024)} %token_.3) | copy-start | bytes 13828
  0.0 11.7 %copy-start.12 = (f32[768]{0:T(1024)S(1)}, f32[768]{0:T(1024)}, u32[]{:S(2)}) copy-start(f32[768]{0:T(1024)} %gain.3) | copy-start | bytes 9220
  3.6 11.2 %copy-start.13 = (bf16[36,1152]{1,0:T(8,128)(2,1)S(1)}, bf16[36,1152]{1,0:T(8,128)(2,1)}, u32[]{:S(2)}) copy-start(bf16[36,1152]{1,0:T(8,128)(2,1)} %get-tuple-element.37) | copy-start | bytes 248836
  3.6 11.2 %collective-permute-start = (bf16[36,1152]{1,0:T(8,128)(2,1)}, bf16[36,1152]{1,0:T(8,128)(2,1)S(1)}, u32[]{:S(2)}, u32[]{:S(2)}) collective-permute-start(bf16[36,1152]{1,0:T(8,128)(2,1)} %get-tuple-element.37), channel_id=1, source_target_pairs={{0,4},{1,5},{2,6},{3,7},{4,0},{5,1},{6,2},{7,3},{8,12},{9,13},{10,... | collective-permute-start | bytes 248840 | tf_op jit(solution)/shard_map/ppermute | solution.py:130
  7.7 4.0 %collective-permute-start.1 = (bf16[2,48,128]{2,1,0:T(8,128)(2,1)}, bf16[2,48,128]{2,1,0:T(8,128)(2,1)S(1)}, u32[]{:S(2)}, u32[]{:S(2)}) collective-permute-start(bf16[2,48,128]{2,1,0:T(8,128)(2,1)} %get-tuple-element.34), channel_id=1, source_target_pairs={{0,8},{8,0},{16,24},{24,16},{1,9},{9,1},{17,25},{25,17},{2,10},{10... | collective-permute-start | bytes 73736 | tf_op jit(solution)/shard_map/ppermute | solution.py:130
  7.7 4.0 %collective-permute-start.2 = (bf16[2,48,128]{2,1,0:T(8,128)(2,1)}, bf16[2,48,128]{2,1,0:T(8,128)(2,1)S(1)}, u32[]{:S(2)}, u32[]{:S(2)}) collective-permute-start(bf16[2,48,128]{2,1,0:T(8,128)(2,1)} %get-tuple-element.35), channel_id=1, source_target_pairs={{8,16},{24,0},{16,8},{0,24},{9,17},{25,1},{17,9},{1,25},{10,18},{2... | collective-permute-start | bytes 73736 | tf_op jit(solution)/shard_map/ppermute | solution.py:509
  9.3 15.0 %copy-start.5 = (bf16[768,768]{1,0:T(8,128)(2,1)S(1)}, bf16[768,768]{1,0:T(8,128)(2,1)}, u32[]{:S(2)}) copy-start(bf16[768,768]{1,0:T(8,128)(2,1)} %refs_3_.7) | copy-start | bytes 3538948
  11.7 12.6 %copy-start.4 = (bf16[768,768]{1,0:T(8,128)(2,1)S(1)}, bf16[768,768]{1,0:T(8,128)(2,1)}, u32[]{:S(2)}) copy-start(bf16[768,768]{1,0:T(8,128)(2,1)} %refs_0_.3) | copy-start | bytes 3538948
  13.9 8.0 %collective-permute-start.8 = (bf16[1,72,768]{2,1,0:T(8,128)(2,1)S(1)}, bf16[1,72,768]{2,1,0:T(8,128)(2,1)S(1)}, u32[]{:S(2)}, u32[]{:S(2)}) collective-permute-start(bf16[1,72,768]{2,1,0:T(8,128)(2,1)S(1)} %bitcast.14), channel_id=1, source_target_pairs={{0,16},{8,24},{16,0},{24,8},{1,17},{9,25},{17,1},{25,9},{2,18},{10... | collective-permute-start | bytes 331784 | tf_op jit(solution)/shard_map/ppermute | solution.py:130
  14.9 9.5 %copy-start.3 = (bf16[768,768]{1,0:T(8,128)(2,1)S(1)}, bf16[768,768]{1,0:T(8,128)(2,1)}, u32[]{:S(2)}) copy-start(bf16[768,768]{1,0:T(8,128)(2,1)} %refs_13_.1) | copy-start | bytes 3538948
  14.9 7.1 %collective-permute-start.3 = (bf16[2,36,640]{2,1,0:T(8,128)(2,1)S(1)}, bf16[2,36,640]{2,1,0:T(8,128)(2,1)S(1)}, u32[]{:S(2)}, u32[]{:S(2)}) collective-permute-start(bf16[2,36,640]{2,1,0:T(8,128)(2,1)S(1)} %pad_maximum_fusion.4), channel_id=1, source_target_pairs={{0,2},{1,3},{2,0},{3,1},{4,6},{5,7},{6,4},{7,5},{8,10},{9,11},{10,... | collective-permute-start | bytes 276488 | tf_op jit(solution)/shard_map/ppermute | solution.py:130
  16.6 5.4 %collective-permute-start.5 = (bf16[2,36,512]{2,1,0:T(8,128)(2,1)S(1)}, bf16[2,36,512]{2,1,0:T(8,128)(2,1)S(1)}, u32[]{:S(2)}, u32[]{:S(2)}) collective-permute-start(bf16[2,36,512]{2,1,0:T(8,128)(2,1)S(1)} %pad_maximum_fusion.5), channel_id=1, source_target_pairs={{0,1},{1,0},{2,3},{3,2},{4,5},{5,4},{6,7},{7,6},{8,9},{9,8},{10,11... | collective-permute-start | bytes 221192 | tf_op jit(solution)/shard_map/ppermute | solution.py:130
  18.1 6.2 %copy-start.2 = (bf16[768,768]{1,0:T(8,128)(2,1)S(1)}, bf16[768,768]{1,0:T(8,128)(2,1)}, u32[]{:S(2)}) copy-start(bf16[768,768]{1,0:T(8,128)(2,1)} %refs_12_.1) | copy-start | bytes 3538948
  20.4 3.9 %copy-start.1 = (bf16[768,768]{1,0:T(8,128)(2,1)S(1)}, bf16[768,768]{1,0:T(8,128)(2,1)}, u32[]{:S(2)}) copy-start(bf16[768,768]{1,0:T(8,128)(2,1)} %refs_11_.1) | copy-start | bytes 3538948
  21.9 2.4 %collective-permute-start.9 = (bf16[2,72,768]{2,1,0:T(8,128)(2,1)S(1)}, bf16[2,72,768]{2,1,0:T(8,128)(2,1)S(1)}, u32[]{:S(2)}, u32[]{:S(2)}) collective-permute-start(bf16[2,72,768]{2,1,0:T(8,128)(2,1)S(1)} %pad_maximum_fusion.near), channel_id=1, source_target_pairs={{0,8},{8,0},{16,24},{24,16},{1,9},{9,1},{17,25},{25,17},{2,10},{10... | collective-permute-start | bytes 663560 | tf_op jit(solution)/shard_map/ppermute | solution.py:130
  22.0 7.5 %collective-permute-start.4 = (bf16[4,36,640]{2,1,0:T(8,128)(2,1)S(1)}, bf16[4,36,640]{2,1,0:T(8,128)(2,1)S(1)}, u32[]{:S(2)}, u32[]{:S(2)}) collective-permute-start(bf16[4,36,640]{2,1,0:T(8,128)(2,1)S(1)} %pad_maximum_fusion.2.refs_0_), channel_id=1, source_target_pairs={{0,1},{1,0},{2,3},{3,2},{4,5},{5,4},{6,7},{7,6},{8,9},{9,8},{10,11... | collective-permute-start | bytes 552968 | tf_op jit(solution)/shard_map/ppermute | solution.py:130
  22.7 6.3 %collective-permute-start.6 = (bf16[4,36,512]{2,1,0:T(8,128)(2,1)S(1)}, bf16[4,36,512]{2,1,0:T(8,128)(2,1)S(1)}, u32[]{:S(2)}, u32[]{:S(2)}) collective-permute-start(bf16[4,36,512]{2,1,0:T(8,128)(2,1)S(1)} %pad_maximum_fusion.3.refs_2_), channel_id=1, source_target_pairs={{0,2},{1,3},{2,0},{3,1},{4,6},{5,7},{6,4},{7,5},{8,10},{9,11},{10,... | collective-permute-start | bytes 442376 | tf_op jit(solution)/shard_map/ppermute | solution.py:130
  23.4 4.7 %collective-permute-start.7 = (bf16[1,72,768]{2,1,0:T(8,128)(2,1)S(1)}, bf16[1,72,768]{2,1,0:T(8,128)(2,1)S(1)}, u32[]{:S(2)}, u32[]{:S(2)}) collective-permute-start(bf16[1,72,768]{2,1,0:T(8,128)(2,1)S(1)} %bitcast.12), channel_id=1, source_target_pairs={{0,16},{8,24},{16,0},{24,8},{1,17},{9,25},{17,1},{25,9},{2,18},{10... | collective-permute-start | bytes 331784 | tf_op jit(solution)/shard_map/ppermute | solution.py:130
  29.6 1.8 %collective-permute-start.10 = (bf16[2,72,768]{2,1,0:T(8,128)(2,1)S(1)}, bf16[2,72,768]{2,1,0:T(8,128)(2,1)S(1)}, u32[]{:S(2)}, u32[]{:S(2)}) collective-permute-start(bf16[2,72,768]{2,1,0:T(8,128)(2,1)S(1)} %pad_maximum_fusion.1.near), channel_id=1, source_target_pairs={{0,8},{8,0},{16,24},{24,16},{1,9},{9,1},{17,25},{25,17},{2,10},{10... | collective-permute-start | bytes 663560 | tf_op jit(solution)/shard_map/ppermute | solution.py:130

commit v10 on v9

--- a/solution.py
+++ b/solution.py
@@ -408,26 +408,28 @@
     _, k_near, v_near, _, _ = parts[-1]
     rows, width = parts[-1][4].shape
     x = stack(far)
-    for c in range(0, width, 2 * LANES):
+    scale = LOG2E / HEAD_DIM**0.5
+    lane = iota((rows, 2 * LANES), 1)
+    groups = head_groups(width)
+    work = [(s, base, heads) for s in range(samples) for base, heads in groups]
+    chunks = list(range(0, width, 2 * LANES))
+    for i, c in enumerate(chunks):
+        work.insert(min(2 * i + 1, (samples - 1) * len(groups) + i), c)
+
+    def fill(c):
         lanes = slice(c, c + 2 * LANES)
         k = jnp.concatenate([k_near[:, lanes].astype(F32), dot(x, wk[:, lanes])], axis=0)
         kt[lanes] = k.T.astype(BF16)
-    v[: v_near.shape[0]] = v_near[...]
-    v[v_near.shape[0] :] = dot(x, wv[...]).astype(BF16)
-    scale = LOG2E / HEAD_DIM**0.5
-    lane = iota((rows, 2 * LANES), 1)
-    work = [
-        (s, base, heads[i : i + 2])
-        for s in range(samples)
-        for base, heads in head_groups(width)
-        for i in range(0, len(heads), 2)
-    ]
+        v[: v_near.shape[0], lanes] = v_near[:, lanes]
+        v[v_near.shape[0] :, lanes] = dot(x, wv[:, lanes]).astype(BF16)
 
     def channels(base, h):
         low = h * HEAD_DIM - base
         return (lane >= low) & (lane < low + HEAD_DIM)
 
     def score(item):
+        if isinstance(item, int):
+            return fill(item)
         s, base, heads = item
         q, keys = parts[s][0], parts[s][1] if s < samples - 1 else kt
         mine = q[:, base : base + 2 * LANES].astype(F32)
@@ -436,6 +438,8 @@
         return item, dot(mine, keys[base : base + 2 * LANES]) * scale + some
 
     def soften(item):
+        if item is None:
+            return None
         place, sc = item
         e = jnp.exp2(sc - jnp.max(sc, -1, keepdims=True))
         return place, e.astype(BF16), inverse(jnp.sum(e, -1, keepdims=True))
@@ -443,6 +447,8 @@
     mixes = {}
 
     def mix(item):
+        if item is None:
+            return
         (s, base, heads), e, share = item
         values = parts[s][2] if s < samples - 1 else v
         o = dot(e, values[:, base : base + 2 * LANES]) * share
@@ -453,7 +459,7 @@
 
     def close(s):
         tiles = {}
-        for base, _ in head_groups(width):
+        for base, _ in groups:
             for t in range(2):
                 at = base + t * LANES
                 part = mixes[s, base][:, t * LANES : (t + 1) * LANES]
@@ -529,6 +535,7 @@
             bias, got, _ = lax.optimization_barrier((bias, got, token_norm))
             held = [jnp.stack([bias[:, lanes], got[:, lanes]]) for lanes in (slice(0, split), slice(split, None))]
             inner = after(inner, held, token_norm)
+    last = swap(norms[-1], "row", row_bits[0])
     for i in range(1, len(bits) - 1):
         held = [widen(h, "sample", order[i], token_norm) for h, order in zip(held, orders)]
     halves = []
@@ -538,8 +545,12 @@
     weights = (query_weight, key_weight, value_weight, gate_weight, out_weight)
     for s in range(samples):
         near = norms[s]
+        others = (mixed, parts, halves) if s == samples - 1 else (mixed, parts)
         for bit in row_bits[:-1]:
-            near = widen(near, "row", bit, mixed, *((parts, halves) if s == samples - 1 else parts))
+            if s == samples - 1 and bit == row_bits[0]:
+                near = jnp.concatenate([near, after(last, *others)], axis=0)
+            else:
+                near = widen(near, "row", bit, *others)
         far = swap(near, "row", row_bits[-1])
         near = after(near, held)
         blocks = (near, far) if s < samples - 1 else (near,)

time: 35.8 us -> 35.1 us (0.980)
  Pallas kernels: 18.9 us -> 18.2 us
    pallas_call x1, Pallas kernels: 4.26 us -> 3.53 us  [attend(): pl.pallas_call(functools.partial(attend_kernel, len(parts)), out_shape=ja...]
  transfers between devices with their start and end apart: 11 -> 11, of which waited for: 3 -> 3; matrix products, arithmetic and copies ran while one was open for 0% -> 0% of each run, Pallas kernels for 31% -> 32%
where the time goes in v10:
time: 35.1 us; the launch traced here: 34.9 us
  Pallas kernels  18.2 us (52%)
  starting transfers between devices  12.3 us (35%)
  waiting for transfers between devices  3.94 us (11%)
    ppermute x10, starting transfers between devices, swap(): lax.ppermute(held, axis, [(i, i ^ far) for i in range(lax.axis_size(axis))])  10.6 us
    pallas_call x2, Pallas kernels, atom_attention(): pl.pallas_call(functools.partial(atom_kernel, sample), out_shape=jax.Shap...  4.62 us
    ppermute x10, waiting for transfers between devices, swap(): lax.ppermute(held, axis, [(i, i ^ far) for i in range(lax.axis_size(axis))])  3.94 us
    pallas_call x1, Pallas kernels, pair_bias(): pl.pallas_call(bias_kernel, grid=(1,), out_shape=[jax.ShapeDtypeStruct((c...  3.57 us
    pallas_call x1, Pallas kernels, attend(): pl.pallas_call(functools.partial(attend_kernel, len(parts)), out_shape=ja...  3.53 us
    pallas_call x2, Pallas kernels, gather_tokens(): pl.pallas_call(functools.partial(gather_kernel, sample), out_shape=[jax.S...  3.51 us
    pallas_call x2, Pallas kernels, project(): pl.pallas_call(project_kernel, out_shape=[jax.ShapeDtypeStruct((rows, wid...  2.21 us
    ppermute x1, starting transfers between devices, shards(): lax.ppermute(outer, 'row', odd_pairs + [(j, i) for i, j in odd_pairs])  1.63 us
  transfers between devices with their start and end apart: 11, of which 3 were waited for; matrix products, arithmetic and copies ran while one was open for 0% of the time, Pallas kernels for 32%

profile of v10, /device:TPU:0, one launch (start us, length us, event | category | flops | bytes accessed | tf_op | source)
XLA Modules:
  0.0 34.9 jit_solution(12003065543979341116)
XLA Ops:
  0.0 3.6 %pair_bias.1 = (bf16[36,1152]{1,0:T(8,128)(2,1)}, bf16[2,48,128]{2,1,0:T(8,128)(2,1)}, bf16[2,48,128]{2,1,0:T(8,128)(2,1)}) custom-call(bf16[2,1152,128]{2,1,0:T(8,128)(2,1)} %feat.7, bf16[2,1152,128]{2,1,0:T(8,128)(2,1)} %feat.7, bf16[36,72,128]{2,1,0:T(8,128)(2,1)} %bitcast.16, s32[36]{0:T(128)} %mask.1, bf16[16,128]{1,0:T(8,128)(2,1)} %bitcast.17), custom_call_target="tpu_custom_call" | custom-call | flops 60000000 | bytes 1000 | tf_op jit(solution)/shard_map/pair_bias/pallas_call | solution.py:102
  3.6 4.0 %collective-permute-start = (bf16[36,1152]{1,0:T(8,128)(2,1)}, bf16[36,1152]{1,0:T(8,128)(2,1)S(1)}, u32[]{:S(2)}, u32[]{:S(2)}) collective-permute-start(bf16[36,1152]{1,0:T(8,128)(2,1)} %get-tuple-element.37), channel_id=1, source_target_pairs={{0,4},{1,5},{2,6},{3,7},{4,0},{5,1},{6,2},{7,3},{8,12},{9,13},{10,... | collective-permute-start | bytes 248840 | tf_op jit(solution)/shard_map/ppermute | solution.py:130
  7.7 0.0 collective-permute-start.1
  7.7 1.6 %collective-permute-start.2 = (bf16[2,48,128]{2,1,0:T(8,128)(2,1)}, bf16[2,48,128]{2,1,0:T(8,128)(2,1)S(1)}, u32[]{:S(2)}, u32[]{:S(2)}) collective-permute-start(bf16[2,48,128]{2,1,0:T(8,128)(2,1)} %get-tuple-element.35), channel_id=1, source_target_pairs={{8,16},{24,0},{16,8},{0,24},{9,17},{25,1},{17,9},{1,25},{10,18},{2... | collective-permute-start | bytes 73736 | tf_op jit(solution)/shard_map/ppermute | solution.py:515
  9.3 0.0 copy-start.5
  9.3 2.4 %atom_attention.2.mixed = bf16[1152,128]{1,0:T(8,128)(2,1)S(1)} custom-call(bf16[2,1152,128]{2,1,0:T(8,128)(2,1)S(1)} %copy-done, bf16[128,128]{1,0:T(8,128)(2,1)S(1)} %copy-done.7, bf16[128,128]{1,0:T(8,128)(2,1)S(1)} %copy-done.8, bf16[128,128]{1,0:T(8,128)(2,1)S(1)} %copy-done.9), custom_call_target="tpu_custom_call" | custom-call | flops 80000000 | bytes 1000 | tf_op jit(solution)/shard_map/atom_attention/pallas_call | solution.py:239
  11.7 0.0 collective-permute-done.1.refs_0_
  11.7 0.0 collective-permute-done.2.refs_1_
  11.7 0.0 copy-start.4
  11.8 2.1 %gather_tokens.2 = (f32[72,768]{1,0:T(8,128)S(1)}, bf16[72,768]{1,0:T(8,128)(2,1)S(1)}) custom-call(bf16[1152,128]{1,0:T(8,128)(2,1)S(1)} %atom_attention.2.mixed, bf16[2,1152,128]{2,1,0:T(8,128)(2,1)S(1)} %copy-done, s32[1152]{0:T(1024)S(1)} %copy-done.11, bf16[128,128]{1,0:T(8,128)(2,1)S(1)} %copy-done.10, bf16[128,768]{1,0:T(8,128)(2,1)S(1)} %copy-done.6, ...), custom_call_target="tpu_custom_call" | custom-call | flops 20000000 | bytes 1000 | tf_op jit(solution)/shard_map/gather_tokens/pallas_call | solution.py:309
  13.9 1.0 %collective-permute-start.8 = (bf16[1,72,768]{2,1,0:T(8,128)(2,1)S(1)}, bf16[1,72,768]{2,1,0:T(8,128)(2,1)S(1)}, u32[]{:S(2)}, u32[]{:S(2)}) collective-permute-start(bf16[1,72,768]{2,1,0:T(8,128)(2,1)S(1)} %bitcast.14), channel_id=1, source_target_pairs={{0,16},{8,24},{16,0},{24,8},{1,17},{9,25},{17,1},{25,9},{2,18},{10... | collective-permute-start | bytes 331784 | tf_op jit(solution)/shard_map/ppermute | solution.py:130
  14.8 0.0 collective-permute-done
  14.9 0.0 copy-start.3
  14.9 1.6 %collective-permute-start.3 = (bf16[2,36,640]{2,1,0:T(8,128)(2,1)S(1)}, bf16[2,36,640]{2,1,0:T(8,128)(2,1)S(1)}, u32[]{:S(2)}, u32[]{:S(2)}) collective-permute-start(bf16[2,36,640]{2,1,0:T(8,128)(2,1)S(1)} %pad_maximum_fusion.4), channel_id=1, source_target_pairs={{0,2},{1,3},{2,0},{3,1},{4,6},{5,7},{6,4},{7,5},{8,10},{9,11},{10,... | collective-permute-start | bytes 276488 | tf_op jit(solution)/shard_map/ppermute | solution.py:130
  16.6 1.6 %collective-permute-start.5 = (bf16[2,36,512]{2,1,0:T(8,128)(2,1)S(1)}, bf16[2,36,512]{2,1,0:T(8,128)(2,1)S(1)}, u32[]{:S(2)}, u32[]{:S(2)}) collective-permute-start(bf16[2,36,512]{2,1,0:T(8,128)(2,1)S(1)} %pad_maximum_fusion.5), channel_id=1, source_target_pairs={{0,1},{1,0},{2,3},{3,2},{4,5},{5,4},{6,7},{7,6},{8,9},{9,8},{10,11... | collective-permute-start | bytes 221192 | tf_op jit(solution)/shard_map/ppermute | solution.py:130
  18.2 2.3 %atom_attention.3.mixed = bf16[1152,128]{1,0:T(8,128)(2,1)S(1)} custom-call(bf16[2,1152,128]{2,1,0:T(8,128)(2,1)S(1)} %copy-done, bf16[2,48,128]{2,1,0:T(8,128)(2,1)S(1)} %collective-permute-done.1.refs_0_, bf16[2,48,128]{2,1,0:T(8,128)(2,1)S(1)} %collective-permute-done.2.refs_1_, bf16[128,128]{1,0:T(8,128)(2,1)S(1)} %copy-done.7, ...), custom_call_target="tpu_custom_call" | custom-call | flops 80000000 | bytes 1000 | tf_op jit(solution)/shard_map/atom_attention/pallas_call | solution.py:239
  20.4 0.0 copy-start.1
  20.4 1.4 %gather_tokens.3 = (f32[72,768]{1,0:T(8,128)S(1)}, bf16[72,768]{1,0:T(8,128)(2,1)S(1)}) custom-call(bf16[1152,128]{1,0:T(8,128)(2,1)S(1)} %atom_attention.3.mixed, bf16[2,1152,128]{2,1,0:T(8,128)(2,1)S(1)} %copy-done, s32[1152]{0:T(1024)S(1)} %copy-done.11, bf16[128,128]{1,0:T(8,128)(2,1)S(1)} %copy-done.10, bf16[128,768]{1,0:T(8,128)(2,1)S(1)} %copy-done.6, ...), custom_call_target="tpu_custom_call" | custom-call | flops 20000000 | bytes 1000 | tf_op jit(solution)/shard_map/gather_tokens/pallas_call | solution.py:309
  21.9 0.0 collective-permute-done.8
  21.9 0.1 collective-permute-start.9
  22.0 0.0 collective-permute-done.3
  22.0 0.7 %collective-permute-start.4 = (bf16[4,36,640]{2,1,0:T(8,128)(2,1)S(1)}, bf16[4,36,640]{2,1,0:T(8,128)(2,1)S(1)}, u32[]{:S(2)}, u32[]{:S(2)}) collective-permute-start(bf16[4,36,640]{2,1,0:T(8,128)(2,1)S(1)} %pad_maximum_fusion.2.refs_0_), channel_id=1, source_target_pairs={{0,1},{1,0},{2,3},{3,2},{4,5},{5,4},{6,7},{7,6},{8,9},{9,8},{10,11... | collective-permute-start | bytes 552968 | tf_op jit(solution)/shard_map/ppermute | solution.py:130
  22.7 0.7 %collective-permute-start.6 = (bf16[4,36,512]{2,1,0:T(8,128)(2,1)S(1)}, bf16[4,36,512]{2,1,0:T(8,128)(2,1)S(1)}, u32[]{:S(2)}, u32[]{:S(2)}) collective-permute-start(bf16[4,36,512]{2,1,0:T(8,128)(2,1)S(1)} %pad_maximum_fusion.3.refs_2_), channel_id=1, source_target_pairs={{0,2},{1,3},{2,0},{3,1},{4,6},{5,7},{6,4},{7,5},{8,10},{9,11},{10,... | collective-permute-start | bytes 442376 | tf_op jit(solution)/shard_map/ppermute | solution.py:130
  23.4 0.9 %collective-permute-start.7 = (bf16[1,72,768]{2,1,0:T(8,128)(2,1)S(1)}, bf16[1,72,768]{2,1,0:T(8,128)(2,1)S(1)}, u32[]{:S(2)}, u32[]{:S(2)}) collective-permute-start(bf16[1,72,768]{2,1,0:T(8,128)(2,1)S(1)} %bitcast.12), channel_id=1, source_target_pairs={{0,16},{8,24},{16,0},{24,8},{1,17},{9,25},{17,1},{25,9},{2,18},{10... | collective-permute-start | bytes 331784 | tf_op jit(solution)/shard_map/ppermute | solution.py:130
  24.4 1.3 %project.2 = (bf16[72,768]{1,0:T(8,128)(2,1)S(1)}, bf16[768,288]{1,0:T(8,128)(2,1)S(1)}, bf16[288,768]{1,0:T(8,128)(2,1)S(1)}, f32[72,768]{1,0:T(8,128)S(1)}) custom-call(bf16[2,72,768]{2,1,0:T(8,128)(2,1)S(1)} %pad_maximum_fusion.near, bf16[2,72,768]{2,1,0:T(8,128)(2,1)S(1)} %collective-permute-done.9.refs_0_, bf16[768,768]{1,0:T(8,128)(2,1)S(1)} %copy-done.4, ...), custom_call_target="tpu_custom_call" | custom-call | flops 40000000 | bytes 1000 | tf_op jit(solution)/shard_map/project/pallas_call | solution.py:351
  25.6 2.5 %collective-permute-done.7 = bf16[1,72,768]{2,1,0:T(8,128)(2,1)S(1)} collective-permute-done((bf16[1,72,768]{2,1,0:T(8,128)(2,1)S(1)}, bf16[1,72,768]{2,1,0:T(8,128)(2,1)S(1)}, u32[]{:S(2)}, u32[]{:S(2)}) %collective-permute-start.7) | collective-permute-done | bytes 110624 | tf_op jit(solution)/shard_map/ppermute | solution.py:130
  28.1 0.9 %collective-permute-done.6.refs_3_ = bf16[4,36,512]{2,1,0:T(8,128)(2,1)S(1)} collective-permute-done((bf16[4,36,512]{2,1,0:T(8,128)(2,1)S(1)}, bf16[4,36,512]{2,1,0:T(8,128)(2,1)S(1)}, u32[]{:S(2)}, u32[]{:S(2)}) %collective-permute-start.6) | collective-permute-done | bytes 147488 | tf_op jit(solution)/shard_map/ppermute | solution.py:130
  29.0 0.5 %collective-permute-done.4.refs_1_ = bf16[4,36,640]{2,1,0:T(8,128)(2,1)S(1)} collective-permute-done((bf16[4,36,640]{2,1,0:T(8,128)(2,1)S(1)}, bf16[4,36,640]{2,1,0:T(8,128)(2,1)S(1)}, u32[]{:S(2)}, u32[]{:S(2)}) %collective-permute-start.4) | collective-permute-done | bytes 184352 | tf_op jit(solution)/shard_map/ppermute | solution.py:130
  29.6 0.1 collective-permute-start.10
  29.7 0.8 %turn_bias.1.bias = f32[1152,288]{1,0:T(8,128)S(1)} custom-call(bf16[4,36,640]{2,1,0:T(8,128)(2,1)S(1)} %pad_maximum_fusion.2.refs_0_, bf16[4,36,640]{2,1,0:T(8,128)(2,1)S(1)} %collective-permute-done.4.refs_1_, bf16[4,36,512]{2,1,0:T(8,128)(2,1)S(1)} %pad_maximum_fusion.3.refs_2_, bf16[4,36,512]{2,1,0:T(8,128)(2,1)S(1)} %collective-permute-done.6.refs_3_), custom_call_target="tpu_custom_call" | custom-call | flops 20000000 | bytes 1000 | tf_op jit(solution)/shard_map/turn_bias/pallas_call | solution.py:393
  30.4 0.9 %project.3 = (bf16[72,768]{1,0:T(8,128)(2,1)S(1)}, bf16[144,768]{1,0:T(8,128)(2,1)S(1)}, bf16[144,768]{1,0:T(8,128)(2,1)S(1)}, f32[72,768]{1,0:T(8,128)S(1)}) custom-call(bf16[2,72,768]{2,1,0:T(8,128)(2,1)S(1)} %pad_maximum_fusion.1.near, bf16[768,768]{1,0:T(8,128)(2,1)S(1)} %copy-done.4, bf16[768,768]{1,0:T(8,128)(2,1)S(1)} %copy-done.1, ...), custom_call_target="tpu_custom_call" | custom-call | flops 40000000 | bytes 1000 | tf_op jit(solution)/shard_map/project/pallas_call | solution.py:351
  31.4 3.5 %attend.1 = bf16[2,72,768]{2,1,0:T(8,128)(2,1)} custom-call(f32[1152,288]{1,0:T(8,128)S(1)} %turn_bias.1.bias, bf16[72,768]{1,0:T(8,128)(2,1)S(1)} %get-tuple-element.45.refs_0_, bf16[768,288]{1,0:T(8,128)(2,1)S(1)} %get-tuple-element.46.refs_1_, bf16[288,768]{1,0:T(8,128)(2,1)S(1)} %get-tuple-element.47.refs_2_, f32[72,768]{1,0:T(8,128)S(1)} %get-tuple-element.48.refs_3_, ...), custom_call_target="tpu_custom_call" | custom-call | flops 60000000 | bytes 1000 | tf_op jit(solution)/shard_map/attend/pallas_call | solution.py:479
  (35 shorter events, 0.2 us)
Async XLA Ops:
  0.0 9.3 %copy-start = (bf16[2,1152,128]{2,1,0:T(8,128)(2,1)S(1)}, bf16[2,1152,128]{2,1,0:T(8,128)(2,1)}, u32[]{:S(2)}) copy-start(bf16[2,1152,128]{2,1,0:T(8,128)(2,1)} %feat.7) | copy-start | bytes 1769476
  0.0 9.3 %copy-start.7 = (bf16[128,128]{1,0:T(8,128)(2,1)S(1)}, bf16[128,128]{1,0:T(8,128)(2,1)}, u32[]{:S(2)}) copy-start(bf16[128,128]{1,0:T(8,128)(2,1)} %refs_2_.7) | copy-start | bytes 98308
  0.0 9.3 %copy-start.8 = (bf16[128,128]{1,0:T(8,128)(2,1)S(1)}, bf16[128,128]{1,0:T(8,128)(2,1)}, u32[]{:S(2)}) copy-start(bf16[128,128]{1,0:T(8,128)(2,1)} %refs_3_.5) | copy-start | bytes 98308
  0.0 9.3 %copy-start.9 = (bf16[128,128]{1,0:T(8,128)(2,1)S(1)}, bf16[128,128]{1,0:T(8,128)(2,1)}, u32[]{:S(2)}) copy-start(bf16[128,128]{1,0:T(8,128)(2,1)} %refs_4_.5) | copy-start | bytes 98308
  0.0 11.7 %copy-start.6 = (bf16[128,768]{1,0:T(8,128)(2,1)S(1)}, bf16[128,768]{1,0:T(8,128)(2,1)}, u32[]{:S(2)}) copy-start(bf16[128,768]{1,0:T(8,128)(2,1)} %agg.3) | copy-start | bytes 589828
  0.0 11.7 %copy-start.10 = (bf16[128,128]{1,0:T(8,128)(2,1)S(1)}, bf16[128,128]{1,0:T(8,128)(2,1)}, u32[]{:S(2)}) copy-start(bf16[128,128]{1,0:T(8,128)(2,1)} %wo.3) | copy-start | bytes 98308
  0.0 11.7 %copy-start.11 = (s32[1152]{0:T(1024)S(1)}, s32[1152]{0:T(1024)}, u32[]{:S(2)}) copy-start(s32[1152]{0:T(1024)} %token_.3) | copy-start | bytes 13828
  0.0 11.7 %copy-start.12 = (f32[768]{0:T(1024)S(1)}, f32[768]{0:T(1024)}, u32[]{:S(2)}) copy-start(f32[768]{0:T(1024)} %gain.3) | copy-start | bytes 9220
  3.6 11.2 %copy-start.13 = (bf16[36,1152]{1,0:T(8,128)(2,1)S(1)}, bf16[36,1152]{1,0:T(8,128)(2,1)}, u32[]{:S(2)}) copy-start(bf16[36,1152]{1,0:T(8,128)(2,1)} %get-tuple-element.37) | copy-start | bytes 248836
  3.6 11.2 %collective-permute-start = (bf16[36,1152]{1,0:T(8,128)(2,1)}, bf16[36,1152]{1,0:T(8,128)(2,1)S(1)}, u32[]{:S(2)}, u32[]{:S(2)}) collective-permute-start(bf16[36,1152]{1,0:T(8,128)(2,1)} %get-tuple-element.37), channel_id=1, source_target_pairs={{0,4},{1,5},{2,6},{3,7},{4,0},{5,1},{6,2},{7,3},{8,12},{9,13},{10,... | collective-permute-start | bytes 248840 | tf_op jit(solution)/shard_map/ppermute | solution.py:130
  7.7 4.0 %collective-permute-start.1 = (bf16[2,48,128]{2,1,0:T(8,128)(2,1)}, bf16[2,48,128]{2,1,0:T(8,128)(2,1)S(1)}, u32[]{:S(2)}, u32[]{:S(2)}) collective-permute-start(bf16[2,48,128]{2,1,0:T(8,128)(2,1)} %get-tuple-element.34), channel_id=1, source_target_pairs={{0,8},{8,0},{16,24},{24,16},{1,9},{9,1},{17,25},{25,17},{2,10},{10... | collective-permute-start | bytes 73736 | tf_op jit(solution)/shard_map/ppermute | solution.py:130
  7.7 4.0 %collective-permute-start.2 = (bf16[2,48,128]{2,1,0:T(8,128)(2,1)}, bf16[2,48,128]{2,1,0:T(8,128)(2,1)S(1)}, u32[]{:S(2)}, u32[]{:S(2)}) collective-permute-start(bf16[2,48,128]{2,1,0:T(8,128)(2,1)} %get-tuple-element.35), channel_id=1, source_target_pairs={{8,16},{24,0},{16,8},{0,24},{9,17},{25,1},{17,9},{1,25},{10,18},{2... | collective-permute-start | bytes 73736 | tf_op jit(solution)/shard_map/ppermute | solution.py:515
  9.3 15.0 %copy-start.5 = (bf16[768,768]{1,0:T(8,128)(2,1)S(1)}, bf16[768,768]{1,0:T(8,128)(2,1)}, u32[]{:S(2)}) copy-start(bf16[768,768]{1,0:T(8,128)(2,1)} %refs_3_.7) | copy-start | bytes 3538948
  11.7 12.6 %copy-start.4 = (bf16[768,768]{1,0:T(8,128)(2,1)S(1)}, bf16[768,768]{1,0:T(8,128)(2,1)}, u32[]{:S(2)}) copy-start(bf16[768,768]{1,0:T(8,128)(2,1)} %refs_0_.3) | copy-start | bytes 3538948
  13.9 8.0 %collective-permute-start.8 = (bf16[1,72,768]{2,1,0:T(8,128)(2,1)S(1)}, bf16[1,72,768]{2,1,0:T(8,128)(2,1)S(1)}, u32[]{:S(2)}, u32[]{:S(2)}) collective-permute-start(bf16[1,72,768]{2,1,0:T(8,128)(2,1)S(1)} %bitcast.14), channel_id=1, source_target_pairs={{0,16},{8,24},{16,0},{24,8},{1,17},{9,25},{17,1},{25,9},{2,18},{10... | collective-permute-start | bytes 331784 | tf_op jit(solution)/shard_map/ppermute | solution.py:130
  14.9 9.5 %copy-start.3 = (bf16[768,768]{1,0:T(8,128)(2,1)S(1)}, bf16[768,768]{1,0:T(8,128)(2,1)}, u32[]{:S(2)}) copy-start(bf16[768,768]{1,0:T(8,128)(2,1)} %refs_13_.1) | copy-start | bytes 3538948
  14.9 7.1 %collective-permute-start.3 = (bf16[2,36,640]{2,1,0:T(8,128)(2,1)S(1)}, bf16[2,36,640]{2,1,0:T(8,128)(2,1)S(1)}, u32[]{:S(2)}, u32[]{:S(2)}) collective-permute-start(bf16[2,36,640]{2,1,0:T(8,128)(2,1)S(1)} %pad_maximum_fusion.4), channel_id=1, source_target_pairs={{0,2},{1,3},{2,0},{3,1},{4,6},{5,7},{6,4},{7,5},{8,10},{9,11},{10,... | collective-permute-start | bytes 276488 | tf_op jit(solution)/shard_map/ppermute | solution.py:130
  16.6 5.4 %collective-permute-start.5 = (bf16[2,36,512]{2,1,0:T(8,128)(2,1)S(1)}, bf16[2,36,512]{2,1,0:T(8,128)(2,1)S(1)}, u32[]{:S(2)}, u32[]{:S(2)}) collective-permute-start(bf16[2,36,512]{2,1,0:T(8,128)(2,1)S(1)} %pad_maximum_fusion.5), channel_id=1, source_target_pairs={{0,1},{1,0},{2,3},{3,2},{4,5},{5,4},{6,7},{7,6},{8,9},{9,8},{10,11... | collective-permute-start | bytes 221192 | tf_op jit(solution)/shard_map/ppermute | solution.py:130
  18.1 6.2 %copy-start.2 = (bf16[768,768]{1,0:T(8,128)(2,1)S(1)}, bf16[768,768]{1,0:T(8,128)(2,1)}, u32[]{:S(2)}) copy-start(bf16[768,768]{1,0:T(8,128)(2,1)} %refs_12_.1) | copy-start | bytes 3538948
  20.4 3.9 %copy-start.1 = (bf16[768,768]{1,0:T(8,128)(2,1)S(1)}, bf16[768,768]{1,0:T(8,128)(2,1)}, u32[]{:S(2)}) copy-start(bf16[768,768]{1,0:T(8,128)(2,1)} %refs_11_.1) | copy-start | bytes 3538948
  21.9 2.4 %collective-permute-start.9 = (bf16[2,72,768]{2,1,0:T(8,128)(2,1)S(1)}, bf16[2,72,768]{2,1,0:T(8,128)(2,1)S(1)}, u32[]{:S(2)}, u32[]{:S(2)}) collective-permute-start(bf16[2,72,768]{2,1,0:T(8,128)(2,1)S(1)} %pad_maximum_fusion.near), channel_id=1, source_target_pairs={{0,8},{8,0},{16,24},{24,16},{1,9},{9,1},{17,25},{25,17},{2,10},{10... | collective-permute-start | bytes 663560 | tf_op jit(solution)/shard_map/ppermute | solution.py:130
  22.0 7.5 %collective-permute-start.4 = (bf16[4,36,640]{2,1,0:T(8,128)(2,1)S(1)}, bf16[4,36,640]{2,1,0:T(8,128)(2,1)S(1)}, u32[]{:S(2)}, u32[]{:S(2)}) collective-permute-start(bf16[4,36,640]{2,1,0:T(8,128)(2,1)S(1)} %pad_maximum_fusion.2.refs_0_), channel_id=1, source_target_pairs={{0,1},{1,0},{2,3},{3,2},{4,5},{5,4},{6,7},{7,6},{8,9},{9,8},{10,11... | collective-permute-start | bytes 552968 | tf_op jit(solution)/shard_map/ppermute | solution.py:130
  22.7 6.3 %collective-permute-start.6 = (bf16[4,36,512]{2,1,0:T(8,128)(2,1)S(1)}, bf16[4,36,512]{2,1,0:T(8,128)(2,1)S(1)}, u32[]{:S(2)}, u32[]{:S(2)}) collective-permute-start(bf16[4,36,512]{2,1,0:T(8,128)(2,1)S(1)} %pad_maximum_fusion.3.refs_2_), channel_id=1, source_target_pairs={{0,2},{1,3},{2,0},{3,1},{4,6},{5,7},{6,4},{7,5},{8,10},{9,11},{10,... | collective-permute-start | bytes 442376 | tf_op jit(solution)/shard_map/ppermute | solution.py:130
  23.4 4.7 %collective-permute-start.7 = (bf16[1,72,768]{2,1,0:T(8,128)(2,1)S(1)}, bf16[1,72,768]{2,1,0:T(8,128)(2,1)S(1)}, u32[]{:S(2)}, u32[]{:S(2)}) collective-permute-start(bf16[1,72,768]{2,1,0:T(8,128)(2,1)S(1)} %bitcast.12), channel_id=1, source_target_pairs={{0,16},{8,24},{16,0},{24,8},{1,17},{9,25},{17,1},{25,9},{2,18},{10... | collective-permute-start | bytes 331784 | tf_op jit(solution)/shard_map/ppermute | solution.py:130
  29.6 1.8 %collective-permute-start.10 = (bf16[2,72,768]{2,1,0:T(8,128)(2,1)S(1)}, bf16[2,72,768]{2,1,0:T(8,128)(2,1)S(1)}, u32[]{:S(2)}, u32[]{:S(2)}) collective-permute-start(bf16[2,72,768]{2,1,0:T(8,128)(2,1)S(1)} %pad_maximum_fusion.1.near), channel_id=1, source_target_pairs={{0,8},{8,0},{16,24},{24,16},{1,9},{9,1},{17,25},{25,17},{2,10},{10... | collective-permute-start | bytes 663560 | tf_op jit(solution)/shard_map/ppermute | solution.py:130

commit v11 on v10

--- a/solution.py
+++ b/solution.py
@@ -61,13 +61,31 @@
     return held
 
 
-def bias_kernel(head, tail, pair, mask, weight, out, inner, outer, normed):
+def normalise_kernel(pair, normed):
+    for k in range(0, pair.shape[0], 6):
+        normed[k : k + 6] = layer_norm(pair[k : k + 6].astype(F32))
+
+
+def normalise_pairs(pair_cond):
+    rows, cols, chans = pair_cond.shape
+    vmem = pl.BlockSpec(memory_space=pltpu.VMEM)
+    return pl.pallas_call(
+        normalise_kernel,
+        out_shape=jax.ShapeDtypeStruct((cols, rows, chans), F32),
+        in_specs=[vmem],
+        out_specs=vmem,
+        compiler_params=pltpu.CompilerParams(vmem_limit_bytes=8 * MIB),
+        cost_estimate=cost(1),
+        name="normalise_pairs",
+    )(jnp.transpose(pair_cond, (1, 0, 2)))
+
+
+def bias_kernel(feat, normed, mask, weight, out, inner, outer):
     odd = lax.axis_index("row") % 2 == 1
-    inner[...] = jnp.where(odd, head[...], tail[...])
-    outer[...] = jnp.where(odd, tail[...], head[...])
-    cols, rows, chans = pair.shape
-    for k in range(0, cols, 6):
-        normed[k : k + 6] = layer_norm(pair[k : k + 6].astype(F32))
+    head, tail = feat[:, :RIM], feat[:, feat.shape[1] - RIM :]
+    inner[...] = jnp.where(odd, head, tail)
+    outer[...] = jnp.where(odd, tail, head)
+    cols, rows, chans = normed.shape
     spread = (iota((HEADS, LANES), 1) // SUB == iota((HEADS, LANES), 0)).astype(BF16)
     wide = lax.dot_general(weight[...], spread, (((0,), (0,)), ((), ())), preferred_element_type=F32).astype(BF16)
     tall = cols * SUB
@@ -92,34 +110,22 @@
 
 
 def pair_bias(feat, pair_cond, token_mask, pair_weight):
-    rows, cols, chans = pair_cond.shape
-    samples, atoms, width = feat.shape
-    edge = (samples, RIM, width)
-
-    def whole(*shape):
-        return pl.BlockSpec(shape, lambda i: (0,) * len(shape))
-
+    rows, cols, _ = pair_cond.shape
+    edge = (feat.shape[0], RIM, feat.shape[2])
+    vmem = pl.BlockSpec(memory_space=pltpu.VMEM)
     return pl.pallas_call(
         bias_kernel,
-        grid=(1,),
         out_shape=[
             jax.ShapeDtypeStruct((cols, rows * HEADS), BF16),
             jax.ShapeDtypeStruct(edge, BF16),
             jax.ShapeDtypeStruct(edge, BF16),
         ],
-        in_specs=[
-            pl.BlockSpec(edge, lambda i: (0, 0, 0)),
-            pl.BlockSpec(edge, lambda i: (0, atoms // RIM - 1, 0)),
-            whole(cols, rows, chans),
-            whole(cols),
-            whole(HEADS, chans),
-        ],
-        out_specs=[whole(cols, rows * HEADS), whole(*edge), whole(*edge)],
-        scratch_shapes=[pltpu.VMEM((cols, rows, chans), F32)],
-        compiler_params=pltpu.CompilerParams(vmem_limit_bytes=60 * MIB),
+        in_specs=[vmem] * 4,
+        out_specs=[vmem] * 3,
+        compiler_params=pltpu.CompilerParams(vmem_limit_bytes=8 * MIB),
         cost_estimate=cost(3),
         name="pair_bias",
-    )(feat, feat, jnp.transpose(pair_cond, (1, 0, 2)), token_mask, pair_weight.T)
+    )(feat, normalise_pairs(pair_cond), token_mask, pair_weight.T)
 
 
 def after(value, *others):
@@ -331,75 +337,90 @@
     return jnp.concatenate([blocks[j].astype(F32) for j in range(blocks.shape[0])], axis=0).astype(BF16)
 
 
-def project_kernel(near, *refs):
-    *far, wq, wk, wv, wg, wo, q, k, v, gate = refs
-    x = jnp.concatenate([stack(blocks) for blocks in (near, *far)], axis=0)
+def project_kernel(near, far, wq, wk, wv, wg, wo, q, kt, v, gate):
+    x = jnp.concatenate([stack(near), stack(far)], axis=0)
     q[...] = dot(near[0], wq[...]).astype(BF16)
     gate[...] = jax.nn.sigmoid(dot(near[0], wg[...]))
-    if far:
-        for c in range(0, x.shape[1], 2 * LANES):
-            k[c : c + 2 * LANES] = dot(x, wk[:, c : c + 2 * LANES]).T.astype(BF16)
-    else:
-        k[...] = dot(x, wk[...]).astype(BF16)
+    for c in range(0, x.shape[1], 2 * LANES):
+        kt[c : c + 2 * LANES] = dot(x, wk[:, c : c + 2 * LANES]).T.astype(BF16)
     v[...] = dot(x, wv[...]).astype(BF16)
 
 
-def project(blocks, wq, wk, wv, wg, wo):
-    half, rows, width = blocks[0].shape
-    keys = len(blocks) * half * rows
+def project(near, far, wq, wk, wv, wg, wo):
+    half, rows, width = near.shape
+    keys = 2 * half * rows
     vmem = pl.BlockSpec(memory_space=pltpu.VMEM)
     return pl.pallas_call(
         project_kernel,
         out_shape=[
             jax.ShapeDtypeStruct((rows, width), BF16),
-            jax.ShapeDtypeStruct((width, keys) if len(blocks) > 1 else (keys, width), BF16),
+            jax.ShapeDtypeStruct((width, keys), BF16),
             jax.ShapeDtypeStruct((keys, width), BF16),
             jax.ShapeDtypeStruct((rows, width), F32),
         ],
-        in_specs=[vmem] * (5 + len(blocks)),
+        in_specs=[vmem] * 7,
         out_specs=[vmem] * 4,
         compiler_params=pltpu.CompilerParams(vmem_limit_bytes=24 * MIB),
         cost_estimate=cost(2),
         name="project",
-    )(*blocks, wq, wk, wv, wg, wo)
-
-
-def turn_kernel(orders, row_bits, *refs):
-    *halves, out, tall = refs
+    )(near, far, wq, wk, wv, wg, wo)
+
+
+def turn_kernel(orders, row_bits, near, wq, wk, wv, wg, *refs):
+    *halves, q, k, v, gate, out, tall = refs
+    x = stack(near)
+    width = x.shape[1]
+
+    def project_columns(c):
+        lanes = slice(c, c + 2 * LANES)
+        q[:, lanes] = dot(near[0], wq[:, lanes]).astype(BF16)
+        k[:, lanes] = dot(x, wk[:, lanes]).astype(BF16)
+        v[:, lanes] = dot(x, wv[:, lanes]).astype(BF16)
+        gate[:, lanes] = jax.nn.sigmoid(dot(near[0], wg[:, lanes]))
+
     rows = out.shape[0] // HEADS
     me = lax.axis_index("sample")
     at = 0
-    for near, far, bits in zip(halves[::2], halves[1::2], orders):
-        half, cols, wide = near.shape
+    for i, (mine, other, bits) in enumerate(zip(halves[::2], halves[1::2], orders)):
+        half, cols, wide = mine.shape
         places = places_of(bits)
         for j in range(2 * half):
             place = sum(jnp.where(me ^ j == p, i, 0) for i, p in enumerate(places))
-            block = jnp.where(place < half, near[place % half], far[place % half])
+            block = jnp.where(place < half, mine[place % half], other[place % half])
             tall[j * cols : (j + 1) * cols, at : at + wide] = block.astype(F32)
         at += wide
     starts = [pl.multiple_of((lax.axis_index("row") ^ p) * rows, SUB) for p in places_of(row_bits)]
     for g in range(rows // SUB):
+        if g * 2 * LANES < width:
+            project_columns(g * 2 * LANES)
         lanes = slice(g * LANES, (g + 1) * LANES)
         turned = jnp.concatenate([tall[pl.ds(start, rows), lanes] for start in starts], axis=0).T
         for h in range(HEADS):
             out[h * rows + g * SUB : h * rows + (g + 1) * SUB] = turned[h * SUB : (h + 1) * SUB] * LOG2E
 
 
-def turn_bias(orders, row_bits, halves):
+def turn_bias(orders, row_bits, halves, near, wq, wk, wv, wg):
     half, cols, _ = halves[0].shape
     keys = 2 * half * cols
-    wide = sum(near.shape[2] for near in halves[::2])
+    wide = sum(part.shape[2] for part in halves[::2])
+    blocks, rows, width = near.shape
     vmem = pl.BlockSpec(memory_space=pltpu.VMEM)
     return pl.pallas_call(
         functools.partial(turn_kernel, orders, row_bits),
-        out_shape=jax.ShapeDtypeStruct((wide, keys), F32),
-        in_specs=[vmem] * len(halves),
-        out_specs=vmem,
+        out_shape=[
+            jax.ShapeDtypeStruct((rows, width), BF16),
+            jax.ShapeDtypeStruct((blocks * rows, width), BF16),
+            jax.ShapeDtypeStruct((blocks * rows, width), BF16),
+            jax.ShapeDtypeStruct((rows, width), F32),
+            jax.ShapeDtypeStruct((wide, keys), F32),
+        ],
+        in_specs=[vmem] * (5 + len(halves)),
+        out_specs=[vmem] * 5,
         scratch_shapes=[pltpu.VMEM((keys, wide), F32)],
         compiler_params=pltpu.CompilerParams(vmem_limit_bytes=24 * MIB),
         cost_estimate=cost(1),
         name="turn_bias",
-    )(*halves)
+    )(near, wq, wk, wv, wg, *halves)
 
 
 def attend_kernel(samples, bias, *refs):
@@ -553,9 +574,11 @@
                 near = widen(near, "row", bit, *others)
         far = swap(near, "row", row_bits[-1])
         near = after(near, held)
-        blocks = (near, far) if s < samples - 1 else (near,)
-        parts.append((*project(blocks, *weights), inputs[s]))
-    bias = turn_bias(orders, row_bits, after(halves, near))
+        if s < samples - 1:
+            parts.append((*project(near, far, *weights), inputs[s]))
+        else:
+            *part, bias = turn_bias(orders, row_bits, halves, near, *weights[:4])
+            parts.append((*part, inputs[s]))
     return attend(bias, parts, far, key_weight, value_weight, out_weight)
 
 

time: 35.1 us -> 34.9 us (level)
  Pallas kernels: 18.2 us -> 16.6 us
  local copies, waits for them, and re-layouts: 0.08 us -> 1.25 us
    unnamed x28 -> x32, local copies, waits for them, and re-layouts: 0.06 us -> 1.23 us
    pallas_call x1 -> x2, Pallas kernels: 3.57 us -> 2.55 us  [the longest x1 1.66 us: pair_bias(): pl.pallas_call(bias_kernel, out_shape=[jax.ShapeDtypeStruct((cols, rows *...]
    pallas_call x2 -> x1, Pallas kernels: 2.21 us -> 1.28 us  [project(): pl.pallas_call(project_kernel, out_shape=[jax.ShapeDtypeStruct((rows, wid...]
    ppermute x10, starting transfers between devices: 10.6 us -> 11 us  [swap(): lax.ppermute(held, axis, [(i, i ^ far) for i in range(lax.axis_size(axis))])]
  transfers between devices with their start and end apart: 11 -> 11, of which waited for: 3 -> 4; matrix products, arithmetic and copies ran while one was open for 0% -> 0% of each run, Pallas kernels for 32% -> 30%
where the time goes in v11:
time: 34.9 us; the launch traced here: 34.8 us
  Pallas kernels  16.6 us (48%)
  starting transfers between devices  12.6 us (36%)
  waiting for transfers between devices  3.77 us (11%)
  local copies, waits for them, and re-layouts  1.25 us (4%)
    ppermute x10, starting transfers between devices, swap(): lax.ppermute(held, axis, [(i, i ^ far) for i in range(lax.axis_size(axis))])  11 us
    pallas_call x2, Pallas kernels, atom_attention(): pl.pallas_call(functools.partial(atom_kernel, sample), out_shape=jax.Shap...  4.62 us
    ppermute x10, waiting for transfers between devices, swap(): lax.ppermute(held, axis, [(i, i ^ far) for i in range(lax.axis_size(axis))])  3.77 us
    pallas_call x1, Pallas kernels, attend(): pl.pallas_call(functools.partial(attend_kernel, len(parts)), out_shape=ja...  3.59 us
    pallas_call x2, Pallas kernels, gather_tokens(): pl.pallas_call(functools.partial(gather_kernel, sample), out_shape=[jax.S...  3.51 us
    pallas_call x1, Pallas kernels, pair_bias(): pl.pallas_call(bias_kernel, out_shape=[jax.ShapeDtypeStruct((cols, rows *...  1.66 us
    ppermute x1, starting transfers between devices, shards(): lax.ppermute(outer, 'row', odd_pairs + [(j, i) for i, j in odd_pairs])  1.63 us
    pallas_call x1, Pallas kernels, project(): pl.pallas_call(project_kernel, out_shape=[jax.ShapeDtypeStruct((rows, wid...  1.28 us
  transfers between devices with their start and end apart: 11, of which 4 were waited for; matrix products, arithmetic and copies ran while one was open for 0% of the time, Pallas kernels for 30%

profile of v11, /device:TPU:0, one launch (start us, length us, event | category | flops | bytes accessed | tf_op | source)
XLA Modules:
  0.0 34.8 jit_solution(15959641377398207196)
XLA Ops:
  0.0 1.2 %copy-done.7 = bf16[72,36,128]{2,0,1:T(8,128)(2,1)S(1)} copy-done((bf16[72,36,128]{2,0,1:T(8,128)(2,1)S(1)}, bf16[72,36,128]{2,0,1:T(8,128)(2,1)}, u32[]{:S(2)}) %copy-start.7) | copy-done | bytes 663576
  1.2 0.9 %normalise_pairs.1.normed = f32[36,72,128]{2,1,0:T(8,128)S(1)} custom-call(bf16[36,72,128]{2,1,0:T(8,128)(2,1)S(1)} %bitcast.12), custom_call_target="tpu_custom_call" | custom-call | flops 20000000 | bytes 1000 | tf_op jit(solution)/shard_map/normalise_pairs/pallas_call | solution.py:72
  2.1 0.0 copy-start.8
  2.1 0.0 copy-start.9
  2.1 0.0 copy-start.10
  2.1 0.0 copy-start.6
  2.1 0.0 copy-start.11
  2.1 0.0 copy-start.12
  2.2 0.0 copy-start.13
  2.2 1.7 %pair_bias.1 = (bf16[36,1152]{1,0:T(8,128)(2,1)S(1)}, bf16[2,48,128]{2,1,0:T(8,128)(2,1)S(1)}, bf16[2,48,128]{2,1,0:T(8,128)(2,1)S(1)}) custom-call(bf16[2,1152,128]{2,1,0:T(8,128)(2,1)S(1)} %copy-done, f32[36,72,128]{2,1,0:T(8,128)S(1)} %normalise_pairs.1.normed, s32[36]{0:T(128)S(1)} %copy-done.15, bf16[16,128]{1,0:T(8,128)(2,1)S(1)} %bitcast.17), custom_call_target="tpu_custom_call" | custom-call | flops 60000000 | bytes 1000 | tf_op jit(solution)/shard_map/pair_bias/pallas_call | solution.py:116
  3.8 4.1 %collective-permute-start.1 = (bf16[36,1152]{1,0:T(8,128)(2,1)S(1)}, bf16[36,1152]{1,0:T(8,128)(2,1)S(1)}, u32[]{:S(2)}, u32[]{:S(2)}) collective-permute-start(bf16[36,1152]{1,0:T(8,128)(2,1)S(1)} %get-tuple-element.34), channel_id=1, source_target_pairs={{0,4},{1,5},{2,6},{3,7},{4,0},{5,1},{6,2},{7,3},{8,12},{9,13},{10,... | collective-permute-start | bytes 248840 | tf_op jit(solution)/shard_map/ppermute | solution.py:136
  7.9 1.6 %collective-permute-start.2 = (bf16[2,48,128]{2,1,0:T(8,128)(2,1)S(1)}, bf16[2,48,128]{2,1,0:T(8,128)(2,1)S(1)}, u32[]{:S(2)}, u32[]{:S(2)}) collective-permute-start(bf16[2,48,128]{2,1,0:T(8,128)(2,1)S(1)} %get-tuple-element.32), channel_id=1, source_target_pairs={{8,16},{24,0},{16,8},{0,24},{9,17},{25,1},{17,9},{1,25},{10,18},{2... | collective-permute-start | bytes 73736 | tf_op jit(solution)/shard_map/ppermute | solution.py:536
  9.6 2.4 %atom_attention.2.mixed = bf16[1152,128]{1,0:T(8,128)(2,1)S(1)} custom-call(bf16[2,1152,128]{2,1,0:T(8,128)(2,1)S(1)} %copy-done, bf16[128,128]{1,0:T(8,128)(2,1)S(1)} %copy-done.8, bf16[128,128]{1,0:T(8,128)(2,1)S(1)} %copy-done.9, bf16[128,128]{1,0:T(8,128)(2,1)S(1)} %copy-done.10), custom_call_target="tpu_custom_call" | custom-call | flops 80000000 | bytes 1000 | tf_op jit(solution)/shard_map/atom_attention/pallas_call | solution.py:245
  12.0 0.0 copy-start.4
  12.0 2.1 %gather_tokens.2 = (f32[72,768]{1,0:T(8,128)S(1)}, bf16[72,768]{1,0:T(8,128)(2,1)S(1)}) custom-call(bf16[1152,128]{1,0:T(8,128)(2,1)S(1)} %atom_attention.2.mixed, bf16[2,1152,128]{2,1,0:T(8,128)(2,1)S(1)} %copy-done, s32[1152]{0:T(1024)S(1)} %copy-done.12, bf16[128,128]{1,0:T(8,128)(2,1)S(1)} %copy-done.11, bf16[128,768]{1,0:T(8,128)(2,1)S(1)} %copy-done.6, ...), custom_call_target="tpu_custom_call" | custom-call | flops 20000000 | bytes 1000 | tf_op jit(solution)/shard_map/gather_tokens/pallas_call | solution.py:315
  14.1 0.8 %collective-permute-start.4 = (bf16[1,72,768]{2,1,0:T(8,128)(2,1)S(1)}, bf16[1,72,768]{2,1,0:T(8,128)(2,1)S(1)}, u32[]{:S(2)}, u32[]{:S(2)}) collective-permute-start(bf16[1,72,768]{2,1,0:T(8,128)(2,1)S(1)} %bitcast.15), channel_id=1, source_target_pairs={{0,16},{8,24},{16,0},{24,8},{1,17},{9,25},{17,1},{25,9},{2,18},{10... | collective-permute-start | bytes 331784 | tf_op jit(solution)/shard_map/ppermute | solution.py:136
  15.0 1.6 %collective-permute-start.6 = (bf16[2,36,512]{2,1,0:T(8,128)(2,1)S(1)}, bf16[2,36,512]{2,1,0:T(8,128)(2,1)S(1)}, u32[]{:S(2)}, u32[]{:S(2)}) collective-permute-start(bf16[2,36,512]{2,1,0:T(8,128)(2,1)S(1)} %pad_maximum_fusion.5), channel_id=1, source_target_pairs={{0,1},{1,0},{2,3},{3,2},{4,5},{5,4},{6,7},{7,6},{8,9},{9,8},{10,11... | collective-permute-start | bytes 221192 | tf_op jit(solution)/shard_map/ppermute | solution.py:136
  16.6 1.6 %collective-permute-start.5 = (bf16[2,36,640]{2,1,0:T(8,128)(2,1)S(1)}, bf16[2,36,640]{2,1,0:T(8,128)(2,1)S(1)}, u32[]{:S(2)}, u32[]{:S(2)}) collective-permute-start(bf16[2,36,640]{2,1,0:T(8,128)(2,1)S(1)} %pad_maximum_fusion.4), channel_id=1, source_target_pairs={{0,2},{1,3},{2,0},{3,1},{4,6},{5,7},{6,4},{7,5},{8,10},{9,11},{10,... | collective-permute-start | bytes 276488 | tf_op jit(solution)/shard_map/ppermute | solution.py:136
  18.2 2.3 %atom_attention.3.mixed = bf16[1152,128]{1,0:T(8,128)(2,1)S(1)} custom-call(bf16[2,1152,128]{2,1,0:T(8,128)(2,1)S(1)} %copy-done, bf16[2,48,128]{2,1,0:T(8,128)(2,1)S(1)} %collective-permute-done.refs_0_, bf16[2,48,128]{2,1,0:T(8,128)(2,1)S(1)} %collective-permute-done.2.refs_1_, bf16[128,128]{1,0:T(8,128)(2,1)S(1)} %copy-done.8, ...), custom_call_target="tpu_custom_call" | custom-call | flops 80000000 | bytes 1000 | tf_op jit(solution)/shard_map/atom_attention/pallas_call | solution.py:245
  20.5 1.4 %gather_tokens.3 = (f32[72,768]{1,0:T(8,128)S(1)}, bf16[72,768]{1,0:T(8,128)(2,1)S(1)}) custom-call(bf16[1152,128]{1,0:T(8,128)(2,1)S(1)} %atom_attention.3.mixed, bf16[2,1152,128]{2,1,0:T(8,128)(2,1)S(1)} %copy-done, s32[1152]{0:T(1024)S(1)} %copy-done.12, bf16[128,128]{1,0:T(8,128)(2,1)S(1)} %copy-done.11, bf16[128,768]{1,0:T(8,128)(2,1)S(1)} %copy-done.6, ...), custom_call_target="tpu_custom_call" | custom-call | flops 20000000 | bytes 1000 | tf_op jit(solution)/shard_map/gather_tokens/pallas_call | solution.py:315
  21.9 0.1 collective-permute-start.7
  22.1 0.6 %collective-permute-start.8 = (bf16[4,36,640]{2,1,0:T(8,128)(2,1)S(1)}, bf16[4,36,640]{2,1,0:T(8,128)(2,1)S(1)}, u32[]{:S(2)}, u32[]{:S(2)}) collective-permute-start(bf16[4,36,640]{2,1,0:T(8,128)(2,1)S(1)} %pad_maximum_fusion.2.refs_0_), channel_id=1, source_target_pairs={{0,1},{1,0},{2,3},{3,2},{4,5},{5,4},{6,7},{7,6},{8,9},{9,8},{10,11... | collective-permute-start | bytes 552968 | tf_op jit(solution)/shard_map/ppermute | solution.py:136
  22.7 1.0 %collective-permute-start.9 = (bf16[4,36,512]{2,1,0:T(8,128)(2,1)S(1)}, bf16[4,36,512]{2,1,0:T(8,128)(2,1)S(1)}, u32[]{:S(2)}, u32[]{:S(2)}) collective-permute-start(bf16[4,36,512]{2,1,0:T(8,128)(2,1)S(1)} %pad_maximum_fusion.3.refs_2_), channel_id=1, source_target_pairs={{0,2},{1,3},{2,0},{3,1},{4,6},{5,7},{6,4},{7,5},{8,10},{9,11},{10,... | collective-permute-start | bytes 442376 | tf_op jit(solution)/shard_map/ppermute | solution.py:136
  23.7 1.2 %collective-permute-start.3 = (bf16[1,72,768]{2,1,0:T(8,128)(2,1)S(1)}, bf16[1,72,768]{2,1,0:T(8,128)(2,1)S(1)}, u32[]{:S(2)}, u32[]{:S(2)}) collective-permute-start(bf16[1,72,768]{2,1,0:T(8,128)(2,1)S(1)} %bitcast.13), channel_id=1, source_target_pairs={{0,16},{8,24},{16,0},{24,8},{1,17},{9,25},{17,1},{25,9},{2,18},{10... | collective-permute-start | bytes 331784 | tf_op jit(solution)/shard_map/ppermute | solution.py:136
  24.9 1.3 %project.1 = (bf16[72,768]{1,0:T(8,128)(2,1)S(1)}, bf16[768,288]{1,0:T(8,128)(2,1)S(1)}, bf16[288,768]{1,0:T(8,128)(2,1)S(1)}, f32[72,768]{1,0:T(8,128)S(1)}) custom-call(bf16[2,72,768]{2,1,0:T(8,128)(2,1)S(1)} %pad_maximum_fusion.near, bf16[2,72,768]{2,1,0:T(8,128)(2,1)S(1)} %collective-permute-done.7.far, bf16[768,768]{1,0:T(8,128)(2,1)S(1)} %copy-done.4, ...), custom_call_target="tpu_custom_call" | custom-call | flops 40000000 | bytes 1000 | tf_op jit(solution)/shard_map/project/pallas_call | solution.py:353
  26.2 2.2 %collective-permute-done.3 = bf16[1,72,768]{2,1,0:T(8,128)(2,1)S(1)} collective-permute-done((bf16[1,72,768]{2,1,0:T(8,128)(2,1)S(1)}, bf16[1,72,768]{2,1,0:T(8,128)(2,1)S(1)}, u32[]{:S(2)}, u32[]{:S(2)}) %collective-permute-start.3) | collective-permute-done | bytes 110624 | tf_op jit(solution)/shard_map/ppermute | solution.py:136
  28.4 0.7 %collective-permute-done.9.refs_3_ = bf16[4,36,512]{2,1,0:T(8,128)(2,1)S(1)} collective-permute-done((bf16[4,36,512]{2,1,0:T(8,128)(2,1)S(1)}, bf16[4,36,512]{2,1,0:T(8,128)(2,1)S(1)}, u32[]{:S(2)}, u32[]{:S(2)}) %collective-permute-start.9) | collective-permute-done | bytes 147488 | tf_op jit(solution)/shard_map/ppermute | solution.py:136
  29.1 0.5 %collective-permute-done.8.refs_1_ = bf16[4,36,640]{2,1,0:T(8,128)(2,1)S(1)} collective-permute-done((bf16[4,36,640]{2,1,0:T(8,128)(2,1)S(1)}, bf16[4,36,640]{2,1,0:T(8,128)(2,1)S(1)}, u32[]{:S(2)}, u32[]{:S(2)}) %collective-permute-start.8) | collective-permute-done | bytes 184352 | tf_op jit(solution)/shard_map/ppermute | solution.py:136
  29.6 0.1 collective-permute-start.10
  29.7 1.1 %turn_bias.1 = (bf16[72,768]{1,0:T(8,128)(2,1)S(1)}, bf16[144,768]{1,0:T(8,128)(2,1)S(1)}, bf16[144,768]{1,0:T(8,128)(2,1)S(1)}, f32[72,768]{1,0:T(8,128)S(1)}, f32[1152,288]{1,0:T(8,128)S(1)}) custom-call(bf16[2,72,768]{2,1,0:T(8,128)(2,1)S(1)} %pad_maximum_fusion.1.near, bf16[768,768]{1,0:T(8,128)(2,1)S(1)} %copy-done.4, bf16[768,768]{1,0:T(8,128)(2,1)S(1)} %copy-done.1, ...), custom_call_target="tpu_custom_call" | custom-call | flops 20000000 | bytes 1000 | tf_op jit(solution)/shard_map/turn_bias/pallas_call | solution.py:408
  30.8 0.4 %collective-permute-done.10.refs_10_ = bf16[2,72,768]{2,1,0:T(8,128)(2,1)S(1)} collective-permute-done((bf16[2,72,768]{2,1,0:T(8,128)(2,1)S(1)}, bf16[2,72,768]{2,1,0:T(8,128)(2,1)S(1)}, u32[]{:S(2)}, u32[]{:S(2)}) %collective-permute-start.10) | collective-permute-done | bytes 221216 | tf_op jit(solution)/shard_map/ppermute | solution.py:136
  31.2 3.6 %attend.1 = bf16[2,72,768]{2,1,0:T(8,128)(2,1)} custom-call(f32[1152,288]{1,0:T(8,128)S(1)} %get-tuple-element.49.bias, bf16[72,768]{1,0:T(8,128)(2,1)S(1)} %get-tuple-element.42.refs_0_, bf16[768,288]{1,0:T(8,128)(2,1)S(1)} %get-tuple-element.43.refs_1_, bf16[288,768]{1,0:T(8,128)(2,1)S(1)} %get-tuple-element.44.refs_2_, ...), custom_call_target="tpu_custom_call" | custom-call | flops 60000000 | bytes 1000 | tf_op jit(solution)/shard_map/attend/pallas_call | solution.py:500
  (39 shorter events, 0.2 us)
Async XLA Ops:
  0.0 2.1 %copy-start = (bf16[2,1152,128]{2,1,0:T(8,128)(2,1)S(1)}, bf16[2,1152,128]{2,1,0:T(8,128)(2,1)}, u32[]{:S(2)}) copy-start(bf16[2,1152,128]{2,1,0:T(8,128)(2,1)} %feat.9) | copy-start | bytes 1769476
  0.0 1.2 %copy-start.7 = (bf16[72,36,128]{2,0,1:T(8,128)(2,1)S(1)}, bf16[72,36,128]{2,0,1:T(8,128)(2,1)}, u32[]{:S(2)}) copy-start(bf16[72,36,128]{2,0,1:T(8,128)(2,1)} %param.18) | copy-start | bytes 1990660
  1.2 0.9 %copy-start.14 = (bf16[128,16]{0,1:T(8,128)(2,1)S(1)}, bf16[128,16]{0,1:T(8,128)(2,1)}, u32[]{:S(2)}) copy-start(bf16[128,16]{0,1:T(8,128)(2,1)} %param.25) | copy-start | bytes 12292
  1.2 1.0 %copy-start.15 = (s32[36]{0:T(128)S(1)}, s32[36]{0:T(128)}, u32[]{:S(2)}) copy-start(s32[36]{0:T(128)} %mask.1) | copy-start | bytes 436
  2.1 7.5 %copy-start.8 = (bf16[128,128]{1,0:T(8,128)(2,1)S(1)}, bf16[128,128]{1,0:T(8,128)(2,1)}, u32[]{:S(2)}) copy-start(bf16[128,128]{1,0:T(8,128)(2,1)} %refs_2_.5) | copy-start | bytes 98308
  2.1 7.5 %copy-start.9 = (bf16[128,128]{1,0:T(8,128)(2,1)S(1)}, bf16[128,128]{1,0:T(8,128)(2,1)}, u32[]{:S(2)}) copy-start(bf16[128,128]{1,0:T(8,128)(2,1)} %refs_3_.3) | copy-start | bytes 98308
  2.1 7.5 %copy-start.10 = (bf16[128,128]{1,0:T(8,128)(2,1)S(1)}, bf16[128,128]{1,0:T(8,128)(2,1)}, u32[]{:S(2)}) copy-start(bf16[128,128]{1,0:T(8,128)(2,1)} %refs_4_.3) | copy-start | bytes 98308
  2.1 9.9 %copy-start.6 = (bf16[128,768]{1,0:T(8,128)(2,1)S(1)}, bf16[128,768]{1,0:T(8,128)(2,1)}, u32[]{:S(2)}) copy-start(bf16[128,768]{1,0:T(8,128)(2,1)} %agg.3) | copy-start | bytes 589828
  2.1 9.9 %copy-start.11 = (bf16[128,128]{1,0:T(8,128)(2,1)S(1)}, bf16[128,128]{1,0:T(8,128)(2,1)}, u32[]{:S(2)}) copy-start(bf16[128,128]{1,0:T(8,128)(2,1)} %wo.4) | copy-start | bytes 98308
  2.1 9.9 %copy-start.12 = (s32[1152]{0:T(1024)S(1)}, s32[1152]{0:T(1024)}, u32[]{:S(2)}) copy-start(s32[1152]{0:T(1024)} %token_.3) | copy-start | bytes 13828
  2.2 9.8 %copy-start.13 = (f32[768]{0:T(1024)S(1)}, f32[768]{0:T(1024)}, u32[]{:S(2)}) copy-start(f32[768]{0:T(1024)} %gain.3) | copy-start | bytes 9220
  3.8 11.1 %collective-permute-start.1 = (bf16[36,1152]{1,0:T(8,128)(2,1)S(1)}, bf16[36,1152]{1,0:T(8,128)(2,1)S(1)}, u32[]{:S(2)}, u32[]{:S(2)}) collective-permute-start(bf16[36,1152]{1,0:T(8,128)(2,1)S(1)} %get-tuple-element.34), channel_id=1, source_target_pairs={{0,4},{1,5},{2,6},{3,7},{4,0},{5,1},{6,2},{7,3},{8,12},{9,13},{10,... | collective-permute-start | bytes 248840 | tf_op jit(solution)/shard_map/ppermute | solution.py:136
  7.9 4.0 %collective-permute-start = (bf16[2,48,128]{2,1,0:T(8,128)(2,1)S(1)}, bf16[2,48,128]{2,1,0:T(8,128)(2,1)S(1)}, u32[]{:S(2)}, u32[]{:S(2)}) collective-permute-start(bf16[2,48,128]{2,1,0:T(8,128)(2,1)S(1)} %get-tuple-element.30), channel_id=1, source_target_pairs={{0,8},{8,0},{16,24},{24,16},{1,9},{9,1},{17,25},{25,17},{2,10},{10... | collective-permute-start | bytes 73736 | tf_op jit(solution)/shard_map/ppermute | solution.py:136
  7.9 4.0 %collective-permute-start.2 = (bf16[2,48,128]{2,1,0:T(8,128)(2,1)S(1)}, bf16[2,48,128]{2,1,0:T(8,128)(2,1)S(1)}, u32[]{:S(2)}, u32[]{:S(2)}) collective-permute-start(bf16[2,48,128]{2,1,0:T(8,128)(2,1)S(1)} %get-tuple-element.32), channel_id=1, source_target_pairs={{8,16},{24,0},{16,8},{0,24},{9,17},{25,1},{17,9},{1,25},{10,18},{2... | collective-permute-start | bytes 73736 | tf_op jit(solution)/shard_map/ppermute | solution.py:536
  9.6 15.3 %copy-start.5 = (bf16[768,768]{1,0:T(8,128)(2,1)S(1)}, bf16[768,768]{1,0:T(8,128)(2,1)}, u32[]{:S(2)}) copy-start(bf16[768,768]{1,0:T(8,128)(2,1)} %wg.3) | copy-start | bytes 3538948
  12.0 12.9 %copy-start.4 = (bf16[768,768]{1,0:T(8,128)(2,1)S(1)}, bf16[768,768]{1,0:T(8,128)(2,1)}, u32[]{:S(2)}) copy-start(bf16[768,768]{1,0:T(8,128)(2,1)} %wq.3) | copy-start | bytes 3538948
  14.1 7.8 %collective-permute-start.4 = (bf16[1,72,768]{2,1,0:T(8,128)(2,1)S(1)}, bf16[1,72,768]{2,1,0:T(8,128)(2,1)S(1)}, u32[]{:S(2)}, u32[]{:S(2)}) collective-permute-start(bf16[1,72,768]{2,1,0:T(8,128)(2,1)S(1)} %bitcast.15), channel_id=1, source_target_pairs={{0,16},{8,24},{16,0},{24,8},{1,17},{9,25},{17,1},{25,9},{2,18},{10... | collective-permute-start | bytes 331784 | tf_op jit(solution)/shard_map/ppermute | solution.py:136
  15.0 7.0 %collective-permute-start.6 = (bf16[2,36,512]{2,1,0:T(8,128)(2,1)S(1)}, bf16[2,36,512]{2,1,0:T(8,128)(2,1)S(1)}, u32[]{:S(2)}, u32[]{:S(2)}) collective-permute-start(bf16[2,36,512]{2,1,0:T(8,128)(2,1)S(1)} %pad_maximum_fusion.5), channel_id=1, source_target_pairs={{0,1},{1,0},{2,3},{3,2},{4,5},{5,4},{6,7},{7,6},{8,9},{9,8},{10,11... | collective-permute-start | bytes 221192 | tf_op jit(solution)/shard_map/ppermute | solution.py:136
  16.5 8.4 %copy-start.3 = (bf16[768,768]{1,0:T(8,128)(2,1)S(1)}, bf16[768,768]{1,0:T(8,128)(2,1)}, u32[]{:S(2)}) copy-start(bf16[768,768]{1,0:T(8,128)(2,1)} %refs_13_.1) | copy-start | bytes 3538948
  16.6 5.5 %collective-permute-start.5 = (bf16[2,36,640]{2,1,0:T(8,128)(2,1)S(1)}, bf16[2,36,640]{2,1,0:T(8,128)(2,1)S(1)}, u32[]{:S(2)}, u32[]{:S(2)}) collective-permute-start(bf16[2,36,640]{2,1,0:T(8,128)(2,1)S(1)} %pad_maximum_fusion.4), channel_id=1, source_target_pairs={{0,2},{1,3},{2,0},{3,1},{4,6},{5,7},{6,4},{7,5},{8,10},{9,11},{10,... | collective-permute-start | bytes 276488 | tf_op jit(solution)/shard_map/ppermute | solution.py:136
  18.2 6.7 %copy-start.2 = (bf16[768,768]{1,0:T(8,128)(2,1)S(1)}, bf16[768,768]{1,0:T(8,128)(2,1)}, u32[]{:S(2)}) copy-start(bf16[768,768]{1,0:T(8,128)(2,1)} %refs_12_.1) | copy-start | bytes 3538948
  20.5 4.5 %copy-start.1 = (bf16[768,768]{1,0:T(8,128)(2,1)S(1)}, bf16[768,768]{1,0:T(8,128)(2,1)}, u32[]{:S(2)}) copy-start(bf16[768,768]{1,0:T(8,128)(2,1)} %refs_11_.1) | copy-start | bytes 3538948
  21.9 3.0 %collective-permute-start.7 = (bf16[2,72,768]{2,1,0:T(8,128)(2,1)S(1)}, bf16[2,72,768]{2,1,0:T(8,128)(2,1)S(1)}, u32[]{:S(2)}, u32[]{:S(2)}) collective-permute-start(bf16[2,72,768]{2,1,0:T(8,128)(2,1)S(1)} %pad_maximum_fusion.near), channel_id=1, source_target_pairs={{0,8},{8,0},{16,24},{24,16},{1,9},{9,1},{17,25},{25,17},{2,10},{10... | collective-permute-start | bytes 663560 | tf_op jit(solution)/shard_map/ppermute | solution.py:136
  22.1 7.5 %collective-permute-start.8 = (bf16[4,36,640]{2,1,0:T(8,128)(2,1)S(1)}, bf16[4,36,640]{2,1,0:T(8,128)(2,1)S(1)}, u32[]{:S(2)}, u32[]{:S(2)}) collective-permute-start(bf16[4,36,640]{2,1,0:T(8,128)(2,1)S(1)} %pad_maximum_fusion.2.refs_0_), channel_id=1, source_target_pairs={{0,1},{1,0},{2,3},{3,2},{4,5},{5,4},{6,7},{7,6},{8,9},{9,8},{10,11... | collective-permute-start | bytes 552968 | tf_op jit(solution)/shard_map/ppermute | solution.py:136
  22.7 6.4 %collective-permute-start.9 = (bf16[4,36,512]{2,1,0:T(8,128)(2,1)S(1)}, bf16[4,36,512]{2,1,0:T(8,128)(2,1)S(1)}, u32[]{:S(2)}, u32[]{:S(2)}) collective-permute-start(bf16[4,36,512]{2,1,0:T(8,128)(2,1)S(1)} %pad_maximum_fusion.3.refs_2_), channel_id=1, source_target_pairs={{0,2},{1,3},{2,0},{3,1},{4,6},{5,7},{6,4},{7,5},{8,10},{9,11},{10,... | collective-permute-start | bytes 442376 | tf_op jit(solution)/shard_map/ppermute | solution.py:136
  23.7 4.7 %collective-permute-start.3 = (bf16[1,72,768]{2,1,0:T(8,128)(2,1)S(1)}, bf16[1,72,768]{2,1,0:T(8,128)(2,1)S(1)}, u32[]{:S(2)}, u32[]{:S(2)}) collective-permute-start(bf16[1,72,768]{2,1,0:T(8,128)(2,1)S(1)} %bitcast.13), channel_id=1, source_target_pairs={{0,16},{8,24},{16,0},{24,8},{1,17},{9,25},{17,1},{25,9},{2,18},{10... | collective-permute-start | bytes 331784 | tf_op jit(solution)/shard_map/ppermute | solution.py:136
  29.6 1.5 %collective-permute-start.10 = (bf16[2,72,768]{2,1,0:T(8,128)(2,1)S(1)}, bf16[2,72,768]{2,1,0:T(8,128)(2,1)S(1)}, u32[]{:S(2)}, u32[]{:S(2)}) collective-permute-start(bf16[2,72,768]{2,1,0:T(8,128)(2,1)S(1)} %pad_maximum_fusion.1.near), channel_id=1, source_target_pairs={{0,8},{8,0},{16,24},{24,16},{1,9},{9,1},{17,25},{25,17},{2,10},{10... | collective-permute-start | bytes 663560 | tf_op jit(solution)/shard_map/ppermute | solution.py:136

commit v12 on v11

--- a/solution.py
+++ b/solution.py
@@ -80,7 +80,7 @@
     )(jnp.transpose(pair_cond, (1, 0, 2)))
 
 
-def bias_kernel(feat, normed, mask, weight, out, inner, outer):
+def bias_kernel(feat, normed, mask, weight, out, inner, outer, whole):
     odd = lax.axis_index("row") % 2 == 1
     head, tail = feat[:, :RIM], feat[:, feat.shape[1] - RIM :]
     inner[...] = jnp.where(odd, head, tail)
@@ -93,20 +93,26 @@
     open_row = jnp.broadcast_to(mask[...].reshape(1, cols), (LANES, cols)).astype(BF16)
     open_key = dot_nt(key_of.astype(BF16), open_row) > 0.5
     picked = (iota((cols, tall), 1) // SUB == iota((cols, tall), 0)).astype(BF16)
-    row = iota((tall, LANES), 0)
-    mine = iota((tall, LANES), 1) % SUB == row % SUB
-    apart = lax.axis_index("sample") * cols + row // SUB - lax.axis_index("row") * rows - row % SUB
-
-    def weigh(g):
-        x = normed[:, g * SUB : (g + 1) * SUB].reshape(tall, chans).astype(BF16)
-        raw = jnp.where(open_key | (apart == g * SUB), dot(x, wide), -30000.0)
-        return g, jnp.where(mine, raw, 0.0).astype(BF16)
+    batch = 3
+    row = iota((batch * tall, LANES), 0)
+    mine = iota((batch * tall, LANES), 1) % SUB == row % SUB
+    query = row // tall * SUB + row % SUB
+    apart = lax.axis_index("sample") * cols + row % tall // SUB - lax.axis_index("row") * rows - query
+    open_key = jnp.concatenate([open_key] * batch, axis=0)
+
+    def weigh(first):
+        x = [normed[:, g * SUB : (g + 1) * SUB].reshape(tall, chans) for g in range(first, first + batch)]
+        raw = dot(jnp.concatenate(x, axis=0).astype(BF16), wide)
+        raw = jnp.where(open_key | (apart == first * SUB), raw, -30000.0)
+        return first, jnp.where(mine, raw, 0.0).astype(BF16)
 
     def pick(item):
-        g, raw = item
-        out[:, g * LANES : (g + 1) * LANES] = dot(picked, raw).astype(BF16)
-
-    skewed(range(rows // SUB), [weigh, pick])
+        first, raw = item
+        for i in range(batch):
+            whole[(first + i) * cols : (first + i + 1) * cols] = dot(picked, raw[i * tall : (i + 1) * tall])
+
+    skewed(range(0, rows // SUB, batch), [weigh, pick])
+    out[...] = whole[...].astype(BF16)
 
 
 def pair_bias(feat, pair_cond, token_mask, pair_weight):
@@ -116,12 +122,13 @@
     return pl.pallas_call(
         bias_kernel,
         out_shape=[
-            jax.ShapeDtypeStruct((cols, rows * HEADS), BF16),
+            jax.ShapeDtypeStruct((rows // SUB * cols, LANES), BF16),
             jax.ShapeDtypeStruct(edge, BF16),
             jax.ShapeDtypeStruct(edge, BF16),
         ],
         in_specs=[vmem] * 4,
         out_specs=[vmem] * 3,
+        scratch_shapes=[pltpu.VMEM((rows // SUB * cols, LANES), F32)],
         compiler_params=pltpu.CompilerParams(vmem_limit_bytes=8 * MIB),
         cost_estimate=cost(3),
         name="pair_bias",
@@ -367,7 +374,7 @@
 
 
 def turn_kernel(orders, row_bits, near, wq, wk, wv, wg, *refs):
-    *halves, q, k, v, gate, out, tall = refs
+    *halves, q, k, v, gate, out, tall, flat = refs
     x = stack(near)
     width = x.shape[1]
 
@@ -380,15 +387,20 @@
 
     rows = out.shape[0] // HEADS
     me = lax.axis_index("sample")
-    at = 0
-    for i, (mine, other, bits) in enumerate(zip(halves[::2], halves[1::2], orders)):
-        half, cols, wide = mine.shape
+    groups = 0
+    for mine, other, bits in zip(halves[::2], halves[1::2], orders):
+        half, count, _ = mine.shape
+        cols = tall.shape[0] // (2 * half)
         places = places_of(bits)
         for j in range(2 * half):
             place = sum(jnp.where(me ^ j == p, i, 0) for i, p in enumerate(places))
             block = jnp.where(place < half, mine[place % half], other[place % half])
-            tall[j * cols : (j + 1) * cols, at : at + wide] = block.astype(F32)
-        at += wide
+            low = groups * cols
+            flat[j, low : low + count] = block.astype(F32)
+            for g in range(count // cols):
+                lanes = slice((groups + g) * LANES, (groups + g + 1) * LANES)
+                tall[j * cols : (j + 1) * cols, lanes] = flat[j, low + g * cols : low + (g + 1) * cols]
+        groups += count // cols
     starts = [pl.multiple_of((lax.axis_index("row") ^ p) * rows, SUB) for p in places_of(row_bits)]
     for g in range(rows // SUB):
         if g * 2 * LANES < width:
@@ -400,10 +412,11 @@
 
 
 def turn_bias(orders, row_bits, halves, near, wq, wk, wv, wg):
-    half, cols, _ = halves[0].shape
-    keys = 2 * half * cols
-    wide = sum(part.shape[2] for part in halves[::2])
     blocks, rows, width = near.shape
+    devices = 2 * halves[0].shape[0]
+    wide = rows * HEADS
+    count = sum(part.shape[1] for part in halves[::2])
+    keys = devices * count * LANES // wide
     vmem = pl.BlockSpec(memory_space=pltpu.VMEM)
     return pl.pallas_call(
         functools.partial(turn_kernel, orders, row_bits),
@@ -416,8 +429,8 @@
         ],
         in_specs=[vmem] * (5 + len(halves)),
         out_specs=[vmem] * 5,
-        scratch_shapes=[pltpu.VMEM((keys, wide), F32)],
-        compiler_params=pltpu.CompilerParams(vmem_limit_bytes=24 * MIB),
+        scratch_shapes=[pltpu.VMEM((keys, wide), F32), pltpu.VMEM((devices, count, LANES), F32)],
+        compiler_params=pltpu.CompilerParams(vmem_limit_bytes=32 * MIB),
         cost_estimate=cost(1),
         name="turn_bias",
     )(near, wq, wk, wv, wg, *halves)
@@ -540,7 +553,7 @@
 
     bits, row_bits = bits_of(lax.axis_size("sample")), bits_of(ranks)
     orders = [bits, bits[:1] + bits[-1:] + bits[1:-1]]
-    split = (bias.shape[1] // LANES + 1) // 2 * LANES
+    split = rows // SUB // 2 * pair_cond.shape[1]
     got = swap(bias, "sample", bits[0])
     norms, inputs = [], []
     for s in range(samples):
@@ -554,7 +567,7 @@
         norms.append(token_norm[None])
         if s == 0:
             bias, got, _ = lax.optimization_barrier((bias, got, token_norm))
-            held = [jnp.stack([bias[:, lanes], got[:, lanes]]) for lanes in (slice(0, split), slice(split, None))]
+            held = [jnp.stack([bias[part], got[part]]) for part in (slice(0, split), slice(split, None))]
             inner = after(inner, held, token_norm)
     last = swap(norms[-1], "row", row_bits[0])
     for i in range(1, len(bits) - 1):

time: 34.9 us -> 34.3 us (0.983)
  transfers between devices with their start and end apart: 11 -> 11, of which waited for: 4 -> 4; matrix products, arithmetic and copies ran while one was open for 0% -> 0% of each run, Pallas kernels for 30% -> 31%
where the time goes in v12:
time: 34.3 us; the launch traced here: 34.2 us
  Pallas kernels  16.5 us (48%)
  starting transfers between devices  12.3 us (36%)
  waiting for transfers between devices  3.62 us (11%)
  local copies, waits for them, and re-layouts  1.25 us (4%)
    ppermute x10, starting transfers between devices, swap(): lax.ppermute(held, axis, [(i, i ^ far) for i in range(lax.axis_size(axis))])  10.7 us
    pallas_call x2, Pallas kernels, atom_attention(): pl.pallas_call(functools.partial(atom_kernel, sample), out_shape=jax.Shap...  4.62 us
    ppermute x10, waiting for transfers between devices, swap(): lax.ppermute(held, axis, [(i, i ^ far) for i in range(lax.axis_size(axis))])  3.61 us
    pallas_call x1, Pallas kernels, attend(): pl.pallas_call(functools.partial(attend_kernel, len(parts)), out_shape=ja...  3.55 us
    pallas_call x2, Pallas kernels, gather_tokens(): pl.pallas_call(functools.partial(gather_kernel, sample), out_shape=[jax.S...  3.51 us
    ppermute x1, starting transfers between devices, shards(): lax.ppermute(outer, 'row', odd_pairs + [(j, i) for i, j in odd_pairs])  1.63 us
    pallas_call x1, Pallas kernels, pair_bias(): pl.pallas_call(bias_kernel, out_shape=[jax.ShapeDtypeStruct((rows // SUB...  1.48 us
    pallas_call x1, Pallas kernels, project(): pl.pallas_call(project_kernel, out_shape=[jax.ShapeDtypeStruct((rows, wid...  1.27 us
  transfers between devices with their start and end apart: 11, of which 4 were waited for; matrix products, arithmetic and copies ran while one was open for 0% of the time, Pallas kernels for 31%

profile of v12, /device:TPU:0, one launch (start us, length us, event | category | flops | bytes accessed | tf_op | source)
XLA Modules:
  0.0 34.2 jit_solution(3184996687285151527)
XLA Ops:
  0.0 1.2 %copy-done.7 = bf16[72,36,128]{2,0,1:T(8,128)(2,1)S(1)} copy-done((bf16[72,36,128]{2,0,1:T(8,128)(2,1)S(1)}, bf16[72,36,128]{2,0,1:T(8,128)(2,1)}, u32[]{:S(2)}) %copy-start.7) | copy-done | bytes 663576
  1.2 0.9 %normalise_pairs.1.normed = f32[36,72,128]{2,1,0:T(8,128)S(1)} custom-call(bf16[36,72,128]{2,1,0:T(8,128)(2,1)S(1)} %bitcast.12), custom_call_target="tpu_custom_call" | custom-call | flops 20000000 | bytes 1000 | tf_op jit(solution)/shard_map/normalise_pairs/pallas_call | solution.py:72
  2.1 0.0 copy-start.8
  2.1 0.0 copy-start.9
  2.1 0.0 copy-start.10
  2.1 0.0 copy-start.6
  2.1 0.0 copy-start.11
  2.2 1.5 %pair_bias.1 = (bf16[324,128]{1,0:T(8,128)(2,1)S(1)}, bf16[2,48,128]{2,1,0:T(8,128)(2,1)S(1)}, bf16[2,48,128]{2,1,0:T(8,128)(2,1)S(1)}) custom-call(bf16[2,1152,128]{2,1,0:T(8,128)(2,1)S(1)} %copy-done, f32[36,72,128]{2,1,0:T(8,128)S(1)} %normalise_pairs.1.normed, s32[36]{0:T(128)S(1)} %copy-done.15, bf16[16,128]{1,0:T(8,128)(2,1)S(1)} %bitcast.17), custom_call_target="tpu_custom_call" | custom-call | flops 60000000 | bytes 1000 | tf_op jit(solution)/shard_map/pair_bias/pallas_call | solution.py:122
  3.7 4.1 %collective-permute-start.1 = (bf16[324,128]{1,0:T(8,128)(2,1)S(1)}, bf16[324,128]{1,0:T(8,128)(2,1)S(1)}, u32[]{:S(2)}, u32[]{:S(2)}) collective-permute-start(bf16[324,128]{1,0:T(8,128)(2,1)S(1)} %get-tuple-element.34), channel_id=1, source_target_pairs={{0,4},{1,5},{2,6},{3,7},{4,0},{5,1},{6,2},{7,3},{8,12},{9,13},{10,... | collective-permute-start | bytes 248840 | tf_op jit(solution)/shard_map/ppermute | solution.py:143
  7.8 1.6 %collective-permute-start.2 = (bf16[2,48,128]{2,1,0:T(8,128)(2,1)S(1)}, bf16[2,48,128]{2,1,0:T(8,128)(2,1)S(1)}, u32[]{:S(2)}, u32[]{:S(2)}) collective-permute-start(bf16[2,48,128]{2,1,0:T(8,128)(2,1)S(1)} %get-tuple-element.32), channel_id=1, source_target_pairs={{8,16},{24,0},{16,8},{0,24},{9,17},{25,1},{17,9},{1,25},{10,18},{2... | collective-permute-start | bytes 73736 | tf_op jit(solution)/shard_map/ppermute | solution.py:549
  9.4 2.4 %atom_attention.2.mixed = bf16[1152,128]{1,0:T(8,128)(2,1)S(1)} custom-call(bf16[2,1152,128]{2,1,0:T(8,128)(2,1)S(1)} %copy-done, bf16[128,128]{1,0:T(8,128)(2,1)S(1)} %copy-done.8, bf16[128,128]{1,0:T(8,128)(2,1)S(1)} %copy-done.9, bf16[128,128]{1,0:T(8,128)(2,1)S(1)} %copy-done.10), custom_call_target="tpu_custom_call" | custom-call | flops 80000000 | bytes 1000 | tf_op jit(solution)/shard_map/atom_attention/pallas_call | solution.py:252
  11.8 0.0 copy-start.4
  11.8 2.1 %gather_tokens.2 = (f32[72,768]{1,0:T(8,128)S(1)}, bf16[72,768]{1,0:T(8,128)(2,1)S(1)}) custom-call(bf16[1152,128]{1,0:T(8,128)(2,1)S(1)} %atom_attention.2.mixed, bf16[2,1152,128]{2,1,0:T(8,128)(2,1)S(1)} %copy-done, s32[1152]{0:T(1024)S(1)} %copy-done.12, bf16[128,128]{1,0:T(8,128)(2,1)S(1)} %copy-done.11, bf16[128,768]{1,0:T(8,128)(2,1)S(1)} %copy-done.6, ...), custom_call_target="tpu_custom_call" | custom-call | flops 20000000 | bytes 1000 | tf_op jit(solution)/shard_map/gather_tokens/pallas_call | solution.py:322
  14.0 0.8 %collective-permute-start.4 = (bf16[1,72,768]{2,1,0:T(8,128)(2,1)S(1)}, bf16[1,72,768]{2,1,0:T(8,128)(2,1)S(1)}, u32[]{:S(2)}, u32[]{:S(2)}) collective-permute-start(bf16[1,72,768]{2,1,0:T(8,128)(2,1)S(1)} %bitcast.15), channel_id=1, source_target_pairs={{0,16},{8,24},{16,0},{24,8},{1,17},{9,25},{17,1},{25,9},{2,18},{10... | collective-permute-start | bytes 331784 | tf_op jit(solution)/shard_map/ppermute | solution.py:143
  14.8 0.0 copy-start.3
  14.8 1.6 %collective-permute-start.6 = (bf16[2,180,128]{2,1,0:T(8,128)(2,1)S(1)}, bf16[2,180,128]{2,1,0:T(8,128)(2,1)S(1)}, u32[]{:S(2)}, u32[]{:S(2)}) collective-permute-start(bf16[2,180,128]{2,1,0:T(8,128)(2,1)S(1)} %pad_maximum_fusion.4), channel_id=1, source_target_pairs={{0,1},{1,0},{2,3},{3,2},{4,5},{5,4},{6,7},{7,6},{8,9},{9,8},{10,11... | collective-permute-start | bytes 276488 | tf_op jit(solution)/shard_map/ppermute | solution.py:143
  16.4 1.6 %collective-permute-start.5 = (bf16[2,144,128]{2,1,0:T(8,128)(2,1)S(1)}, bf16[2,144,128]{2,1,0:T(8,128)(2,1)S(1)}, u32[]{:S(2)}, u32[]{:S(2)}) collective-permute-start(bf16[2,144,128]{2,1,0:T(8,128)(2,1)S(1)} %pad_maximum_fusion.5), channel_id=1, source_target_pairs={{0,2},{1,3},{2,0},{3,1},{4,6},{5,7},{6,4},{7,5},{8,10},{9,11},{10,... | collective-permute-start | bytes 221192 | tf_op jit(solution)/shard_map/ppermute | solution.py:143
  18.0 2.3 %atom_attention.3.mixed = bf16[1152,128]{1,0:T(8,128)(2,1)S(1)} custom-call(bf16[2,1152,128]{2,1,0:T(8,128)(2,1)S(1)} %copy-done, bf16[2,48,128]{2,1,0:T(8,128)(2,1)S(1)} %collective-permute-done.refs_0_, bf16[2,48,128]{2,1,0:T(8,128)(2,1)S(1)} %collective-permute-done.2.refs_1_, bf16[128,128]{1,0:T(8,128)(2,1)S(1)} %copy-done.8, ...), custom_call_target="tpu_custom_call" | custom-call | flops 80000000 | bytes 1000 | tf_op jit(solution)/shard_map/atom_attention/pallas_call | solution.py:252
  20.3 0.0 copy-start.1
  20.3 1.4 %gather_tokens.3 = (f32[72,768]{1,0:T(8,128)S(1)}, bf16[72,768]{1,0:T(8,128)(2,1)S(1)}) custom-call(bf16[1152,128]{1,0:T(8,128)(2,1)S(1)} %atom_attention.3.mixed, bf16[2,1152,128]{2,1,0:T(8,128)(2,1)S(1)} %copy-done, s32[1152]{0:T(1024)S(1)} %copy-done.12, bf16[128,128]{1,0:T(8,128)(2,1)S(1)} %copy-done.11, bf16[128,768]{1,0:T(8,128)(2,1)S(1)} %copy-done.6, ...), custom_call_target="tpu_custom_call" | custom-call | flops 20000000 | bytes 1000 | tf_op jit(solution)/shard_map/gather_tokens/pallas_call | solution.py:322
  21.8 0.1 collective-permute-start.7
  21.9 0.6 %collective-permute-start.9 = (bf16[4,180,128]{2,1,0:T(8,128)(2,1)S(1)}, bf16[4,180,128]{2,1,0:T(8,128)(2,1)S(1)}, u32[]{:S(2)}, u32[]{:S(2)}) collective-permute-start(bf16[4,180,128]{2,1,0:T(8,128)(2,1)S(1)} %pad_maximum_fusion.2.refs_2_), channel_id=1, source_target_pairs={{0,2},{1,3},{2,0},{3,1},{4,6},{5,7},{6,4},{7,5},{8,10},{9,11},{10,... | collective-permute-start | bytes 552968 | tf_op jit(solution)/shard_map/ppermute | solution.py:143
  22.5 0.6 %collective-permute-start.8 = (bf16[4,144,128]{2,1,0:T(8,128)(2,1)S(1)}, bf16[4,144,128]{2,1,0:T(8,128)(2,1)S(1)}, u32[]{:S(2)}, u32[]{:S(2)}) collective-permute-start(bf16[4,144,128]{2,1,0:T(8,128)(2,1)S(1)} %pad_maximum_fusion.3.refs_0_), channel_id=1, source_target_pairs={{0,1},{1,0},{2,3},{3,2},{4,5},{5,4},{6,7},{7,6},{8,9},{9,8},{10,11... | collective-permute-start | bytes 442376 | tf_op jit(solution)/shard_map/ppermute | solution.py:143
  23.1 1.3 %collective-permute-start.3 = (bf16[1,72,768]{2,1,0:T(8,128)(2,1)S(1)}, bf16[1,72,768]{2,1,0:T(8,128)(2,1)S(1)}, u32[]{:S(2)}, u32[]{:S(2)}) collective-permute-start(bf16[1,72,768]{2,1,0:T(8,128)(2,1)S(1)} %bitcast.13), channel_id=1, source_target_pairs={{0,16},{8,24},{16,0},{24,8},{1,17},{9,25},{17,1},{25,9},{2,18},{10... | collective-permute-start | bytes 331784 | tf_op jit(solution)/shard_map/ppermute | solution.py:143
  24.4 1.3 %project.1 = (bf16[72,768]{1,0:T(8,128)(2,1)S(1)}, bf16[768,288]{1,0:T(8,128)(2,1)S(1)}, bf16[288,768]{1,0:T(8,128)(2,1)S(1)}, f32[72,768]{1,0:T(8,128)S(1)}) custom-call(bf16[2,72,768]{2,1,0:T(8,128)(2,1)S(1)} %pad_maximum_fusion.near, bf16[2,72,768]{2,1,0:T(8,128)(2,1)S(1)} %collective-permute-done.7.far, bf16[768,768]{1,0:T(8,128)(2,1)S(1)} %copy-done.4, ...), custom_call_target="tpu_custom_call" | custom-call | flops 40000000 | bytes 1000 | tf_op jit(solution)/shard_map/project/pallas_call | solution.py:360
  25.7 2.2 %collective-permute-done.3 = bf16[1,72,768]{2,1,0:T(8,128)(2,1)S(1)} collective-permute-done((bf16[1,72,768]{2,1,0:T(8,128)(2,1)S(1)}, bf16[1,72,768]{2,1,0:T(8,128)(2,1)S(1)}, u32[]{:S(2)}, u32[]{:S(2)}) %collective-permute-start.3) | collective-permute-done | bytes 110624 | tf_op jit(solution)/shard_map/ppermute | solution.py:143
  27.9 0.5 %collective-permute-done.8.refs_1_ = bf16[4,144,128]{2,1,0:T(8,128)(2,1)S(1)} collective-permute-done((bf16[4,144,128]{2,1,0:T(8,128)(2,1)S(1)}, bf16[4,144,128]{2,1,0:T(8,128)(2,1)S(1)}, u32[]{:S(2)}, u32[]{:S(2)}) %collective-permute-start.8) | collective-permute-done | bytes 147488 | tf_op jit(solution)/shard_map/ppermute | solution.py:143
  28.5 0.6 %collective-permute-done.9.refs_3_ = bf16[4,180,128]{2,1,0:T(8,128)(2,1)S(1)} collective-permute-done((bf16[4,180,128]{2,1,0:T(8,128)(2,1)S(1)}, bf16[4,180,128]{2,1,0:T(8,128)(2,1)S(1)}, u32[]{:S(2)}, u32[]{:S(2)}) %collective-permute-start.9) | collective-permute-done | bytes 184352 | tf_op jit(solution)/shard_map/ppermute | solution.py:143
  29.1 0.1 collective-permute-start.10
  29.2 1.2 %turn_bias.1 = (bf16[72,768]{1,0:T(8,128)(2,1)S(1)}, bf16[144,768]{1,0:T(8,128)(2,1)S(1)}, bf16[144,768]{1,0:T(8,128)(2,1)S(1)}, f32[72,768]{1,0:T(8,128)S(1)}, f32[1152,288]{1,0:T(8,128)S(1)}) custom-call(bf16[2,72,768]{2,1,0:T(8,128)(2,1)S(1)} %pad_maximum_fusion.1.near, bf16[768,768]{1,0:T(8,128)(2,1)S(1)} %copy-done.4, bf16[768,768]{1,0:T(8,128)(2,1)S(1)} %copy-done.1, ...), custom_call_target="tpu_custom_call" | custom-call | flops 20000000 | bytes 1000 | tf_op jit(solution)/shard_map/turn_bias/pallas_call | solution.py:421
  30.4 0.2 collective-permute-done.10.refs_10_
  30.6 3.5 %attend.1 = bf16[2,72,768]{2,1,0:T(8,128)(2,1)} custom-call(f32[1152,288]{1,0:T(8,128)S(1)} %get-tuple-element.49.bias, bf16[72,768]{1,0:T(8,128)(2,1)S(1)} %get-tuple-element.42.refs_0_, bf16[768,288]{1,0:T(8,128)(2,1)S(1)} %get-tuple-element.43.refs_1_, bf16[288,768]{1,0:T(8,128)(2,1)S(1)} %get-tuple-element.44.refs_2_, ...), custom_call_target="tpu_custom_call" | custom-call | flops 60000000 | bytes 1000 | tf_op jit(solution)/shard_map/attend/pallas_call | solution.py:513
  (39 shorter events, 0.2 us)
Async XLA Ops:
  0.0 2.1 %copy-start = (bf16[2,1152,128]{2,1,0:T(8,128)(2,1)S(1)}, bf16[2,1152,128]{2,1,0:T(8,128)(2,1)}, u32[]{:S(2)}) copy-start(bf16[2,1152,128]{2,1,0:T(8,128)(2,1)} %feat.9) | copy-start | bytes 1769476
  0.0 1.2 %copy-start.7 = (bf16[72,36,128]{2,0,1:T(8,128)(2,1)S(1)}, bf16[72,36,128]{2,0,1:T(8,128)(2,1)}, u32[]{:S(2)}) copy-start(bf16[72,36,128]{2,0,1:T(8,128)(2,1)} %param.18) | copy-start | bytes 1990660
  1.2 0.9 %copy-start.14 = (bf16[128,16]{0,1:T(8,128)(2,1)S(1)}, bf16[128,16]{0,1:T(8,128)(2,1)}, u32[]{:S(2)}) copy-start(bf16[128,16]{0,1:T(8,128)(2,1)} %param.25) | copy-start | bytes 12292
  1.2 1.0 %copy-start.15 = (s32[36]{0:T(128)S(1)}, s32[36]{0:T(128)}, u32[]{:S(2)}) copy-start(s32[36]{0:T(128)} %mask.1) | copy-start | bytes 436
  2.1 7.3 %copy-start.8 = (bf16[128,128]{1,0:T(8,128)(2,1)S(1)}, bf16[128,128]{1,0:T(8,128)(2,1)}, u32[]{:S(2)}) copy-start(bf16[128,128]{1,0:T(8,128)(2,1)} %refs_2_.5) | copy-start | bytes 98308
  2.1 7.3 %copy-start.9 = (bf16[128,128]{1,0:T(8,128)(2,1)S(1)}, bf16[128,128]{1,0:T(8,128)(2,1)}, u32[]{:S(2)}) copy-start(bf16[128,128]{1,0:T(8,128)(2,1)} %refs_3_.3) | copy-start | bytes 98308
  2.1 7.3 %copy-start.10 = (bf16[128,128]{1,0:T(8,128)(2,1)S(1)}, bf16[128,128]{1,0:T(8,128)(2,1)}, u32[]{:S(2)}) copy-start(bf16[128,128]{1,0:T(8,128)(2,1)} %refs_4_.3) | copy-start | bytes 98308
  2.1 9.7 %copy-start.6 = (bf16[128,768]{1,0:T(8,128)(2,1)S(1)}, bf16[128,768]{1,0:T(8,128)(2,1)}, u32[]{:S(2)}) copy-start(bf16[128,768]{1,0:T(8,128)(2,1)} %agg.3) | copy-start | bytes 589828
  2.1 9.7 %copy-start.11 = (bf16[128,128]{1,0:T(8,128)(2,1)S(1)}, bf16[128,128]{1,0:T(8,128)(2,1)}, u32[]{:S(2)}) copy-start(bf16[128,128]{1,0:T(8,128)(2,1)} %wo.4) | copy-start | bytes 98308
  2.1 9.7 %copy-start.12 = (s32[1152]{0:T(1024)S(1)}, s32[1152]{0:T(1024)}, u32[]{:S(2)}) copy-start(s32[1152]{0:T(1024)} %token_.3) | copy-start | bytes 13828
  2.2 9.7 %copy-start.13 = (f32[768]{0:T(1024)S(1)}, f32[768]{0:T(1024)}, u32[]{:S(2)}) copy-start(f32[768]{0:T(1024)} %gain.3) | copy-start | bytes 9220
  3.7 11.1 %collective-permute-start.1 = (bf16[324,128]{1,0:T(8,128)(2,1)S(1)}, bf16[324,128]{1,0:T(8,128)(2,1)S(1)}, u32[]{:S(2)}, u32[]{:S(2)}) collective-permute-start(bf16[324,128]{1,0:T(8,128)(2,1)S(1)} %get-tuple-element.34), channel_id=1, source_target_pairs={{0,4},{1,5},{2,6},{3,7},{4,0},{5,1},{6,2},{7,3},{8,12},{9,13},{10,... | collective-permute-start | bytes 248840 | tf_op jit(solution)/shard_map/ppermute | solution.py:143
  7.8 4.0 %collective-permute-start = (bf16[2,48,128]{2,1,0:T(8,128)(2,1)S(1)}, bf16[2,48,128]{2,1,0:T(8,128)(2,1)S(1)}, u32[]{:S(2)}, u32[]{:S(2)}) collective-permute-start(bf16[2,48,128]{2,1,0:T(8,128)(2,1)S(1)} %get-tuple-element.30), channel_id=1, source_target_pairs={{0,8},{8,0},{16,24},{24,16},{1,9},{9,1},{17,25},{25,17},{2,10},{10... | collective-permute-start | bytes 73736 | tf_op jit(solution)/shard_map/ppermute | solution.py:143
  7.8 4.0 %collective-permute-start.2 = (bf16[2,48,128]{2,1,0:T(8,128)(2,1)S(1)}, bf16[2,48,128]{2,1,0:T(8,128)(2,1)S(1)}, u32[]{:S(2)}, u32[]{:S(2)}) collective-permute-start(bf16[2,48,128]{2,1,0:T(8,128)(2,1)S(1)} %get-tuple-element.32), channel_id=1, source_target_pairs={{8,16},{24,0},{16,8},{0,24},{9,17},{25,1},{17,9},{1,25},{10,18},{2... | collective-permute-start | bytes 73736 | tf_op jit(solution)/shard_map/ppermute | solution.py:549
  9.4 15.0 %copy-start.5 = (bf16[768,768]{1,0:T(8,128)(2,1)S(1)}, bf16[768,768]{1,0:T(8,128)(2,1)}, u32[]{:S(2)}) copy-start(bf16[768,768]{1,0:T(8,128)(2,1)} %wg.3) | copy-start | bytes 3538948
  11.8 12.6 %copy-start.4 = (bf16[768,768]{1,0:T(8,128)(2,1)S(1)}, bf16[768,768]{1,0:T(8,128)(2,1)}, u32[]{:S(2)}) copy-start(bf16[768,768]{1,0:T(8,128)(2,1)} %wq.3) | copy-start | bytes 3538948
  14.0 7.8 %collective-permute-start.4 = (bf16[1,72,768]{2,1,0:T(8,128)(2,1)S(1)}, bf16[1,72,768]{2,1,0:T(8,128)(2,1)S(1)}, u32[]{:S(2)}, u32[]{:S(2)}) collective-permute-start(bf16[1,72,768]{2,1,0:T(8,128)(2,1)S(1)} %bitcast.15), channel_id=1, source_target_pairs={{0,16},{8,24},{16,0},{24,8},{1,17},{9,25},{17,1},{25,9},{2,18},{10... | collective-permute-start | bytes 331784 | tf_op jit(solution)/shard_map/ppermute | solution.py:143
  14.8 9.6 %copy-start.3 = (bf16[768,768]{1,0:T(8,128)(2,1)S(1)}, bf16[768,768]{1,0:T(8,128)(2,1)}, u32[]{:S(2)}) copy-start(bf16[768,768]{1,0:T(8,128)(2,1)} %refs_13_.1) | copy-start | bytes 3538948
  14.8 7.1 %collective-permute-start.6 = (bf16[2,180,128]{2,1,0:T(8,128)(2,1)S(1)}, bf16[2,180,128]{2,1,0:T(8,128)(2,1)S(1)}, u32[]{:S(2)}, u32[]{:S(2)}) collective-permute-start(bf16[2,180,128]{2,1,0:T(8,128)(2,1)S(1)} %pad_maximum_fusion.4), channel_id=1, source_target_pairs={{0,1},{1,0},{2,3},{3,2},{4,5},{5,4},{6,7},{7,6},{8,9},{9,8},{10,11... | collective-permute-start | bytes 276488 | tf_op jit(solution)/shard_map/ppermute | solution.py:143
  16.4 5.5 %collective-permute-start.5 = (bf16[2,144,128]{2,1,0:T(8,128)(2,1)S(1)}, bf16[2,144,128]{2,1,0:T(8,128)(2,1)S(1)}, u32[]{:S(2)}, u32[]{:S(2)}) collective-permute-start(bf16[2,144,128]{2,1,0:T(8,128)(2,1)S(1)} %pad_maximum_fusion.5), channel_id=1, source_target_pairs={{0,2},{1,3},{2,0},{3,1},{4,6},{5,7},{6,4},{7,5},{8,10},{9,11},{10,... | collective-permute-start | bytes 221192 | tf_op jit(solution)/shard_map/ppermute | solution.py:143
  18.0 6.4 %copy-start.2 = (bf16[768,768]{1,0:T(8,128)(2,1)S(1)}, bf16[768,768]{1,0:T(8,128)(2,1)}, u32[]{:S(2)}) copy-start(bf16[768,768]{1,0:T(8,128)(2,1)} %refs_12_.1) | copy-start | bytes 3538948
  20.3 4.1 %copy-start.1 = (bf16[768,768]{1,0:T(8,128)(2,1)S(1)}, bf16[768,768]{1,0:T(8,128)(2,1)}, u32[]{:S(2)}) copy-start(bf16[768,768]{1,0:T(8,128)(2,1)} %refs_11_.1) | copy-start | bytes 3538948
  21.8 2.6 %collective-permute-start.7 = (bf16[2,72,768]{2,1,0:T(8,128)(2,1)S(1)}, bf16[2,72,768]{2,1,0:T(8,128)(2,1)S(1)}, u32[]{:S(2)}, u32[]{:S(2)}) collective-permute-start(bf16[2,72,768]{2,1,0:T(8,128)(2,1)S(1)} %pad_maximum_fusion.near), channel_id=1, source_target_pairs={{0,8},{8,0},{16,24},{24,16},{1,9},{9,1},{17,25},{25,17},{2,10},{10... | collective-permute-start | bytes 663560 | tf_op jit(solution)/shard_map/ppermute | solution.py:143
  21.9 7.2 %collective-permute-start.9 = (bf16[4,180,128]{2,1,0:T(8,128)(2,1)S(1)}, bf16[4,180,128]{2,1,0:T(8,128)(2,1)S(1)}, u32[]{:S(2)}, u32[]{:S(2)}) collective-permute-start(bf16[4,180,128]{2,1,0:T(8,128)(2,1)S(1)} %pad_maximum_fusion.2.refs_2_), channel_id=1, source_target_pairs={{0,2},{1,3},{2,0},{3,1},{4,6},{5,7},{6,4},{7,5},{8,10},{9,11},{10,... | collective-permute-start | bytes 552968 | tf_op jit(solution)/shard_map/ppermute | solution.py:143
  22.5 6.0 %collective-permute-start.8 = (bf16[4,144,128]{2,1,0:T(8,128)(2,1)S(1)}, bf16[4,144,128]{2,1,0:T(8,128)(2,1)S(1)}, u32[]{:S(2)}, u32[]{:S(2)}) collective-permute-start(bf16[4,144,128]{2,1,0:T(8,128)(2,1)S(1)} %pad_maximum_fusion.3.refs_0_), channel_id=1, source_target_pairs={{0,1},{1,0},{2,3},{3,2},{4,5},{5,4},{6,7},{7,6},{8,9},{9,8},{10,11... | collective-permute-start | bytes 442376 | tf_op jit(solution)/shard_map/ppermute | solution.py:143
  23.1 4.8 %collective-permute-start.3 = (bf16[1,72,768]{2,1,0:T(8,128)(2,1)S(1)}, bf16[1,72,768]{2,1,0:T(8,128)(2,1)S(1)}, u32[]{:S(2)}, u32[]{:S(2)}) collective-permute-start(bf16[1,72,768]{2,1,0:T(8,128)(2,1)S(1)} %bitcast.13), channel_id=1, source_target_pairs={{0,16},{8,24},{16,0},{24,8},{1,17},{9,25},{17,1},{25,9},{2,18},{10... | collective-permute-start | bytes 331784 | tf_op jit(solution)/shard_map/ppermute | solution.py:143
  29.1 1.5 %collective-permute-start.10 = (bf16[2,72,768]{2,1,0:T(8,128)(2,1)S(1)}, bf16[2,72,768]{2,1,0:T(8,128)(2,1)S(1)}, u32[]{:S(2)}, u32[]{:S(2)}) collective-permute-start(bf16[2,72,768]{2,1,0:T(8,128)(2,1)S(1)} %pad_maximum_fusion.1.near), channel_id=1, source_target_pairs={{0,8},{8,0},{16,24},{24,16},{1,9},{9,1},{17,25},{25,17},{2,10},{10... | collective-permute-start | bytes 663560 | tf_op jit(solution)/shard_map/ppermute | solution.py:143

commit v13 on v12

--- a/solution.py
+++ b/solution.py
@@ -94,22 +94,24 @@
     open_key = dot_nt(key_of.astype(BF16), open_row) > 0.5
     picked = (iota((cols, tall), 1) // SUB == iota((cols, tall), 0)).astype(BF16)
     batch = 3
-    row = iota((batch * tall, LANES), 0)
-    mine = iota((batch * tall, LANES), 1) % SUB == row % SUB
-    query = row // tall * SUB + row % SUB
-    apart = lax.axis_index("sample") * cols + row % tall // SUB - lax.axis_index("row") * rows - query
-    open_key = jnp.concatenate([open_key] * batch, axis=0)
+    row = iota((tall, LANES), 0)
+    mine = iota((tall, LANES), 1) % SUB == row % SUB
+    own = lax.axis_index("sample") * cols + row // SUB - lax.axis_index("row") * rows - row % SUB
+    own = jnp.where(mine, own, -1)
+    kept = mine & open_key
+    base = jnp.where(mine & ~open_key, -30000.0, 0.0)
 
     def weigh(first):
-        x = [normed[:, g * SUB : (g + 1) * SUB].reshape(tall, chans) for g in range(first, first + batch)]
-        raw = dot(jnp.concatenate(x, axis=0).astype(BF16), wide)
-        raw = jnp.where(open_key | (apart == first * SUB), raw, -30000.0)
-        return first, jnp.where(mine, raw, 0.0).astype(BF16)
+        out = []
+        for g in range(first, first + batch):
+            raw = dot(normed[:, g * SUB : (g + 1) * SUB].reshape(tall, chans).astype(BF16), wide)
+            out.append(jnp.where(kept | (own == g * SUB), raw, base).astype(BF16))
+        return first, out
 
     def pick(item):
-        first, raw = item
-        for i in range(batch):
-            whole[(first + i) * cols : (first + i + 1) * cols] = dot(picked, raw[i * tall : (i + 1) * tall])
+        first, out = item
+        for i, raw in enumerate(out):
+            whole[(first + i) * cols : (first + i + 1) * cols] = dot(picked, raw)
 
     skewed(range(0, rows // SUB, batch), [weigh, pick])
     out[...] = whole[...].astype(BF16)
@@ -443,7 +445,7 @@
     rows, width = parts[-1][4].shape
     x = stack(far)
     scale = LOG2E / HEAD_DIM**0.5
-    lane = iota((rows, 2 * LANES), 1)
+    lane = iota((rows, LANES), 1)
     groups = head_groups(width)
     work = [(s, base, heads) for s in range(samples) for base, heads in groups]
     chunks = list(range(0, width, 2 * LANES))
@@ -457,17 +459,25 @@
         v[: v_near.shape[0], lanes] = v_near[:, lanes]
         v[v_near.shape[0] :, lanes] = dot(x, wv[:, lanes]).astype(BF16)
 
-    def channels(base, h):
-        low = h * HEAD_DIM - base
+    def tiles_of(h):
+        return range(h * HEAD_DIM // LANES * LANES, (h + 1) * HEAD_DIM, LANES)
+
+    def channels(at, h):
+        low = h * HEAD_DIM - at
         return (lane >= low) & (lane < low + HEAD_DIM)
+
+    blank = jnp.zeros((rows, LANES), F32)
 
     def score(item):
         if isinstance(item, int):
             return fill(item)
         s, base, heads = item
         q, keys = parts[s][0], parts[s][1] if s < samples - 1 else kt
-        mine = q[:, base : base + 2 * LANES].astype(F32)
-        mine = jnp.concatenate([jnp.where(channels(base, h), mine, 0.0) for h in heads], axis=0).astype(BF16)
+        both = [(at, q[:, at : at + LANES].astype(F32)) for at in (base, base + LANES)]
+        mine = [
+            [jnp.where(channels(at, h), part, 0.0) if at in tiles_of(h) else blank for at, part in both] for h in heads
+        ]
+        mine = jnp.concatenate([jnp.concatenate(pair, axis=1) for pair in mine], axis=0).astype(BF16)
         some = bias[heads[0] * rows : (heads[-1] + 1) * rows]
         return item, dot(mine, keys[base : base + 2 * LANES]) * scale + some
 
@@ -485,21 +495,18 @@
             return
         (s, base, heads), e, share = item
         values = parts[s][2] if s < samples - 1 else v
-        o = dot(e, values[:, base : base + 2 * LANES]) * share
+        o = dot(e, values[:, base : base + 2 * LANES])
         for i, h in enumerate(heads):
-            mixes[s, base] = jnp.where(channels(base, h), o[i * rows : (i + 1) * rows], mixes.get((s, base), 0.0))
+            part = slice(i * rows, (i + 1) * rows)
+            for at in tiles_of(h):
+                one = o[part, at - base : at - base + LANES] * share[part]
+                mixes[s, at] = jnp.where(channels(at, h), one, mixes.get((s, at), 0.0))
         if h == HEADS - 1:
             close(s)
 
     def close(s):
-        tiles = {}
-        for base, _ in groups:
-            for t in range(2):
-                at = base + t * LANES
-                part = mixes[s, base][:, t * LANES : (t + 1) * LANES]
-                tiles[at] = tiles[at] + part if at in tiles else part
         gate, token_in = parts[s][3:]
-        gated = jnp.concatenate([tiles[at] for at in range(0, width, LANES)], axis=1) * gate[...]
+        gated = jnp.concatenate([mixes[s, at] for at in range(0, width, LANES)], axis=1) * gate[...]
         out[s] = (token_in[...] + dot(gated.astype(BF16), wo[...])).astype(BF16)
 
     skewed(work, [score, soften, mix])

time: 34.3 us -> 33.9 us (0.988)
  Pallas kernels: 16.5 us -> 16.1 us
    pallas_call x1, Pallas kernels: 1.48 us -> 1.03 us  [pair_bias(): pl.pallas_call(bias_kernel, out_shape=[jax.ShapeDtypeStruct((rows // SUB...]
  transfers between devices with their start and end apart: 11 -> 11, of which waited for: 4 -> 4; matrix products, arithmetic and copies ran while one was open for 0% -> 0% of each run, Pallas kernels for 31% -> 32%
where the time goes in v13:
time: 33.9 us; the launch traced here: 33.7 us
  Pallas kernels  16.1 us (47%)
  starting transfers between devices  12.3 us (36%)
  waiting for transfers between devices  3.62 us (11%)
  local copies, waits for them, and re-layouts  1.25 us (4%)
    ppermute x10, starting transfers between devices, swap(): lax.ppermute(held, axis, [(i, i ^ far) for i in range(lax.axis_size(axis))])  10.7 us
    pallas_call x2, Pallas kernels, atom_attention(): pl.pallas_call(functools.partial(atom_kernel, sample), out_shape=jax.Shap...  4.62 us
    ppermute x10, waiting for transfers between devices, swap(): lax.ppermute(held, axis, [(i, i ^ far) for i in range(lax.axis_size(axis))])  3.61 us
    pallas_call x1, Pallas kernels, attend(): pl.pallas_call(functools.partial(attend_kernel, len(parts)), out_shape=ja...  3.55 us
    pallas_call x2, Pallas kernels, gather_tokens(): pl.pallas_call(functools.partial(gather_kernel, sample), out_shape=[jax.S...  3.51 us
    ppermute x1, starting transfers between devices, shards(): lax.ppermute(outer, 'row', odd_pairs + [(j, i) for i, j in odd_pairs])  1.63 us
    pallas_call x1, Pallas kernels, project(): pl.pallas_call(project_kernel, out_shape=[jax.ShapeDtypeStruct((rows, wid...  1.27 us
    unnamed x32, local copies, waits for them, and re-layouts  1.23 us
  transfers between devices with their start and end apart: 11, of which 4 were waited for; matrix products, arithmetic and copies ran while one was open for 0% of the time, Pallas kernels for 32%

profile of v13, /device:TPU:0, one launch (start us, length us, event | category | flops | bytes accessed | tf_op | source)
XLA Modules:
  0.0 33.7 jit_solution(2893231665067444678)
XLA Ops:
  0.0 1.2 %copy-done.7 = bf16[72,36,128]{2,0,1:T(8,128)(2,1)S(1)} copy-done((bf16[72,36,128]{2,0,1:T(8,128)(2,1)S(1)}, bf16[72,36,128]{2,0,1:T(8,128)(2,1)}, u32[]{:S(2)}) %copy-start.7) | copy-done | bytes 663576
  1.2 0.9 %normalise_pairs.1.normed = f32[36,72,128]{2,1,0:T(8,128)S(1)} custom-call(bf16[36,72,128]{2,1,0:T(8,128)(2,1)S(1)} %bitcast.12), custom_call_target="tpu_custom_call" | custom-call | flops 20000000 | bytes 1000 | tf_op jit(solution)/shard_map/normalise_pairs/pallas_call | solution.py:72
  2.1 0.0 copy-start.8
  2.1 0.0 copy-start.9
  2.1 0.0 copy-start.10
  2.1 0.0 copy-start.6
  2.1 0.0 copy-start.11
  2.1 0.0 copy-start.12
  2.2 0.0 copy-start.13
  2.2 1.0 %pair_bias.1 = (bf16[324,128]{1,0:T(8,128)(2,1)S(1)}, bf16[2,48,128]{2,1,0:T(8,128)(2,1)S(1)}, bf16[2,48,128]{2,1,0:T(8,128)(2,1)S(1)}) custom-call(bf16[2,1152,128]{2,1,0:T(8,128)(2,1)S(1)} %copy-done, f32[36,72,128]{2,1,0:T(8,128)S(1)} %normalise_pairs.1.normed, s32[36]{0:T(128)S(1)} %copy-done.15, bf16[16,128]{1,0:T(8,128)(2,1)S(1)} %bitcast.17), custom_call_target="tpu_custom_call" | custom-call | flops 60000000 | bytes 1000 | tf_op jit(solution)/shard_map/pair_bias/pallas_call | solution.py:124
  3.2 4.1 %collective-permute-start.1 = (bf16[324,128]{1,0:T(8,128)(2,1)S(1)}, bf16[324,128]{1,0:T(8,128)(2,1)S(1)}, u32[]{:S(2)}, u32[]{:S(2)}) collective-permute-start(bf16[324,128]{1,0:T(8,128)(2,1)S(1)} %get-tuple-element.34), channel_id=1, source_target_pairs={{0,4},{1,5},{2,6},{3,7},{4,0},{5,1},{6,2},{7,3},{8,12},{9,13},{10,... | collective-permute-start | bytes 248840 | tf_op jit(solution)/shard_map/ppermute | solution.py:145
  7.3 1.6 %collective-permute-start.2 = (bf16[2,48,128]{2,1,0:T(8,128)(2,1)S(1)}, bf16[2,48,128]{2,1,0:T(8,128)(2,1)S(1)}, u32[]{:S(2)}, u32[]{:S(2)}) collective-permute-start(bf16[2,48,128]{2,1,0:T(8,128)(2,1)S(1)} %get-tuple-element.32), channel_id=1, source_target_pairs={{8,16},{24,0},{16,8},{0,24},{9,17},{25,1},{17,9},{1,25},{10,18},{2... | collective-permute-start | bytes 73736 | tf_op jit(solution)/shard_map/ppermute | solution.py:556
  9.0 2.4 %atom_attention.2.mixed = bf16[1152,128]{1,0:T(8,128)(2,1)S(1)} custom-call(bf16[2,1152,128]{2,1,0:T(8,128)(2,1)S(1)} %copy-done, bf16[128,128]{1,0:T(8,128)(2,1)S(1)} %copy-done.8, bf16[128,128]{1,0:T(8,128)(2,1)S(1)} %copy-done.9, bf16[128,128]{1,0:T(8,128)(2,1)S(1)} %copy-done.10), custom_call_target="tpu_custom_call" | custom-call | flops 80000000 | bytes 1000 | tf_op jit(solution)/shard_map/atom_attention/pallas_call | solution.py:254
  11.4 0.0 copy-start.4
  11.4 2.1 %gather_tokens.2 = (f32[72,768]{1,0:T(8,128)S(1)}, bf16[72,768]{1,0:T(8,128)(2,1)S(1)}) custom-call(bf16[1152,128]{1,0:T(8,128)(2,1)S(1)} %atom_attention.2.mixed, bf16[2,1152,128]{2,1,0:T(8,128)(2,1)S(1)} %copy-done, s32[1152]{0:T(1024)S(1)} %copy-done.12, bf16[128,128]{1,0:T(8,128)(2,1)S(1)} %copy-done.11, bf16[128,768]{1,0:T(8,128)(2,1)S(1)} %copy-done.6, ...), custom_call_target="tpu_custom_call" | custom-call | flops 20000000 | bytes 1000 | tf_op jit(solution)/shard_map/gather_tokens/pallas_call | solution.py:324
  13.5 0.8 %collective-permute-start.4 = (bf16[1,72,768]{2,1,0:T(8,128)(2,1)S(1)}, bf16[1,72,768]{2,1,0:T(8,128)(2,1)S(1)}, u32[]{:S(2)}, u32[]{:S(2)}) collective-permute-start(bf16[1,72,768]{2,1,0:T(8,128)(2,1)S(1)} %bitcast.15), channel_id=1, source_target_pairs={{0,16},{8,24},{16,0},{24,8},{1,17},{9,25},{17,1},{25,9},{2,18},{10... | collective-permute-start | bytes 331784 | tf_op jit(solution)/shard_map/ppermute | solution.py:145
  14.4 1.6 %collective-permute-start.6 = (bf16[2,180,128]{2,1,0:T(8,128)(2,1)S(1)}, bf16[2,180,128]{2,1,0:T(8,128)(2,1)S(1)}, u32[]{:S(2)}, u32[]{:S(2)}) collective-permute-start(bf16[2,180,128]{2,1,0:T(8,128)(2,1)S(1)} %pad_maximum_fusion.4), channel_id=1, source_target_pairs={{0,1},{1,0},{2,3},{3,2},{4,5},{5,4},{6,7},{7,6},{8,9},{9,8},{10,11... | collective-permute-start | bytes 276488 | tf_op jit(solution)/shard_map/ppermute | solution.py:145
  15.9 1.6 %collective-permute-start.5 = (bf16[2,144,128]{2,1,0:T(8,128)(2,1)S(1)}, bf16[2,144,128]{2,1,0:T(8,128)(2,1)S(1)}, u32[]{:S(2)}, u32[]{:S(2)}) collective-permute-start(bf16[2,144,128]{2,1,0:T(8,128)(2,1)S(1)} %pad_maximum_fusion.5), channel_id=1, source_target_pairs={{0,2},{1,3},{2,0},{3,1},{4,6},{5,7},{6,4},{7,5},{8,10},{9,11},{10,... | collective-permute-start | bytes 221192 | tf_op jit(solution)/shard_map/ppermute | solution.py:145
  17.6 2.3 %atom_attention.3.mixed = bf16[1152,128]{1,0:T(8,128)(2,1)S(1)} custom-call(bf16[2,1152,128]{2,1,0:T(8,128)(2,1)S(1)} %copy-done, bf16[2,48,128]{2,1,0:T(8,128)(2,1)S(1)} %collective-permute-done.refs_0_, bf16[2,48,128]{2,1,0:T(8,128)(2,1)S(1)} %collective-permute-done.2.refs_1_, bf16[128,128]{1,0:T(8,128)(2,1)S(1)} %copy-done.8, ...), custom_call_target="tpu_custom_call" | custom-call | flops 80000000 | bytes 1000 | tf_op jit(solution)/shard_map/atom_attention/pallas_call | solution.py:254
  19.8 1.4 %gather_tokens.3 = (f32[72,768]{1,0:T(8,128)S(1)}, bf16[72,768]{1,0:T(8,128)(2,1)S(1)}) custom-call(bf16[1152,128]{1,0:T(8,128)(2,1)S(1)} %atom_attention.3.mixed, bf16[2,1152,128]{2,1,0:T(8,128)(2,1)S(1)} %copy-done, s32[1152]{0:T(1024)S(1)} %copy-done.12, bf16[128,128]{1,0:T(8,128)(2,1)S(1)} %copy-done.11, bf16[128,768]{1,0:T(8,128)(2,1)S(1)} %copy-done.6, ...), custom_call_target="tpu_custom_call" | custom-call | flops 20000000 | bytes 1000 | tf_op jit(solution)/shard_map/gather_tokens/pallas_call | solution.py:324
  21.3 0.1 collective-permute-start.7
  21.4 0.6 %collective-permute-start.9 = (bf16[4,180,128]{2,1,0:T(8,128)(2,1)S(1)}, bf16[4,180,128]{2,1,0:T(8,128)(2,1)S(1)}, u32[]{:S(2)}, u32[]{:S(2)}) collective-permute-start(bf16[4,180,128]{2,1,0:T(8,128)(2,1)S(1)} %pad_maximum_fusion.2.refs_2_), channel_id=1, source_target_pairs={{0,2},{1,3},{2,0},{3,1},{4,6},{5,7},{6,4},{7,5},{8,10},{9,11},{10,... | collective-permute-start | bytes 552968 | tf_op jit(solution)/shard_map/ppermute | solution.py:145
  22.0 0.6 %collective-permute-start.8 = (bf16[4,144,128]{2,1,0:T(8,128)(2,1)S(1)}, bf16[4,144,128]{2,1,0:T(8,128)(2,1)S(1)}, u32[]{:S(2)}, u32[]{:S(2)}) collective-permute-start(bf16[4,144,128]{2,1,0:T(8,128)(2,1)S(1)} %pad_maximum_fusion.3.refs_0_), channel_id=1, source_target_pairs={{0,1},{1,0},{2,3},{3,2},{4,5},{5,4},{6,7},{7,6},{8,9},{9,8},{10,11... | collective-permute-start | bytes 442376 | tf_op jit(solution)/shard_map/ppermute | solution.py:145
  22.6 1.3 %collective-permute-start.3 = (bf16[1,72,768]{2,1,0:T(8,128)(2,1)S(1)}, bf16[1,72,768]{2,1,0:T(8,128)(2,1)S(1)}, u32[]{:S(2)}, u32[]{:S(2)}) collective-permute-start(bf16[1,72,768]{2,1,0:T(8,128)(2,1)S(1)} %bitcast.13), channel_id=1, source_target_pairs={{0,16},{8,24},{16,0},{24,8},{1,17},{9,25},{17,1},{25,9},{2,18},{10... | collective-permute-start | bytes 331784 | tf_op jit(solution)/shard_map/ppermute | solution.py:145
  24.0 1.3 %project.1 = (bf16[72,768]{1,0:T(8,128)(2,1)S(1)}, bf16[768,288]{1,0:T(8,128)(2,1)S(1)}, bf16[288,768]{1,0:T(8,128)(2,1)S(1)}, f32[72,768]{1,0:T(8,128)S(1)}) custom-call(bf16[2,72,768]{2,1,0:T(8,128)(2,1)S(1)} %pad_maximum_fusion.near, bf16[2,72,768]{2,1,0:T(8,128)(2,1)S(1)} %collective-permute-done.7.far, bf16[768,768]{1,0:T(8,128)(2,1)S(1)} %copy-done.4, ...), custom_call_target="tpu_custom_call" | custom-call | flops 40000000 | bytes 1000 | tf_op jit(solution)/shard_map/project/pallas_call | solution.py:362
  25.2 2.2 %collective-permute-done.3 = bf16[1,72,768]{2,1,0:T(8,128)(2,1)S(1)} collective-permute-done((bf16[1,72,768]{2,1,0:T(8,128)(2,1)S(1)}, bf16[1,72,768]{2,1,0:T(8,128)(2,1)S(1)}, u32[]{:S(2)}, u32[]{:S(2)}) %collective-permute-start.3) | collective-permute-done | bytes 110624 | tf_op jit(solution)/shard_map/ppermute | solution.py:145
  27.5 0.5 %collective-permute-done.8.refs_1_ = bf16[4,144,128]{2,1,0:T(8,128)(2,1)S(1)} collective-permute-done((bf16[4,144,128]{2,1,0:T(8,128)(2,1)S(1)}, bf16[4,144,128]{2,1,0:T(8,128)(2,1)S(1)}, u32[]{:S(2)}, u32[]{:S(2)}) %collective-permute-start.8) | collective-permute-done | bytes 147488 | tf_op jit(solution)/shard_map/ppermute | solution.py:145
  28.0 0.6 %collective-permute-done.9.refs_3_ = bf16[4,180,128]{2,1,0:T(8,128)(2,1)S(1)} collective-permute-done((bf16[4,180,128]{2,1,0:T(8,128)(2,1)S(1)}, bf16[4,180,128]{2,1,0:T(8,128)(2,1)S(1)}, u32[]{:S(2)}, u32[]{:S(2)}) %collective-permute-start.9) | collective-permute-done | bytes 184352 | tf_op jit(solution)/shard_map/ppermute | solution.py:145
  28.6 0.1 collective-permute-start.10
  28.7 1.2 %turn_bias.1 = (bf16[72,768]{1,0:T(8,128)(2,1)S(1)}, bf16[144,768]{1,0:T(8,128)(2,1)S(1)}, bf16[144,768]{1,0:T(8,128)(2,1)S(1)}, f32[72,768]{1,0:T(8,128)S(1)}, f32[1152,288]{1,0:T(8,128)S(1)}) custom-call(bf16[2,72,768]{2,1,0:T(8,128)(2,1)S(1)} %pad_maximum_fusion.1.near, bf16[768,768]{1,0:T(8,128)(2,1)S(1)} %copy-done.4, bf16[768,768]{1,0:T(8,128)(2,1)S(1)} %copy-done.1, ...), custom_call_target="tpu_custom_call" | custom-call | flops 20000000 | bytes 1000 | tf_op jit(solution)/shard_map/turn_bias/pallas_call | solution.py:423
  29.9 0.2 collective-permute-done.10.refs_10_
  30.2 3.5 %attend.1 = bf16[2,72,768]{2,1,0:T(8,128)(2,1)} custom-call(f32[1152,288]{1,0:T(8,128)S(1)} %get-tuple-element.49.bias, bf16[72,768]{1,0:T(8,128)(2,1)S(1)} %get-tuple-element.42.refs_0_, bf16[768,288]{1,0:T(8,128)(2,1)S(1)} %get-tuple-element.43.refs_1_, bf16[288,768]{1,0:T(8,128)(2,1)S(1)} %get-tuple-element.44.refs_2_, ...), custom_call_target="tpu_custom_call" | custom-call | flops 60000000 | bytes 1000 | tf_op jit(solution)/shard_map/attend/pallas_call | solution.py:520
  (39 shorter events, 0.2 us)
Async XLA Ops:
  0.0 2.1 %copy-start = (bf16[2,1152,128]{2,1,0:T(8,128)(2,1)S(1)}, bf16[2,1152,128]{2,1,0:T(8,128)(2,1)}, u32[]{:S(2)}) copy-start(bf16[2,1152,128]{2,1,0:T(8,128)(2,1)} %feat.9) | copy-start | bytes 1769476
  0.0 1.2 %copy-start.7 = (bf16[72,36,128]{2,0,1:T(8,128)(2,1)S(1)}, bf16[72,36,128]{2,0,1:T(8,128)(2,1)}, u32[]{:S(2)}) copy-start(bf16[72,36,128]{2,0,1:T(8,128)(2,1)} %param.18) | copy-start | bytes 1990660
  1.2 0.9 %copy-start.14 = (bf16[128,16]{0,1:T(8,128)(2,1)S(1)}, bf16[128,16]{0,1:T(8,128)(2,1)}, u32[]{:S(2)}) copy-start(bf16[128,16]{0,1:T(8,128)(2,1)} %param.25) | copy-start | bytes 12292
  1.2 1.0 %copy-start.15 = (s32[36]{0:T(128)S(1)}, s32[36]{0:T(128)}, u32[]{:S(2)}) copy-start(s32[36]{0:T(128)} %mask.1) | copy-start | bytes 436
  2.1 6.9 %copy-start.8 = (bf16[128,128]{1,0:T(8,128)(2,1)S(1)}, bf16[128,128]{1,0:T(8,128)(2,1)}, u32[]{:S(2)}) copy-start(bf16[128,128]{1,0:T(8,128)(2,1)} %refs_2_.5) | copy-start | bytes 98308
  2.1 6.9 %copy-start.9 = (bf16[128,128]{1,0:T(8,128)(2,1)S(1)}, bf16[128,128]{1,0:T(8,128)(2,1)}, u32[]{:S(2)}) copy-start(bf16[128,128]{1,0:T(8,128)(2,1)} %refs_3_.3) | copy-start | bytes 98308
  2.1 6.9 %copy-start.10 = (bf16[128,128]{1,0:T(8,128)(2,1)S(1)}, bf16[128,128]{1,0:T(8,128)(2,1)}, u32[]{:S(2)}) copy-start(bf16[128,128]{1,0:T(8,128)(2,1)} %refs_4_.3) | copy-start | bytes 98308
  2.1 9.2 %copy-start.6 = (bf16[128,768]{1,0:T(8,128)(2,1)S(1)}, bf16[128,768]{1,0:T(8,128)(2,1)}, u32[]{:S(2)}) copy-start(bf16[128,768]{1,0:T(8,128)(2,1)} %agg.3) | copy-start | bytes 589828
  2.1 9.2 %copy-start.11 = (bf16[128,128]{1,0:T(8,128)(2,1)S(1)}, bf16[128,128]{1,0:T(8,128)(2,1)}, u32[]{:S(2)}) copy-start(bf16[128,128]{1,0:T(8,128)(2,1)} %wo.4) | copy-start | bytes 98308
  2.1 9.2 %copy-start.12 = (s32[1152]{0:T(1024)S(1)}, s32[1152]{0:T(1024)}, u32[]{:S(2)}) copy-start(s32[1152]{0:T(1024)} %token_.3) | copy-start | bytes 13828
  2.2 9.2 %copy-start.13 = (f32[768]{0:T(1024)S(1)}, f32[768]{0:T(1024)}, u32[]{:S(2)}) copy-start(f32[768]{0:T(1024)} %gain.3) | copy-start | bytes 9220
  3.2 11.1 %collective-permute-start.1 = (bf16[324,128]{1,0:T(8,128)(2,1)S(1)}, bf16[324,128]{1,0:T(8,128)(2,1)S(1)}, u32[]{:S(2)}, u32[]{:S(2)}) collective-permute-start(bf16[324,128]{1,0:T(8,128)(2,1)S(1)} %get-tuple-element.34), channel_id=1, source_target_pairs={{0,4},{1,5},{2,6},{3,7},{4,0},{5,1},{6,2},{7,3},{8,12},{9,13},{10,... | collective-permute-start | bytes 248840 | tf_op jit(solution)/shard_map/ppermute | solution.py:145
  7.3 4.0 %collective-permute-start = (bf16[2,48,128]{2,1,0:T(8,128)(2,1)S(1)}, bf16[2,48,128]{2,1,0:T(8,128)(2,1)S(1)}, u32[]{:S(2)}, u32[]{:S(2)}) collective-permute-start(bf16[2,48,128]{2,1,0:T(8,128)(2,1)S(1)} %get-tuple-element.30), channel_id=1, source_target_pairs={{0,8},{8,0},{16,24},{24,16},{1,9},{9,1},{17,25},{25,17},{2,10},{10... | collective-permute-start | bytes 73736 | tf_op jit(solution)/shard_map/ppermute | solution.py:145
  7.3 4.0 %collective-permute-start.2 = (bf16[2,48,128]{2,1,0:T(8,128)(2,1)S(1)}, bf16[2,48,128]{2,1,0:T(8,128)(2,1)S(1)}, u32[]{:S(2)}, u32[]{:S(2)}) collective-permute-start(bf16[2,48,128]{2,1,0:T(8,128)(2,1)S(1)} %get-tuple-element.32), channel_id=1, source_target_pairs={{8,16},{24,0},{16,8},{0,24},{9,17},{25,1},{17,9},{1,25},{10,18},{2... | collective-permute-start | bytes 73736 | tf_op jit(solution)/shard_map/ppermute | solution.py:556
  8.9 15.0 %copy-start.5 = (bf16[768,768]{1,0:T(8,128)(2,1)S(1)}, bf16[768,768]{1,0:T(8,128)(2,1)}, u32[]{:S(2)}) copy-start(bf16[768,768]{1,0:T(8,128)(2,1)} %wg.3) | copy-start | bytes 3538948
  11.4 12.6 %copy-start.4 = (bf16[768,768]{1,0:T(8,128)(2,1)S(1)}, bf16[768,768]{1,0:T(8,128)(2,1)}, u32[]{:S(2)}) copy-start(bf16[768,768]{1,0:T(8,128)(2,1)} %wq.3) | copy-start | bytes 3538948
  13.5 7.8 %collective-permute-start.4 = (bf16[1,72,768]{2,1,0:T(8,128)(2,1)S(1)}, bf16[1,72,768]{2,1,0:T(8,128)(2,1)S(1)}, u32[]{:S(2)}, u32[]{:S(2)}) collective-permute-start(bf16[1,72,768]{2,1,0:T(8,128)(2,1)S(1)} %bitcast.15), channel_id=1, source_target_pairs={{0,16},{8,24},{16,0},{24,8},{1,17},{9,25},{17,1},{25,9},{2,18},{10... | collective-permute-start | bytes 331784 | tf_op jit(solution)/shard_map/ppermute | solution.py:145
  14.3 9.6 %copy-start.3 = (bf16[768,768]{1,0:T(8,128)(2,1)S(1)}, bf16[768,768]{1,0:T(8,128)(2,1)}, u32[]{:S(2)}) copy-start(bf16[768,768]{1,0:T(8,128)(2,1)} %refs_13_.1) | copy-start | bytes 3538948
  14.4 7.0 %collective-permute-start.6 = (bf16[2,180,128]{2,1,0:T(8,128)(2,1)S(1)}, bf16[2,180,128]{2,1,0:T(8,128)(2,1)S(1)}, u32[]{:S(2)}, u32[]{:S(2)}) collective-permute-start(bf16[2,180,128]{2,1,0:T(8,128)(2,1)S(1)} %pad_maximum_fusion.4), channel_id=1, source_target_pairs={{0,1},{1,0},{2,3},{3,2},{4,5},{5,4},{6,7},{7,6},{8,9},{9,8},{10,11... | collective-permute-start | bytes 276488 | tf_op jit(solution)/shard_map/ppermute | solution.py:145
  15.9 5.5 %collective-permute-start.5 = (bf16[2,144,128]{2,1,0:T(8,128)(2,1)S(1)}, bf16[2,144,128]{2,1,0:T(8,128)(2,1)S(1)}, u32[]{:S(2)}, u32[]{:S(2)}) collective-permute-start(bf16[2,144,128]{2,1,0:T(8,128)(2,1)S(1)} %pad_maximum_fusion.5), channel_id=1, source_target_pairs={{0,2},{1,3},{2,0},{3,1},{4,6},{5,7},{6,4},{7,5},{8,10},{9,11},{10,... | collective-permute-start | bytes 221192 | tf_op jit(solution)/shard_map/ppermute | solution.py:145
  17.6 6.4 %copy-start.2 = (bf16[768,768]{1,0:T(8,128)(2,1)S(1)}, bf16[768,768]{1,0:T(8,128)(2,1)}, u32[]{:S(2)}) copy-start(bf16[768,768]{1,0:T(8,128)(2,1)} %refs_12_.1) | copy-start | bytes 3538948
  19.8 4.1 %copy-start.1 = (bf16[768,768]{1,0:T(8,128)(2,1)S(1)}, bf16[768,768]{1,0:T(8,128)(2,1)}, u32[]{:S(2)}) copy-start(bf16[768,768]{1,0:T(8,128)(2,1)} %refs_11_.1) | copy-start | bytes 3538948
  21.3 2.6 %collective-permute-start.7 = (bf16[2,72,768]{2,1,0:T(8,128)(2,1)S(1)}, bf16[2,72,768]{2,1,0:T(8,128)(2,1)S(1)}, u32[]{:S(2)}, u32[]{:S(2)}) collective-permute-start(bf16[2,72,768]{2,1,0:T(8,128)(2,1)S(1)} %pad_maximum_fusion.near), channel_id=1, source_target_pairs={{0,8},{8,0},{16,24},{24,16},{1,9},{9,1},{17,25},{25,17},{2,10},{10... | collective-permute-start | bytes 663560 | tf_op jit(solution)/shard_map/ppermute | solution.py:145
  21.4 7.2 %collective-permute-start.9 = (bf16[4,180,128]{2,1,0:T(8,128)(2,1)S(1)}, bf16[4,180,128]{2,1,0:T(8,128)(2,1)S(1)}, u32[]{:S(2)}, u32[]{:S(2)}) collective-permute-start(bf16[4,180,128]{2,1,0:T(8,128)(2,1)S(1)} %pad_maximum_fusion.2.refs_2_), channel_id=1, source_target_pairs={{0,2},{1,3},{2,0},{3,1},{4,6},{5,7},{6,4},{7,5},{8,10},{9,11},{10,... | collective-permute-start | bytes 552968 | tf_op jit(solution)/shard_map/ppermute | solution.py:145
  22.0 6.0 %collective-permute-start.8 = (bf16[4,144,128]{2,1,0:T(8,128)(2,1)S(1)}, bf16[4,144,128]{2,1,0:T(8,128)(2,1)S(1)}, u32[]{:S(2)}, u32[]{:S(2)}) collective-permute-start(bf16[4,144,128]{2,1,0:T(8,128)(2,1)S(1)} %pad_maximum_fusion.3.refs_0_), channel_id=1, source_target_pairs={{0,1},{1,0},{2,3},{3,2},{4,5},{5,4},{6,7},{7,6},{8,9},{9,8},{10,11... | collective-permute-start | bytes 442376 | tf_op jit(solution)/shard_map/ppermute | solution.py:145
  22.6 4.8 %collective-permute-start.3 = (bf16[1,72,768]{2,1,0:T(8,128)(2,1)S(1)}, bf16[1,72,768]{2,1,0:T(8,128)(2,1)S(1)}, u32[]{:S(2)}, u32[]{:S(2)}) collective-permute-start(bf16[1,72,768]{2,1,0:T(8,128)(2,1)S(1)} %bitcast.13), channel_id=1, source_target_pairs={{0,16},{8,24},{16,0},{24,8},{1,17},{9,25},{17,1},{25,9},{2,18},{10... | collective-permute-start | bytes 331784 | tf_op jit(solution)/shard_map/ppermute | solution.py:145
  28.6 1.5 %collective-permute-start.10 = (bf16[2,72,768]{2,1,0:T(8,128)(2,1)S(1)}, bf16[2,72,768]{2,1,0:T(8,128)(2,1)S(1)}, u32[]{:S(2)}, u32[]{:S(2)}) collective-permute-start(bf16[2,72,768]{2,1,0:T(8,128)(2,1)S(1)} %pad_maximum_fusion.1.near), channel_id=1, source_target_pairs={{0,8},{8,0},{16,24},{24,16},{1,9},{9,1},{17,25},{25,17},{2,10},{10... | collective-permute-start | bytes 663560 | tf_op jit(solution)/shard_map/ppermute | solution.py:145

commit v14 on v13

--- a/solution.py
+++ b/solution.py
@@ -346,12 +346,37 @@
     return jnp.concatenate([blocks[j].astype(F32) for j in range(blocks.shape[0])], axis=0).astype(BF16)
 
 
-def project_kernel(near, far, wq, wk, wv, wg, wo, q, kt, v, gate):
+def tiles_of(h):
+    return range(h * HEAD_DIM // LANES * LANES, (h + 1) * HEAD_DIM, LANES)
+
+
+def channels(rows, at, h):
+    lane = iota((rows, LANES), 1)
+    low = h * HEAD_DIM - at
+    return (lane >= low) & (lane < low + HEAD_DIM)
+
+
+def head_scores(q, kt, base, heads):
+    rows = q.shape[0]
+    blank = jnp.zeros((rows, LANES), F32)
+    both = [(at, q[:, at : at + LANES].astype(F32)) for at in (base, base + LANES)]
+    mine = [
+        [jnp.where(channels(rows, at, h), part, 0.0) if at in tiles_of(h) else blank for at, part in both]
+        for h in heads
+    ]
+    mine = jnp.concatenate([jnp.concatenate(pair, axis=1) for pair in mine], axis=0).astype(BF16)
+    return dot(mine, kt[base : base + 2 * LANES]) * (LOG2E / HEAD_DIM**0.5)
+
+
+def project_kernel(near, far, wq, wk, wv, wg, wo, scores, v, gate, q, kt):
     x = jnp.concatenate([stack(near), stack(far)], axis=0)
+    rows = near.shape[1]
     q[...] = dot(near[0], wq[...]).astype(BF16)
-    gate[...] = jax.nn.sigmoid(dot(near[0], wg[...]))
     for c in range(0, x.shape[1], 2 * LANES):
         kt[c : c + 2 * LANES] = dot(x, wk[:, c : c + 2 * LANES]).T.astype(BF16)
+    for base, heads in head_groups(x.shape[1]):
+        scores[heads[0] * rows : (heads[-1] + 1) * rows] = head_scores(q, kt, base, heads)
+    gate[...] = jax.nn.sigmoid(dot(near[0], wg[...]))
     v[...] = dot(x, wv[...]).astype(BF16)
 
 
@@ -362,13 +387,13 @@
     return pl.pallas_call(
         project_kernel,
         out_shape=[
-            jax.ShapeDtypeStruct((rows, width), BF16),
-            jax.ShapeDtypeStruct((width, keys), BF16),
+            jax.ShapeDtypeStruct((HEADS * rows, keys), F32),
             jax.ShapeDtypeStruct((keys, width), BF16),
             jax.ShapeDtypeStruct((rows, width), F32),
         ],
         in_specs=[vmem] * 7,
-        out_specs=[vmem] * 4,
+        out_specs=[vmem] * 3,
+        scratch_shapes=[pltpu.VMEM((rows, width), BF16), pltpu.VMEM((width, keys), BF16)],
         compiler_params=pltpu.CompilerParams(vmem_limit_bytes=24 * MIB),
         cost_estimate=cost(2),
         name="project",
@@ -439,13 +464,11 @@
 
 
 def attend_kernel(samples, bias, *refs):
-    parts, refs = [refs[5 * s : 5 * s + 5] for s in range(samples)], refs[5 * samples :]
-    far, wk, wv, wo, out, kt, v = refs
-    _, k_near, v_near, _, _ = parts[-1]
-    rows, width = parts[-1][4].shape
+    parts, refs = [refs[4 * s : 4 * s + 4] for s in range(samples - 1)], refs[4 * (samples - 1) :]
+    q, k_near, v_near, gate_last, token_last, far, wk, wv, wo, out, kt, v = refs
+    parts.append((None, v, gate_last, token_last))
+    rows, width = token_last.shape
     x = stack(far)
-    scale = LOG2E / HEAD_DIM**0.5
-    lane = iota((rows, LANES), 1)
     groups = head_groups(width)
     work = [(s, base, heads) for s in range(samples) for base, heads in groups]
     chunks = list(range(0, width, 2 * LANES))
@@ -459,27 +482,12 @@
         v[: v_near.shape[0], lanes] = v_near[:, lanes]
         v[v_near.shape[0] :, lanes] = dot(x, wv[:, lanes]).astype(BF16)
 
-    def tiles_of(h):
-        return range(h * HEAD_DIM // LANES * LANES, (h + 1) * HEAD_DIM, LANES)
-
-    def channels(at, h):
-        low = h * HEAD_DIM - at
-        return (lane >= low) & (lane < low + HEAD_DIM)
-
-    blank = jnp.zeros((rows, LANES), F32)
-
     def score(item):
         if isinstance(item, int):
             return fill(item)
         s, base, heads = item
-        q, keys = parts[s][0], parts[s][1] if s < samples - 1 else kt
-        both = [(at, q[:, at : at + LANES].astype(F32)) for at in (base, base + LANES)]
-        mine = [
-            [jnp.where(channels(at, h), part, 0.0) if at in tiles_of(h) else blank for at, part in both] for h in heads
-        ]
-        mine = jnp.concatenate([jnp.concatenate(pair, axis=1) for pair in mine], axis=0).astype(BF16)
-        some = bias[heads[0] * rows : (heads[-1] + 1) * rows]
-        return item, dot(mine, keys[base : base + 2 * LANES]) * scale + some
+        part = slice(heads[0] * rows, (heads[-1] + 1) * rows)
+        return item, (parts[s][0][part] if s < samples - 1 else head_scores(q, kt, base, heads)) + bias[part]
 
     def soften(item):
         if item is None:
@@ -494,18 +502,17 @@
         if item is None:
             return
         (s, base, heads), e, share = item
-        values = parts[s][2] if s < samples - 1 else v
-        o = dot(e, values[:, base : base + 2 * LANES])
+        o = dot(e, parts[s][1][:, base : base + 2 * LANES])
         for i, h in enumerate(heads):
             part = slice(i * rows, (i + 1) * rows)
             for at in tiles_of(h):
                 one = o[part, at - base : at - base + LANES] * share[part]
-                mixes[s, at] = jnp.where(channels(at, h), one, mixes.get((s, at), 0.0))
+                mixes[s, at] = jnp.where(channels(rows, at, h), one, mixes.get((s, at), 0.0))
         if h == HEADS - 1:
             close(s)
 
     def close(s):
-        gate, token_in = parts[s][3:]
+        gate, token_in = parts[s][2:]
         gated = jnp.concatenate([mixes[s, at] for at in range(0, width, LANES)], axis=1) * gate[...]
         out[s] = (token_in[...] + dot(gated.astype(BF16), wo[...])).astype(BF16)
 

time: 33.9 us -> 33.7 us (level)
  waiting for transfers between devices: 3.62 us -> 3.19 us
    pallas_call x1, Pallas kernels: 1.27 us -> 1.7 us  [project(): pl.pallas_call(project_kernel, out_shape=[jax.ShapeDtypeStruct((HEADS * r...]
    ppermute x10, waiting for transfers between devices: 3.61 us -> 3.19 us  [swap(): lax.ppermute(held, axis, [(i, i ^ far) for i in range(lax.axis_size(axis))])]
  transfers between devices with their start and end apart: 11 -> 11, of which waited for: 4 -> 4; matrix products, arithmetic and copies ran while one was open for 0% -> 0% of each run, Pallas kernels for 32% -> 33%
where the time goes in v14:
time: 33.7 us; the launch traced here: 33.5 us
  Pallas kernels  16.3 us (48%)
  starting transfers between devices  12.3 us (36%)
  waiting for transfers between devices  3.19 us (9%)
  local copies, waits for them, and re-layouts  1.25 us (4%)
    ppermute x10, starting transfers between devices, swap(): lax.ppermute(held, axis, [(i, i ^ far) for i in range(lax.axis_size(axis))])  10.7 us
    pallas_call x2, Pallas kernels, atom_attention(): pl.pallas_call(functools.partial(atom_kernel, sample), out_shape=jax.Shap...  4.62 us
    pallas_call x2, Pallas kernels, gather_tokens(): pl.pallas_call(functools.partial(gather_kernel, sample), out_shape=[jax.S...  3.51 us
    pallas_call x1, Pallas kernels, attend(): pl.pallas_call(functools.partial(attend_kernel, len(parts)), out_shape=ja...  3.36 us
    ppermute x10, waiting for transfers between devices, swap(): lax.ppermute(held, axis, [(i, i ^ far) for i in range(lax.axis_size(axis))])  3.19 us
    pallas_call x1, Pallas kernels, project(): pl.pallas_call(project_kernel, out_shape=[jax.ShapeDtypeStruct((HEADS * r...  1.7 us
    ppermute x1, starting transfers between devices, shards(): lax.ppermute(outer, 'row', odd_pairs + [(j, i) for i, j in odd_pairs])  1.63 us
    unnamed x32, local copies, waits for them, and re-layouts  1.23 us
  transfers between devices with their start and end apart: 11, of which 4 were waited for; matrix products, arithmetic and copies ran while one was open for 0% of the time, Pallas kernels for 33%

profile of v14, /device:TPU:0, one launch (start us, length us, event | category | flops | bytes accessed | tf_op | source)
XLA Modules:
  0.0 33.5 jit_solution(10362872196538849468)
XLA Ops:
  0.0 1.2 %copy-done.7 = bf16[72,36,128]{2,0,1:T(8,128)(2,1)S(1)} copy-done((bf16[72,36,128]{2,0,1:T(8,128)(2,1)S(1)}, bf16[72,36,128]{2,0,1:T(8,128)(2,1)}, u32[]{:S(2)}) %copy-start.7) | copy-done | bytes 663576
  1.2 0.9 %normalise_pairs.1.normed = f32[36,72,128]{2,1,0:T(8,128)S(1)} custom-call(bf16[36,72,128]{2,1,0:T(8,128)(2,1)S(1)} %bitcast.12), custom_call_target="tpu_custom_call" | custom-call | flops 20000000 | bytes 1000 | tf_op jit(solution)/shard_map/normalise_pairs/pallas_call | solution.py:72
  2.1 0.0 copy-start.8
  2.1 0.0 copy-start.9
  2.1 0.0 copy-start.10
  2.1 0.0 copy-start.6
  2.1 0.0 copy-start.12
  2.2 0.0 copy-start.13
  2.2 1.0 %pair_bias.1 = (bf16[324,128]{1,0:T(8,128)(2,1)S(1)}, bf16[2,48,128]{2,1,0:T(8,128)(2,1)S(1)}, bf16[2,48,128]{2,1,0:T(8,128)(2,1)S(1)}) custom-call(bf16[2,1152,128]{2,1,0:T(8,128)(2,1)S(1)} %copy-done, f32[36,72,128]{2,1,0:T(8,128)S(1)} %normalise_pairs.1.normed, s32[36]{0:T(128)S(1)} %copy-done.15, bf16[16,128]{1,0:T(8,128)(2,1)S(1)} %bitcast.17), custom_call_target="tpu_custom_call" | custom-call | flops 60000000 | bytes 1000 | tf_op jit(solution)/shard_map/pair_bias/pallas_call | solution.py:124
  3.2 4.1 %collective-permute-start.1 = (bf16[324,128]{1,0:T(8,128)(2,1)S(1)}, bf16[324,128]{1,0:T(8,128)(2,1)S(1)}, u32[]{:S(2)}, u32[]{:S(2)}) collective-permute-start(bf16[324,128]{1,0:T(8,128)(2,1)S(1)} %get-tuple-element.33), channel_id=1, source_target_pairs={{0,4},{1,5},{2,6},{3,7},{4,0},{5,1},{6,2},{7,3},{8,12},{9,13},{10,... | collective-permute-start | bytes 248840 | tf_op jit(solution)/shard_map/ppermute | solution.py:145
  7.3 1.6 %collective-permute-start.2 = (bf16[2,48,128]{2,1,0:T(8,128)(2,1)S(1)}, bf16[2,48,128]{2,1,0:T(8,128)(2,1)S(1)}, u32[]{:S(2)}, u32[]{:S(2)}) collective-permute-start(bf16[2,48,128]{2,1,0:T(8,128)(2,1)S(1)} %get-tuple-element.31), channel_id=1, source_target_pairs={{8,16},{24,0},{16,8},{0,24},{9,17},{25,1},{17,9},{1,25},{10,18},{2... | collective-permute-start | bytes 73736 | tf_op jit(solution)/shard_map/ppermute | solution.py:563
  9.0 2.4 %atom_attention.2.mixed = bf16[1152,128]{1,0:T(8,128)(2,1)S(1)} custom-call(bf16[2,1152,128]{2,1,0:T(8,128)(2,1)S(1)} %copy-done, bf16[128,128]{1,0:T(8,128)(2,1)S(1)} %copy-done.8, bf16[128,128]{1,0:T(8,128)(2,1)S(1)} %copy-done.9, bf16[128,128]{1,0:T(8,128)(2,1)S(1)} %copy-done.10), custom_call_target="tpu_custom_call" | custom-call | flops 80000000 | bytes 1000 | tf_op jit(solution)/shard_map/atom_attention/pallas_call | solution.py:254
  11.4 0.0 copy-start.4
  11.4 2.1 %gather_tokens.2 = (f32[72,768]{1,0:T(8,128)S(1)}, bf16[72,768]{1,0:T(8,128)(2,1)S(1)}) custom-call(bf16[1152,128]{1,0:T(8,128)(2,1)S(1)} %atom_attention.2.mixed, bf16[2,1152,128]{2,1,0:T(8,128)(2,1)S(1)} %copy-done, s32[1152]{0:T(1024)S(1)} %copy-done.12, bf16[128,128]{1,0:T(8,128)(2,1)S(1)} %copy-done.11, bf16[128,768]{1,0:T(8,128)(2,1)S(1)} %copy-done.6, ...), custom_call_target="tpu_custom_call" | custom-call | flops 20000000 | bytes 1000 | tf_op jit(solution)/shard_map/gather_tokens/pallas_call | solution.py:324
  13.5 0.8 %collective-permute-start.4 = (bf16[1,72,768]{2,1,0:T(8,128)(2,1)S(1)}, bf16[1,72,768]{2,1,0:T(8,128)(2,1)S(1)}, u32[]{:S(2)}, u32[]{:S(2)}) collective-permute-start(bf16[1,72,768]{2,1,0:T(8,128)(2,1)S(1)} %bitcast.15), channel_id=1, source_target_pairs={{0,16},{8,24},{16,0},{24,8},{1,17},{9,25},{17,1},{25,9},{2,18},{10... | collective-permute-start | bytes 331784 | tf_op jit(solution)/shard_map/ppermute | solution.py:145
  14.3 0.0 copy-start.3
  14.4 1.6 %collective-permute-start.6 = (bf16[2,180,128]{2,1,0:T(8,128)(2,1)S(1)}, bf16[2,180,128]{2,1,0:T(8,128)(2,1)S(1)}, u32[]{:S(2)}, u32[]{:S(2)}) collective-permute-start(bf16[2,180,128]{2,1,0:T(8,128)(2,1)S(1)} %pad_maximum_fusion.4), channel_id=1, source_target_pairs={{0,1},{1,0},{2,3},{3,2},{4,5},{5,4},{6,7},{7,6},{8,9},{9,8},{10,11... | collective-permute-start | bytes 276488 | tf_op jit(solution)/shard_map/ppermute | solution.py:145
  15.9 1.6 %collective-permute-start.5 = (bf16[2,144,128]{2,1,0:T(8,128)(2,1)S(1)}, bf16[2,144,128]{2,1,0:T(8,128)(2,1)S(1)}, u32[]{:S(2)}, u32[]{:S(2)}) collective-permute-start(bf16[2,144,128]{2,1,0:T(8,128)(2,1)S(1)} %pad_maximum_fusion.5), channel_id=1, source_target_pairs={{0,2},{1,3},{2,0},{3,1},{4,6},{5,7},{6,4},{7,5},{8,10},{9,11},{10,... | collective-permute-start | bytes 221192 | tf_op jit(solution)/shard_map/ppermute | solution.py:145
  17.6 2.3 %atom_attention.3.mixed = bf16[1152,128]{1,0:T(8,128)(2,1)S(1)} custom-call(bf16[2,1152,128]{2,1,0:T(8,128)(2,1)S(1)} %copy-done, bf16[2,48,128]{2,1,0:T(8,128)(2,1)S(1)} %collective-permute-done.refs_0_, bf16[2,48,128]{2,1,0:T(8,128)(2,1)S(1)} %collective-permute-done.2.refs_1_, bf16[128,128]{1,0:T(8,128)(2,1)S(1)} %copy-done.8, ...), custom_call_target="tpu_custom_call" | custom-call | flops 80000000 | bytes 1000 | tf_op jit(solution)/shard_map/atom_attention/pallas_call | solution.py:254
  19.8 1.4 %gather_tokens.3 = (f32[72,768]{1,0:T(8,128)S(1)}, bf16[72,768]{1,0:T(8,128)(2,1)S(1)}) custom-call(bf16[1152,128]{1,0:T(8,128)(2,1)S(1)} %atom_attention.3.mixed, bf16[2,1152,128]{2,1,0:T(8,128)(2,1)S(1)} %copy-done, s32[1152]{0:T(1024)S(1)} %copy-done.12, bf16[128,128]{1,0:T(8,128)(2,1)S(1)} %copy-done.11, bf16[128,768]{1,0:T(8,128)(2,1)S(1)} %copy-done.6, ...), custom_call_target="tpu_custom_call" | custom-call | flops 20000000 | bytes 1000 | tf_op jit(solution)/shard_map/gather_tokens/pallas_call | solution.py:324
  21.3 0.1 collective-permute-start.7
  21.4 0.6 %collective-permute-start.9 = (bf16[4,180,128]{2,1,0:T(8,128)(2,1)S(1)}, bf16[4,180,128]{2,1,0:T(8,128)(2,1)S(1)}, u32[]{:S(2)}, u32[]{:S(2)}) collective-permute-start(bf16[4,180,128]{2,1,0:T(8,128)(2,1)S(1)} %pad_maximum_fusion.2.refs_2_), channel_id=1, source_target_pairs={{0,2},{1,3},{2,0},{3,1},{4,6},{5,7},{6,4},{7,5},{8,10},{9,11},{10,... | collective-permute-start | bytes 552968 | tf_op jit(solution)/shard_map/ppermute | solution.py:145
  22.0 0.6 %collective-permute-start.8 = (bf16[4,144,128]{2,1,0:T(8,128)(2,1)S(1)}, bf16[4,144,128]{2,1,0:T(8,128)(2,1)S(1)}, u32[]{:S(2)}, u32[]{:S(2)}) collective-permute-start(bf16[4,144,128]{2,1,0:T(8,128)(2,1)S(1)} %pad_maximum_fusion.3.refs_0_), channel_id=1, source_target_pairs={{0,1},{1,0},{2,3},{3,2},{4,5},{5,4},{6,7},{7,6},{8,9},{9,8},{10,11... | collective-permute-start | bytes 442376 | tf_op jit(solution)/shard_map/ppermute | solution.py:145
  22.6 1.3 %collective-permute-start.3 = (bf16[1,72,768]{2,1,0:T(8,128)(2,1)S(1)}, bf16[1,72,768]{2,1,0:T(8,128)(2,1)S(1)}, u32[]{:S(2)}, u32[]{:S(2)}) collective-permute-start(bf16[1,72,768]{2,1,0:T(8,128)(2,1)S(1)} %bitcast.13), channel_id=1, source_target_pairs={{0,16},{8,24},{16,0},{24,8},{1,17},{9,25},{17,1},{25,9},{2,18},{10... | collective-permute-start | bytes 331784 | tf_op jit(solution)/shard_map/ppermute | solution.py:145
  24.0 1.7 %project.1 = (f32[1152,288]{1,0:T(8,128)S(1)}, bf16[288,768]{1,0:T(8,128)(2,1)S(1)}, f32[72,768]{1,0:T(8,128)S(1)}) custom-call(bf16[2,72,768]{2,1,0:T(8,128)(2,1)S(1)} %pad_maximum_fusion.near, bf16[2,72,768]{2,1,0:T(8,128)(2,1)S(1)} %collective-permute-done.7.far, bf16[768,768]{1,0:T(8,128)(2,1)S(1)} %copy-done.4, bf16[768,768]{1,0:T(8,128)(2,1)S(1)} %copy-done.1, ...), custom_call_target="tpu_custom_call" | custom-call | flops 40000000 | bytes 1000 | tf_op jit(solution)/shard_map/project/pallas_call | solution.py:387
  25.7 1.8 %collective-permute-done.3 = bf16[1,72,768]{2,1,0:T(8,128)(2,1)S(1)} collective-permute-done((bf16[1,72,768]{2,1,0:T(8,128)(2,1)S(1)}, bf16[1,72,768]{2,1,0:T(8,128)(2,1)S(1)}, u32[]{:S(2)}, u32[]{:S(2)}) %collective-permute-start.3) | collective-permute-done | bytes 110624 | tf_op jit(solution)/shard_map/ppermute | solution.py:145
  27.5 0.5 %collective-permute-done.8.refs_1_ = bf16[4,144,128]{2,1,0:T(8,128)(2,1)S(1)} collective-permute-done((bf16[4,144,128]{2,1,0:T(8,128)(2,1)S(1)}, bf16[4,144,128]{2,1,0:T(8,128)(2,1)S(1)}, u32[]{:S(2)}, u32[]{:S(2)}) %collective-permute-start.8) | collective-permute-done | bytes 147488 | tf_op jit(solution)/shard_map/ppermute | solution.py:145
  28.0 0.6 %collective-permute-done.9.refs_3_ = bf16[4,180,128]{2,1,0:T(8,128)(2,1)S(1)} collective-permute-done((bf16[4,180,128]{2,1,0:T(8,128)(2,1)S(1)}, bf16[4,180,128]{2,1,0:T(8,128)(2,1)S(1)}, u32[]{:S(2)}, u32[]{:S(2)}) %collective-permute-start.9) | collective-permute-done | bytes 184352 | tf_op jit(solution)/shard_map/ppermute | solution.py:145
  28.6 0.1 collective-permute-start.10
  28.7 1.2 %turn_bias.1 = (bf16[72,768]{1,0:T(8,128)(2,1)S(1)}, bf16[144,768]{1,0:T(8,128)(2,1)S(1)}, bf16[144,768]{1,0:T(8,128)(2,1)S(1)}, f32[72,768]{1,0:T(8,128)S(1)}, f32[1152,288]{1,0:T(8,128)S(1)}) custom-call(bf16[2,72,768]{2,1,0:T(8,128)(2,1)S(1)} %pad_maximum_fusion.1.near, bf16[768,768]{1,0:T(8,128)(2,1)S(1)} %copy-done.4, bf16[768,768]{1,0:T(8,128)(2,1)S(1)} %copy-done.1, ...), custom_call_target="tpu_custom_call" | custom-call | flops 20000000 | bytes 1000 | tf_op jit(solution)/shard_map/turn_bias/pallas_call | solution.py:448
  29.9 0.2 collective-permute-done.10.refs_9_
  30.2 3.4 %attend.1 = bf16[2,72,768]{2,1,0:T(8,128)(2,1)} custom-call(f32[1152,288]{1,0:T(8,128)S(1)} %get-tuple-element.47.bias, f32[1152,288]{1,0:T(8,128)S(1)} %get-tuple-element.41.refs_0_, bf16[288,768]{1,0:T(8,128)(2,1)S(1)} %get-tuple-element.42.refs_1_, f32[72,768]{1,0:T(8,128)S(1)} %get-tuple-element.43.refs_2_, f32[72,768]{1,0:T(8,128)S(1)} %get-tuple-element.44.refs_3_, ...), custom_call_target="tpu_custom_call" | custom-call | flops 60000000 | bytes 1000 | tf_op jit(solution)/shard_map/attend/pallas_call | solution.py:527
  (39 shorter events, 0.2 us)
Async XLA Ops:
  0.0 2.1 %copy-start = (bf16[2,1152,128]{2,1,0:T(8,128)(2,1)S(1)}, bf16[2,1152,128]{2,1,0:T(8,128)(2,1)}, u32[]{:S(2)}) copy-start(bf16[2,1152,128]{2,1,0:T(8,128)(2,1)} %feat.9) | copy-start | bytes 1769476
  0.0 1.2 %copy-start.7 = (bf16[72,36,128]{2,0,1:T(8,128)(2,1)S(1)}, bf16[72,36,128]{2,0,1:T(8,128)(2,1)}, u32[]{:S(2)}) copy-start(bf16[72,36,128]{2,0,1:T(8,128)(2,1)} %param.18) | copy-start | bytes 1990660
  1.2 0.9 %copy-start.14 = (bf16[128,16]{0,1:T(8,128)(2,1)S(1)}, bf16[128,16]{0,1:T(8,128)(2,1)}, u32[]{:S(2)}) copy-start(bf16[128,16]{0,1:T(8,128)(2,1)} %param.25) | copy-start | bytes 12292
  1.2 1.0 %copy-start.15 = (s32[36]{0:T(128)S(1)}, s32[36]{0:T(128)}, u32[]{:S(2)}) copy-start(s32[36]{0:T(128)} %mask.1) | copy-start | bytes 436
  2.1 6.9 %copy-start.8 = (bf16[128,128]{1,0:T(8,128)(2,1)S(1)}, bf16[128,128]{1,0:T(8,128)(2,1)}, u32[]{:S(2)}) copy-start(bf16[128,128]{1,0:T(8,128)(2,1)} %refs_2_.5) | copy-start | bytes 98308
  2.1 6.9 %copy-start.9 = (bf16[128,128]{1,0:T(8,128)(2,1)S(1)}, bf16[128,128]{1,0:T(8,128)(2,1)}, u32[]{:S(2)}) copy-start(bf16[128,128]{1,0:T(8,128)(2,1)} %refs_3_.3) | copy-start | bytes 98308
  2.1 6.9 %copy-start.10 = (bf16[128,128]{1,0:T(8,128)(2,1)S(1)}, bf16[128,128]{1,0:T(8,128)(2,1)}, u32[]{:S(2)}) copy-start(bf16[128,128]{1,0:T(8,128)(2,1)} %refs_4_.3) | copy-start | bytes 98308
  2.1 9.2 %copy-start.6 = (bf16[128,768]{1,0:T(8,128)(2,1)S(1)}, bf16[128,768]{1,0:T(8,128)(2,1)}, u32[]{:S(2)}) copy-start(bf16[128,768]{1,0:T(8,128)(2,1)} %agg.3) | copy-start | bytes 589828
  2.1 9.2 %copy-start.11 = (bf16[128,128]{1,0:T(8,128)(2,1)S(1)}, bf16[128,128]{1,0:T(8,128)(2,1)}, u32[]{:S(2)}) copy-start(bf16[128,128]{1,0:T(8,128)(2,1)} %wo.4) | copy-start | bytes 98308
  2.1 9.2 %copy-start.12 = (s32[1152]{0:T(1024)S(1)}, s32[1152]{0:T(1024)}, u32[]{:S(2)}) copy-start(s32[1152]{0:T(1024)} %token_.3) | copy-start | bytes 13828
  2.2 9.2 %copy-start.13 = (f32[768]{0:T(1024)S(1)}, f32[768]{0:T(1024)}, u32[]{:S(2)}) copy-start(f32[768]{0:T(1024)} %gain.3) | copy-start | bytes 9220
  3.2 11.1 %collective-permute-start.1 = (bf16[324,128]{1,0:T(8,128)(2,1)S(1)}, bf16[324,128]{1,0:T(8,128)(2,1)S(1)}, u32[]{:S(2)}, u32[]{:S(2)}) collective-permute-start(bf16[324,128]{1,0:T(8,128)(2,1)S(1)} %get-tuple-element.33), channel_id=1, source_target_pairs={{0,4},{1,5},{2,6},{3,7},{4,0},{5,1},{6,2},{7,3},{8,12},{9,13},{10,... | collective-permute-start | bytes 248840 | tf_op jit(solution)/shard_map/ppermute | solution.py:145
  7.3 4.0 %collective-permute-start = (bf16[2,48,128]{2,1,0:T(8,128)(2,1)S(1)}, bf16[2,48,128]{2,1,0:T(8,128)(2,1)S(1)}, u32[]{:S(2)}, u32[]{:S(2)}) collective-permute-start(bf16[2,48,128]{2,1,0:T(8,128)(2,1)S(1)} %get-tuple-element.29), channel_id=1, source_target_pairs={{0,8},{8,0},{16,24},{24,16},{1,9},{9,1},{17,25},{25,17},{2,10},{10... | collective-permute-start | bytes 73736 | tf_op jit(solution)/shard_map/ppermute | solution.py:145
  7.3 4.0 %collective-permute-start.2 = (bf16[2,48,128]{2,1,0:T(8,128)(2,1)S(1)}, bf16[2,48,128]{2,1,0:T(8,128)(2,1)S(1)}, u32[]{:S(2)}, u32[]{:S(2)}) collective-permute-start(bf16[2,48,128]{2,1,0:T(8,128)(2,1)S(1)} %get-tuple-element.31), channel_id=1, source_target_pairs={{8,16},{24,0},{16,8},{0,24},{9,17},{25,1},{17,9},{1,25},{10,18},{2... | collective-permute-start | bytes 73736 | tf_op jit(solution)/shard_map/ppermute | solution.py:563
  8.9 15.0 %copy-start.5 = (bf16[768,768]{1,0:T(8,128)(2,1)S(1)}, bf16[768,768]{1,0:T(8,128)(2,1)}, u32[]{:S(2)}) copy-start(bf16[768,768]{1,0:T(8,128)(2,1)} %wg.3) | copy-start | bytes 3538948
  11.4 12.6 %copy-start.4 = (bf16[768,768]{1,0:T(8,128)(2,1)S(1)}, bf16[768,768]{1,0:T(8,128)(2,1)}, u32[]{:S(2)}) copy-start(bf16[768,768]{1,0:T(8,128)(2,1)} %wq.3) | copy-start | bytes 3538948
  13.5 7.8 %collective-permute-start.4 = (bf16[1,72,768]{2,1,0:T(8,128)(2,1)S(1)}, bf16[1,72,768]{2,1,0:T(8,128)(2,1)S(1)}, u32[]{:S(2)}, u32[]{:S(2)}) collective-permute-start(bf16[1,72,768]{2,1,0:T(8,128)(2,1)S(1)} %bitcast.15), channel_id=1, source_target_pairs={{0,16},{8,24},{16,0},{24,8},{1,17},{9,25},{17,1},{25,9},{2,18},{10... | collective-permute-start | bytes 331784 | tf_op jit(solution)/shard_map/ppermute | solution.py:145
  14.3 9.6 %copy-start.3 = (bf16[768,768]{1,0:T(8,128)(2,1)S(1)}, bf16[768,768]{1,0:T(8,128)(2,1)}, u32[]{:S(2)}) copy-start(bf16[768,768]{1,0:T(8,128)(2,1)} %refs_12_.1) | copy-start | bytes 3538948
  14.4 7.0 %collective-permute-start.6 = (bf16[2,180,128]{2,1,0:T(8,128)(2,1)S(1)}, bf16[2,180,128]{2,1,0:T(8,128)(2,1)S(1)}, u32[]{:S(2)}, u32[]{:S(2)}) collective-permute-start(bf16[2,180,128]{2,1,0:T(8,128)(2,1)S(1)} %pad_maximum_fusion.4), channel_id=1, source_target_pairs={{0,1},{1,0},{2,3},{3,2},{4,5},{5,4},{6,7},{7,6},{8,9},{9,8},{10,11... | collective-permute-start | bytes 276488 | tf_op jit(solution)/shard_map/ppermute | solution.py:145
  15.9 5.5 %collective-permute-start.5 = (bf16[2,144,128]{2,1,0:T(8,128)(2,1)S(1)}, bf16[2,144,128]{2,1,0:T(8,128)(2,1)S(1)}, u32[]{:S(2)}, u32[]{:S(2)}) collective-permute-start(bf16[2,144,128]{2,1,0:T(8,128)(2,1)S(1)} %pad_maximum_fusion.5), channel_id=1, source_target_pairs={{0,2},{1,3},{2,0},{3,1},{4,6},{5,7},{6,4},{7,5},{8,10},{9,11},{10,... | collective-permute-start | bytes 221192 | tf_op jit(solution)/shard_map/ppermute | solution.py:145
  17.6 6.4 %copy-start.2 = (bf16[768,768]{1,0:T(8,128)(2,1)S(1)}, bf16[768,768]{1,0:T(8,128)(2,1)}, u32[]{:S(2)}) copy-start(bf16[768,768]{1,0:T(8,128)(2,1)} %refs_11_.1) | copy-start | bytes 3538948
  19.8 4.1 %copy-start.1 = (bf16[768,768]{1,0:T(8,128)(2,1)S(1)}, bf16[768,768]{1,0:T(8,128)(2,1)}, u32[]{:S(2)}) copy-start(bf16[768,768]{1,0:T(8,128)(2,1)} %refs_10_.1) | copy-start | bytes 3538948
  21.3 2.6 %collective-permute-start.7 = (bf16[2,72,768]{2,1,0:T(8,128)(2,1)S(1)}, bf16[2,72,768]{2,1,0:T(8,128)(2,1)S(1)}, u32[]{:S(2)}, u32[]{:S(2)}) collective-permute-start(bf16[2,72,768]{2,1,0:T(8,128)(2,1)S(1)} %pad_maximum_fusion.near), channel_id=1, source_target_pairs={{0,8},{8,0},{16,24},{24,16},{1,9},{9,1},{17,25},{25,17},{2,10},{10... | collective-permute-start | bytes 663560 | tf_op jit(solution)/shard_map/ppermute | solution.py:145
  21.4 7.2 %collective-permute-start.9 = (bf16[4,180,128]{2,1,0:T(8,128)(2,1)S(1)}, bf16[4,180,128]{2,1,0:T(8,128)(2,1)S(1)}, u32[]{:S(2)}, u32[]{:S(2)}) collective-permute-start(bf16[4,180,128]{2,1,0:T(8,128)(2,1)S(1)} %pad_maximum_fusion.2.refs_2_), channel_id=1, source_target_pairs={{0,2},{1,3},{2,0},{3,1},{4,6},{5,7},{6,4},{7,5},{8,10},{9,11},{10,... | collective-permute-start | bytes 552968 | tf_op jit(solution)/shard_map/ppermute | solution.py:145
  22.0 6.0 %collective-permute-start.8 = (bf16[4,144,128]{2,1,0:T(8,128)(2,1)S(1)}, bf16[4,144,128]{2,1,0:T(8,128)(2,1)S(1)}, u32[]{:S(2)}, u32[]{:S(2)}) collective-permute-start(bf16[4,144,128]{2,1,0:T(8,128)(2,1)S(1)} %pad_maximum_fusion.3.refs_0_), channel_id=1, source_target_pairs={{0,1},{1,0},{2,3},{3,2},{4,5},{5,4},{6,7},{7,6},{8,9},{9,8},{10,11... | collective-permute-start | bytes 442376 | tf_op jit(solution)/shard_map/ppermute | solution.py:145
  22.6 4.8 %collective-permute-start.3 = (bf16[1,72,768]{2,1,0:T(8,128)(2,1)S(1)}, bf16[1,72,768]{2,1,0:T(8,128)(2,1)S(1)}, u32[]{:S(2)}, u32[]{:S(2)}) collective-permute-start(bf16[1,72,768]{2,1,0:T(8,128)(2,1)S(1)} %bitcast.13), channel_id=1, source_target_pairs={{0,16},{8,24},{16,0},{24,8},{1,17},{9,25},{17,1},{25,9},{2,18},{10... | collective-permute-start | bytes 331784 | tf_op jit(solution)/shard_map/ppermute | solution.py:145
  28.6 1.5 %collective-permute-start.10 = (bf16[2,72,768]{2,1,0:T(8,128)(2,1)S(1)}, bf16[2,72,768]{2,1,0:T(8,128)(2,1)S(1)}, u32[]{:S(2)}, u32[]{:S(2)}) collective-permute-start(bf16[2,72,768]{2,1,0:T(8,128)(2,1)S(1)} %pad_maximum_fusion.1.near), channel_id=1, source_target_pairs={{0,8},{8,0},{16,24},{24,16},{1,9},{9,1},{17,25},{25,17},{2,10},{10... | collective-permute-start | bytes 663560 | tf_op jit(solution)/shard_map/ppermute | solution.py:145

commit v15 on v14

--- a/solution.py
+++ b/solution.py
@@ -470,10 +470,12 @@
     rows, width = token_last.shape
     x = stack(far)
     groups = head_groups(width)
-    work = [(s, base, heads) for s in range(samples) for base, heads in groups]
+    work = [
+        (s, base, heads[i : i + 3]) for s in range(samples) for base, heads in groups for i in range(0, len(heads), 3)
+    ]
     chunks = list(range(0, width, 2 * LANES))
     for i, c in enumerate(chunks):
-        work.insert(min(2 * i + 1, (samples - 1) * len(groups) + i), c)
+        work.insert(min(2 * i + 1, (samples - 1) * len(work) // samples), c)
 
     def fill(c):
         lanes = slice(c, c + 2 * LANES)
@@ -508,13 +510,19 @@
             for at in tiles_of(h):
                 one = o[part, at - base : at - base + LANES] * share[part]
                 mixes[s, at] = jnp.where(channels(rows, at, h), one, mixes.get((s, at), 0.0))
+        if (h + 1) * HEAD_DIM % LANES == 0:
+            close(s, h)
+
+    sums = {}
+
+    def close(s, h):
+        _, _, gate, token_in = parts[s]
+        lanes = slice((h - 7) * HEAD_DIM, (h + 1) * HEAD_DIM)
+        mixed = jnp.concatenate([mixes[s, at] for at in range(lanes.start, lanes.stop, LANES)], axis=1)
+        part = dot((mixed * gate[:, lanes]).astype(BF16), wo[lanes])
+        sums[s] = sums[s] + part if s in sums else part
         if h == HEADS - 1:
-            close(s)
-
-    def close(s):
-        gate, token_in = parts[s][2:]
-        gated = jnp.concatenate([mixes[s, at] for at in range(0, width, LANES)], axis=1) * gate[...]
-        out[s] = (token_in[...] + dot(gated.astype(BF16), wo[...])).astype(BF16)
+            out[s] = (token_in[...] + sums[s]).astype(BF16)
 
     skewed(work, [score, soften, mix])
 

time: 33.7 us -> 34 us (level)
  no operation moved by 1% of the time
where the time goes in v15:
time: 34 us; the launch traced here: 33.8 us
  Pallas kernels  16.6 us (49%)
  starting transfers between devices  12.3 us (36%)
  waiting for transfers between devices  3.19 us (9%)
  local copies, waits for them, and re-layouts  1.25 us (4%)
    ppermute x10, starting transfers between devices, swap(): lax.ppermute(held, axis, [(i, i ^ far) for i in range(lax.axis_size(axis))])  10.7 us
    pallas_call x2, Pallas kernels, atom_attention(): pl.pallas_call(functools.partial(atom_kernel, sample), out_shape=jax.Shap...  4.62 us
    pallas_call x1, Pallas kernels, attend(): pl.pallas_call(functools.partial(attend_kernel, len(parts)), out_shape=ja...  3.65 us
    pallas_call x2, Pallas kernels, gather_tokens(): pl.pallas_call(functools.partial(gather_kernel, sample), out_shape=[jax.S...  3.51 us
    ppermute x10, waiting for transfers between devices, swap(): lax.ppermute(held, axis, [(i, i ^ far) for i in range(lax.axis_size(axis))])  3.19 us
    pallas_call x1, Pallas kernels, project(): pl.pallas_call(project_kernel, out_shape=[jax.ShapeDtypeStruct((HEADS * r...  1.7 us
    ppermute x1, starting transfers between devices, shards(): lax.ppermute(outer, 'row', odd_pairs + [(j, i) for i, j in odd_pairs])  1.63 us
    unnamed x32, local copies, waits for them, and re-layouts  1.23 us
  transfers between devices with their start and end apart: 11, of which 4 were waited for; matrix products, arithmetic and copies ran while one was open for 0% of the time, Pallas kernels for 33%

profile of v15, /device:TPU:0, one launch (start us, length us, event | category | flops | bytes accessed | tf_op | source)
XLA Modules:
  0.0 33.8 jit_solution(15051200432951285352)
XLA Ops:
  0.0 1.2 %copy-done.7 = bf16[72,36,128]{2,0,1:T(8,128)(2,1)S(1)} copy-done((bf16[72,36,128]{2,0,1:T(8,128)(2,1)S(1)}, bf16[72,36,128]{2,0,1:T(8,128)(2,1)}, u32[]{:S(2)}) %copy-start.7) | copy-done | bytes 663576
  1.2 0.9 %normalise_pairs.1.normed = f32[36,72,128]{2,1,0:T(8,128)S(1)} custom-call(bf16[36,72,128]{2,1,0:T(8,128)(2,1)S(1)} %bitcast.12), custom_call_target="tpu_custom_call" | custom-call | flops 20000000 | bytes 1000 | tf_op jit(solution)/shard_map/normalise_pairs/pallas_call | solution.py:72
  2.1 0.0 copy-start.8
  2.1 0.0 copy-start.9
  2.1 0.0 copy-start.10
  2.1 0.0 copy-start.6
  2.1 0.0 copy-start.11
  2.1 0.0 copy-start.12
  2.2 0.0 copy-start.13
  2.2 1.0 %pair_bias.1 = (bf16[324,128]{1,0:T(8,128)(2,1)S(1)}, bf16[2,48,128]{2,1,0:T(8,128)(2,1)S(1)}, bf16[2,48,128]{2,1,0:T(8,128)(2,1)S(1)}) custom-call(bf16[2,1152,128]{2,1,0:T(8,128)(2,1)S(1)} %copy-done, f32[36,72,128]{2,1,0:T(8,128)S(1)} %normalise_pairs.1.normed, s32[36]{0:T(128)S(1)} %copy-done.15, bf16[16,128]{1,0:T(8,128)(2,1)S(1)} %bitcast.17), custom_call_target="tpu_custom_call" | custom-call | flops 60000000 | bytes 1000 | tf_op jit(solution)/shard_map/pair_bias/pallas_call | solution.py:124
  3.2 4.1 %collective-permute-start.1 = (bf16[324,128]{1,0:T(8,128)(2,1)S(1)}, bf16[324,128]{1,0:T(8,128)(2,1)S(1)}, u32[]{:S(2)}, u32[]{:S(2)}) collective-permute-start(bf16[324,128]{1,0:T(8,128)(2,1)S(1)} %get-tuple-element.33), channel_id=1, source_target_pairs={{0,4},{1,5},{2,6},{3,7},{4,0},{5,1},{6,2},{7,3},{8,12},{9,13},{10,... | collective-permute-start | bytes 248840 | tf_op jit(solution)/shard_map/ppermute | solution.py:145
  7.3 1.6 %collective-permute-start.2 = (bf16[2,48,128]{2,1,0:T(8,128)(2,1)S(1)}, bf16[2,48,128]{2,1,0:T(8,128)(2,1)S(1)}, u32[]{:S(2)}, u32[]{:S(2)}) collective-permute-start(bf16[2,48,128]{2,1,0:T(8,128)(2,1)S(1)} %get-tuple-element.31), channel_id=1, source_target_pairs={{8,16},{24,0},{16,8},{0,24},{9,17},{25,1},{17,9},{1,25},{10,18},{2... | collective-permute-start | bytes 73736 | tf_op jit(solution)/shard_map/ppermute | solution.py:571
  9.0 2.4 %atom_attention.2.mixed = bf16[1152,128]{1,0:T(8,128)(2,1)S(1)} custom-call(bf16[2,1152,128]{2,1,0:T(8,128)(2,1)S(1)} %copy-done, bf16[128,128]{1,0:T(8,128)(2,1)S(1)} %copy-done.8, bf16[128,128]{1,0:T(8,128)(2,1)S(1)} %copy-done.9, bf16[128,128]{1,0:T(8,128)(2,1)S(1)} %copy-done.10), custom_call_target="tpu_custom_call" | custom-call | flops 80000000 | bytes 1000 | tf_op jit(solution)/shard_map/atom_attention/pallas_call | solution.py:254
  11.4 0.0 copy-start.4
  11.4 2.1 %gather_tokens.2 = (f32[72,768]{1,0:T(8,128)S(1)}, bf16[72,768]{1,0:T(8,128)(2,1)S(1)}) custom-call(bf16[1152,128]{1,0:T(8,128)(2,1)S(1)} %atom_attention.2.mixed, bf16[2,1152,128]{2,1,0:T(8,128)(2,1)S(1)} %copy-done, s32[1152]{0:T(1024)S(1)} %copy-done.12, bf16[128,128]{1,0:T(8,128)(2,1)S(1)} %copy-done.11, bf16[128,768]{1,0:T(8,128)(2,1)S(1)} %copy-done.6, ...), custom_call_target="tpu_custom_call" | custom-call | flops 20000000 | bytes 1000 | tf_op jit(solution)/shard_map/gather_tokens/pallas_call | solution.py:324
  13.5 0.8 %collective-permute-start.4 = (bf16[1,72,768]{2,1,0:T(8,128)(2,1)S(1)}, bf16[1,72,768]{2,1,0:T(8,128)(2,1)S(1)}, u32[]{:S(2)}, u32[]{:S(2)}) collective-permute-start(bf16[1,72,768]{2,1,0:T(8,128)(2,1)S(1)} %bitcast.15), channel_id=1, source_target_pairs={{0,16},{8,24},{16,0},{24,8},{1,17},{9,25},{17,1},{25,9},{2,18},{10... | collective-permute-start | bytes 331784 | tf_op jit(solution)/shard_map/ppermute | solution.py:145
  14.4 1.6 %collective-permute-start.6 = (bf16[2,180,128]{2,1,0:T(8,128)(2,1)S(1)}, bf16[2,180,128]{2,1,0:T(8,128)(2,1)S(1)}, u32[]{:S(2)}, u32[]{:S(2)}) collective-permute-start(bf16[2,180,128]{2,1,0:T(8,128)(2,1)S(1)} %pad_maximum_fusion.4), channel_id=1, source_target_pairs={{0,1},{1,0},{2,3},{3,2},{4,5},{5,4},{6,7},{7,6},{8,9},{9,8},{10,11... | collective-permute-start | bytes 276488 | tf_op jit(solution)/shard_map/ppermute | solution.py:145
  15.9 1.6 %collective-permute-start.5 = (bf16[2,144,128]{2,1,0:T(8,128)(2,1)S(1)}, bf16[2,144,128]{2,1,0:T(8,128)(2,1)S(1)}, u32[]{:S(2)}, u32[]{:S(2)}) collective-permute-start(bf16[2,144,128]{2,1,0:T(8,128)(2,1)S(1)} %pad_maximum_fusion.5), channel_id=1, source_target_pairs={{0,2},{1,3},{2,0},{3,1},{4,6},{5,7},{6,4},{7,5},{8,10},{9,11},{10,... | collective-permute-start | bytes 221192 | tf_op jit(solution)/shard_map/ppermute | solution.py:145
  17.6 2.3 %atom_attention.3.mixed = bf16[1152,128]{1,0:T(8,128)(2,1)S(1)} custom-call(bf16[2,1152,128]{2,1,0:T(8,128)(2,1)S(1)} %copy-done, bf16[2,48,128]{2,1,0:T(8,128)(2,1)S(1)} %collective-permute-done.refs_0_, bf16[2,48,128]{2,1,0:T(8,128)(2,1)S(1)} %collective-permute-done.2.refs_1_, bf16[128,128]{1,0:T(8,128)(2,1)S(1)} %copy-done.8, ...), custom_call_target="tpu_custom_call" | custom-call | flops 80000000 | bytes 1000 | tf_op jit(solution)/shard_map/atom_attention/pallas_call | solution.py:254
  19.8 1.4 %gather_tokens.3 = (f32[72,768]{1,0:T(8,128)S(1)}, bf16[72,768]{1,0:T(8,128)(2,1)S(1)}) custom-call(bf16[1152,128]{1,0:T(8,128)(2,1)S(1)} %atom_attention.3.mixed, bf16[2,1152,128]{2,1,0:T(8,128)(2,1)S(1)} %copy-done, s32[1152]{0:T(1024)S(1)} %copy-done.12, bf16[128,128]{1,0:T(8,128)(2,1)S(1)} %copy-done.11, bf16[128,768]{1,0:T(8,128)(2,1)S(1)} %copy-done.6, ...), custom_call_target="tpu_custom_call" | custom-call | flops 20000000 | bytes 1000 | tf_op jit(solution)/shard_map/gather_tokens/pallas_call | solution.py:324
  21.3 0.1 collective-permute-start.7
  21.4 0.6 %collective-permute-start.9 = (bf16[4,180,128]{2,1,0:T(8,128)(2,1)S(1)}, bf16[4,180,128]{2,1,0:T(8,128)(2,1)S(1)}, u32[]{:S(2)}, u32[]{:S(2)}) collective-permute-start(bf16[4,180,128]{2,1,0:T(8,128)(2,1)S(1)} %pad_maximum_fusion.2.refs_2_), channel_id=1, source_target_pairs={{0,2},{1,3},{2,0},{3,1},{4,6},{5,7},{6,4},{7,5},{8,10},{9,11},{10,... | collective-permute-start | bytes 552968 | tf_op jit(solution)/shard_map/ppermute | solution.py:145
  22.0 0.6 %collective-permute-start.8 = (bf16[4,144,128]{2,1,0:T(8,128)(2,1)S(1)}, bf16[4,144,128]{2,1,0:T(8,128)(2,1)S(1)}, u32[]{:S(2)}, u32[]{:S(2)}) collective-permute-start(bf16[4,144,128]{2,1,0:T(8,128)(2,1)S(1)} %pad_maximum_fusion.3.refs_0_), channel_id=1, source_target_pairs={{0,1},{1,0},{2,3},{3,2},{4,5},{5,4},{6,7},{7,6},{8,9},{9,8},{10,11... | collective-permute-start | bytes 442376 | tf_op jit(solution)/shard_map/ppermute | solution.py:145
  22.6 1.3 %collective-permute-start.3 = (bf16[1,72,768]{2,1,0:T(8,128)(2,1)S(1)}, bf16[1,72,768]{2,1,0:T(8,128)(2,1)S(1)}, u32[]{:S(2)}, u32[]{:S(2)}) collective-permute-start(bf16[1,72,768]{2,1,0:T(8,128)(2,1)S(1)} %bitcast.13), channel_id=1, source_target_pairs={{0,16},{8,24},{16,0},{24,8},{1,17},{9,25},{17,1},{25,9},{2,18},{10... | collective-permute-start | bytes 331784 | tf_op jit(solution)/shard_map/ppermute | solution.py:145
  24.0 1.7 %project.1 = (f32[1152,288]{1,0:T(8,128)S(1)}, bf16[288,768]{1,0:T(8,128)(2,1)S(1)}, f32[72,768]{1,0:T(8,128)S(1)}) custom-call(bf16[2,72,768]{2,1,0:T(8,128)(2,1)S(1)} %pad_maximum_fusion.near, bf16[2,72,768]{2,1,0:T(8,128)(2,1)S(1)} %collective-permute-done.7.far, bf16[768,768]{1,0:T(8,128)(2,1)S(1)} %copy-done.4, bf16[768,768]{1,0:T(8,128)(2,1)S(1)} %copy-done.1, ...), custom_call_target="tpu_custom_call" | custom-call | flops 40000000 | bytes 1000 | tf_op jit(solution)/shard_map/project/pallas_call | solution.py:387
  25.7 1.8 %collective-permute-done.3 = bf16[1,72,768]{2,1,0:T(8,128)(2,1)S(1)} collective-permute-done((bf16[1,72,768]{2,1,0:T(8,128)(2,1)S(1)}, bf16[1,72,768]{2,1,0:T(8,128)(2,1)S(1)}, u32[]{:S(2)}, u32[]{:S(2)}) %collective-permute-start.3) | collective-permute-done | bytes 110624 | tf_op jit(solution)/shard_map/ppermute | solution.py:145
  27.5 0.5 %collective-permute-done.8.refs_1_ = bf16[4,144,128]{2,1,0:T(8,128)(2,1)S(1)} collective-permute-done((bf16[4,144,128]{2,1,0:T(8,128)(2,1)S(1)}, bf16[4,144,128]{2,1,0:T(8,128)(2,1)S(1)}, u32[]{:S(2)}, u32[]{:S(2)}) %collective-permute-start.8) | collective-permute-done | bytes 147488 | tf_op jit(solution)/shard_map/ppermute | solution.py:145
  28.0 0.6 %collective-permute-done.9.refs_3_ = bf16[4,180,128]{2,1,0:T(8,128)(2,1)S(1)} collective-permute-done((bf16[4,180,128]{2,1,0:T(8,128)(2,1)S(1)}, bf16[4,180,128]{2,1,0:T(8,128)(2,1)S(1)}, u32[]{:S(2)}, u32[]{:S(2)}) %collective-permute-start.9) | collective-permute-done | bytes 184352 | tf_op jit(solution)/shard_map/ppermute | solution.py:145
  28.6 0.1 collective-permute-start.10
  28.7 1.2 %turn_bias.1 = (bf16[72,768]{1,0:T(8,128)(2,1)S(1)}, bf16[144,768]{1,0:T(8,128)(2,1)S(1)}, bf16[144,768]{1,0:T(8,128)(2,1)S(1)}, f32[72,768]{1,0:T(8,128)S(1)}, f32[1152,288]{1,0:T(8,128)S(1)}) custom-call(bf16[2,72,768]{2,1,0:T(8,128)(2,1)S(1)} %pad_maximum_fusion.1.near, bf16[768,768]{1,0:T(8,128)(2,1)S(1)} %copy-done.4, bf16[768,768]{1,0:T(8,128)(2,1)S(1)} %copy-done.1, ...), custom_call_target="tpu_custom_call" | custom-call | flops 20000000 | bytes 1000 | tf_op jit(solution)/shard_map/turn_bias/pallas_call | solution.py:448
  29.9 0.2 collective-permute-done.10.refs_9_
  30.2 3.7 %attend.1 = bf16[2,72,768]{2,1,0:T(8,128)(2,1)} custom-call(f32[1152,288]{1,0:T(8,128)S(1)} %get-tuple-element.47.bias, f32[1152,288]{1,0:T(8,128)S(1)} %get-tuple-element.41.refs_0_, bf16[288,768]{1,0:T(8,128)(2,1)S(1)} %get-tuple-element.42.refs_1_, f32[72,768]{1,0:T(8,128)S(1)} %get-tuple-element.43.refs_2_, f32[72,768]{1,0:T(8,128)S(1)} %get-tuple-element.44.refs_3_, ...), custom_call_target="tpu_custom_call" | custom-call | flops 60000000 | bytes 1000 | tf_op jit(solution)/shard_map/attend/pallas_call | solution.py:535
  (39 shorter events, 0.2 us)
Async XLA Ops:
  0.0 2.1 %copy-start = (bf16[2,1152,128]{2,1,0:T(8,128)(2,1)S(1)}, bf16[2,1152,128]{2,1,0:T(8,128)(2,1)}, u32[]{:S(2)}) copy-start(bf16[2,1152,128]{2,1,0:T(8,128)(2,1)} %feat.9) | copy-start | bytes 1769476
  0.0 1.2 %copy-start.7 = (bf16[72,36,128]{2,0,1:T(8,128)(2,1)S(1)}, bf16[72,36,128]{2,0,1:T(8,128)(2,1)}, u32[]{:S(2)}) copy-start(bf16[72,36,128]{2,0,1:T(8,128)(2,1)} %param.18) | copy-start | bytes 1990660
  1.2 0.9 %copy-start.14 = (bf16[128,16]{0,1:T(8,128)(2,1)S(1)}, bf16[128,16]{0,1:T(8,128)(2,1)}, u32[]{:S(2)}) copy-start(bf16[128,16]{0,1:T(8,128)(2,1)} %param.25) | copy-start | bytes 12292
  1.2 1.0 %copy-start.15 = (s32[36]{0:T(128)S(1)}, s32[36]{0:T(128)}, u32[]{:S(2)}) copy-start(s32[36]{0:T(128)} %mask.1) | copy-start | bytes 436
  2.1 6.9 %copy-start.8 = (bf16[128,128]{1,0:T(8,128)(2,1)S(1)}, bf16[128,128]{1,0:T(8,128)(2,1)}, u32[]{:S(2)}) copy-start(bf16[128,128]{1,0:T(8,128)(2,1)} %refs_2_.5) | copy-start | bytes 98308
  2.1 6.9 %copy-start.9 = (bf16[128,128]{1,0:T(8,128)(2,1)S(1)}, bf16[128,128]{1,0:T(8,128)(2,1)}, u32[]{:S(2)}) copy-start(bf16[128,128]{1,0:T(8,128)(2,1)} %refs_3_.3) | copy-start | bytes 98308
  2.1 6.9 %copy-start.10 = (bf16[128,128]{1,0:T(8,128)(2,1)S(1)}, bf16[128,128]{1,0:T(8,128)(2,1)}, u32[]{:S(2)}) copy-start(bf16[128,128]{1,0:T(8,128)(2,1)} %refs_4_.3) | copy-start | bytes 98308
  2.1 9.2 %copy-start.6 = (bf16[128,768]{1,0:T(8,128)(2,1)S(1)}, bf16[128,768]{1,0:T(8,128)(2,1)}, u32[]{:S(2)}) copy-start(bf16[128,768]{1,0:T(8,128)(2,1)} %agg.3) | copy-start | bytes 589828
  2.1 9.2 %copy-start.11 = (bf16[128,128]{1,0:T(8,128)(2,1)S(1)}, bf16[128,128]{1,0:T(8,128)(2,1)}, u32[]{:S(2)}) copy-start(bf16[128,128]{1,0:T(8,128)(2,1)} %wo.4) | copy-start | bytes 98308
  2.1 9.2 %copy-start.12 = (s32[1152]{0:T(1024)S(1)}, s32[1152]{0:T(1024)}, u32[]{:S(2)}) copy-start(s32[1152]{0:T(1024)} %token_.3) | copy-start | bytes 13828
  2.2 9.2 %copy-start.13 = (f32[768]{0:T(1024)S(1)}, f32[768]{0:T(1024)}, u32[]{:S(2)}) copy-start(f32[768]{0:T(1024)} %gain.3) | copy-start | bytes 9220
  3.2 11.1 %collective-permute-start.1 = (bf16[324,128]{1,0:T(8,128)(2,1)S(1)}, bf16[324,128]{1,0:T(8,128)(2,1)S(1)}, u32[]{:S(2)}, u32[]{:S(2)}) collective-permute-start(bf16[324,128]{1,0:T(8,128)(2,1)S(1)} %get-tuple-element.33), channel_id=1, source_target_pairs={{0,4},{1,5},{2,6},{3,7},{4,0},{5,1},{6,2},{7,3},{8,12},{9,13},{10,... | collective-permute-start | bytes 248840 | tf_op jit(solution)/shard_map/ppermute | solution.py:145
  7.3 4.0 %collective-permute-start = (bf16[2,48,128]{2,1,0:T(8,128)(2,1)S(1)}, bf16[2,48,128]{2,1,0:T(8,128)(2,1)S(1)}, u32[]{:S(2)}, u32[]{:S(2)}) collective-permute-start(bf16[2,48,128]{2,1,0:T(8,128)(2,1)S(1)} %get-tuple-element.29), channel_id=1, source_target_pairs={{0,8},{8,0},{16,24},{24,16},{1,9},{9,1},{17,25},{25,17},{2,10},{10... | collective-permute-start | bytes 73736 | tf_op jit(solution)/shard_map/ppermute | solution.py:145
  7.3 4.0 %collective-permute-start.2 = (bf16[2,48,128]{2,1,0:T(8,128)(2,1)S(1)}, bf16[2,48,128]{2,1,0:T(8,128)(2,1)S(1)}, u32[]{:S(2)}, u32[]{:S(2)}) collective-permute-start(bf16[2,48,128]{2,1,0:T(8,128)(2,1)S(1)} %get-tuple-element.31), channel_id=1, source_target_pairs={{8,16},{24,0},{16,8},{0,24},{9,17},{25,1},{17,9},{1,25},{10,18},{2... | collective-permute-start | bytes 73736 | tf_op jit(solution)/shard_map/ppermute | solution.py:571
  8.9 15.0 %copy-start.5 = (bf16[768,768]{1,0:T(8,128)(2,1)S(1)}, bf16[768,768]{1,0:T(8,128)(2,1)}, u32[]{:S(2)}) copy-start(bf16[768,768]{1,0:T(8,128)(2,1)} %wg.3) | copy-start | bytes 3538948
  11.4 12.6 %copy-start.4 = (bf16[768,768]{1,0:T(8,128)(2,1)S(1)}, bf16[768,768]{1,0:T(8,128)(2,1)}, u32[]{:S(2)}) copy-start(bf16[768,768]{1,0:T(8,128)(2,1)} %wq.3) | copy-start | bytes 3538948
  13.5 7.8 %collective-permute-start.4 = (bf16[1,72,768]{2,1,0:T(8,128)(2,1)S(1)}, bf16[1,72,768]{2,1,0:T(8,128)(2,1)S(1)}, u32[]{:S(2)}, u32[]{:S(2)}) collective-permute-start(bf16[1,72,768]{2,1,0:T(8,128)(2,1)S(1)} %bitcast.15), channel_id=1, source_target_pairs={{0,16},{8,24},{16,0},{24,8},{1,17},{9,25},{17,1},{25,9},{2,18},{10... | collective-permute-start | bytes 331784 | tf_op jit(solution)/shard_map/ppermute | solution.py:145
  14.3 9.6 %copy-start.3 = (bf16[768,768]{1,0:T(8,128)(2,1)S(1)}, bf16[768,768]{1,0:T(8,128)(2,1)}, u32[]{:S(2)}) copy-start(bf16[768,768]{1,0:T(8,128)(2,1)} %refs_12_.1) | copy-start | bytes 3538948
  14.4 7.0 %collective-permute-start.6 = (bf16[2,180,128]{2,1,0:T(8,128)(2,1)S(1)}, bf16[2,180,128]{2,1,0:T(8,128)(2,1)S(1)}, u32[]{:S(2)}, u32[]{:S(2)}) collective-permute-start(bf16[2,180,128]{2,1,0:T(8,128)(2,1)S(1)} %pad_maximum_fusion.4), channel_id=1, source_target_pairs={{0,1},{1,0},{2,3},{3,2},{4,5},{5,4},{6,7},{7,6},{8,9},{9,8},{10,11... | collective-permute-start | bytes 276488 | tf_op jit(solution)/shard_map/ppermute | solution.py:145
  15.9 5.5 %collective-permute-start.5 = (bf16[2,144,128]{2,1,0:T(8,128)(2,1)S(1)}, bf16[2,144,128]{2,1,0:T(8,128)(2,1)S(1)}, u32[]{:S(2)}, u32[]{:S(2)}) collective-permute-start(bf16[2,144,128]{2,1,0:T(8,128)(2,1)S(1)} %pad_maximum_fusion.5), channel_id=1, source_target_pairs={{0,2},{1,3},{2,0},{3,1},{4,6},{5,7},{6,4},{7,5},{8,10},{9,11},{10,... | collective-permute-start | bytes 221192 | tf_op jit(solution)/shard_map/ppermute | solution.py:145
  17.6 6.4 %copy-start.2 = (bf16[768,768]{1,0:T(8,128)(2,1)S(1)}, bf16[768,768]{1,0:T(8,128)(2,1)}, u32[]{:S(2)}) copy-start(bf16[768,768]{1,0:T(8,128)(2,1)} %refs_11_.1) | copy-start | bytes 3538948
  19.8 4.1 %copy-start.1 = (bf16[768,768]{1,0:T(8,128)(2,1)S(1)}, bf16[768,768]{1,0:T(8,128)(2,1)}, u32[]{:S(2)}) copy-start(bf16[768,768]{1,0:T(8,128)(2,1)} %refs_10_.1) | copy-start | bytes 3538948
  21.3 2.6 %collective-permute-start.7 = (bf16[2,72,768]{2,1,0:T(8,128)(2,1)S(1)}, bf16[2,72,768]{2,1,0:T(8,128)(2,1)S(1)}, u32[]{:S(2)}, u32[]{:S(2)}) collective-permute-start(bf16[2,72,768]{2,1,0:T(8,128)(2,1)S(1)} %pad_maximum_fusion.near), channel_id=1, source_target_pairs={{0,8},{8,0},{16,24},{24,16},{1,9},{9,1},{17,25},{25,17},{2,10},{10... | collective-permute-start | bytes 663560 | tf_op jit(solution)/shard_map/ppermute | solution.py:145
  21.4 7.2 %collective-permute-start.9 = (bf16[4,180,128]{2,1,0:T(8,128)(2,1)S(1)}, bf16[4,180,128]{2,1,0:T(8,128)(2,1)S(1)}, u32[]{:S(2)}, u32[]{:S(2)}) collective-permute-start(bf16[4,180,128]{2,1,0:T(8,128)(2,1)S(1)} %pad_maximum_fusion.2.refs_2_), channel_id=1, source_target_pairs={{0,2},{1,3},{2,0},{3,1},{4,6},{5,7},{6,4},{7,5},{8,10},{9,11},{10,... | collective-permute-start | bytes 552968 | tf_op jit(solution)/shard_map/ppermute | solution.py:145
  22.0 6.0 %collective-permute-start.8 = (bf16[4,144,128]{2,1,0:T(8,128)(2,1)S(1)}, bf16[4,144,128]{2,1,0:T(8,128)(2,1)S(1)}, u32[]{:S(2)}, u32[]{:S(2)}) collective-permute-start(bf16[4,144,128]{2,1,0:T(8,128)(2,1)S(1)} %pad_maximum_fusion.3.refs_0_), channel_id=1, source_target_pairs={{0,1},{1,0},{2,3},{3,2},{4,5},{5,4},{6,7},{7,6},{8,9},{9,8},{10,11... | collective-permute-start | bytes 442376 | tf_op jit(solution)/shard_map/ppermute | solution.py:145
  22.6 4.8 %collective-permute-start.3 = (bf16[1,72,768]{2,1,0:T(8,128)(2,1)S(1)}, bf16[1,72,768]{2,1,0:T(8,128)(2,1)S(1)}, u32[]{:S(2)}, u32[]{:S(2)}) collective-permute-start(bf16[1,72,768]{2,1,0:T(8,128)(2,1)S(1)} %bitcast.13), channel_id=1, source_target_pairs={{0,16},{8,24},{16,0},{24,8},{1,17},{9,25},{17,1},{25,9},{2,18},{10... | collective-permute-start | bytes 331784 | tf_op jit(solution)/shard_map/ppermute | solution.py:145
  28.6 1.5 %collective-permute-start.10 = (bf16[2,72,768]{2,1,0:T(8,128)(2,1)S(1)}, bf16[2,72,768]{2,1,0:T(8,128)(2,1)S(1)}, u32[]{:S(2)}, u32[]{:S(2)}) collective-permute-start(bf16[2,72,768]{2,1,0:T(8,128)(2,1)S(1)} %pad_maximum_fusion.1.near), channel_id=1, source_target_pairs={{0,8},{8,0},{16,24},{24,16},{1,9},{9,1},{17,25},{25,17},{2,10},{10... | collective-permute-start | bytes 663560 | tf_op jit(solution)/shard_map/ppermute | solution.py:145

commit v16 on v14

--- a/solution.py
+++ b/solution.py
@@ -470,10 +470,10 @@
     rows, width = token_last.shape
     x = stack(far)
     groups = head_groups(width)
-    work = [(s, base, heads) for s in range(samples) for base, heads in groups]
+    work = [(s, groups[i : i + 2]) for s in range(samples) for i in range(0, len(groups), 2)]
     chunks = list(range(0, width, 2 * LANES))
     for i, c in enumerate(chunks):
-        work.insert(min(2 * i + 1, (samples - 1) * len(groups) + i), c)
+        work.insert(min(2 * i + 1, (samples - 1) * len(groups) // 2 + i), c)
 
     def fill(c):
         lanes = slice(c, c + 2 * LANES)
@@ -485,9 +485,11 @@
     def score(item):
         if isinstance(item, int):
             return fill(item)
-        s, base, heads = item
-        part = slice(heads[0] * rows, (heads[-1] + 1) * rows)
-        return item, (parts[s][0][part] if s < samples - 1 else head_scores(q, kt, base, heads)) + bias[part]
+        s, pair = item
+        part = slice(pair[0][1][0] * rows, (pair[-1][1][-1] + 1) * rows)
+        if s < samples - 1:
+            return item, parts[s][0][part] + bias[part]
+        return item, jnp.concatenate([head_scores(q, kt, *group) for group in pair], axis=0) + bias[part]
 
     def soften(item):
         if item is None:
@@ -501,13 +503,17 @@
     def mix(item):
         if item is None:
             return
-        (s, base, heads), e, share = item
-        o = dot(e, parts[s][1][:, base : base + 2 * LANES])
-        for i, h in enumerate(heads):
-            part = slice(i * rows, (i + 1) * rows)
-            for at in tiles_of(h):
-                one = o[part, at - base : at - base + LANES] * share[part]
-                mixes[s, at] = jnp.where(channels(rows, at, h), one, mixes.get((s, at), 0.0))
+        (s, pair), e, share = item
+        first = pair[0][1][0]
+        for base, heads in pair:
+            low = (heads[0] - first) * rows
+            o = dot(e[low : low + len(heads) * rows], parts[s][1][:, base : base + 2 * LANES])
+            for i, h in enumerate(heads):
+                part = slice(i * rows, (i + 1) * rows)
+                own = share[low + i * rows : low + (i + 1) * rows]
+                for at in tiles_of(h):
+                    one = o[part, at - base : at - base + LANES] * own
+                    mixes[s, at] = jnp.where(channels(rows, at, h), one, mixes.get((s, at), 0.0))
         if h == HEADS - 1:
             close(s)
 

time: 33.7 us -> 33.7 us (level)
  no operation moved by 1% of the time
where the time goes in v16:
time: 33.7 us; the launch traced here: 33.6 us
  Pallas kernels  16.3 us (48%)
  starting transfers between devices  12.3 us (36%)
  waiting for transfers between devices  3.19 us (9%)
  local copies, waits for them, and re-layouts  1.25 us (4%)
    ppermute x10, starting transfers between devices, swap(): lax.ppermute(held, axis, [(i, i ^ far) for i in range(lax.axis_size(axis))])  10.7 us
    pallas_call x2, Pallas kernels, atom_attention(): pl.pallas_call(functools.partial(atom_kernel, sample), out_shape=jax.Shap...  4.62 us
    pallas_call x2, Pallas kernels, gather_tokens(): pl.pallas_call(functools.partial(gather_kernel, sample), out_shape=[jax.S...  3.51 us
    pallas_call x1, Pallas kernels, attend(): pl.pallas_call(functools.partial(attend_kernel, len(parts)), out_shape=ja...  3.37 us
    ppermute x10, waiting for transfers between devices, swap(): lax.ppermute(held, axis, [(i, i ^ far) for i in range(lax.axis_size(axis))])  3.19 us
    pallas_call x1, Pallas kernels, project(): pl.pallas_call(project_kernel, out_shape=[jax.ShapeDtypeStruct((HEADS * r...  1.7 us
    ppermute x1, starting transfers between devices, shards(): lax.ppermute(outer, 'row', odd_pairs + [(j, i) for i, j in odd_pairs])  1.63 us
    unnamed x32, local copies, waits for them, and re-layouts  1.23 us
  transfers between devices with their start and end apart: 11, of which 4 were waited for; matrix products, arithmetic and copies ran while one was open for 0% of the time, Pallas kernels for 33%

profile of v16, /device:TPU:0, one launch (start us, length us, event | category | flops | bytes accessed | tf_op | source)
XLA Modules:
  0.0 33.6 jit_solution(7881675317142138689)
XLA Ops:
  0.0 1.2 %copy-done.7 = bf16[72,36,128]{2,0,1:T(8,128)(2,1)S(1)} copy-done((bf16[72,36,128]{2,0,1:T(8,128)(2,1)S(1)}, bf16[72,36,128]{2,0,1:T(8,128)(2,1)}, u32[]{:S(2)}) %copy-start.7) | copy-done | bytes 663576
  1.2 0.9 %normalise_pairs.1.normed = f32[36,72,128]{2,1,0:T(8,128)S(1)} custom-call(bf16[36,72,128]{2,1,0:T(8,128)(2,1)S(1)} %bitcast.12), custom_call_target="tpu_custom_call" | custom-call | flops 20000000 | bytes 1000 | tf_op jit(solution)/shard_map/normalise_pairs/pallas_call | solution.py:72
  2.1 0.0 copy-start.8
  2.1 0.0 copy-start.9
  2.1 0.0 copy-start.10
  2.1 0.0 copy-start.6
  2.1 0.0 copy-start.12
  2.2 0.0 copy-start.13
  2.2 1.0 %pair_bias.1 = (bf16[324,128]{1,0:T(8,128)(2,1)S(1)}, bf16[2,48,128]{2,1,0:T(8,128)(2,1)S(1)}, bf16[2,48,128]{2,1,0:T(8,128)(2,1)S(1)}) custom-call(bf16[2,1152,128]{2,1,0:T(8,128)(2,1)S(1)} %copy-done, f32[36,72,128]{2,1,0:T(8,128)S(1)} %normalise_pairs.1.normed, s32[36]{0:T(128)S(1)} %copy-done.15, bf16[16,128]{1,0:T(8,128)(2,1)S(1)} %bitcast.17), custom_call_target="tpu_custom_call" | custom-call | flops 60000000 | bytes 1000 | tf_op jit(solution)/shard_map/pair_bias/pallas_call | solution.py:124
  3.2 4.1 %collective-permute-start.1 = (bf16[324,128]{1,0:T(8,128)(2,1)S(1)}, bf16[324,128]{1,0:T(8,128)(2,1)S(1)}, u32[]{:S(2)}, u32[]{:S(2)}) collective-permute-start(bf16[324,128]{1,0:T(8,128)(2,1)S(1)} %get-tuple-element.33), channel_id=1, source_target_pairs={{0,4},{1,5},{2,6},{3,7},{4,0},{5,1},{6,2},{7,3},{8,12},{9,13},{10,... | collective-permute-start | bytes 248840 | tf_op jit(solution)/shard_map/ppermute | solution.py:145
  7.3 1.6 %collective-permute-start.2 = (bf16[2,48,128]{2,1,0:T(8,128)(2,1)S(1)}, bf16[2,48,128]{2,1,0:T(8,128)(2,1)S(1)}, u32[]{:S(2)}, u32[]{:S(2)}) collective-permute-start(bf16[2,48,128]{2,1,0:T(8,128)(2,1)S(1)} %get-tuple-element.31), channel_id=1, source_target_pairs={{8,16},{24,0},{16,8},{0,24},{9,17},{25,1},{17,9},{1,25},{10,18},{2... | collective-permute-start | bytes 73736 | tf_op jit(solution)/shard_map/ppermute | solution.py:569
  9.0 2.4 %atom_attention.2.mixed = bf16[1152,128]{1,0:T(8,128)(2,1)S(1)} custom-call(bf16[2,1152,128]{2,1,0:T(8,128)(2,1)S(1)} %copy-done, bf16[128,128]{1,0:T(8,128)(2,1)S(1)} %copy-done.8, bf16[128,128]{1,0:T(8,128)(2,1)S(1)} %copy-done.9, bf16[128,128]{1,0:T(8,128)(2,1)S(1)} %copy-done.10), custom_call_target="tpu_custom_call" | custom-call | flops 80000000 | bytes 1000 | tf_op jit(solution)/shard_map/atom_attention/pallas_call | solution.py:254
  11.4 0.0 copy-start.4
  11.4 2.1 %gather_tokens.2 = (f32[72,768]{1,0:T(8,128)S(1)}, bf16[72,768]{1,0:T(8,128)(2,1)S(1)}) custom-call(bf16[1152,128]{1,0:T(8,128)(2,1)S(1)} %atom_attention.2.mixed, bf16[2,1152,128]{2,1,0:T(8,128)(2,1)S(1)} %copy-done, s32[1152]{0:T(1024)S(1)} %copy-done.12, bf16[128,128]{1,0:T(8,128)(2,1)S(1)} %copy-done.11, bf16[128,768]{1,0:T(8,128)(2,1)S(1)} %copy-done.6, ...), custom_call_target="tpu_custom_call" | custom-call | flops 20000000 | bytes 1000 | tf_op jit(solution)/shard_map/gather_tokens/pallas_call | solution.py:324
  13.5 0.8 %collective-permute-start.4 = (bf16[1,72,768]{2,1,0:T(8,128)(2,1)S(1)}, bf16[1,72,768]{2,1,0:T(8,128)(2,1)S(1)}, u32[]{:S(2)}, u32[]{:S(2)}) collective-permute-start(bf16[1,72,768]{2,1,0:T(8,128)(2,1)S(1)} %bitcast.15), channel_id=1, source_target_pairs={{0,16},{8,24},{16,0},{24,8},{1,17},{9,25},{17,1},{25,9},{2,18},{10... | collective-permute-start | bytes 331784 | tf_op jit(solution)/shard_map/ppermute | solution.py:145
  14.3 0.0 copy-start.3
  14.4 1.6 %collective-permute-start.6 = (bf16[2,180,128]{2,1,0:T(8,128)(2,1)S(1)}, bf16[2,180,128]{2,1,0:T(8,128)(2,1)S(1)}, u32[]{:S(2)}, u32[]{:S(2)}) collective-permute-start(bf16[2,180,128]{2,1,0:T(8,128)(2,1)S(1)} %pad_maximum_fusion.4), channel_id=1, source_target_pairs={{0,1},{1,0},{2,3},{3,2},{4,5},{5,4},{6,7},{7,6},{8,9},{9,8},{10,11... | collective-permute-start | bytes 276488 | tf_op jit(solution)/shard_map/ppermute | solution.py:145
  15.9 1.6 %collective-permute-start.5 = (bf16[2,144,128]{2,1,0:T(8,128)(2,1)S(1)}, bf16[2,144,128]{2,1,0:T(8,128)(2,1)S(1)}, u32[]{:S(2)}, u32[]{:S(2)}) collective-permute-start(bf16[2,144,128]{2,1,0:T(8,128)(2,1)S(1)} %pad_maximum_fusion.5), channel_id=1, source_target_pairs={{0,2},{1,3},{2,0},{3,1},{4,6},{5,7},{6,4},{7,5},{8,10},{9,11},{10,... | collective-permute-start | bytes 221192 | tf_op jit(solution)/shard_map/ppermute | solution.py:145
  17.6 2.3 %atom_attention.3.mixed = bf16[1152,128]{1,0:T(8,128)(2,1)S(1)} custom-call(bf16[2,1152,128]{2,1,0:T(8,128)(2,1)S(1)} %copy-done, bf16[2,48,128]{2,1,0:T(8,128)(2,1)S(1)} %collective-permute-done.refs_0_, bf16[2,48,128]{2,1,0:T(8,128)(2,1)S(1)} %collective-permute-done.2.refs_1_, bf16[128,128]{1,0:T(8,128)(2,1)S(1)} %copy-done.8, ...), custom_call_target="tpu_custom_call" | custom-call | flops 80000000 | bytes 1000 | tf_op jit(solution)/shard_map/atom_attention/pallas_call | solution.py:254
  19.8 1.4 %gather_tokens.3 = (f32[72,768]{1,0:T(8,128)S(1)}, bf16[72,768]{1,0:T(8,128)(2,1)S(1)}) custom-call(bf16[1152,128]{1,0:T(8,128)(2,1)S(1)} %atom_attention.3.mixed, bf16[2,1152,128]{2,1,0:T(8,128)(2,1)S(1)} %copy-done, s32[1152]{0:T(1024)S(1)} %copy-done.12, bf16[128,128]{1,0:T(8,128)(2,1)S(1)} %copy-done.11, bf16[128,768]{1,0:T(8,128)(2,1)S(1)} %copy-done.6, ...), custom_call_target="tpu_custom_call" | custom-call | flops 20000000 | bytes 1000 | tf_op jit(solution)/shard_map/gather_tokens/pallas_call | solution.py:324
  21.3 0.1 collective-permute-start.7
  21.4 0.6 %collective-permute-start.9 = (bf16[4,180,128]{2,1,0:T(8,128)(2,1)S(1)}, bf16[4,180,128]{2,1,0:T(8,128)(2,1)S(1)}, u32[]{:S(2)}, u32[]{:S(2)}) collective-permute-start(bf16[4,180,128]{2,1,0:T(8,128)(2,1)S(1)} %pad_maximum_fusion.2.refs_2_), channel_id=1, source_target_pairs={{0,2},{1,3},{2,0},{3,1},{4,6},{5,7},{6,4},{7,5},{8,10},{9,11},{10,... | collective-permute-start | bytes 552968 | tf_op jit(solution)/shard_map/ppermute | solution.py:145
  22.0 0.6 %collective-permute-start.8 = (bf16[4,144,128]{2,1,0:T(8,128)(2,1)S(1)}, bf16[4,144,128]{2,1,0:T(8,128)(2,1)S(1)}, u32[]{:S(2)}, u32[]{:S(2)}) collective-permute-start(bf16[4,144,128]{2,1,0:T(8,128)(2,1)S(1)} %pad_maximum_fusion.3.refs_0_), channel_id=1, source_target_pairs={{0,1},{1,0},{2,3},{3,2},{4,5},{5,4},{6,7},{7,6},{8,9},{9,8},{10,11... | collective-permute-start | bytes 442376 | tf_op jit(solution)/shard_map/ppermute | solution.py:145
  22.6 1.3 %collective-permute-start.3 = (bf16[1,72,768]{2,1,0:T(8,128)(2,1)S(1)}, bf16[1,72,768]{2,1,0:T(8,128)(2,1)S(1)}, u32[]{:S(2)}, u32[]{:S(2)}) collective-permute-start(bf16[1,72,768]{2,1,0:T(8,128)(2,1)S(1)} %bitcast.13), channel_id=1, source_target_pairs={{0,16},{8,24},{16,0},{24,8},{1,17},{9,25},{17,1},{25,9},{2,18},{10... | collective-permute-start | bytes 331784 | tf_op jit(solution)/shard_map/ppermute | solution.py:145
  24.0 1.7 %project.1 = (f32[1152,288]{1,0:T(8,128)S(1)}, bf16[288,768]{1,0:T(8,128)(2,1)S(1)}, f32[72,768]{1,0:T(8,128)S(1)}) custom-call(bf16[2,72,768]{2,1,0:T(8,128)(2,1)S(1)} %pad_maximum_fusion.near, bf16[2,72,768]{2,1,0:T(8,128)(2,1)S(1)} %collective-permute-done.7.far, bf16[768,768]{1,0:T(8,128)(2,1)S(1)} %copy-done.4, bf16[768,768]{1,0:T(8,128)(2,1)S(1)} %copy-done.1, ...), custom_call_target="tpu_custom_call" | custom-call | flops 40000000 | bytes 1000 | tf_op jit(solution)/shard_map/project/pallas_call | solution.py:387
  25.7 1.8 %collective-permute-done.3 = bf16[1,72,768]{2,1,0:T(8,128)(2,1)S(1)} collective-permute-done((bf16[1,72,768]{2,1,0:T(8,128)(2,1)S(1)}, bf16[1,72,768]{2,1,0:T(8,128)(2,1)S(1)}, u32[]{:S(2)}, u32[]{:S(2)}) %collective-permute-start.3) | collective-permute-done | bytes 110624 | tf_op jit(solution)/shard_map/ppermute | solution.py:145
  27.5 0.5 %collective-permute-done.8.refs_1_ = bf16[4,144,128]{2,1,0:T(8,128)(2,1)S(1)} collective-permute-done((bf16[4,144,128]{2,1,0:T(8,128)(2,1)S(1)}, bf16[4,144,128]{2,1,0:T(8,128)(2,1)S(1)}, u32[]{:S(2)}, u32[]{:S(2)}) %collective-permute-start.8) | collective-permute-done | bytes 147488 | tf_op jit(solution)/shard_map/ppermute | solution.py:145
  28.0 0.6 %collective-permute-done.9.refs_3_ = bf16[4,180,128]{2,1,0:T(8,128)(2,1)S(1)} collective-permute-done((bf16[4,180,128]{2,1,0:T(8,128)(2,1)S(1)}, bf16[4,180,128]{2,1,0:T(8,128)(2,1)S(1)}, u32[]{:S(2)}, u32[]{:S(2)}) %collective-permute-start.9) | collective-permute-done | bytes 184352 | tf_op jit(solution)/shard_map/ppermute | solution.py:145
  28.6 0.1 collective-permute-start.10
  28.7 1.2 %turn_bias.1 = (bf16[72,768]{1,0:T(8,128)(2,1)S(1)}, bf16[144,768]{1,0:T(8,128)(2,1)S(1)}, bf16[144,768]{1,0:T(8,128)(2,1)S(1)}, f32[72,768]{1,0:T(8,128)S(1)}, f32[1152,288]{1,0:T(8,128)S(1)}) custom-call(bf16[2,72,768]{2,1,0:T(8,128)(2,1)S(1)} %pad_maximum_fusion.1.near, bf16[768,768]{1,0:T(8,128)(2,1)S(1)} %copy-done.4, bf16[768,768]{1,0:T(8,128)(2,1)S(1)} %copy-done.1, ...), custom_call_target="tpu_custom_call" | custom-call | flops 20000000 | bytes 1000 | tf_op jit(solution)/shard_map/turn_bias/pallas_call | solution.py:448
  29.9 0.2 collective-permute-done.10.refs_9_
  30.2 3.4 %attend.1 = bf16[2,72,768]{2,1,0:T(8,128)(2,1)} custom-call(f32[1152,288]{1,0:T(8,128)S(1)} %get-tuple-element.47.bias, f32[1152,288]{1,0:T(8,128)S(1)} %get-tuple-element.41.refs_0_, bf16[288,768]{1,0:T(8,128)(2,1)S(1)} %get-tuple-element.42.refs_1_, f32[72,768]{1,0:T(8,128)S(1)} %get-tuple-element.43.refs_2_, f32[72,768]{1,0:T(8,128)S(1)} %get-tuple-element.44.refs_3_, ...), custom_call_target="tpu_custom_call" | custom-call | flops 60000000 | bytes 1000 | tf_op jit(solution)/shard_map/attend/pallas_call | solution.py:533
  (39 shorter events, 0.2 us)
Async XLA Ops:
  0.0 2.1 %copy-start = (bf16[2,1152,128]{2,1,0:T(8,128)(2,1)S(1)}, bf16[2,1152,128]{2,1,0:T(8,128)(2,1)}, u32[]{:S(2)}) copy-start(bf16[2,1152,128]{2,1,0:T(8,128)(2,1)} %feat.9) | copy-start | bytes 1769476
  0.0 1.2 %copy-start.7 = (bf16[72,36,128]{2,0,1:T(8,128)(2,1)S(1)}, bf16[72,36,128]{2,0,1:T(8,128)(2,1)}, u32[]{:S(2)}) copy-start(bf16[72,36,128]{2,0,1:T(8,128)(2,1)} %param.18) | copy-start | bytes 1990660
  1.2 0.9 %copy-start.14 = (bf16[128,16]{0,1:T(8,128)(2,1)S(1)}, bf16[128,16]{0,1:T(8,128)(2,1)}, u32[]{:S(2)}) copy-start(bf16[128,16]{0,1:T(8,128)(2,1)} %param.25) | copy-start | bytes 12292
  1.2 1.0 %copy-start.15 = (s32[36]{0:T(128)S(1)}, s32[36]{0:T(128)}, u32[]{:S(2)}) copy-start(s32[36]{0:T(128)} %mask.1) | copy-start | bytes 436
  2.1 6.9 %copy-start.8 = (bf16[128,128]{1,0:T(8,128)(2,1)S(1)}, bf16[128,128]{1,0:T(8,128)(2,1)}, u32[]{:S(2)}) copy-start(bf16[128,128]{1,0:T(8,128)(2,1)} %refs_2_.5) | copy-start | bytes 98308
  2.1 6.9 %copy-start.9 = (bf16[128,128]{1,0:T(8,128)(2,1)S(1)}, bf16[128,128]{1,0:T(8,128)(2,1)}, u32[]{:S(2)}) copy-start(bf16[128,128]{1,0:T(8,128)(2,1)} %refs_3_.3) | copy-start | bytes 98308
  2.1 6.9 %copy-start.10 = (bf16[128,128]{1,0:T(8,128)(2,1)S(1)}, bf16[128,128]{1,0:T(8,128)(2,1)}, u32[]{:S(2)}) copy-start(bf16[128,128]{1,0:T(8,128)(2,1)} %refs_4_.3) | copy-start | bytes 98308
  2.1 9.2 %copy-start.6 = (bf16[128,768]{1,0:T(8,128)(2,1)S(1)}, bf16[128,768]{1,0:T(8,128)(2,1)}, u32[]{:S(2)}) copy-start(bf16[128,768]{1,0:T(8,128)(2,1)} %agg.3) | copy-start | bytes 589828
  2.1 9.2 %copy-start.11 = (bf16[128,128]{1,0:T(8,128)(2,1)S(1)}, bf16[128,128]{1,0:T(8,128)(2,1)}, u32[]{:S(2)}) copy-start(bf16[128,128]{1,0:T(8,128)(2,1)} %wo.4) | copy-start | bytes 98308
  2.1 9.2 %copy-start.12 = (s32[1152]{0:T(1024)S(1)}, s32[1152]{0:T(1024)}, u32[]{:S(2)}) copy-start(s32[1152]{0:T(1024)} %token_.3) | copy-start | bytes 13828
  2.2 9.2 %copy-start.13 = (f32[768]{0:T(1024)S(1)}, f32[768]{0:T(1024)}, u32[]{:S(2)}) copy-start(f32[768]{0:T(1024)} %gain.3) | copy-start | bytes 9220
  3.2 11.1 %collective-permute-start.1 = (bf16[324,128]{1,0:T(8,128)(2,1)S(1)}, bf16[324,128]{1,0:T(8,128)(2,1)S(1)}, u32[]{:S(2)}, u32[]{:S(2)}) collective-permute-start(bf16[324,128]{1,0:T(8,128)(2,1)S(1)} %get-tuple-element.33), channel_id=1, source_target_pairs={{0,4},{1,5},{2,6},{3,7},{4,0},{5,1},{6,2},{7,3},{8,12},{9,13},{10,... | collective-permute-start | bytes 248840 | tf_op jit(solution)/shard_map/ppermute | solution.py:145
  7.3 4.0 %collective-permute-start = (bf16[2,48,128]{2,1,0:T(8,128)(2,1)S(1)}, bf16[2,48,128]{2,1,0:T(8,128)(2,1)S(1)}, u32[]{:S(2)}, u32[]{:S(2)}) collective-permute-start(bf16[2,48,128]{2,1,0:T(8,128)(2,1)S(1)} %get-tuple-element.29), channel_id=1, source_target_pairs={{0,8},{8,0},{16,24},{24,16},{1,9},{9,1},{17,25},{25,17},{2,10},{10... | collective-permute-start | bytes 73736 | tf_op jit(solution)/shard_map/ppermute | solution.py:145
  7.3 4.0 %collective-permute-start.2 = (bf16[2,48,128]{2,1,0:T(8,128)(2,1)S(1)}, bf16[2,48,128]{2,1,0:T(8,128)(2,1)S(1)}, u32[]{:S(2)}, u32[]{:S(2)}) collective-permute-start(bf16[2,48,128]{2,1,0:T(8,128)(2,1)S(1)} %get-tuple-element.31), channel_id=1, source_target_pairs={{8,16},{24,0},{16,8},{0,24},{9,17},{25,1},{17,9},{1,25},{10,18},{2... | collective-permute-start | bytes 73736 | tf_op jit(solution)/shard_map/ppermute | solution.py:569
  8.9 15.0 %copy-start.5 = (bf16[768,768]{1,0:T(8,128)(2,1)S(1)}, bf16[768,768]{1,0:T(8,128)(2,1)}, u32[]{:S(2)}) copy-start(bf16[768,768]{1,0:T(8,128)(2,1)} %wg.3) | copy-start | bytes 3538948
  11.4 12.6 %copy-start.4 = (bf16[768,768]{1,0:T(8,128)(2,1)S(1)}, bf16[768,768]{1,0:T(8,128)(2,1)}, u32[]{:S(2)}) copy-start(bf16[768,768]{1,0:T(8,128)(2,1)} %wq.3) | copy-start | bytes 3538948
  13.5 7.8 %collective-permute-start.4 = (bf16[1,72,768]{2,1,0:T(8,128)(2,1)S(1)}, bf16[1,72,768]{2,1,0:T(8,128)(2,1)S(1)}, u32[]{:S(2)}, u32[]{:S(2)}) collective-permute-start(bf16[1,72,768]{2,1,0:T(8,128)(2,1)S(1)} %bitcast.15), channel_id=1, source_target_pairs={{0,16},{8,24},{16,0},{24,8},{1,17},{9,25},{17,1},{25,9},{2,18},{10... | collective-permute-start | bytes 331784 | tf_op jit(solution)/shard_map/ppermute | solution.py:145
  14.3 9.6 %copy-start.3 = (bf16[768,768]{1,0:T(8,128)(2,1)S(1)}, bf16[768,768]{1,0:T(8,128)(2,1)}, u32[]{:S(2)}) copy-start(bf16[768,768]{1,0:T(8,128)(2,1)} %refs_12_.1) | copy-start | bytes 3538948
  14.4 7.0 %collective-permute-start.6 = (bf16[2,180,128]{2,1,0:T(8,128)(2,1)S(1)}, bf16[2,180,128]{2,1,0:T(8,128)(2,1)S(1)}, u32[]{:S(2)}, u32[]{:S(2)}) collective-permute-start(bf16[2,180,128]{2,1,0:T(8,128)(2,1)S(1)} %pad_maximum_fusion.4), channel_id=1, source_target_pairs={{0,1},{1,0},{2,3},{3,2},{4,5},{5,4},{6,7},{7,6},{8,9},{9,8},{10,11... | collective-permute-start | bytes 276488 | tf_op jit(solution)/shard_map/ppermute | solution.py:145
  15.9 5.5 %collective-permute-start.5 = (bf16[2,144,128]{2,1,0:T(8,128)(2,1)S(1)}, bf16[2,144,128]{2,1,0:T(8,128)(2,1)S(1)}, u32[]{:S(2)}, u32[]{:S(2)}) collective-permute-start(bf16[2,144,128]{2,1,0:T(8,128)(2,1)S(1)} %pad_maximum_fusion.5), channel_id=1, source_target_pairs={{0,2},{1,3},{2,0},{3,1},{4,6},{5,7},{6,4},{7,5},{8,10},{9,11},{10,... | collective-permute-start | bytes 221192 | tf_op jit(solution)/shard_map/ppermute | solution.py:145
  17.6 6.4 %copy-start.2 = (bf16[768,768]{1,0:T(8,128)(2,1)S(1)}, bf16[768,768]{1,0:T(8,128)(2,1)}, u32[]{:S(2)}) copy-start(bf16[768,768]{1,0:T(8,128)(2,1)} %refs_11_.1) | copy-start | bytes 3538948
  19.8 4.1 %copy-start.1 = (bf16[768,768]{1,0:T(8,128)(2,1)S(1)}, bf16[768,768]{1,0:T(8,128)(2,1)}, u32[]{:S(2)}) copy-start(bf16[768,768]{1,0:T(8,128)(2,1)} %refs_10_.1) | copy-start | bytes 3538948
  21.3 2.6 %collective-permute-start.7 = (bf16[2,72,768]{2,1,0:T(8,128)(2,1)S(1)}, bf16[2,72,768]{2,1,0:T(8,128)(2,1)S(1)}, u32[]{:S(2)}, u32[]{:S(2)}) collective-permute-start(bf16[2,72,768]{2,1,0:T(8,128)(2,1)S(1)} %pad_maximum_fusion.near), channel_id=1, source_target_pairs={{0,8},{8,0},{16,24},{24,16},{1,9},{9,1},{17,25},{25,17},{2,10},{10... | collective-permute-start | bytes 663560 | tf_op jit(solution)/shard_map/ppermute | solution.py:145
  21.4 7.2 %collective-permute-start.9 = (bf16[4,180,128]{2,1,0:T(8,128)(2,1)S(1)}, bf16[4,180,128]{2,1,0:T(8,128)(2,1)S(1)}, u32[]{:S(2)}, u32[]{:S(2)}) collective-permute-start(bf16[4,180,128]{2,1,0:T(8,128)(2,1)S(1)} %pad_maximum_fusion.2.refs_2_), channel_id=1, source_target_pairs={{0,2},{1,3},{2,0},{3,1},{4,6},{5,7},{6,4},{7,5},{8,10},{9,11},{10,... | collective-permute-start | bytes 552968 | tf_op jit(solution)/shard_map/ppermute | solution.py:145
  22.0 6.0 %collective-permute-start.8 = (bf16[4,144,128]{2,1,0:T(8,128)(2,1)S(1)}, bf16[4,144,128]{2,1,0:T(8,128)(2,1)S(1)}, u32[]{:S(2)}, u32[]{:S(2)}) collective-permute-start(bf16[4,144,128]{2,1,0:T(8,128)(2,1)S(1)} %pad_maximum_fusion.3.refs_0_), channel_id=1, source_target_pairs={{0,1},{1,0},{2,3},{3,2},{4,5},{5,4},{6,7},{7,6},{8,9},{9,8},{10,11... | collective-permute-start | bytes 442376 | tf_op jit(solution)/shard_map/ppermute | solution.py:145
  22.6 4.8 %collective-permute-start.3 = (bf16[1,72,768]{2,1,0:T(8,128)(2,1)S(1)}, bf16[1,72,768]{2,1,0:T(8,128)(2,1)S(1)}, u32[]{:S(2)}, u32[]{:S(2)}) collective-permute-start(bf16[1,72,768]{2,1,0:T(8,128)(2,1)S(1)} %bitcast.13), channel_id=1, source_target_pairs={{0,16},{8,24},{16,0},{24,8},{1,17},{9,25},{17,1},{25,9},{2,18},{10... | collective-permute-start | bytes 331784 | tf_op jit(solution)/shard_map/ppermute | solution.py:145
  28.6 1.5 %collective-permute-start.10 = (bf16[2,72,768]{2,1,0:T(8,128)(2,1)S(1)}, bf16[2,72,768]{2,1,0:T(8,128)(2,1)S(1)}, u32[]{:S(2)}, u32[]{:S(2)}) collective-permute-start(bf16[2,72,768]{2,1,0:T(8,128)(2,1)S(1)} %pad_maximum_fusion.1.near), channel_id=1, source_target_pairs={{0,8},{8,0},{16,24},{24,16},{1,9},{9,1},{17,25},{25,17},{2,10},{10... | collective-permute-start | bytes 663560 | tf_op jit(solution)/shard_map/ppermute | solution.py:145

commit v17 on v14

--- a/solution.py
+++ b/solution.py
@@ -62,8 +62,20 @@
 
 
 def normalise_kernel(pair, normed):
-    for k in range(0, pair.shape[0], 6):
-        normed[k : k + 6] = layer_norm(pair[k : k + 6].astype(F32))
+    cols, rows, chans = pair.shape
+    evenly = jnp.full((chans, chans), 1.0 / chans, BF16)
+    step = 6
+
+    def centre(k):
+        x = pair[k : k + step].astype(F32).reshape(step * rows, chans)
+        return k, x - dot(x.astype(BF16), evenly)
+
+    def scale(item):
+        k, x = item
+        x = x * lax.rsqrt(jnp.mean(x * x, -1, keepdims=True) + 1e-05)
+        normed[k : k + step] = x.reshape(step, rows, chans)
+
+    skewed(range(0, cols, step), [centre, scale])
 
 
 def normalise_pairs(pair_cond):

time: 33.7 us -> 33.4 us (level)
  no operation moved by 1% of the time
where the time goes in v17:
time: 33.4 us; the launch traced here: 33.3 us
  Pallas kernels  16 us (48%)
  starting transfers between devices  12.3 us (37%)
  waiting for transfers between devices  3.19 us (10%)
  local copies, waits for them, and re-layouts  1.32 us (4%)
    ppermute x10, starting transfers between devices, swap(): lax.ppermute(held, axis, [(i, i ^ far) for i in range(lax.axis_size(axis))])  10.7 us
    pallas_call x2, Pallas kernels, atom_attention(): pl.pallas_call(functools.partial(atom_kernel, sample), out_shape=jax.Shap...  4.62 us
    pallas_call x2, Pallas kernels, gather_tokens(): pl.pallas_call(functools.partial(gather_kernel, sample), out_shape=[jax.S...  3.51 us
    pallas_call x1, Pallas kernels, attend(): pl.pallas_call(functools.partial(attend_kernel, len(parts)), out_shape=ja...  3.36 us
    ppermute x10, waiting for transfers between devices, swap(): lax.ppermute(held, axis, [(i, i ^ far) for i in range(lax.axis_size(axis))])  3.19 us
    pallas_call x1, Pallas kernels, project(): pl.pallas_call(project_kernel, out_shape=[jax.ShapeDtypeStruct((HEADS * r...  1.7 us
    ppermute x1, starting transfers between devices, shards(): lax.ppermute(outer, 'row', odd_pairs + [(j, i) for i, j in odd_pairs])  1.63 us
    unnamed x32, local copies, waits for them, and re-layouts  1.3 us
  transfers between devices with their start and end apart: 11, of which 4 were waited for; matrix products, arithmetic and copies ran while one was open for 0% of the time, Pallas kernels for 33%

profile of v17, /device:TPU:0, one launch (start us, length us, event | category | flops | bytes accessed | tf_op | source)
XLA Modules:
  0.0 33.3 jit_solution(11381175582780274225)
XLA Ops:
  0.0 1.2 %copy-done.7 = bf16[72,36,128]{2,0,1:T(8,128)(2,1)S(1)} copy-done((bf16[72,36,128]{2,0,1:T(8,128)(2,1)S(1)}, bf16[72,36,128]{2,0,1:T(8,128)(2,1)}, u32[]{:S(2)}) %copy-start.7) | copy-done | bytes 663576
  1.2 0.6 %normalise_pairs.1.normed = f32[36,72,128]{2,1,0:T(8,128)S(1)} custom-call(bf16[36,72,128]{2,1,0:T(8,128)(2,1)S(1)} %bitcast.12), custom_call_target="tpu_custom_call" | custom-call | flops 20000000 | bytes 1000 | tf_op jit(solution)/shard_map/normalise_pairs/pallas_call | solution.py:84
  1.7 0.0 copy-start.8
  1.8 0.0 copy-start.9
  1.8 0.0 copy-start.10
  1.8 0.1 copy-done.14
  1.9 0.0 copy-start.13
  1.9 1.0 %pair_bias.1 = (bf16[324,128]{1,0:T(8,128)(2,1)S(1)}, bf16[2,48,128]{2,1,0:T(8,128)(2,1)S(1)}, bf16[2,48,128]{2,1,0:T(8,128)(2,1)S(1)}) custom-call(bf16[2,1152,128]{2,1,0:T(8,128)(2,1)S(1)} %copy-done, f32[36,72,128]{2,1,0:T(8,128)S(1)} %normalise_pairs.1.normed, s32[36]{0:T(128)S(1)} %copy-done.15, bf16[16,128]{1,0:T(8,128)(2,1)S(1)} %bitcast.17), custom_call_target="tpu_custom_call" | custom-call | flops 60000000 | bytes 1000 | tf_op jit(solution)/shard_map/pair_bias/pallas_call | solution.py:136
  2.9 4.1 %collective-permute-start.1 = (bf16[324,128]{1,0:T(8,128)(2,1)S(1)}, bf16[324,128]{1,0:T(8,128)(2,1)S(1)}, u32[]{:S(2)}, u32[]{:S(2)}) collective-permute-start(bf16[324,128]{1,0:T(8,128)(2,1)S(1)} %get-tuple-element.33), channel_id=1, source_target_pairs={{0,4},{1,5},{2,6},{3,7},{4,0},{5,1},{6,2},{7,3},{8,12},{9,13},{10,... | collective-permute-start | bytes 248840 | tf_op jit(solution)/shard_map/ppermute | solution.py:157
  7.0 1.6 %collective-permute-start.2 = (bf16[2,48,128]{2,1,0:T(8,128)(2,1)S(1)}, bf16[2,48,128]{2,1,0:T(8,128)(2,1)S(1)}, u32[]{:S(2)}, u32[]{:S(2)}) collective-permute-start(bf16[2,48,128]{2,1,0:T(8,128)(2,1)S(1)} %get-tuple-element.31), channel_id=1, source_target_pairs={{8,16},{24,0},{16,8},{0,24},{9,17},{25,1},{17,9},{1,25},{10,18},{2... | collective-permute-start | bytes 73736 | tf_op jit(solution)/shard_map/ppermute | solution.py:575
  8.7 2.4 %atom_attention.2.mixed = bf16[1152,128]{1,0:T(8,128)(2,1)S(1)} custom-call(bf16[2,1152,128]{2,1,0:T(8,128)(2,1)S(1)} %copy-done, bf16[128,128]{1,0:T(8,128)(2,1)S(1)} %copy-done.8, bf16[128,128]{1,0:T(8,128)(2,1)S(1)} %copy-done.9, bf16[128,128]{1,0:T(8,128)(2,1)S(1)} %copy-done.10), custom_call_target="tpu_custom_call" | custom-call | flops 80000000 | bytes 1000 | tf_op jit(solution)/shard_map/atom_attention/pallas_call | solution.py:266
  11.1 0.0 copy-start.4
  11.1 2.1 %gather_tokens.2 = (f32[72,768]{1,0:T(8,128)S(1)}, bf16[72,768]{1,0:T(8,128)(2,1)S(1)}) custom-call(bf16[1152,128]{1,0:T(8,128)(2,1)S(1)} %atom_attention.2.mixed, bf16[2,1152,128]{2,1,0:T(8,128)(2,1)S(1)} %copy-done, s32[1152]{0:T(1024)S(1)} %copy-done.12, bf16[128,128]{1,0:T(8,128)(2,1)S(1)} %copy-done.11, bf16[128,768]{1,0:T(8,128)(2,1)S(1)} %copy-done.6, ...), custom_call_target="tpu_custom_call" | custom-call | flops 20000000 | bytes 1000 | tf_op jit(solution)/shard_map/gather_tokens/pallas_call | solution.py:336
  13.2 0.8 %collective-permute-start.4 = (bf16[1,72,768]{2,1,0:T(8,128)(2,1)S(1)}, bf16[1,72,768]{2,1,0:T(8,128)(2,1)S(1)}, u32[]{:S(2)}, u32[]{:S(2)}) collective-permute-start(bf16[1,72,768]{2,1,0:T(8,128)(2,1)S(1)} %bitcast.15), channel_id=1, source_target_pairs={{0,16},{8,24},{16,0},{24,8},{1,17},{9,25},{17,1},{25,9},{2,18},{10... | collective-permute-start | bytes 331784 | tf_op jit(solution)/shard_map/ppermute | solution.py:157
  14.0 0.0 copy-start.3
  14.1 1.6 %collective-permute-start.6 = (bf16[2,180,128]{2,1,0:T(8,128)(2,1)S(1)}, bf16[2,180,128]{2,1,0:T(8,128)(2,1)S(1)}, u32[]{:S(2)}, u32[]{:S(2)}) collective-permute-start(bf16[2,180,128]{2,1,0:T(8,128)(2,1)S(1)} %pad_maximum_fusion.4), channel_id=1, source_target_pairs={{0,1},{1,0},{2,3},{3,2},{4,5},{5,4},{6,7},{7,6},{8,9},{9,8},{10,11... | collective-permute-start | bytes 276488 | tf_op jit(solution)/shard_map/ppermute | solution.py:157
  15.6 1.6 %collective-permute-start.5 = (bf16[2,144,128]{2,1,0:T(8,128)(2,1)S(1)}, bf16[2,144,128]{2,1,0:T(8,128)(2,1)S(1)}, u32[]{:S(2)}, u32[]{:S(2)}) collective-permute-start(bf16[2,144,128]{2,1,0:T(8,128)(2,1)S(1)} %pad_maximum_fusion.5), channel_id=1, source_target_pairs={{0,2},{1,3},{2,0},{3,1},{4,6},{5,7},{6,4},{7,5},{8,10},{9,11},{10,... | collective-permute-start | bytes 221192 | tf_op jit(solution)/shard_map/ppermute | solution.py:157
  17.3 2.3 %atom_attention.3.mixed = bf16[1152,128]{1,0:T(8,128)(2,1)S(1)} custom-call(bf16[2,1152,128]{2,1,0:T(8,128)(2,1)S(1)} %copy-done, bf16[2,48,128]{2,1,0:T(8,128)(2,1)S(1)} %collective-permute-done.refs_0_, bf16[2,48,128]{2,1,0:T(8,128)(2,1)S(1)} %collective-permute-done.2.refs_1_, bf16[128,128]{1,0:T(8,128)(2,1)S(1)} %copy-done.8, ...), custom_call_target="tpu_custom_call" | custom-call | flops 80000000 | bytes 1000 | tf_op jit(solution)/shard_map/atom_attention/pallas_call | solution.py:266
  19.6 0.0 copy-start.1
  19.6 1.4 %gather_tokens.3 = (f32[72,768]{1,0:T(8,128)S(1)}, bf16[72,768]{1,0:T(8,128)(2,1)S(1)}) custom-call(bf16[1152,128]{1,0:T(8,128)(2,1)S(1)} %atom_attention.3.mixed, bf16[2,1152,128]{2,1,0:T(8,128)(2,1)S(1)} %copy-done, s32[1152]{0:T(1024)S(1)} %copy-done.12, bf16[128,128]{1,0:T(8,128)(2,1)S(1)} %copy-done.11, bf16[128,768]{1,0:T(8,128)(2,1)S(1)} %copy-done.6, ...), custom_call_target="tpu_custom_call" | custom-call | flops 20000000 | bytes 1000 | tf_op jit(solution)/shard_map/gather_tokens/pallas_call | solution.py:336
  21.0 0.1 collective-permute-start.7
  21.2 0.6 %collective-permute-start.9 = (bf16[4,180,128]{2,1,0:T(8,128)(2,1)S(1)}, bf16[4,180,128]{2,1,0:T(8,128)(2,1)S(1)}, u32[]{:S(2)}, u32[]{:S(2)}) collective-permute-start(bf16[4,180,128]{2,1,0:T(8,128)(2,1)S(1)} %pad_maximum_fusion.2.refs_2_), channel_id=1, source_target_pairs={{0,2},{1,3},{2,0},{3,1},{4,6},{5,7},{6,4},{7,5},{8,10},{9,11},{10,... | collective-permute-start | bytes 552968 | tf_op jit(solution)/shard_map/ppermute | solution.py:157
  21.8 0.6 %collective-permute-start.8 = (bf16[4,144,128]{2,1,0:T(8,128)(2,1)S(1)}, bf16[4,144,128]{2,1,0:T(8,128)(2,1)S(1)}, u32[]{:S(2)}, u32[]{:S(2)}) collective-permute-start(bf16[4,144,128]{2,1,0:T(8,128)(2,1)S(1)} %pad_maximum_fusion.3.refs_0_), channel_id=1, source_target_pairs={{0,1},{1,0},{2,3},{3,2},{4,5},{5,4},{6,7},{7,6},{8,9},{9,8},{10,11... | collective-permute-start | bytes 442376 | tf_op jit(solution)/shard_map/ppermute | solution.py:157
  22.3 1.3 %collective-permute-start.3 = (bf16[1,72,768]{2,1,0:T(8,128)(2,1)S(1)}, bf16[1,72,768]{2,1,0:T(8,128)(2,1)S(1)}, u32[]{:S(2)}, u32[]{:S(2)}) collective-permute-start(bf16[1,72,768]{2,1,0:T(8,128)(2,1)S(1)} %bitcast.13), channel_id=1, source_target_pairs={{0,16},{8,24},{16,0},{24,8},{1,17},{9,25},{17,1},{25,9},{2,18},{10... | collective-permute-start | bytes 331784 | tf_op jit(solution)/shard_map/ppermute | solution.py:157
  23.7 1.7 %project.1 = (f32[1152,288]{1,0:T(8,128)S(1)}, bf16[288,768]{1,0:T(8,128)(2,1)S(1)}, f32[72,768]{1,0:T(8,128)S(1)}) custom-call(bf16[2,72,768]{2,1,0:T(8,128)(2,1)S(1)} %pad_maximum_fusion.near, bf16[2,72,768]{2,1,0:T(8,128)(2,1)S(1)} %collective-permute-done.7.far, bf16[768,768]{1,0:T(8,128)(2,1)S(1)} %copy-done.4, bf16[768,768]{1,0:T(8,128)(2,1)S(1)} %copy-done.1, ...), custom_call_target="tpu_custom_call" | custom-call | flops 40000000 | bytes 1000 | tf_op jit(solution)/shard_map/project/pallas_call | solution.py:399
  25.4 1.8 %collective-permute-done.3 = bf16[1,72,768]{2,1,0:T(8,128)(2,1)S(1)} collective-permute-done((bf16[1,72,768]{2,1,0:T(8,128)(2,1)S(1)}, bf16[1,72,768]{2,1,0:T(8,128)(2,1)S(1)}, u32[]{:S(2)}, u32[]{:S(2)}) %collective-permute-start.3) | collective-permute-done | bytes 110624 | tf_op jit(solution)/shard_map/ppermute | solution.py:157
  27.2 0.6 %collective-permute-done.8.refs_1_ = bf16[4,144,128]{2,1,0:T(8,128)(2,1)S(1)} collective-permute-done((bf16[4,144,128]{2,1,0:T(8,128)(2,1)S(1)}, bf16[4,144,128]{2,1,0:T(8,128)(2,1)S(1)}, u32[]{:S(2)}, u32[]{:S(2)}) %collective-permute-start.8) | collective-permute-done | bytes 147488 | tf_op jit(solution)/shard_map/ppermute | solution.py:157
  27.7 0.6 %collective-permute-done.9.refs_3_ = bf16[4,180,128]{2,1,0:T(8,128)(2,1)S(1)} collective-permute-done((bf16[4,180,128]{2,1,0:T(8,128)(2,1)S(1)}, bf16[4,180,128]{2,1,0:T(8,128)(2,1)S(1)}, u32[]{:S(2)}, u32[]{:S(2)}) %collective-permute-start.9) | collective-permute-done | bytes 184352 | tf_op jit(solution)/shard_map/ppermute | solution.py:157
  28.4 0.1 collective-permute-start.10
  28.4 1.2 %turn_bias.1 = (bf16[72,768]{1,0:T(8,128)(2,1)S(1)}, bf16[144,768]{1,0:T(8,128)(2,1)S(1)}, bf16[144,768]{1,0:T(8,128)(2,1)S(1)}, f32[72,768]{1,0:T(8,128)S(1)}, f32[1152,288]{1,0:T(8,128)S(1)}) custom-call(bf16[2,72,768]{2,1,0:T(8,128)(2,1)S(1)} %pad_maximum_fusion.1.near, bf16[768,768]{1,0:T(8,128)(2,1)S(1)} %copy-done.4, bf16[768,768]{1,0:T(8,128)(2,1)S(1)} %copy-done.1, ...), custom_call_target="tpu_custom_call" | custom-call | flops 20000000 | bytes 1000 | tf_op jit(solution)/shard_map/turn_bias/pallas_call | solution.py:460
  29.7 0.2 collective-permute-done.10.refs_9_
  29.9 3.4 %attend.1 = bf16[2,72,768]{2,1,0:T(8,128)(2,1)} custom-call(f32[1152,288]{1,0:T(8,128)S(1)} %get-tuple-element.47.bias, f32[1152,288]{1,0:T(8,128)S(1)} %get-tuple-element.41.refs_0_, bf16[288,768]{1,0:T(8,128)(2,1)S(1)} %get-tuple-element.42.refs_1_, f32[72,768]{1,0:T(8,128)S(1)} %get-tuple-element.43.refs_2_, f32[72,768]{1,0:T(8,128)S(1)} %get-tuple-element.44.refs_3_, ...), custom_call_target="tpu_custom_call" | custom-call | flops 60000000 | bytes 1000 | tf_op jit(solution)/shard_map/attend/pallas_call | solution.py:539
  (39 shorter events, 0.2 us)
Async XLA Ops:
  0.0 1.8 %copy-start = (bf16[2,1152,128]{2,1,0:T(8,128)(2,1)S(1)}, bf16[2,1152,128]{2,1,0:T(8,128)(2,1)}, u32[]{:S(2)}) copy-start(bf16[2,1152,128]{2,1,0:T(8,128)(2,1)} %feat.9) | copy-start | bytes 1769476
  0.0 1.2 %copy-start.7 = (bf16[72,36,128]{2,0,1:T(8,128)(2,1)S(1)}, bf16[72,36,128]{2,0,1:T(8,128)(2,1)}, u32[]{:S(2)}) copy-start(bf16[72,36,128]{2,0,1:T(8,128)(2,1)} %param.18) | copy-start | bytes 1990660
  1.2 0.7 %copy-start.14 = (bf16[128,16]{0,1:T(8,128)(2,1)S(1)}, bf16[128,16]{0,1:T(8,128)(2,1)}, u32[]{:S(2)}) copy-start(bf16[128,16]{0,1:T(8,128)(2,1)} %param.25) | copy-start | bytes 12292
  1.2 0.7 %copy-start.15 = (s32[36]{0:T(128)S(1)}, s32[36]{0:T(128)}, u32[]{:S(2)}) copy-start(s32[36]{0:T(128)} %mask.1) | copy-start | bytes 436
  1.7 6.9 %copy-start.8 = (bf16[128,128]{1,0:T(8,128)(2,1)S(1)}, bf16[128,128]{1,0:T(8,128)(2,1)}, u32[]{:S(2)}) copy-start(bf16[128,128]{1,0:T(8,128)(2,1)} %refs_2_.5) | copy-start | bytes 98308
  1.8 6.9 %copy-start.9 = (bf16[128,128]{1,0:T(8,128)(2,1)S(1)}, bf16[128,128]{1,0:T(8,128)(2,1)}, u32[]{:S(2)}) copy-start(bf16[128,128]{1,0:T(8,128)(2,1)} %refs_3_.3) | copy-start | bytes 98308
  1.8 6.9 %copy-start.10 = (bf16[128,128]{1,0:T(8,128)(2,1)S(1)}, bf16[128,128]{1,0:T(8,128)(2,1)}, u32[]{:S(2)}) copy-start(bf16[128,128]{1,0:T(8,128)(2,1)} %refs_4_.3) | copy-start | bytes 98308
  1.9 9.2 %copy-start.6 = (bf16[128,768]{1,0:T(8,128)(2,1)S(1)}, bf16[128,768]{1,0:T(8,128)(2,1)}, u32[]{:S(2)}) copy-start(bf16[128,768]{1,0:T(8,128)(2,1)} %agg.3) | copy-start | bytes 589828
  1.9 9.2 %copy-start.11 = (bf16[128,128]{1,0:T(8,128)(2,1)S(1)}, bf16[128,128]{1,0:T(8,128)(2,1)}, u32[]{:S(2)}) copy-start(bf16[128,128]{1,0:T(8,128)(2,1)} %wo.4) | copy-start | bytes 98308
  1.9 9.2 %copy-start.12 = (s32[1152]{0:T(1024)S(1)}, s32[1152]{0:T(1024)}, u32[]{:S(2)}) copy-start(s32[1152]{0:T(1024)} %token_.3) | copy-start | bytes 13828
  1.9 9.2 %copy-start.13 = (f32[768]{0:T(1024)S(1)}, f32[768]{0:T(1024)}, u32[]{:S(2)}) copy-start(f32[768]{0:T(1024)} %gain.3) | copy-start | bytes 9220
  2.9 11.1 %collective-permute-start.1 = (bf16[324,128]{1,0:T(8,128)(2,1)S(1)}, bf16[324,128]{1,0:T(8,128)(2,1)S(1)}, u32[]{:S(2)}, u32[]{:S(2)}) collective-permute-start(bf16[324,128]{1,0:T(8,128)(2,1)S(1)} %get-tuple-element.33), channel_id=1, source_target_pairs={{0,4},{1,5},{2,6},{3,7},{4,0},{5,1},{6,2},{7,3},{8,12},{9,13},{10,... | collective-permute-start | bytes 248840 | tf_op jit(solution)/shard_map/ppermute | solution.py:157
  7.0 4.0 %collective-permute-start = (bf16[2,48,128]{2,1,0:T(8,128)(2,1)S(1)}, bf16[2,48,128]{2,1,0:T(8,128)(2,1)S(1)}, u32[]{:S(2)}, u32[]{:S(2)}) collective-permute-start(bf16[2,48,128]{2,1,0:T(8,128)(2,1)S(1)} %get-tuple-element.29), channel_id=1, source_target_pairs={{0,8},{8,0},{16,24},{24,16},{1,9},{9,1},{17,25},{25,17},{2,10},{10... | collective-permute-start | bytes 73736 | tf_op jit(solution)/shard_map/ppermute | solution.py:157
  7.0 4.0 %collective-permute-start.2 = (bf16[2,48,128]{2,1,0:T(8,128)(2,1)S(1)}, bf16[2,48,128]{2,1,0:T(8,128)(2,1)S(1)}, u32[]{:S(2)}, u32[]{:S(2)}) collective-permute-start(bf16[2,48,128]{2,1,0:T(8,128)(2,1)S(1)} %get-tuple-element.31), channel_id=1, source_target_pairs={{8,16},{24,0},{16,8},{0,24},{9,17},{25,1},{17,9},{1,25},{10,18},{2... | collective-permute-start | bytes 73736 | tf_op jit(solution)/shard_map/ppermute | solution.py:575
  8.7 15.0 %copy-start.5 = (bf16[768,768]{1,0:T(8,128)(2,1)S(1)}, bf16[768,768]{1,0:T(8,128)(2,1)}, u32[]{:S(2)}) copy-start(bf16[768,768]{1,0:T(8,128)(2,1)} %wg.3) | copy-start | bytes 3538948
  11.1 12.6 %copy-start.4 = (bf16[768,768]{1,0:T(8,128)(2,1)S(1)}, bf16[768,768]{1,0:T(8,128)(2,1)}, u32[]{:S(2)}) copy-start(bf16[768,768]{1,0:T(8,128)(2,1)} %wq.3) | copy-start | bytes 3538948
  13.2 7.8 %collective-permute-start.4 = (bf16[1,72,768]{2,1,0:T(8,128)(2,1)S(1)}, bf16[1,72,768]{2,1,0:T(8,128)(2,1)S(1)}, u32[]{:S(2)}, u32[]{:S(2)}) collective-permute-start(bf16[1,72,768]{2,1,0:T(8,128)(2,1)S(1)} %bitcast.15), channel_id=1, source_target_pairs={{0,16},{8,24},{16,0},{24,8},{1,17},{9,25},{17,1},{25,9},{2,18},{10... | collective-permute-start | bytes 331784 | tf_op jit(solution)/shard_map/ppermute | solution.py:157
  14.0 9.6 %copy-start.3 = (bf16[768,768]{1,0:T(8,128)(2,1)S(1)}, bf16[768,768]{1,0:T(8,128)(2,1)}, u32[]{:S(2)}) copy-start(bf16[768,768]{1,0:T(8,128)(2,1)} %refs_12_.1) | copy-start | bytes 3538948
  14.1 7.1 %collective-permute-start.6 = (bf16[2,180,128]{2,1,0:T(8,128)(2,1)S(1)}, bf16[2,180,128]{2,1,0:T(8,128)(2,1)S(1)}, u32[]{:S(2)}, u32[]{:S(2)}) collective-permute-start(bf16[2,180,128]{2,1,0:T(8,128)(2,1)S(1)} %pad_maximum_fusion.4), channel_id=1, source_target_pairs={{0,1},{1,0},{2,3},{3,2},{4,5},{5,4},{6,7},{7,6},{8,9},{9,8},{10,11... | collective-permute-start | bytes 276488 | tf_op jit(solution)/shard_map/ppermute | solution.py:157
  15.6 5.5 %collective-permute-start.5 = (bf16[2,144,128]{2,1,0:T(8,128)(2,1)S(1)}, bf16[2,144,128]{2,1,0:T(8,128)(2,1)S(1)}, u32[]{:S(2)}, u32[]{:S(2)}) collective-permute-start(bf16[2,144,128]{2,1,0:T(8,128)(2,1)S(1)} %pad_maximum_fusion.5), channel_id=1, source_target_pairs={{0,2},{1,3},{2,0},{3,1},{4,6},{5,7},{6,4},{7,5},{8,10},{9,11},{10,... | collective-permute-start | bytes 221192 | tf_op jit(solution)/shard_map/ppermute | solution.py:157
  17.3 6.4 %copy-start.2 = (bf16[768,768]{1,0:T(8,128)(2,1)S(1)}, bf16[768,768]{1,0:T(8,128)(2,1)}, u32[]{:S(2)}) copy-start(bf16[768,768]{1,0:T(8,128)(2,1)} %refs_11_.1) | copy-start | bytes 3538948
  19.6 4.1 %copy-start.1 = (bf16[768,768]{1,0:T(8,128)(2,1)S(1)}, bf16[768,768]{1,0:T(8,128)(2,1)}, u32[]{:S(2)}) copy-start(bf16[768,768]{1,0:T(8,128)(2,1)} %refs_10_.1) | copy-start | bytes 3538948
  21.0 2.6 %collective-permute-start.7 = (bf16[2,72,768]{2,1,0:T(8,128)(2,1)S(1)}, bf16[2,72,768]{2,1,0:T(8,128)(2,1)S(1)}, u32[]{:S(2)}, u32[]{:S(2)}) collective-permute-start(bf16[2,72,768]{2,1,0:T(8,128)(2,1)S(1)} %pad_maximum_fusion.near), channel_id=1, source_target_pairs={{0,8},{8,0},{16,24},{24,16},{1,9},{9,1},{17,25},{25,17},{2,10},{10... | collective-permute-start | bytes 663560 | tf_op jit(solution)/shard_map/ppermute | solution.py:157
  21.2 7.2 %collective-permute-start.9 = (bf16[4,180,128]{2,1,0:T(8,128)(2,1)S(1)}, bf16[4,180,128]{2,1,0:T(8,128)(2,1)S(1)}, u32[]{:S(2)}, u32[]{:S(2)}) collective-permute-start(bf16[4,180,128]{2,1,0:T(8,128)(2,1)S(1)} %pad_maximum_fusion.2.refs_2_), channel_id=1, source_target_pairs={{0,2},{1,3},{2,0},{3,1},{4,6},{5,7},{6,4},{7,5},{8,10},{9,11},{10,... | collective-permute-start | bytes 552968 | tf_op jit(solution)/shard_map/ppermute | solution.py:157
  21.8 6.0 %collective-permute-start.8 = (bf16[4,144,128]{2,1,0:T(8,128)(2,1)S(1)}, bf16[4,144,128]{2,1,0:T(8,128)(2,1)S(1)}, u32[]{:S(2)}, u32[]{:S(2)}) collective-permute-start(bf16[4,144,128]{2,1,0:T(8,128)(2,1)S(1)} %pad_maximum_fusion.3.refs_0_), channel_id=1, source_target_pairs={{0,1},{1,0},{2,3},{3,2},{4,5},{5,4},{6,7},{7,6},{8,9},{9,8},{10,11... | collective-permute-start | bytes 442376 | tf_op jit(solution)/shard_map/ppermute | solution.py:157
  22.3 4.8 %collective-permute-start.3 = (bf16[1,72,768]{2,1,0:T(8,128)(2,1)S(1)}, bf16[1,72,768]{2,1,0:T(8,128)(2,1)S(1)}, u32[]{:S(2)}, u32[]{:S(2)}) collective-permute-start(bf16[1,72,768]{2,1,0:T(8,128)(2,1)S(1)} %bitcast.13), channel_id=1, source_target_pairs={{0,16},{8,24},{16,0},{24,8},{1,17},{9,25},{17,1},{25,9},{2,18},{10... | collective-permute-start | bytes 331784 | tf_op jit(solution)/shard_map/ppermute | solution.py:157
  28.4 1.5 %collective-permute-start.10 = (bf16[2,72,768]{2,1,0:T(8,128)(2,1)S(1)}, bf16[2,72,768]{2,1,0:T(8,128)(2,1)S(1)}, u32[]{:S(2)}, u32[]{:S(2)}) collective-permute-start(bf16[2,72,768]{2,1,0:T(8,128)(2,1)S(1)} %pad_maximum_fusion.1.near), channel_id=1, source_target_pairs={{0,8},{8,0},{16,24},{24,16},{1,9},{9,1},{17,25},{25,17},{2,10},{10... | collective-permute-start | bytes 663560 | tf_op jit(solution)/shard_map/ppermute | solution.py:157

commit v18 on v17

--- a/solution.py
+++ b/solution.py
@@ -227,13 +227,15 @@
     *halo, wq, wk, wv, mixed, qs, ks, vs = refs
     atoms, chans = feat.shape[1:]
     wqkv = jnp.concatenate([wq[...], wk[...], wv[...]], axis=1)
+    evenly = jnp.full((chans, chans), 1.0 / chans, BF16)
 
     def normalise(at):
         if isinstance(at, int):
             part = feat[sample, at : at + LANES]
         else:
             at, part = at
-        return at, layer_norm(part.astype(F32)).astype(BF16)
+        x = part.astype(F32) - dot(part, evenly)
+        return at, (x * lax.rsqrt(jnp.mean(x * x, -1, keepdims=True) + 1e-05)).astype(BF16)
 
     def project_atoms(item):
         at, normed = item

time: 33.4 us -> 36.1 us (1.081)
  Pallas kernels: 16 us -> 18.9 us
    pallas_call x2, Pallas kernels: 4.62 us -> 7.55 us  [atom_attention(): pl.pallas_call(functools.partial(atom_kernel, sample), out_shape=jax.Shap...]
  transfers between devices with their start and end apart: 11 -> 11, of which waited for: 4 -> 4; matrix products, arithmetic and copies ran while one was open for 0% -> 0% of each run, Pallas kernels for 33% -> 39%
where the time goes in v18:
time: 36.1 us; the launch traced here: 36 us
  Pallas kernels  18.9 us (52%)
  starting transfers between devices  12.3 us (34%)
  waiting for transfers between devices  3.03 us (8%)
  local copies, waits for them, and re-layouts  1.32 us (4%)
    ppermute x10, starting transfers between devices, swap(): lax.ppermute(held, axis, [(i, i ^ far) for i in range(lax.axis_size(axis))])  10.6 us
    pallas_call x2, Pallas kernels, atom_attention(): pl.pallas_call(functools.partial(atom_kernel, sample), out_shape=jax.Shap...  7.55 us
    pallas_call x2, Pallas kernels, gather_tokens(): pl.pallas_call(functools.partial(gather_kernel, sample), out_shape=[jax.S...  3.51 us
    pallas_call x1, Pallas kernels, attend(): pl.pallas_call(functools.partial(attend_kernel, len(parts)), out_shape=ja...  3.36 us
    ppermute x10, waiting for transfers between devices, swap(): lax.ppermute(held, axis, [(i, i ^ far) for i in range(lax.axis_size(axis))])  3.03 us
    pallas_call x1, Pallas kernels, project(): pl.pallas_call(project_kernel, out_shape=[jax.ShapeDtypeStruct((HEADS * r...  1.7 us
    ppermute x1, starting transfers between devices, shards(): lax.ppermute(outer, 'row', odd_pairs + [(j, i) for i, j in odd_pairs])  1.63 us
    unnamed x32, local copies, waits for them, and re-layouts  1.3 us
  transfers between devices with their start and end apart: 11, of which 4 were waited for; matrix products, arithmetic and copies ran while one was open for 0% of the time, Pallas kernels for 39%

profile of v18, /device:TPU:0, one launch (start us, length us, event | category | flops | bytes accessed | tf_op | source)
XLA Modules:
  0.0 36.0 jit_solution(8533842013841874332)
XLA Ops:
  0.0 1.2 %copy-done.7 = bf16[72,36,128]{2,0,1:T(8,128)(2,1)S(1)} copy-done((bf16[72,36,128]{2,0,1:T(8,128)(2,1)S(1)}, bf16[72,36,128]{2,0,1:T(8,128)(2,1)}, u32[]{:S(2)}) %copy-start.7) | copy-done | bytes 663576
  1.2 0.6 %normalise_pairs.1.normed = f32[36,72,128]{2,1,0:T(8,128)S(1)} custom-call(bf16[36,72,128]{2,1,0:T(8,128)(2,1)S(1)} %bitcast.12), custom_call_target="tpu_custom_call" | custom-call | flops 20000000 | bytes 1000 | tf_op jit(solution)/shard_map/normalise_pairs/pallas_call | solution.py:84
  1.7 0.0 copy-start.8
  1.8 0.0 copy-start.9
  1.8 0.0 copy-start.10
  1.8 0.1 copy-done.14
  1.9 0.0 copy-start.13
  1.9 1.0 %pair_bias.1 = (bf16[324,128]{1,0:T(8,128)(2,1)S(1)}, bf16[2,48,128]{2,1,0:T(8,128)(2,1)S(1)}, bf16[2,48,128]{2,1,0:T(8,128)(2,1)S(1)}) custom-call(bf16[2,1152,128]{2,1,0:T(8,128)(2,1)S(1)} %copy-done, f32[36,72,128]{2,1,0:T(8,128)S(1)} %normalise_pairs.1.normed, s32[36]{0:T(128)S(1)} %copy-done.15, bf16[16,128]{1,0:T(8,128)(2,1)S(1)} %bitcast.17), custom_call_target="tpu_custom_call" | custom-call | flops 60000000 | bytes 1000 | tf_op jit(solution)/shard_map/pair_bias/pallas_call | solution.py:136
  2.9 4.1 %collective-permute-start.1 = (bf16[324,128]{1,0:T(8,128)(2,1)S(1)}, bf16[324,128]{1,0:T(8,128)(2,1)S(1)}, u32[]{:S(2)}, u32[]{:S(2)}) collective-permute-start(bf16[324,128]{1,0:T(8,128)(2,1)S(1)} %get-tuple-element.33), channel_id=1, source_target_pairs={{0,4},{1,5},{2,6},{3,7},{4,0},{5,1},{6,2},{7,3},{8,12},{9,13},{10,... | collective-permute-start | bytes 248840 | tf_op jit(solution)/shard_map/ppermute | solution.py:157
  7.0 1.6 %collective-permute-start.2 = (bf16[2,48,128]{2,1,0:T(8,128)(2,1)S(1)}, bf16[2,48,128]{2,1,0:T(8,128)(2,1)S(1)}, u32[]{:S(2)}, u32[]{:S(2)}) collective-permute-start(bf16[2,48,128]{2,1,0:T(8,128)(2,1)S(1)} %get-tuple-element.31), channel_id=1, source_target_pairs={{8,16},{24,0},{16,8},{0,24},{9,17},{25,1},{17,9},{1,25},{10,18},{2... | collective-permute-start | bytes 73736 | tf_op jit(solution)/shard_map/ppermute | solution.py:577
  8.7 3.6 %atom_attention.2.mixed = bf16[1152,128]{1,0:T(8,128)(2,1)S(1)} custom-call(bf16[2,1152,128]{2,1,0:T(8,128)(2,1)S(1)} %copy-done, bf16[128,128]{1,0:T(8,128)(2,1)S(1)} %copy-done.8, bf16[128,128]{1,0:T(8,128)(2,1)S(1)} %copy-done.9, bf16[128,128]{1,0:T(8,128)(2,1)S(1)} %copy-done.10), custom_call_target="tpu_custom_call" | custom-call | flops 80000000 | bytes 1000 | tf_op jit(solution)/shard_map/atom_attention/pallas_call | solution.py:268
  12.3 0.0 copy-start.4
  12.3 2.1 %gather_tokens.2 = (f32[72,768]{1,0:T(8,128)S(1)}, bf16[72,768]{1,0:T(8,128)(2,1)S(1)}) custom-call(bf16[1152,128]{1,0:T(8,128)(2,1)S(1)} %atom_attention.2.mixed, bf16[2,1152,128]{2,1,0:T(8,128)(2,1)S(1)} %copy-done, s32[1152]{0:T(1024)S(1)} %copy-done.12, bf16[128,128]{1,0:T(8,128)(2,1)S(1)} %copy-done.11, bf16[128,768]{1,0:T(8,128)(2,1)S(1)} %copy-done.6, ...), custom_call_target="tpu_custom_call" | custom-call | flops 20000000 | bytes 1000 | tf_op jit(solution)/shard_map/gather_tokens/pallas_call | solution.py:338
  14.4 0.6 %collective-permute-start.4 = (bf16[1,72,768]{2,1,0:T(8,128)(2,1)S(1)}, bf16[1,72,768]{2,1,0:T(8,128)(2,1)S(1)}, u32[]{:S(2)}, u32[]{:S(2)}) collective-permute-start(bf16[1,72,768]{2,1,0:T(8,128)(2,1)S(1)} %bitcast.15), channel_id=1, source_target_pairs={{0,16},{8,24},{16,0},{24,8},{1,17},{9,25},{17,1},{25,9},{2,18},{10... | collective-permute-start | bytes 331784 | tf_op jit(solution)/shard_map/ppermute | solution.py:157
  15.0 0.0 copy-start.3
  15.1 1.5 %collective-permute-start.6 = (bf16[2,180,128]{2,1,0:T(8,128)(2,1)S(1)}, bf16[2,180,128]{2,1,0:T(8,128)(2,1)S(1)}, u32[]{:S(2)}, u32[]{:S(2)}) collective-permute-start(bf16[2,180,128]{2,1,0:T(8,128)(2,1)S(1)} %pad_maximum_fusion.4), channel_id=1, source_target_pairs={{0,1},{1,0},{2,3},{3,2},{4,5},{5,4},{6,7},{7,6},{8,9},{9,8},{10,11... | collective-permute-start | bytes 276488 | tf_op jit(solution)/shard_map/ppermute | solution.py:157
  16.6 1.7 %collective-permute-start.5 = (bf16[2,144,128]{2,1,0:T(8,128)(2,1)S(1)}, bf16[2,144,128]{2,1,0:T(8,128)(2,1)S(1)}, u32[]{:S(2)}, u32[]{:S(2)}) collective-permute-start(bf16[2,144,128]{2,1,0:T(8,128)(2,1)S(1)} %pad_maximum_fusion.5), channel_id=1, source_target_pairs={{0,2},{1,3},{2,0},{3,1},{4,6},{5,7},{6,4},{7,5},{8,10},{9,11},{10,... | collective-permute-start | bytes 221192 | tf_op jit(solution)/shard_map/ppermute | solution.py:157
  18.3 4.0 %atom_attention.3.mixed = bf16[1152,128]{1,0:T(8,128)(2,1)S(1)} custom-call(bf16[2,1152,128]{2,1,0:T(8,128)(2,1)S(1)} %copy-done, bf16[2,48,128]{2,1,0:T(8,128)(2,1)S(1)} %collective-permute-done.refs_0_, bf16[2,48,128]{2,1,0:T(8,128)(2,1)S(1)} %collective-permute-done.2.refs_1_, bf16[128,128]{1,0:T(8,128)(2,1)S(1)} %copy-done.8, ...), custom_call_target="tpu_custom_call" | custom-call | flops 80000000 | bytes 1000 | tf_op jit(solution)/shard_map/atom_attention/pallas_call | solution.py:268
  22.3 0.0 copy-start.1
  22.3 1.4 %gather_tokens.3 = (f32[72,768]{1,0:T(8,128)S(1)}, bf16[72,768]{1,0:T(8,128)(2,1)S(1)}) custom-call(bf16[1152,128]{1,0:T(8,128)(2,1)S(1)} %atom_attention.3.mixed, bf16[2,1152,128]{2,1,0:T(8,128)(2,1)S(1)} %copy-done, s32[1152]{0:T(1024)S(1)} %copy-done.12, bf16[128,128]{1,0:T(8,128)(2,1)S(1)} %copy-done.11, bf16[128,768]{1,0:T(8,128)(2,1)S(1)} %copy-done.6, ...), custom_call_target="tpu_custom_call" | custom-call | flops 20000000 | bytes 1000 | tf_op jit(solution)/shard_map/gather_tokens/pallas_call | solution.py:338
  23.7 0.1 collective-permute-start.7
  23.9 0.5 %collective-permute-start.9 = (bf16[4,180,128]{2,1,0:T(8,128)(2,1)S(1)}, bf16[4,180,128]{2,1,0:T(8,128)(2,1)S(1)}, u32[]{:S(2)}, u32[]{:S(2)}) collective-permute-start(bf16[4,180,128]{2,1,0:T(8,128)(2,1)S(1)} %pad_maximum_fusion.2.refs_2_), channel_id=1, source_target_pairs={{0,2},{1,3},{2,0},{3,1},{4,6},{5,7},{6,4},{7,5},{8,10},{9,11},{10,... | collective-permute-start | bytes 552968 | tf_op jit(solution)/shard_map/ppermute | solution.py:157
  24.4 0.6 %collective-permute-start.8 = (bf16[4,144,128]{2,1,0:T(8,128)(2,1)S(1)}, bf16[4,144,128]{2,1,0:T(8,128)(2,1)S(1)}, u32[]{:S(2)}, u32[]{:S(2)}) collective-permute-start(bf16[4,144,128]{2,1,0:T(8,128)(2,1)S(1)} %pad_maximum_fusion.3.refs_0_), channel_id=1, source_target_pairs={{0,1},{1,0},{2,3},{3,2},{4,5},{5,4},{6,7},{7,6},{8,9},{9,8},{10,11... | collective-permute-start | bytes 442376 | tf_op jit(solution)/shard_map/ppermute | solution.py:157
  25.0 1.5 %collective-permute-start.3 = (bf16[1,72,768]{2,1,0:T(8,128)(2,1)S(1)}, bf16[1,72,768]{2,1,0:T(8,128)(2,1)S(1)}, u32[]{:S(2)}, u32[]{:S(2)}) collective-permute-start(bf16[1,72,768]{2,1,0:T(8,128)(2,1)S(1)} %bitcast.13), channel_id=1, source_target_pairs={{0,16},{8,24},{16,0},{24,8},{1,17},{9,25},{17,1},{25,9},{2,18},{10... | collective-permute-start | bytes 331784 | tf_op jit(solution)/shard_map/ppermute | solution.py:157
  26.6 1.7 %project.1 = (f32[1152,288]{1,0:T(8,128)S(1)}, bf16[288,768]{1,0:T(8,128)(2,1)S(1)}, f32[72,768]{1,0:T(8,128)S(1)}) custom-call(bf16[2,72,768]{2,1,0:T(8,128)(2,1)S(1)} %pad_maximum_fusion.near, bf16[2,72,768]{2,1,0:T(8,128)(2,1)S(1)} %collective-permute-done.7.far, bf16[768,768]{1,0:T(8,128)(2,1)S(1)} %copy-done.4, bf16[768,768]{1,0:T(8,128)(2,1)S(1)} %copy-done.1, ...), custom_call_target="tpu_custom_call" | custom-call | flops 40000000 | bytes 1000 | tf_op jit(solution)/shard_map/project/pallas_call | solution.py:401
  28.3 1.6 %collective-permute-done.3 = bf16[1,72,768]{2,1,0:T(8,128)(2,1)S(1)} collective-permute-done((bf16[1,72,768]{2,1,0:T(8,128)(2,1)S(1)}, bf16[1,72,768]{2,1,0:T(8,128)(2,1)S(1)}, u32[]{:S(2)}, u32[]{:S(2)}) %collective-permute-start.3) | collective-permute-done | bytes 110624 | tf_op jit(solution)/shard_map/ppermute | solution.py:157
  29.9 0.5 %collective-permute-done.8.refs_1_ = bf16[4,144,128]{2,1,0:T(8,128)(2,1)S(1)} collective-permute-done((bf16[4,144,128]{2,1,0:T(8,128)(2,1)S(1)}, bf16[4,144,128]{2,1,0:T(8,128)(2,1)S(1)}, u32[]{:S(2)}, u32[]{:S(2)}) %collective-permute-start.8) | collective-permute-done | bytes 147488 | tf_op jit(solution)/shard_map/ppermute | solution.py:157
  30.4 0.6 %collective-permute-done.9.refs_3_ = bf16[4,180,128]{2,1,0:T(8,128)(2,1)S(1)} collective-permute-done((bf16[4,180,128]{2,1,0:T(8,128)(2,1)S(1)}, bf16[4,180,128]{2,1,0:T(8,128)(2,1)S(1)}, u32[]{:S(2)}, u32[]{:S(2)}) %collective-permute-start.9) | collective-permute-done | bytes 184352 | tf_op jit(solution)/shard_map/ppermute | solution.py:157
  31.1 0.1 collective-permute-start.10
  31.1 1.2 %turn_bias.1 = (bf16[72,768]{1,0:T(8,128)(2,1)S(1)}, bf16[144,768]{1,0:T(8,128)(2,1)S(1)}, bf16[144,768]{1,0:T(8,128)(2,1)S(1)}, f32[72,768]{1,0:T(8,128)S(1)}, f32[1152,288]{1,0:T(8,128)S(1)}) custom-call(bf16[2,72,768]{2,1,0:T(8,128)(2,1)S(1)} %pad_maximum_fusion.1.near, bf16[768,768]{1,0:T(8,128)(2,1)S(1)} %copy-done.4, bf16[768,768]{1,0:T(8,128)(2,1)S(1)} %copy-done.1, ...), custom_call_target="tpu_custom_call" | custom-call | flops 20000000 | bytes 1000 | tf_op jit(solution)/shard_map/turn_bias/pallas_call | solution.py:462
  32.4 0.2 collective-permute-done.10.refs_9_
  32.6 3.4 %attend.1 = bf16[2,72,768]{2,1,0:T(8,128)(2,1)} custom-call(f32[1152,288]{1,0:T(8,128)S(1)} %get-tuple-element.47.bias, f32[1152,288]{1,0:T(8,128)S(1)} %get-tuple-element.41.refs_0_, bf16[288,768]{1,0:T(8,128)(2,1)S(1)} %get-tuple-element.42.refs_1_, f32[72,768]{1,0:T(8,128)S(1)} %get-tuple-element.43.refs_2_, f32[72,768]{1,0:T(8,128)S(1)} %get-tuple-element.44.refs_3_, ...), custom_call_target="tpu_custom_call" | custom-call | flops 60000000 | bytes 1000 | tf_op jit(solution)/shard_map/attend/pallas_call | solution.py:541
  (39 shorter events, 0.2 us)
Async XLA Ops:
  0.0 1.8 %copy-start = (bf16[2,1152,128]{2,1,0:T(8,128)(2,1)S(1)}, bf16[2,1152,128]{2,1,0:T(8,128)(2,1)}, u32[]{:S(2)}) copy-start(bf16[2,1152,128]{2,1,0:T(8,128)(2,1)} %feat.9) | copy-start | bytes 1769476
  0.0 1.2 %copy-start.7 = (bf16[72,36,128]{2,0,1:T(8,128)(2,1)S(1)}, bf16[72,36,128]{2,0,1:T(8,128)(2,1)}, u32[]{:S(2)}) copy-start(bf16[72,36,128]{2,0,1:T(8,128)(2,1)} %param.18) | copy-start | bytes 1990660
  1.2 0.7 %copy-start.14 = (bf16[128,16]{0,1:T(8,128)(2,1)S(1)}, bf16[128,16]{0,1:T(8,128)(2,1)}, u32[]{:S(2)}) copy-start(bf16[128,16]{0,1:T(8,128)(2,1)} %param.25) | copy-start | bytes 12292
  1.2 0.7 %copy-start.15 = (s32[36]{0:T(128)S(1)}, s32[36]{0:T(128)}, u32[]{:S(2)}) copy-start(s32[36]{0:T(128)} %mask.1) | copy-start | bytes 436
  1.7 6.9 %copy-start.8 = (bf16[128,128]{1,0:T(8,128)(2,1)S(1)}, bf16[128,128]{1,0:T(8,128)(2,1)}, u32[]{:S(2)}) copy-start(bf16[128,128]{1,0:T(8,128)(2,1)} %refs_2_.5) | copy-start | bytes 98308
  1.8 6.9 %copy-start.9 = (bf16[128,128]{1,0:T(8,128)(2,1)S(1)}, bf16[128,128]{1,0:T(8,128)(2,1)}, u32[]{:S(2)}) copy-start(bf16[128,128]{1,0:T(8,128)(2,1)} %refs_3_.3) | copy-start | bytes 98308
  1.8 6.9 %copy-start.10 = (bf16[128,128]{1,0:T(8,128)(2,1)S(1)}, bf16[128,128]{1,0:T(8,128)(2,1)}, u32[]{:S(2)}) copy-start(bf16[128,128]{1,0:T(8,128)(2,1)} %refs_4_.3) | copy-start | bytes 98308
  1.9 10.4 %copy-start.6 = (bf16[128,768]{1,0:T(8,128)(2,1)S(1)}, bf16[128,768]{1,0:T(8,128)(2,1)}, u32[]{:S(2)}) copy-start(bf16[128,768]{1,0:T(8,128)(2,1)} %agg.3) | copy-start | bytes 589828
  1.9 10.4 %copy-start.11 = (bf16[128,128]{1,0:T(8,128)(2,1)S(1)}, bf16[128,128]{1,0:T(8,128)(2,1)}, u32[]{:S(2)}) copy-start(bf16[128,128]{1,0:T(8,128)(2,1)} %wo.4) | copy-start | bytes 98308
  1.9 10.4 %copy-start.12 = (s32[1152]{0:T(1024)S(1)}, s32[1152]{0:T(1024)}, u32[]{:S(2)}) copy-start(s32[1152]{0:T(1024)} %token_.3) | copy-start | bytes 13828
  1.9 10.4 %copy-start.13 = (f32[768]{0:T(1024)S(1)}, f32[768]{0:T(1024)}, u32[]{:S(2)}) copy-start(f32[768]{0:T(1024)} %gain.3) | copy-start | bytes 9220
  2.9 12.1 %collective-permute-start.1 = (bf16[324,128]{1,0:T(8,128)(2,1)S(1)}, bf16[324,128]{1,0:T(8,128)(2,1)S(1)}, u32[]{:S(2)}, u32[]{:S(2)}) collective-permute-start(bf16[324,128]{1,0:T(8,128)(2,1)S(1)} %get-tuple-element.33), channel_id=1, source_target_pairs={{0,4},{1,5},{2,6},{3,7},{4,0},{5,1},{6,2},{7,3},{8,12},{9,13},{10,... | collective-permute-start | bytes 248840 | tf_op jit(solution)/shard_map/ppermute | solution.py:157
  7.0 5.2 %collective-permute-start = (bf16[2,48,128]{2,1,0:T(8,128)(2,1)S(1)}, bf16[2,48,128]{2,1,0:T(8,128)(2,1)S(1)}, u32[]{:S(2)}, u32[]{:S(2)}) collective-permute-start(bf16[2,48,128]{2,1,0:T(8,128)(2,1)S(1)} %get-tuple-element.29), channel_id=1, source_target_pairs={{0,8},{8,0},{16,24},{24,16},{1,9},{9,1},{17,25},{25,17},{2,10},{10... | collective-permute-start | bytes 73736 | tf_op jit(solution)/shard_map/ppermute | solution.py:157
  7.0 5.2 %collective-permute-start.2 = (bf16[2,48,128]{2,1,0:T(8,128)(2,1)S(1)}, bf16[2,48,128]{2,1,0:T(8,128)(2,1)S(1)}, u32[]{:S(2)}, u32[]{:S(2)}) collective-permute-start(bf16[2,48,128]{2,1,0:T(8,128)(2,1)S(1)} %get-tuple-element.31), channel_id=1, source_target_pairs={{8,16},{24,0},{16,8},{0,24},{9,17},{25,1},{17,9},{1,25},{10,18},{2... | collective-permute-start | bytes 73736 | tf_op jit(solution)/shard_map/ppermute | solution.py:577
  8.7 17.9 %copy-start.5 = (bf16[768,768]{1,0:T(8,128)(2,1)S(1)}, bf16[768,768]{1,0:T(8,128)(2,1)}, u32[]{:S(2)}) copy-start(bf16[768,768]{1,0:T(8,128)(2,1)} %wg.3) | copy-start | bytes 3538948
  12.3 14.2 %copy-start.4 = (bf16[768,768]{1,0:T(8,128)(2,1)S(1)}, bf16[768,768]{1,0:T(8,128)(2,1)}, u32[]{:S(2)}) copy-start(bf16[768,768]{1,0:T(8,128)(2,1)} %wq.3) | copy-start | bytes 3538948
  14.4 9.3 %collective-permute-start.4 = (bf16[1,72,768]{2,1,0:T(8,128)(2,1)S(1)}, bf16[1,72,768]{2,1,0:T(8,128)(2,1)S(1)}, u32[]{:S(2)}, u32[]{:S(2)}) collective-permute-start(bf16[1,72,768]{2,1,0:T(8,128)(2,1)S(1)} %bitcast.15), channel_id=1, source_target_pairs={{0,16},{8,24},{16,0},{24,8},{1,17},{9,25},{17,1},{25,9},{2,18},{10... | collective-permute-start | bytes 331784 | tf_op jit(solution)/shard_map/ppermute | solution.py:157
  15.0 11.5 %copy-start.3 = (bf16[768,768]{1,0:T(8,128)(2,1)S(1)}, bf16[768,768]{1,0:T(8,128)(2,1)}, u32[]{:S(2)}) copy-start(bf16[768,768]{1,0:T(8,128)(2,1)} %refs_12_.1) | copy-start | bytes 3538948
  15.1 8.8 %collective-permute-start.6 = (bf16[2,180,128]{2,1,0:T(8,128)(2,1)S(1)}, bf16[2,180,128]{2,1,0:T(8,128)(2,1)S(1)}, u32[]{:S(2)}, u32[]{:S(2)}) collective-permute-start(bf16[2,180,128]{2,1,0:T(8,128)(2,1)S(1)} %pad_maximum_fusion.4), channel_id=1, source_target_pairs={{0,1},{1,0},{2,3},{3,2},{4,5},{5,4},{6,7},{7,6},{8,9},{9,8},{10,11... | collective-permute-start | bytes 276488 | tf_op jit(solution)/shard_map/ppermute | solution.py:157
  16.6 7.2 %collective-permute-start.5 = (bf16[2,144,128]{2,1,0:T(8,128)(2,1)S(1)}, bf16[2,144,128]{2,1,0:T(8,128)(2,1)S(1)}, u32[]{:S(2)}, u32[]{:S(2)}) collective-permute-start(bf16[2,144,128]{2,1,0:T(8,128)(2,1)S(1)} %pad_maximum_fusion.5), channel_id=1, source_target_pairs={{0,2},{1,3},{2,0},{3,1},{4,6},{5,7},{6,4},{7,5},{8,10},{9,11},{10,... | collective-permute-start | bytes 221192 | tf_op jit(solution)/shard_map/ppermute | solution.py:157
  18.3 8.3 %copy-start.2 = (bf16[768,768]{1,0:T(8,128)(2,1)S(1)}, bf16[768,768]{1,0:T(8,128)(2,1)}, u32[]{:S(2)}) copy-start(bf16[768,768]{1,0:T(8,128)(2,1)} %refs_11_.1) | copy-start | bytes 3538948
  22.3 4.3 %copy-start.1 = (bf16[768,768]{1,0:T(8,128)(2,1)S(1)}, bf16[768,768]{1,0:T(8,128)(2,1)}, u32[]{:S(2)}) copy-start(bf16[768,768]{1,0:T(8,128)(2,1)} %refs_10_.1) | copy-start | bytes 3538948
  23.7 2.8 %collective-permute-start.7 = (bf16[2,72,768]{2,1,0:T(8,128)(2,1)S(1)}, bf16[2,72,768]{2,1,0:T(8,128)(2,1)S(1)}, u32[]{:S(2)}, u32[]{:S(2)}) collective-permute-start(bf16[2,72,768]{2,1,0:T(8,128)(2,1)S(1)} %pad_maximum_fusion.near), channel_id=1, source_target_pairs={{0,8},{8,0},{16,24},{24,16},{1,9},{9,1},{17,25},{25,17},{2,10},{10... | collective-permute-start | bytes 663560 | tf_op jit(solution)/shard_map/ppermute | solution.py:157
  23.9 7.2 %collective-permute-start.9 = (bf16[4,180,128]{2,1,0:T(8,128)(2,1)S(1)}, bf16[4,180,128]{2,1,0:T(8,128)(2,1)S(1)}, u32[]{:S(2)}, u32[]{:S(2)}) collective-permute-start(bf16[4,180,128]{2,1,0:T(8,128)(2,1)S(1)} %pad_maximum_fusion.2.refs_2_), channel_id=1, source_target_pairs={{0,2},{1,3},{2,0},{3,1},{4,6},{5,7},{6,4},{7,5},{8,10},{9,11},{10,... | collective-permute-start | bytes 552968 | tf_op jit(solution)/shard_map/ppermute | solution.py:157
  24.4 6.0 %collective-permute-start.8 = (bf16[4,144,128]{2,1,0:T(8,128)(2,1)S(1)}, bf16[4,144,128]{2,1,0:T(8,128)(2,1)S(1)}, u32[]{:S(2)}, u32[]{:S(2)}) collective-permute-start(bf16[4,144,128]{2,1,0:T(8,128)(2,1)S(1)} %pad_maximum_fusion.3.refs_0_), channel_id=1, source_target_pairs={{0,1},{1,0},{2,3},{3,2},{4,5},{5,4},{6,7},{7,6},{8,9},{9,8},{10,11... | collective-permute-start | bytes 442376 | tf_op jit(solution)/shard_map/ppermute | solution.py:157
  25.0 4.9 %collective-permute-start.3 = (bf16[1,72,768]{2,1,0:T(8,128)(2,1)S(1)}, bf16[1,72,768]{2,1,0:T(8,128)(2,1)S(1)}, u32[]{:S(2)}, u32[]{:S(2)}) collective-permute-start(bf16[1,72,768]{2,1,0:T(8,128)(2,1)S(1)} %bitcast.13), channel_id=1, source_target_pairs={{0,16},{8,24},{16,0},{24,8},{1,17},{9,25},{17,1},{25,9},{2,18},{10... | collective-permute-start | bytes 331784 | tf_op jit(solution)/shard_map/ppermute | solution.py:157
  31.1 1.5 %collective-permute-start.10 = (bf16[2,72,768]{2,1,0:T(8,128)(2,1)S(1)}, bf16[2,72,768]{2,1,0:T(8,128)(2,1)S(1)}, u32[]{:S(2)}, u32[]{:S(2)}) collective-permute-start(bf16[2,72,768]{2,1,0:T(8,128)(2,1)S(1)} %pad_maximum_fusion.1.near), channel_id=1, source_target_pairs={{0,8},{8,0},{16,24},{24,16},{1,9},{9,1},{17,25},{25,17},{2,10},{10... | collective-permute-start | bytes 663560 | tf_op jit(solution)/shard_map/ppermute | solution.py:157
